TPU v7x, 32 devices: a whole 2x2x4 slice. The times are simulated.
32 devices in a mesh: srow: 4 (over z), scol: 4 (over x, core), trow: 2 (over y).
Axes of the slice: x: 2, y: 2, z: 4, core: 2. Of those that a mesh axis runs over, the one named last changes fastest.
Arguments:
- volume: bfloat16 [8, 8, 16, 128, 128], P(None, 'srow', 'scol', 'trow'), may hold values from -6 to 6
- src_weight: bfloat16 [2, 9, 8, 8], replicated, may hold values from -0.75 to 0.75
- tgt_weight: bfloat16 [2, 9, 8, 8], replicated, may hold values from -0.75 to 0.75
- bias: float32 [2, 8], replicated, may hold values from -3 to 3
Outputs:
- refined: bfloat16 [8, 8, 16, 128, 128], P(None, 'srow', 'scol', 'trow')
All inputs are finite; a program needn't handle non-finite values.
Results may differ from a plain program's by a relative error of at most 0.0036.
Values may be sent and summed in bfloat16 or wider, within the bound.
No kernel may reach another device: no remote copies, remote signals or barrier semaphores. Data moves between devices by JAX's collectives and lax.ppermute only.
A program may use at most 64 MiB of HBM per device.

v0:
```python
import functools

import jax
import jax.numpy as jnp
from jax import lax
from jax.experimental import pallas as pl
from jax.experimental.pallas import tpu as pltpu
from jax.sharding import PartitionSpec as P

BAND = 32
EDGE = 16
SCOPED = 16 * 1024 * 1024
F32 = jnp.float32
BF16 = jnp.bfloat16
VMEM, SMEM, HBM = pltpu.VMEM, pltpu.SMEM, pltpu.HBM
ROW_ODD, COL_ODD, DEEP_ODD, ROW_PAIRED, COL_PAIRED, DEEP_PAIRED = range(6)


def call(body, outs, args, places=None, out_place=VMEM, scratch=(), flops=0, moved=0, aliases=None):
    places = places or {}
    spaces = [places.get(n, VMEM) for n in range(len(args))]
    held = [pltpu.with_memory_space_constraint(a, m) if m in (VMEM, HBM) else a for a, m in zip(args, spaces)]
    return pl.pallas_call(
        body,
        out_shape=tuple(outs),
        in_specs=[pl.BlockSpec(memory_space=m) for m in spaces],
        out_specs=tuple(pl.BlockSpec(memory_space=out_place) for _ in outs),
        scratch_shapes=list(scratch),
        input_output_aliases=aliases or {},
        compiler_params=pltpu.CompilerParams(vmem_limit_bytes=SCOPED),
        cost_estimate=pl.CostEstimate(flops=flops // 1000, bytes_accessed=moved // 1000, transcendentals=0),
    )(*held)


def dot(a, b):
    return jnp.dot(a, b, preferred_element_type=F32)


def operators(parts, src_w_ref, tgt_w_ref, out_refs):
    channels = src_w_ref.shape[1]
    span, small = channels * BAND, channels * EDGE

    def columns(size):
        pick_c = lax.broadcasted_iota(jnp.int32, (channels, channels * size), 1) // size
        pick_r = lax.broadcasted_iota(jnp.int32, (channels, channels * size), 0)
        return (pick_c == pick_r).astype(BF16)

    wide, narrow, single = columns(BAND), columns(EDGE), columns(1)
    row = lax.broadcasted_iota(jnp.int32, (BAND, span), 0)
    shift = row - lax.broadcasted_iota(jnp.int32, (BAND, span), 1) % BAND
    row_s = lax.broadcasted_iota(jnp.int32, (BAND, small), 0)
    col_s = lax.broadcasted_iota(jnp.int32, (BAND, small), 1) % EDGE
    near = ((row_s == 0) & (col_s == EDGE - 1), (row_s == BAND - 1) & (col_s == 0))
    row_1 = lax.broadcasted_iota(jnp.int32, (BAND, channels), 0)
    deep = (row_1 == 0, row_1 == BAND - 1)
    spread = {}

    def taps(ref, layer, o, pick, key):
        key = (key, layer, o)
        if key not in spread:
            spread[key] = lax.dot_general(ref[layer, o], pick, (((0,), (0,)), ((), ())), preferred_element_type=F32)
        return spread[key]

    for (kind, layer), out_ref in zip(parts, out_refs):
        for o in range(channels):
            rows = slice(o * BAND, (o + 1) * BAND)
            for b in range(3):
                if kind == "middle":
                    got = taps(src_w_ref, layer, o, wide, "s")
                    values = {(): jnp.where(shift == 0, got[3 + b][None, :], 0.0)}
                elif kind == "beside":
                    got = taps(src_w_ref, layer, o, wide, "s")
                    values = {(n,): jnp.where(shift == 0, got[6 * n + b][None, :], 0.0) for n in range(2)}
                elif kind == "target":
                    got = taps(tgt_w_ref, layer, o, wide, "t")
                    value = jnp.where(shift == 1, got[b][None, :], 0.0)
                    value = jnp.where(shift == 0, got[3 + b][None, :], value)
                    values = {(): jnp.where(shift == -1, got[6 + b][None, :], value)}
                else:
                    pick, at = (narrow, near) if kind == "near" else (single, deep)
                    got = taps(tgt_w_ref, layer, o, pick, kind)
                    values = {(n,): jnp.where(at[n], got[6 * n + b][None, :], 0.0) for n in range(2)}
                for index, value in values.items():
                    size = value.shape[1]
                    out_ref[(*index, rows, slice(b * size, (b + 1) * size))] = value.astype(BF16)


def operator_shapes(parts, channels):
    span = channels * BAND
    widths = dict(middle=span, beside=span, target=span, near=channels * EDGE, deep=channels)
    lead = dict(middle=(), beside=(2,), target=(), near=(2,), deep=(2,))
    return [VMEM((*lead[kind], span, 3 * widths[kind]), BF16) for kind, _ in parts]


def build_body(parts, src_w_ref, tgt_w_ref, after_ref, *out_refs):
    operators(parts, src_w_ref, tgt_w_ref, out_refs)


def build(parts, src_w, tgt_w, after):
    got = call(
        functools.partial(build_body, parts),
        operator_shapes(parts, src_w.shape[1]),
        (src_w, tgt_w, after),
        {2: pl.ANY},
        flops=len(parts) * 10**7,
        moved=10**6,
    )
    return dict(zip(parts, got))


def band(tile):
    channels, size, width = tile.shape
    return tile.reshape(channels * size, width)


def unband(tile, channels):
    return tile.reshape(channels, tile.shape[0] // channels, tile.shape[1])


def src_operand(tiles, cols):
    return jnp.concatenate([jnp.concatenate(tiles[b : b + cols], axis=1) for b in range(3)], axis=0)


def sent_rows(flag_ref, rows):
    odd = flag_ref[ROW_ODD]
    return ((rows - 1) * (1 - odd), odd), ((rows - 1) * odd, 1 - odd)


def column(mid_ref, rim_ref, i, j, cut):
    last = mid_ref.shape[2] + 1
    return band(rim_ref[:, i, j // last, cut] if j in (0, last) else mid_ref[:, i, j - 1, cut])


def bands_of(depth):
    return [slice(start, start + BAND) for start in range(0, depth, BAND)]


def owed_sums(operator, tiles, out_ref):
    channels, cols, depth, width = out_ref.shape
    cuts = bands_of(depth)
    operand = jnp.concatenate([jnp.concatenate([t for cut in cuts for t in tiles(cut, b)], axis=1) for b in range(3)], axis=0)
    got = dot(operator, operand).astype(BF16)
    for q, cut in enumerate(cuts):
        for j in range(cols):
            at = (q * cols + j) * width
            out_ref[:, j, cut] = unband(got[:, at : at + width], channels)


def inner_sums(mid_ref, rim_ref, flag_ref, beside_ref, out_refs):
    rows, cols = mid_ref.shape[1:3]
    for (i, side), out_ref in zip(sent_rows(flag_ref, rows), out_refs):
        owed_sums(
            beside_ref[side], lambda cut, b: [column(mid_ref, rim_ref, i, j + b, cut) for j in range(cols)], out_ref
        )


def edge_body(mid_ref, rim_ref, cola_ref, colb_ref, beside_ref, flag_ref, a_ref, b_ref, side_ref, *deep_refs):
    rows, cols = mid_ref.shape[1], mid_ref.shape[2] + 2
    odd = flag_ref[COL_ODD]
    side_ref[1 - odd] = cola_ref[...]

    @pl.when(flag_ref[COL_PAIRED] != 0)
    def _():
        side_ref[odd] = colb_ref[...]

    @pl.when(flag_ref[COL_PAIRED] == 0)
    def _():
        side_ref[odd] = jnp.zeros_like(colb_ref)

    def around(i, j, cut):
        if j in (-1, cols):
            return band(side_ref[0 if j < 0 else 1, :, i, cut])
        return column(mid_ref, rim_ref, i, j, cut)

    for (i, side), out_ref in zip(sent_rows(flag_ref, rows), (a_ref, b_ref)):
        owed_sums(beside_ref[side], lambda cut, b: [around(i, j + b - 1, cut) for j in (0, cols - 1)], out_ref)
    sent_depths(mid_ref, rim_ref, flag_ref, deep_refs)


def shifted(tile, step):
    lane = lax.broadcasted_iota(jnp.int32, tile.shape, 1)
    width = tile.shape[1]
    rolled = pltpu.roll(tile.astype(F32), step % width, 1)
    gone = 0 if step == 1 else width - 1
    return jnp.where(lane == gone, 0.0, rolled)


def three(tiles):
    return [jnp.concatenate([shifted(t, step) if step else t.astype(F32) for t in tiles], axis=1) for step in (1, 0, -1)]


def main_body(
    layer, mid_ref, rim_ref, side_ref, middle_ref, beside_ref, target_ref, near_ref, deep_ref, bias_ref, flag_ref, *rest
):
    *deep_halos, accmid_ref, accrim_ref, lane_ref = rest
    channels, rows, mids, depth, width = mid_ref.shape
    cols = mids + 2
    span = channels * BAND
    cuts = bands_of(depth)
    bands = len(cuts)
    out_channel = lax.broadcasted_iota(jnp.int32, (span, 1), 0) // BAND
    bias = jnp.zeros((span, 1), F32)
    for o in range(channels):
        bias = jnp.where(out_channel == o, bias_ref[layer, o], bias)

    def place(j):
        return (accrim_ref, j // (cols - 1)) if j in (0, cols - 1) else (accmid_ref, j - 1)

    for i in range(rows):
        for q, cut in enumerate(cuts):
            tiles = [column(mid_ref, rim_ref, i, j, cut) for j in range(cols)]
            lane_ref[q, 1] = jnp.concatenate(tiles, axis=1)
            for n, step in ((0, 1), (2, -1)):
                lane_ref[q, n] = jnp.concatenate([shifted(t, step).astype(BF16) for t in tiles], axis=1)
        for q, cut in enumerate(cuts):
            total = jnp.broadcast_to(bias, (span, cols * width))
            for a in range(3):
                r = i + a - 1
                if 0 <= r < rows:
                    tiles = [band(side_ref[0, :, r, cut])] + [column(mid_ref, rim_ref, r, j, cut) for j in range(cols)]
                    tiles += [band(side_ref[1, :, r, cut])]
                    operator = middle_ref[...] if a == 1 else beside_ref[a // 2]
                    total = total + dot(operator, src_operand(tiles, cols))
            total = total + dot(target_ref[...], lane_ref[q].reshape(3 * span, cols * width))
            for side, other, start in ((0, q - 1, BAND - EDGE), (1, q + 1, 0)):
                if 0 <= other < bands:
                    parts = [unband(lane_ref[other, n], channels)[:, start : start + EDGE] for n in range(3)]
                    total = total + dot(near_ref[side], jnp.concatenate([band(p) for p in parts], axis=0))
            for j in range(cols):
                acc_ref, at = place(j)
                acc_ref[:, i, at, cut] = unband(total[:, j * width : (j + 1) * width], channels)
        odd = flag_ref[DEEP_ODD]
        for n, halo_ref in enumerate(deep_halos):
            side = (1 - odd) if n == 0 else odd
            cut = pl.ds(pl.multiple_of(side * (depth - BAND), BAND), BAND)
            halo = three([halo_ref[i, :, j * width : (j + 1) * width] for j in range(cols)])
            halo = jnp.concatenate(halo, axis=0)
            if n == 1:
                halo = halo * flag_ref[DEEP_PAIRED].astype(F32)
            got = dot(deep_ref[side], halo.astype(BF16))
            for j in range(cols):
                acc_ref, at = place(j)
                acc_ref[:, i, at, cut] += unband(got[:, j * width : (j + 1) * width], channels)


def finished(x_ref, acc_ref, flag_ref, owed_refs, store):
    rows, cols = x_ref.shape[1:3]
    odd = flag_ref[ROW_ODD]
    paired = flag_ref[ROW_PAIRED].astype(F32)
    for n, i in enumerate([(rows - 1) * (1 - odd), (rows - 1) * odd, *range(1, rows - 1)]):
        for j in range(cols):
            total = acc_ref[:, i, j]
            if n < 2:
                owed = owed_refs[n][:, j].astype(F32)
                total = total + (owed if n == 0 else owed * paired)
            store(i, j, (x_ref[:, i, j].astype(F32) + jnp.maximum(total, 0.0)).astype(BF16))


def sent_columns(rim_ref, flag_ref, col_refs):
    odd = flag_ref[COL_ODD]
    for n, ref in zip((1 - odd, odd), col_refs):
        ref[...] = rim_ref[:, :, n]


def sent_depths(mid_ref, rim_ref, flag_ref, deep_refs):
    channels, rows, mids, depth, _ = mid_ref.shape
    odd = flag_ref[DEEP_ODD]
    shape = (channels, channels * BAND)
    first = lax.broadcasted_iota(jnp.int32, shape, 0) * BAND
    for n, ref in enumerate(deep_refs):
        end = (1 - odd) if n == 0 else odd
        cut = pl.ds(pl.multiple_of(end * (depth - BAND), BAND), BAND)
        pick = (lax.broadcasted_iota(jnp.int32, shape, 1) == first + end * (BAND - 1)).astype(BF16)
        for i in range(rows):
            tiles = [column(mid_ref, rim_ref, i, j, cut) for j in range(mids + 2)]
            ref[i] = dot(pick, jnp.concatenate(tiles, axis=1)).astype(BF16)


def mid_body(x_ref, acc_ref, a_ref, b_ref, flag_ref, out_ref):
    def store(i, j, value):
        out_ref[:, i, j] = value

    finished(x_ref, acc_ref, flag_ref, (a_ref, b_ref), store)


def next_body(mid_ref, rim_ref, acc_ref, outa_ref, outb_ref, beside_ref, flag_ref, out_ref, cola_ref, colb_ref, a_ref, b_ref):
    mid_body(rim_ref, acc_ref, outa_ref, outb_ref, flag_ref, out_ref)
    sent_columns(out_ref, flag_ref, (cola_ref, colb_ref))
    inner_sums(mid_ref, out_ref, flag_ref, beside_ref, (a_ref, b_ref))


def write_mid_body(x_ref, acc_ref, a_ref, b_ref, flag_ref, out_ref, hold_ref, sems):
    rows, mids = x_ref.shape[1:3]
    copies = []

    def store(i, j, value):
        hold_ref[:, i, j] = value
        if j == mids - 1:
            copies.append(pltpu.make_async_copy(hold_ref.at[:, i], out_ref.at[:, i, 1 : mids + 1], sems.at[len(copies)]))
            copies[-1].start()

    finished(x_ref, acc_ref, flag_ref, (a_ref, b_ref), store)
    for copy in copies:
        copy.wait()


def write_rim_body(x_ref, acc_ref, a_ref, b_ref, flag_ref, begun_ref, out_ref, hold_ref, sems):
    last = out_ref.shape[2] - 1
    copies = []

    def store(i, j, value):
        hold_ref[:, i, j] = value
        copies.append(pltpu.make_async_copy(hold_ref.at[:, i, j], out_ref.at[:, i, j * last], sems.at[len(copies)]))
        copies[-1].start()

    finished(x_ref, acc_ref, flag_ref, (a_ref, b_ref), store)
    for copy in copies:
        copy.wait()


def open_body(parts, x_ref, src_w_ref, flag_ref, *rest):
    beside_ref, mid_ref, rim_ref, cola_ref, colb_ref, a_ref, b_ref, src_ref, sems = rest
    last = x_ref.shape[2] - 1
    pairs = (
        (src_w_ref, src_ref),
        (x_ref.at[:, :, 0], rim_ref.at[:, :, 0]),
        (x_ref.at[:, :, last], rim_ref.at[:, :, 1]),
        (x_ref.at[:, :, 1:last], mid_ref),
    )
    copies = [pltpu.make_async_copy(a, b, sems.at[n]) for n, (a, b) in enumerate(pairs)]
    for copy in copies:
        copy.start()
    copies[0].wait()
    operators(parts, src_ref, None, (beside_ref,))
    for copy in copies[1:]:
        copy.wait()
    sent_columns(rim_ref, flag_ref, (cola_ref, colb_ref))
    inner_sums(mid_ref, rim_ref, flag_ref, beside_ref, (a_ref, b_ref))


def swaps(a, b, axis, other):
    count, across = lax.axis_size(axis), lax.axis_size(other)
    pairs = []
    for n in range(count):
        for m in range(across):
            if 0 < n < count - 1:
                target = (n + 1 if n % 2 else n - 1, m)
            else:
                target = (n, m ^ 1)
            pairs.append((n * across + m, target[0] * across + target[1]))
    got_a = lax.ppermute(a, axis, [(n, n ^ 1) for n in range(count)])
    return got_a, lax.ppermute(b, (axis, other), pairs)


def shards(volume, src_weight, tgt_weight, bias):
    layers = src_weight.shape[0]
    channels, rows, cols, depth, width = volume.shape
    axes = ("srow", "scol", "trow")
    at, counts = [lax.axis_index(n) for n in axes], [lax.axis_size(n) for n in axes]
    assert all(count % 2 == 0 for count in counts) and rows > 1 and cols > 2
    paired = [(n > 0) & (n < count - 1) for n, count in zip(at, counts)]
    flags = jnp.stack([n % 2 for n in at] + paired).astype(jnp.int32)
    src_w = jnp.transpose(src_weight, (0, 2, 3, 1))
    tgt_w = jnp.transpose(tgt_weight, (0, 2, 3, 1))
    deep_swaps = 1 if counts[2] == 2 else 2
    mid_shape, rim_shape = ((channels, rows, n, depth, width) for n in (cols - 2, 2))
    line = VMEM((channels, rows, depth, width), BF16)
    owed_mid, owed_rim = (VMEM((channels, n, depth, width), BF16) for n in (cols - 2, 2))
    size = channels * rows * cols * depth * width
    inner_flops = 2 * size // rows * 3 * channels * BAND
    early = [("beside", 0)]
    made = {}
    made[early[0]], mid, rim, col_a, col_b, sum_a, sum_b = call(
        functools.partial(open_body, early),
        operator_shapes(early, channels) + [VMEM(mid_shape, BF16), VMEM(rim_shape, BF16), line, line, owed_mid, owed_mid],
        (volume, src_w, flags),
        {0: HBM, 1: HBM, 2: SMEM},
        scratch=[VMEM(src_w.shape, BF16), pltpu.SemaphoreType.DMA((4,))],
        flops=inner_flops,
        moved=size * 4,
    )
    for layer in range(layers):
        inner = swaps(sum_a, sum_b, "srow", "scol")
        beside = swaps(col_a, col_b, "scol", "trow")
        a, b, side, *deep = call(
            edge_body,
            [owed_rim, owed_rim, VMEM((2, *line.shape), BF16)] + [VMEM((rows, channels, cols * width), BF16)] * deep_swaps,
            (mid, rim, *beside, made["beside", layer], flags),
            {5: SMEM},
            flops=inner_flops,
            moved=size * 2,
        )
        outer = swaps(a, b, "srow", "scol")
        if deep_swaps == 1:
            deeper = [lax.ppermute(deep[0], "trow", [(0, 1), (1, 0)])]
        else:
            deeper = swaps(*deep, "trow", "scol")
        if layer == 0:
            rest = [(kind, n) for n in range(layers) for kind in ("middle", "beside", "target", "near", "deep")]
            made |= build([part for part in rest if part not in early], src_w, tgt_w, a)
        ops = [made[kind, layer] for kind in ("middle", "beside", "target", "near", "deep")]
        acc_mid, acc_rim = call(
            functools.partial(main_body, layer),
            [VMEM(mid_shape, F32), VMEM(rim_shape, F32)],
            (mid, rim, side, *ops, bias, flags, *deeper),
            {8: SMEM, 9: SMEM},
            scratch=[VMEM((depth // BAND, 3, channels * BAND, cols * width), BF16)],
            flops=2 * size * 12 * channels * BAND,
            moved=size * 8,
        )
        mid_args, rim_args = (mid, acc_mid, *inner, flags), (rim, acc_rim, *outer, flags)
        if layer < layers - 1:
            (mid,) = call(mid_body, [VMEM(mid_shape, BF16)], mid_args, {4: SMEM}, flops=size, moved=size * 5)
            rim, col_a, col_b, sum_a, sum_b = call(
                next_body,
                [VMEM(rim_shape, BF16), line, line, owed_mid, owed_mid],
                (mid, *rim_args[:-1], made["beside", layer + 1], flags),
                {6: SMEM},
                flops=inner_flops,
                moved=size * 10,
            )
        else:
            whole = jax.ShapeDtypeStruct(volume.shape, BF16)
            (state,) = call(
                write_mid_body,
                [whole],
                mid_args,
                {4: SMEM},
                out_place=HBM,
                scratch=[VMEM(mid_shape, BF16), pltpu.SemaphoreType.DMA((rows,))],
                flops=size,
                moved=size * 5,
            )
            (state,) = call(
                write_rim_body,
                [whole],
                (*rim_args, state),
                {4: SMEM, 5: HBM},
                out_place=HBM,
                scratch=[VMEM(rim_shape, BF16), pltpu.SemaphoreType.DMA((rows * 2,))],
                flops=size,
                moved=size * 5,
                aliases={5: 0},
            )
    return state


def solution(mesh):
    return jax.shard_map(
        shards,
        mesh=mesh,
        in_specs=(P(None, "srow", "scol", "trow", None), P(), P(), P()),
        out_specs=P(None, "srow", "scol", "trow", None),
        check_vma=False,
    )
```

profile of v0, /device:TPU:0, one launch (start us, length us, event | category | flops | bytes accessed | tf_op | source)
XLA Modules:
  0.0 44.1 jit_solution(255316912118944634)
XLA Ops:
  0.0 0.1 stack.39.flag_ref
  0.1 2.4 %shard_map.46 = (bf16[2,256,768]{2,1,0:T(8,128)(2,1)S(1)}, bf16[8,2,2,64,128]{4,3,2,1,0:T(8,128)(2,1)S(1)}, bf16[8,2,2,64,128]{4,3,2,1,0:T(8,128)(2,1)S(1)}, bf1...) custom-call(bf16[8,2,4,64,128]{4,3,2,1,0:T(8,128)(2,1)} %x_ref.1, ...), custom_call_target="tpu_custom_call" | custom-call | flops 402653 | bytes 2097 | tf_op jit(solution)/shard_map/pallas_call | solution.py:23
  2.5 0.5 %collective-permute-start = (bf16[8,2,64,128]{3,2,1,0:T(8,128)(2,1)S(1)}, bf16[8,2,64,128]{3,2,1,0:T(8,128)(2,1)S(1)}, u32[]{:S(2)}, u32[]{:S(2)}) collective-permute-start(bf16[8,2,64,128]{3,2,1,0:T(8,128)(2,1)S(1)} %get-tuple-element.40), channel_id=1, source_target_pairs={{0,2},{2,0},{4,6},{6,4},{1,3},{3,1},{5,7},{7,5},{8,10},{10,8},{12,... | collective-permute-start | bytes 786440 | tf_op jit(solution)/shard_map/ppermute | solution.py:351
  3.0 2.6 %collective-permute-start.1 = (bf16[8,2,64,128]{3,2,1,0:T(8,128)(2,1)S(1)}, bf16[8,2,64,128]{3,2,1,0:T(8,128)(2,1)S(1)}, u32[]{:S(2)}, u32[]{:S(2)}) collective-permute-start(bf16[8,2,64,128]{3,2,1,0:T(8,128)(2,1)S(1)} %get-tuple-element.41), channel_id=1, source_target_pairs={{0,1},{1,0},{2,4},{3,5},{4,2},{5,3},{6,7},{7,6},{8,9},{9,8},{10,12... | collective-permute-start | bytes 786440 | tf_op jit(solution)/shard_map/ppermute | solution.py:352
  5.6 1.6 %collective-permute-start.3 = (bf16[8,2,64,128]{3,2,1,0:T(8,128)(2,1)S(1)}, bf16[8,2,64,128]{3,2,1,0:T(8,128)(2,1)S(1)}, u32[]{:S(2)}, u32[]{:S(2)}) collective-permute-start(bf16[8,2,64,128]{3,2,1,0:T(8,128)(2,1)S(1)} %get-tuple-element.51), channel_id=1, source_target_pairs={{0,8},{8,0},{16,24},{24,16},{1,9},{9,1},{17,25},{25,17},{2,10},{10... | collective-permute-start | bytes 786440 | tf_op jit(solution)/shard_map/ppermute | solution.py:351
  7.2 0.0 collective-permute-start.4
  7.2 0.0 collective-permute-done.cola_ref
  7.2 2.8 %collective-permute-done.1.colb_ref = bf16[8,2,64,128]{3,2,1,0:T(8,128)(2,1)S(1)} collective-permute-done((bf16[8,2,64,128]{3,2,1,0:T(8,128)(2,1)S(1)}, bf16[8,2,64,128]{3,2,1,0:T(8,128)(2,1)S(1)}, u32[]{:S(2)}, u32[]{:S(2)}) %collective-permute-start.1) | collective-permute-done | bytes 262176 | tf_op jit(solution)/shard_map/ppermute | solution.py:352
  10.0 0.0 copy-start
  10.0 0.0 copy-start.1
  10.0 1.2 %shard_map.47 = (bf16[8,2,64,128]{3,2,1,0:T(8,128)(2,1)S(1)}, bf16[8,2,64,128]{3,2,1,0:T(8,128)(2,1)S(1)}, bf16[2,8,2,64,128]{4,3,2,1,0:T(8,128)(2,1)S(1)}, bf16[2,8,512]{2,1,0:T(8,128)(2,1)S(1)}) custom-call(bf16[8,2,2,64,128]{4,3,2,1,0:T(8,128)(2,1)S(1)} %get-tuple-element.38.mid_ref.x_ref, bf16[8,2,2,64,128]{4,3,2,1,0:T(8,128)(2,1)S(1)} %get-tuple-element.39.rim_ref, ...), custom_call_target="tpu_custom_call" | custom-call | flops 402653 | bytes 1048 | tf_op jit(solution)/shard_map/pallas_call | solution.py:23
  11.2 0.1 collective-permute-start.6
  11.3 3.6 %collective-permute-start.5 = (bf16[8,2,64,128]{3,2,1,0:T(8,128)(2,1)S(1)}, bf16[8,2,64,128]{3,2,1,0:T(8,128)(2,1)S(1)}, u32[]{:S(2)}, u32[]{:S(2)}) collective-permute-start(bf16[8,2,64,128]{3,2,1,0:T(8,128)(2,1)S(1)} %get-tuple-element.44.after_ref), channel_id=1, source_target_pairs={{0,8},{8,0},{16,24},{24,16},{1,9},{9,1},{17,25},{25,17},{2,10},{10... | collective-permute-start | bytes 786440 | tf_op jit(solution)/shard_map/ppermute | solution.py:351
  14.9 1.5 %collective-permute-start.2 = (bf16[2,8,512]{2,1,0:T(8,128)(2,1)S(1)}, bf16[2,8,512]{2,1,0:T(8,128)(2,1)S(1)}, u32[]{:S(2)}, u32[]{:S(2)}) collective-permute-start(bf16[2,8,512]{2,1,0:T(8,128)(2,1)S(1)} %get-tuple-element.49), channel_id=1, source_target_pairs={{0,1},{1,0},{2,3},{3,2},{4,5},{5,4},{6,7},{7,6},{8,9},{9,8},{10,11... | collective-permute-start | bytes 49160 | tf_op jit(solution)/shard_map/ppermute | solution.py:395
  16.4 0.0 copy-done
  16.4 0.0 copy-done.1
  16.4 1.1 %shard_map.48 = (bf16[256,768]{1,0:T(8,128)(2,1)S(1)}, bf16[256,768]{1,0:T(8,128)(2,1)S(1)}, bf16[2,256,384]{2,1,0:T(8,128)(2,1)S(1)}, bf16[2,256,24]{2,1,0:T(8,...) custom-call(bf16[2,8,8,9]{3,2,1,0:T(8,128)(2,1)S(1)} %bitcast.9, ...), custom_call_target="tpu_custom_call" | custom-call | flops 90000 | bytes 1000 | tf_op jit(solution)/shard_map/pallas_call | solution.py:23
  17.5 1.1 %collective-permute-done.2.rest_0_ = bf16[2,8,512]{2,1,0:T(8,128)(2,1)S(1)} collective-permute-done((bf16[2,8,512]{2,1,0:T(8,128)(2,1)S(1)}, bf16[2,8,512]{2,1,0:T(8,128)(2,1)S(1)}, u32[]{:S(2)}, u32[]{:S(2)}) %collective-permute-start.2) | collective-permute-done | bytes 16416 | tf_op jit(solution)/shard_map/ppermute | solution.py:395
  18.6 0.0 copy-start.2
  18.6 0.7 %copy-done.2 = f32[2,8]{1,0:T(2,128)S(1)} copy-done((f32[2,8]{1,0:T(2,128)S(1)}, f32[2,8]{1,0:T(2,128)}, u32[]{:S(2)}) %copy-start.2) | copy-done | bytes 88
  19.3 3.9 %shard_map.49 = (f32[8,2,2,64,128]{4,3,2,1,0:T(8,128)S(1)}, f32[8,2,2,64,128]{4,3,2,1,0:T(8,128)S(1)}) custom-call(bf16[8,2,2,64,128]{4,3,2,1,0:T(8,128)(2,1)S(1)} %get-tuple-element.38.mid_ref.x_ref, bf16[8,2,2,64,128]{4,3,2,1,0:T(8,128)(2,1)S(1)} %get-tuple-element.39.rim_ref, bf16[2,8,2,64,128]{4,3,2,1,0:T(8,128)(2,1)S(1)} %get-tuple-element.43.side_ref, ...), custom_call_target="tpu_custom_call" | custom-call | flops 3221225 | bytes 4194 | tf_op jit(solution)/shard_map/pallas_call | solution.py:23
  23.2 0.0 collective-permute-done.3.a_ref
  23.2 0.0 collective-permute-done.4.b_ref
  23.2 0.8 %shard_map.50.mid_ref.x_ref = bf16[8,2,2,64,128]{4,3,2,1,0:T(8,128)(2,1)S(1)} custom-call(bf16[8,2,2,64,128]{4,3,2,1,0:T(8,128)(2,1)S(1)} %get-tuple-element.38.mid_ref.x_ref, f32[8,2,2,64,128]{4,3,2,1,0:T(8,128)S(1)} %get-tuple-element.50.acc_ref, bf16[8,2,64,128]{3,2,1,0:T(8,128)(2,1)S(1)} %collective-permute-done.3.a_ref, ...), custom_call_target="tpu_custom_call" | custom-call | flops 524 | bytes 2621 | tf_op jit(solution)/shard_map/pallas_call | solution.py:23
  24.0 0.0 collective-permute-done.6.outb_ref
  24.0 0.0 collective-permute-done.5.outa_ref
  24.0 1.4 %shard_map.51 = (bf16[8,2,2,64,128]{4,3,2,1,0:T(8,128)(2,1)S(1)}, bf16[8,2,64,128]{3,2,1,0:T(8,128)(2,1)S(1)}, bf16[8,2,64,128]{3,2,1,0:T(8,128)(2,1)S(1)}, bf16...) custom-call(bf16[8,2,2,64,128]{4,3,2,1,0:T(8,128)(2,1)S(1)} %shard_map.50.mid_ref.x_ref, ...), custom_call_target="tpu_custom_call" | custom-call | flops 402653 | bytes 5242 | tf_op jit(solution)/shard_map/pallas_call | solution.py:23
  25.5 0.1 collective-permute-start.7
  25.6 1.6 %collective-permute-start.8 = (bf16[8,2,64,128]{3,2,1,0:T(8,128)(2,1)S(1)}, bf16[8,2,64,128]{3,2,1,0:T(8,128)(2,1)S(1)}, u32[]{:S(2)}, u32[]{:S(2)}) collective-permute-start(bf16[8,2,64,128]{3,2,1,0:T(8,128)(2,1)S(1)} %get-tuple-element.58), channel_id=1, source_target_pairs={{0,1},{1,0},{2,4},{3,5},{4,2},{5,3},{6,7},{7,6},{8,9},{9,8},{10,12... | collective-permute-start | bytes 786440 | tf_op jit(solution)/shard_map/ppermute | solution.py:352
  27.1 0.0 collective-permute-start.12
  27.1 0.0 collective-permute-start.13
  27.1 0.0 collective-permute-done.7.cola_ref
  27.1 4.8 %collective-permute-done.8.colb_ref = bf16[8,2,64,128]{3,2,1,0:T(8,128)(2,1)S(1)} collective-permute-done((bf16[8,2,64,128]{3,2,1,0:T(8,128)(2,1)S(1)}, bf16[8,2,64,128]{3,2,1,0:T(8,128)(2,1)S(1)}, u32[]{:S(2)}, u32[]{:S(2)}) %collective-permute-start.8) | collective-permute-done | bytes 262176 | tf_op jit(solution)/shard_map/ppermute | solution.py:352
  32.0 1.2 %shard_map.52 = (bf16[8,2,64,128]{3,2,1,0:T(8,128)(2,1)S(1)}, bf16[8,2,64,128]{3,2,1,0:T(8,128)(2,1)S(1)}, bf16[2,8,2,64,128]{4,3,2,1,0:T(8,128)(2,1)S(1)}, bf16[2,8,512]{2,1,0:T(8,128)(2,1)S(1)}) custom-call(bf16[8,2,2,64,128]{4,3,2,1,0:T(8,128)(2,1)S(1)} %shard_map.50.mid_ref.x_ref, bf16[8,2,2,64,128]{4,3,2,1,0:T(8,128)(2,1)S(1)} %get-tuple-element.56.rim_ref.x_ref, ...), custom_call_target="tpu_custom_call" | custom-call | flops 402653 | bytes 1048 | tf_op jit(solution)/shard_map/pallas_call | solution.py:23
  33.2 0.0 collective-permute-start.10
  33.3 0.2 collective-permute-start.11
  33.5 1.5 %collective-permute-start.9 = (bf16[2,8,512]{2,1,0:T(8,128)(2,1)S(1)}, bf16[2,8,512]{2,1,0:T(8,128)(2,1)S(1)}, u32[]{:S(2)}, u32[]{:S(2)}) collective-permute-start(bf16[2,8,512]{2,1,0:T(8,128)(2,1)S(1)} %get-tuple-element.64), channel_id=1, source_target_pairs={{0,1},{1,0},{2,3},{3,2},{4,5},{5,4},{6,7},{7,6},{8,9},{9,8},{10,11... | collective-permute-start | bytes 49160 | tf_op jit(solution)/shard_map/ppermute | solution.py:395
  35.0 2.2 %collective-permute-done.9.rest_0_ = bf16[2,8,512]{2,1,0:T(8,128)(2,1)S(1)} collective-permute-done((bf16[2,8,512]{2,1,0:T(8,128)(2,1)S(1)}, bf16[2,8,512]{2,1,0:T(8,128)(2,1)S(1)}, u32[]{:S(2)}, u32[]{:S(2)}) %collective-permute-start.9) | collective-permute-done | bytes 16416 | tf_op jit(solution)/shard_map/ppermute | solution.py:395
  37.2 3.9 %shard_map.53 = (f32[8,2,2,64,128]{4,3,2,1,0:T(8,128)S(1)}, f32[8,2,2,64,128]{4,3,2,1,0:T(8,128)S(1)}) custom-call(bf16[8,2,2,64,128]{4,3,2,1,0:T(8,128)(2,1)S(1)} %shard_map.50.mid_ref.x_ref, bf16[8,2,2,64,128]{4,3,2,1,0:T(8,128)(2,1)S(1)} %get-tuple-element.56.rim_ref.x_ref, bf16[2,8,2,64,128]{4,3,2,1,0:T(8,128)(2,1)S(1)} %get-tuple-element.59.side_ref, ...), custom_call_target="tpu_custom_call" | custom-call | flops 3221225 | bytes 4194 | tf_op jit(solution)/shard_map/pallas_call | solution.py:23
  41.1 0.0 collective-permute-done.12.a_ref
  41.1 0.0 collective-permute-done.13.b_ref
  41.2 1.5 %shard_map.54.begun_ref = bf16[8,2,4,64,128]{4,3,2,1,0:T(8,128)(2,1)} custom-call(bf16[8,2,2,64,128]{4,3,2,1,0:T(8,128)(2,1)S(1)} %shard_map.50.mid_ref.x_ref, f32[8,2,2,64,128]{4,3,2,1,0:T(8,128)S(1)} %get-tuple-element.68.acc_ref, bf16[8,2,64,128]{3,2,1,0:T(8,128)(2,1)S(1)} %collective-permute-done.12.a_ref, ...), custom_call_target="tpu_custom_call" | custom-call | flops 524 | bytes 2621 | tf_op jit(solution)/shard_map/pallas_call | solution.py:23
  42.7 0.0 collective-permute-done.10.a_ref
  42.7 0.0 collective-permute-done.11.b_ref
  42.7 1.4 %shard_map.55 = bf16[8,2,4,64,128]{4,3,2,1,0:T(8,128)(2,1)} custom-call(bf16[8,2,2,64,128]{4,3,2,1,0:T(8,128)(2,1)S(1)} %get-tuple-element.56.rim_ref.x_ref, f32[8,2,2,64,128]{4,3,2,1,0:T(8,128)S(1)} %get-tuple-element.65.acc_ref, bf16[8,2,64,128]{3,2,1,0:T(8,128)(2,1)S(1)} %collective-permute-done.10.a_ref, ...), custom_call_target="tpu_custom_call", output_to_operand_aliasing={{}: (5, {})} | custom-call | flops 524 | bytes 2621 | tf_op jit(solution)/shard_map/pallas_call | solution.py:23
Async XLA Ops:
  2.5 4.7 %collective-permute-start = (bf16[8,2,64,128]{3,2,1,0:T(8,128)(2,1)S(1)}, bf16[8,2,64,128]{3,2,1,0:T(8,128)(2,1)S(1)}, u32[]{:S(2)}, u32[]{:S(2)}) collective-permute-start(bf16[8,2,64,128]{3,2,1,0:T(8,128)(2,1)S(1)} %get-tuple-element.40), channel_id=1, source_target_pairs={{0,2},{2,0},{4,6},{6,4},{1,3},{3,1},{5,7},{7,5},{8,10},{10,8},{12,... | collective-permute-start | bytes 786440 | tf_op jit(solution)/shard_map/ppermute | solution.py:351
  3.0 6.9 %collective-permute-start.1 = (bf16[8,2,64,128]{3,2,1,0:T(8,128)(2,1)S(1)}, bf16[8,2,64,128]{3,2,1,0:T(8,128)(2,1)S(1)}, u32[]{:S(2)}, u32[]{:S(2)}) collective-permute-start(bf16[8,2,64,128]{3,2,1,0:T(8,128)(2,1)S(1)} %get-tuple-element.41), channel_id=1, source_target_pairs={{0,1},{1,0},{2,4},{3,5},{4,2},{5,3},{6,7},{7,6},{8,9},{9,8},{10,12... | collective-permute-start | bytes 786440 | tf_op jit(solution)/shard_map/ppermute | solution.py:352
  5.6 17.6 %collective-permute-start.3 = (bf16[8,2,64,128]{3,2,1,0:T(8,128)(2,1)S(1)}, bf16[8,2,64,128]{3,2,1,0:T(8,128)(2,1)S(1)}, u32[]{:S(2)}, u32[]{:S(2)}) collective-permute-start(bf16[8,2,64,128]{3,2,1,0:T(8,128)(2,1)S(1)} %get-tuple-element.51), channel_id=1, source_target_pairs={{0,8},{8,0},{16,24},{24,16},{1,9},{9,1},{17,25},{25,17},{2,10},{10... | collective-permute-start | bytes 786440 | tf_op jit(solution)/shard_map/ppermute | solution.py:351
  7.2 16.0 %collective-permute-start.4 = (bf16[8,2,64,128]{3,2,1,0:T(8,128)(2,1)S(1)}, bf16[8,2,64,128]{3,2,1,0:T(8,128)(2,1)S(1)}, u32[]{:S(2)}, u32[]{:S(2)}) collective-permute-start(bf16[8,2,64,128]{3,2,1,0:T(8,128)(2,1)S(1)} %get-tuple-element.52), channel_id=1, source_target_pairs={{0,2},{2,0},{4,6},{6,4},{8,16},{10,18},{12,20},{14,22},{16,8},{18,... | collective-permute-start | bytes 786440 | tf_op jit(solution)/shard_map/ppermute | solution.py:352
  10.0 6.4 %copy-start = (bf16[2,9,8,8]{1,3,2,0:T(8,128)(2,1)S(1)}, bf16[2,9,8,8]{1,3,2,0:T(8,128)(2,1)}, u32[]{:S(2)}) copy-start(bf16[2,9,8,8]{1,3,2,0:T(8,128)(2,1)} %param.5) | copy-start | bytes 6916
  10.0 6.4 %copy-start.1 = (bf16[2,9,8,8]{1,3,2,0:T(8,128)(2,1)S(1)}, bf16[2,9,8,8]{1,3,2,0:T(8,128)(2,1)}, u32[]{:S(2)}) copy-start(bf16[2,9,8,8]{1,3,2,0:T(8,128)(2,1)} %param.6) | copy-start | bytes 6916
  11.2 12.8 %collective-permute-start.6 = (bf16[8,2,64,128]{3,2,1,0:T(8,128)(2,1)S(1)}, bf16[8,2,64,128]{3,2,1,0:T(8,128)(2,1)S(1)}, u32[]{:S(2)}, u32[]{:S(2)}) collective-permute-start(bf16[8,2,64,128]{3,2,1,0:T(8,128)(2,1)S(1)} %get-tuple-element.54), channel_id=1, source_target_pairs={{0,2},{2,0},{4,6},{6,4},{8,16},{10,18},{12,20},{14,22},{16,8},{18,... | collective-permute-start | bytes 786440 | tf_op jit(solution)/shard_map/ppermute | solution.py:352
  11.3 12.7 %collective-permute-start.5 = (bf16[8,2,64,128]{3,2,1,0:T(8,128)(2,1)S(1)}, bf16[8,2,64,128]{3,2,1,0:T(8,128)(2,1)S(1)}, u32[]{:S(2)}, u32[]{:S(2)}) collective-permute-start(bf16[8,2,64,128]{3,2,1,0:T(8,128)(2,1)S(1)} %get-tuple-element.44.after_ref), channel_id=1, source_target_pairs={{0,8},{8,0},{16,24},{24,16},{1,9},{9,1},{17,25},{25,17},{2,10},{10... | collective-permute-start | bytes 786440 | tf_op jit(solution)/shard_map/ppermute | solution.py:351
  14.9 3.7 %collective-permute-start.2 = (bf16[2,8,512]{2,1,0:T(8,128)(2,1)S(1)}, bf16[2,8,512]{2,1,0:T(8,128)(2,1)S(1)}, u32[]{:S(2)}, u32[]{:S(2)}) collective-permute-start(bf16[2,8,512]{2,1,0:T(8,128)(2,1)S(1)} %get-tuple-element.49), channel_id=1, source_target_pairs={{0,1},{1,0},{2,3},{3,2},{4,5},{5,4},{6,7},{7,6},{8,9},{9,8},{10,11... | collective-permute-start | bytes 49160 | tf_op jit(solution)/shard_map/ppermute | solution.py:395
  18.6 0.7 %copy-start.2 = (f32[2,8]{1,0:T(2,128)S(1)}, f32[2,8]{1,0:T(2,128)}, u32[]{:S(2)}) copy-start(f32[2,8]{1,0:T(2,128)} %bias_ref.3) | copy-start | bytes 196
  25.5 1.7 %collective-permute-start.7 = (bf16[8,2,64,128]{3,2,1,0:T(8,128)(2,1)S(1)}, bf16[8,2,64,128]{3,2,1,0:T(8,128)(2,1)S(1)}, u32[]{:S(2)}, u32[]{:S(2)}) collective-permute-start(bf16[8,2,64,128]{3,2,1,0:T(8,128)(2,1)S(1)} %get-tuple-element.57), channel_id=1, source_target_pairs={{0,2},{2,0},{4,6},{6,4},{1,3},{3,1},{5,7},{7,5},{8,10},{10,8},{12,... | collective-permute-start | bytes 786440 | tf_op jit(solution)/shard_map/ppermute | solution.py:351
  25.6 6.4 %collective-permute-start.8 = (bf16[8,2,64,128]{3,2,1,0:T(8,128)(2,1)S(1)}, bf16[8,2,64,128]{3,2,1,0:T(8,128)(2,1)S(1)}, u32[]{:S(2)}, u32[]{:S(2)}) collective-permute-start(bf16[8,2,64,128]{3,2,1,0:T(8,128)(2,1)S(1)} %get-tuple-element.58), channel_id=1, source_target_pairs={{0,1},{1,0},{2,4},{3,5},{4,2},{5,3},{6,7},{7,6},{8,9},{9,8},{10,12... | collective-permute-start | bytes 786440 | tf_op jit(solution)/shard_map/ppermute | solution.py:352
  27.1 14.0 %collective-permute-start.12 = (bf16[8,2,64,128]{3,2,1,0:T(8,128)(2,1)S(1)}, bf16[8,2,64,128]{3,2,1,0:T(8,128)(2,1)S(1)}, u32[]{:S(2)}, u32[]{:S(2)}) collective-permute-start(bf16[8,2,64,128]{3,2,1,0:T(8,128)(2,1)S(1)} %get-tuple-element.69), channel_id=1, source_target_pairs={{0,8},{8,0},{16,24},{24,16},{1,9},{9,1},{17,25},{25,17},{2,10},{10... | collective-permute-start | bytes 786440 | tf_op jit(solution)/shard_map/ppermute | solution.py:351
  27.1 14.0 %collective-permute-start.13 = (bf16[8,2,64,128]{3,2,1,0:T(8,128)(2,1)S(1)}, bf16[8,2,64,128]{3,2,1,0:T(8,128)(2,1)S(1)}, u32[]{:S(2)}, u32[]{:S(2)}) collective-permute-start(bf16[8,2,64,128]{3,2,1,0:T(8,128)(2,1)S(1)} %get-tuple-element.70), channel_id=1, source_target_pairs={{0,2},{2,0},{4,6},{6,4},{8,16},{10,18},{12,20},{14,22},{16,8},{18,... | collective-permute-start | bytes 786440 | tf_op jit(solution)/shard_map/ppermute | solution.py:352
  33.2 9.4 %collective-permute-start.10 = (bf16[8,2,64,128]{3,2,1,0:T(8,128)(2,1)S(1)}, bf16[8,2,64,128]{3,2,1,0:T(8,128)(2,1)S(1)}, u32[]{:S(2)}, u32[]{:S(2)}) collective-permute-start(bf16[8,2,64,128]{3,2,1,0:T(8,128)(2,1)S(1)} %get-tuple-element.66), channel_id=1, source_target_pairs={{0,8},{8,0},{16,24},{24,16},{1,9},{9,1},{17,25},{25,17},{2,10},{10... | collective-permute-start | bytes 786440 | tf_op jit(solution)/shard_map/ppermute | solution.py:351
  33.3 9.4 %collective-permute-start.11 = (bf16[8,2,64,128]{3,2,1,0:T(8,128)(2,1)S(1)}, bf16[8,2,64,128]{3,2,1,0:T(8,128)(2,1)S(1)}, u32[]{:S(2)}, u32[]{:S(2)}) collective-permute-start(bf16[8,2,64,128]{3,2,1,0:T(8,128)(2,1)S(1)} %get-tuple-element.67), channel_id=1, source_target_pairs={{0,2},{2,0},{4,6},{6,4},{8,16},{10,18},{12,20},{14,22},{16,8},{18,... | collective-permute-start | bytes 786440 | tf_op jit(solution)/shard_map/ppermute | solution.py:352
  33.5 3.8 %collective-permute-start.9 = (bf16[2,8,512]{2,1,0:T(8,128)(2,1)S(1)}, bf16[2,8,512]{2,1,0:T(8,128)(2,1)S(1)}, u32[]{:S(2)}, u32[]{:S(2)}) collective-permute-start(bf16[2,8,512]{2,1,0:T(8,128)(2,1)S(1)} %get-tuple-element.64), channel_id=1, source_target_pairs={{0,1},{1,0},{2,3},{3,2},{4,5},{5,4},{6,7},{7,6},{8,9},{9,8},{10,11... | collective-permute-start | bytes 49160 | tf_op jit(solution)/shard_map/ppermute | solution.py:395
where the time goes:
time: 44.3 us; the launch traced here: 44.1 us
  Pallas kernels  18.9 us (43%)
  starting transfers between devices  13.3 us (30%)
  waiting for transfers between devices  11 us (25%)
  local copies, waits for them, and re-layouts  0.77 us (2%)
    pallas_call x10, Pallas kernels, call(): pl.pallas_call(body, out_shape=tuple(outs), in_specs=[pl.BlockSpec(memory...  18.9 us
    ppermute x6, waiting for transfers between devices, swaps(): return (got_a, lax.ppermute(b, (axis, other), pairs))  7.63 us
    ppermute x6, starting transfers between devices, swaps(): got_a = lax.ppermute(a, axis, [(n, n ^ 1) for n in range(count)])  5.8 us
    ppermute x6, starting transfers between devices, swaps(): return (got_a, lax.ppermute(b, (axis, other), pairs))  4.5 us
    ppermute x2, waiting for transfers between devices, shards(): deeper = [lax.ppermute(deep[0], 'trow', [(0, 1), (1, 0)])]  3.32 us
    ppermute x2, starting transfers between devices, shards(): deeper = [lax.ppermute(deep[0], 'trow', [(0, 1), (1, 0)])]  3.04 us
  transfers between devices with their start and end apart: 14, of which 4 were waited for; matrix products, arithmetic and copies ran while one was open for 0% of the time, Pallas kernels for 31%

commit v1 on v0

v1 whole, which is shorter than its diff:
```python
import functools

import jax
import jax.numpy as jnp
from jax import lax
from jax.experimental import pallas as pl
from jax.experimental.pallas import tpu as pltpu
from jax.sharding import PartitionSpec as P

BAND = 32
EDGE = 16
SCOPED = 16 * 1024 * 1024
F32 = jnp.float32
BF16 = jnp.bfloat16
VMEM, HBM = pltpu.VMEM, pltpu.HBM
def parity(axis):
    return lax.axis_index(axis) % 2


def has_second(axis):
    at = lax.axis_index(axis)
    return (at > 0) & (at < lax.axis_size(axis) - 1)


def call(body, outs, args, places=None, out_place=VMEM, scratch=(), aliases=None):
    places = places or {}
    spaces = [places.get(n, VMEM) for n in range(len(args))]
    held = [pltpu.with_memory_space_constraint(a, m) if m in (VMEM, HBM) else a for a, m in zip(args, spaces)]
    return pl.pallas_call(
        body,
        out_shape=tuple(outs),
        in_specs=[pl.BlockSpec(memory_space=m) for m in spaces],
        out_specs=tuple(pl.BlockSpec(memory_space=out_place) for _ in outs),
        scratch_shapes=list(scratch),
        input_output_aliases=aliases or {},
        compiler_params=pltpu.CompilerParams(vmem_limit_bytes=SCOPED),
        cost_estimate=pl.CostEstimate(flops=10**6, bytes_accessed=10**4, transcendentals=0),
    )(*held)


def dot(a, b):
    return jnp.dot(a, b, preferred_element_type=F32)


def operators(parts, src_w_ref, tgt_w_ref, out_refs):
    channels = src_w_ref.shape[1]
    span, small = channels * BAND, channels * EDGE

    def columns(size):
        pick_c = lax.broadcasted_iota(jnp.int32, (channels, channels * size), 1) // size
        pick_r = lax.broadcasted_iota(jnp.int32, (channels, channels * size), 0)
        return (pick_c == pick_r).astype(BF16)

    wide, narrow, single = columns(BAND), columns(EDGE), columns(1)
    row = lax.broadcasted_iota(jnp.int32, (BAND, span), 0)
    shift = row - lax.broadcasted_iota(jnp.int32, (BAND, span), 1) % BAND
    row_s = lax.broadcasted_iota(jnp.int32, (BAND, small), 0)
    col_s = lax.broadcasted_iota(jnp.int32, (BAND, small), 1) % EDGE
    near = ((row_s == 0) & (col_s == EDGE - 1), (row_s == BAND - 1) & (col_s == 0))
    row_1 = lax.broadcasted_iota(jnp.int32, (BAND, channels), 0)
    deep = (row_1 == 0, row_1 == BAND - 1)
    spread = {}

    def taps(ref, layer, o, pick, key):
        key = (key, layer, o)
        if key not in spread:
            spread[key] = lax.dot_general(ref[layer, o], pick, (((0,), (0,)), ((), ())), preferred_element_type=F32)
        return spread[key]

    for (kind, layer), out_ref in zip(parts, out_refs):
        for o in range(channels):
            rows = slice(o * BAND, (o + 1) * BAND)
            for b in range(3):
                if kind == "middle":
                    got = taps(src_w_ref, layer, o, wide, "s")
                    values = {(): jnp.where(shift == 0, got[3 + b][None, :], 0.0)}
                elif kind == "beside":
                    got = taps(src_w_ref, layer, o, wide, "s")
                    values = {(n,): jnp.where(shift == 0, got[6 * n + b][None, :], 0.0) for n in range(2)}
                elif kind == "target":
                    got = taps(tgt_w_ref, layer, o, wide, "t")
                    value = jnp.where(shift == 1, got[b][None, :], 0.0)
                    value = jnp.where(shift == 0, got[3 + b][None, :], value)
                    values = {(): jnp.where(shift == -1, got[6 + b][None, :], value)}
                else:
                    pick, at = (narrow, near) if kind == "near" else (single, deep)
                    got = taps(tgt_w_ref, layer, o, pick, kind)
                    values = {(n,): jnp.where(at[n], got[6 * n + b][None, :], 0.0) for n in range(2)}
                for index, value in values.items():
                    size = value.shape[1]
                    out_ref[(*index, rows, slice(b * size, (b + 1) * size))] = value.astype(BF16)


def operator_shapes(parts, channels):
    span = channels * BAND
    widths = dict(middle=span, beside=span, target=span, near=channels * EDGE, deep=channels)
    lead = dict(middle=(), beside=(2,), target=(), near=(2,), deep=(2,))
    return [VMEM((*lead[kind], span, 3 * widths[kind]), BF16) for kind, _ in parts]


def build_body(parts, src_w_ref, tgt_w_ref, after_ref, *out_refs):
    operators(parts, src_w_ref, tgt_w_ref, out_refs)


def build(parts, src_w, tgt_w, after):
    got = call(
        functools.partial(build_body, parts),
        operator_shapes(parts, src_w.shape[1]),
        (src_w, tgt_w, after),
        {2: pl.ANY},
    )
    return dict(zip(parts, got))


def band(tile):
    channels, size, width = tile.shape
    return tile.reshape(channels * size, width)


def unband(tile, channels):
    return tile.reshape(channels, tile.shape[0] // channels, tile.shape[1])


def src_operand(tiles, cols):
    return jnp.concatenate([jnp.concatenate(tiles[b : b + cols], axis=1) for b in range(3)], axis=0)


def sent_rows(rows):
    odd = parity("srow")
    return ((rows - 1) * (1 - odd), odd), ((rows - 1) * odd, 1 - odd)


def column(mid_ref, rim_ref, i, j, cut):
    last = mid_ref.shape[2] + 1
    return band(rim_ref[:, i, j // last, cut] if j in (0, last) else mid_ref[:, i, j - 1, cut])


def bands_of(depth):
    return [slice(start, start + BAND) for start in range(0, depth, BAND)]


def owed_sums(operator, tiles, out_ref):
    channels, cols, depth, width = out_ref.shape
    cuts = bands_of(depth)
    operand = jnp.concatenate([jnp.concatenate([t for cut in cuts for t in tiles(cut, b)], axis=1) for b in range(3)], axis=0)
    got = dot(operator, operand).astype(BF16)
    for q, cut in enumerate(cuts):
        for j in range(cols):
            at = (q * cols + j) * width
            out_ref[:, j, cut] = unband(got[:, at : at + width], channels)


def inner_sums(mid_ref, rim_ref, beside_ref, out_refs):
    rows, cols = mid_ref.shape[1:3]
    for (i, side), out_ref in zip(sent_rows(rows), out_refs):
        owed_sums(
            beside_ref[side], lambda cut, b: [column(mid_ref, rim_ref, i, j + b, cut) for j in range(cols)], out_ref
        )


def edge_body(mid_ref, rim_ref, cola_ref, colb_ref, beside_ref, after_ref, a_ref, b_ref, side_ref):
    rows, cols = mid_ref.shape[1], mid_ref.shape[2] + 2
    odd, paired = parity("scol"), has_second("scol")
    side_ref[1 - odd] = cola_ref[...]

    @pl.when(paired)
    def _():
        side_ref[odd] = colb_ref[...]

    @pl.when(jnp.logical_not(paired))
    def _():
        side_ref[odd] = jnp.zeros_like(colb_ref)

    def around(i, j, cut):
        if j in (-1, cols):
            return band(side_ref[0 if j < 0 else 1, :, i, cut])
        return column(mid_ref, rim_ref, i, j, cut)

    for (i, side), out_ref in zip(sent_rows(rows), (a_ref, b_ref)):
        owed_sums(beside_ref[side], lambda cut, b: [around(i, j + b - 1, cut) for j in (0, cols - 1)], out_ref)


def shifted(tile, step):
    lane = lax.broadcasted_iota(jnp.int32, tile.shape, 1)
    width = tile.shape[1]
    rolled = pltpu.roll(tile.astype(F32), step % width, 1)
    gone = 0 if step == 1 else width - 1
    return jnp.where(lane == gone, 0.0, rolled)


def three(tiles):
    return [jnp.concatenate([shifted(t, step) if step else t.astype(F32) for t in tiles], axis=1) for step in (1, 0, -1)]


def own_body(
    layer, mid_ref, rim_ref, middle_ref, beside_ref, target_ref, near_ref, bias_ref, after_ref, accmid_ref, accrim_ref, lane_ref
):
    channels, rows, mids, depth, width = mid_ref.shape
    cols = mids + 2
    cuts = bands_of(depth)
    shape = (BAND, cols * width)
    bias = [jnp.broadcast_to(bias_ref[layer : layer + 1, o : o + 1], shape) for o in range(channels)]
    bias = jnp.concatenate(bias, axis=0)
    for i in range(rows):
        for q, cut in enumerate(cuts):
            tiles = [column(mid_ref, rim_ref, i, j, cut) for j in range(cols)]
            lane_ref[q, 1] = jnp.concatenate(tiles, axis=1)
            for n, step in ((0, 1), (2, -1)):
                lane_ref[q, n] = jnp.concatenate([shifted(t, step).astype(BF16) for t in tiles], axis=1)
        for q, cut in enumerate(cuts):
            total = bias + dot(target_ref[...], lane_ref[q].reshape(3 * channels * BAND, cols * width))
            for side, other, start in ((0, q - 1, BAND - EDGE), (1, q + 1, 0)):
                if 0 <= other < len(cuts):
                    parts = [unband(lane_ref[other, n], channels)[:, start : start + EDGE] for n in range(3)]
                    total = total + dot(near_ref[side], jnp.concatenate([band(p) for p in parts], axis=0))
            for n, j in enumerate((0, cols - 1)):
                accrim_ref[:, i, n, cut] = unband(total[:, j * width : (j + 1) * width], channels)
            for j in range(1, cols - 1):
                accmid_ref[:, i, j - 1, cut] = unband(total[:, j * width : (j + 1) * width], channels)
        for a in range(3):
            r = i + a - 1
            if 0 <= r < rows:
                operator = middle_ref[...] if a == 1 else beside_ref[a // 2]
                add_sums(operator, lambda cut, b: [column(mid_ref, rim_ref, r, j + b, cut) for j in range(mids)], accmid_ref, i)


def add_sums(operator, tiles, acc_ref, i):
    channels, _, cols, depth, width = acc_ref.shape
    cuts = bands_of(depth)
    operand = jnp.concatenate([jnp.concatenate([t for cut in cuts for t in tiles(cut, b)], axis=1) for b in range(3)], axis=0)
    got = dot(operator, operand)
    for q, cut in enumerate(cuts):
        for j in range(cols):
            at = (q * cols + j) * width
            acc_ref[:, i, j, cut] += unband(got[:, at : at + width], channels)


def rest_body(
    mid_ref, rim_ref, side_ref, middle_ref, beside_ref, deep_ref, accmid_ref, accrim_ref, *rest
):
    *deep_halos, outmid_ref, outrim_ref = rest
    channels, rows, mids, depth, width = mid_ref.shape
    cols = mids + 2

    def around(r, j, cut):
        if j in (-1, cols):
            return band(side_ref[0 if j < 0 else 1, :, r, cut])
        return column(mid_ref, rim_ref, r, j, cut)

    for i in range(rows):
        for a in range(3):
            r = i + a - 1
            if 0 <= r < rows:
                operator = middle_ref[...] if a == 1 else beside_ref[a // 2]
                add_sums(operator, lambda cut, b: [around(r, j + b - 1, cut) for j in (0, cols - 1)], outrim_ref, i)
        odd = parity("trow")
        for n, halo_ref in enumerate(deep_halos):
            side = (1 - odd) if n == 0 else odd
            cut = pl.ds(pl.multiple_of(side * (depth - BAND), BAND), BAND)
            halo = three([halo_ref[i, :, j * width : (j + 1) * width] for j in range(cols)])
            halo = jnp.concatenate(halo, axis=0)
            if n == 1:
                halo = halo * has_second("trow").astype(F32)
            got = dot(deep_ref[side], halo.astype(BF16))
            for j in range(cols):
                acc_ref, at = (outrim_ref, j // (cols - 1)) if j in (0, cols - 1) else (outmid_ref, j - 1)
                acc_ref[:, i, at, cut] += unband(got[:, j * width : (j + 1) * width], channels)


def finished(x_ref, acc_ref, owed_refs, store):
    rows, cols = x_ref.shape[1:3]
    odd = parity("srow")
    paired = has_second("srow").astype(F32)
    for n, i in enumerate([(rows - 1) * (1 - odd), (rows - 1) * odd, *range(1, rows - 1)]):
        for j in range(cols):
            total = acc_ref[:, i, j]
            if n < 2:
                owed = owed_refs[n][:, j].astype(F32)
                total = total + (owed if n == 0 else owed * paired)
            store(i, j, (x_ref[:, i, j].astype(F32) + jnp.maximum(total, 0.0)).astype(BF16))


def sent_columns(rim_ref, col_refs):
    odd = parity("scol")
    for n, ref in zip((1 - odd, odd), col_refs):
        ref[...] = rim_ref[:, :, n]


def sent_depths(mid_ref, rim_ref, deep_refs):
    channels, rows, mids, depth, _ = mid_ref.shape
    odd = parity("trow")
    shape = (channels, channels * BAND)
    first = lax.broadcasted_iota(jnp.int32, shape, 0) * BAND
    for n, ref in enumerate(deep_refs):
        end = (1 - odd) if n == 0 else odd
        cut = pl.ds(pl.multiple_of(end * (depth - BAND), BAND), BAND)
        pick = (lax.broadcasted_iota(jnp.int32, shape, 1) == first + end * (BAND - 1)).astype(BF16)
        for i in range(rows):
            tiles = [column(mid_ref, rim_ref, i, j, cut) for j in range(mids + 2)]
            ref[i] = dot(pick, jnp.concatenate(tiles, axis=1)).astype(BF16)


def mid_body(x_ref, acc_ref, a_ref, b_ref, out_ref):
    def store(i, j, value):
        out_ref[:, i, j] = value

    finished(x_ref, acc_ref, (a_ref, b_ref), store)


def next_body(mid_ref, rim_ref, acc_ref, outa_ref, outb_ref, beside_ref, out_ref, cola_ref, colb_ref, a_ref, b_ref, *deep_refs):
    mid_body(rim_ref, acc_ref, outa_ref, outb_ref, out_ref)
    sent_columns(out_ref, (cola_ref, colb_ref))
    inner_sums(mid_ref, out_ref, beside_ref, (a_ref, b_ref))
    sent_depths(mid_ref, out_ref, deep_refs)


def last_body(mid_ref, rim_ref, acc_ref, a_ref, b_ref, out_ref, hold_ref, sems):
    rows, mids = mid_ref.shape[1:3]
    copies = [pltpu.make_async_copy(mid_ref, out_ref.at[:, :, 1 : mids + 1], sems.at[0])]
    copies[0].start()

    def store(i, j, value):
        hold_ref[:, i, j] = value
        copy = pltpu.make_async_copy(hold_ref.at[:, i, j], out_ref.at[:, i, j * (mids + 1)], sems.at[len(copies)])
        copy.start()
        copies.append(copy)

    finished(rim_ref, acc_ref, (a_ref, b_ref), store)
    for copy in copies:
        copy.wait()


def open_body(parts, x_ref, src_w_ref, tgt_w_ref, bias_ref, *rest):
    src_ref, tgt_ref, held_ref, beside_ref, mid_ref, rim_ref, cola_ref, colb_ref, a_ref, b_ref, *deep_refs, sems = rest
    last = x_ref.shape[2] - 1
    pairs = (
        (src_w_ref, src_ref),
        (x_ref.at[:, :, 0], rim_ref.at[:, :, 0]),
        (x_ref.at[:, :, last], rim_ref.at[:, :, 1]),
        (x_ref.at[:, :, 1:last], mid_ref),
        (tgt_w_ref, tgt_ref),
        (bias_ref, held_ref),
    )
    copies = [pltpu.make_async_copy(a, b, sems.at[n]) for n, (a, b) in enumerate(pairs)]
    for copy in copies:
        copy.start()
    copies[0].wait()
    operators(parts, src_ref, None, (beside_ref,))
    for copy in copies[1:]:
        copy.wait()
    sent_columns(rim_ref, (cola_ref, colb_ref))
    inner_sums(mid_ref, rim_ref, beside_ref, (a_ref, b_ref))
    sent_depths(mid_ref, rim_ref, deep_refs)


def swaps(a, b, axis, other):
    count, across = lax.axis_size(axis), lax.axis_size(other)
    pairs = []
    for n in range(count):
        for m in range(across):
            if 0 < n < count - 1:
                target = (n + 1 if n % 2 else n - 1, m)
            else:
                target = (n, m ^ 1)
            pairs.append((n * across + m, target[0] * across + target[1]))
    got_a = lax.ppermute(a, axis, [(n, n ^ 1) for n in range(count)])
    return got_a, lax.ppermute(b, (axis, other), pairs)


def shards(volume, src_weight, tgt_weight, bias):
    layers = src_weight.shape[0]
    channels, rows, cols, depth, width = volume.shape
    axes = ("srow", "scol", "trow")
    counts = [lax.axis_size(n) for n in axes]
    assert all(count % 2 == 0 for count in counts) and rows > 1 and cols > 2
    src_w = jnp.transpose(src_weight, (0, 2, 3, 1))
    tgt_w = jnp.transpose(tgt_weight, (0, 2, 3, 1))
    deep_swaps = 1 if counts[2] == 2 else 2
    mid_shape, rim_shape = ((channels, rows, n, depth, width) for n in (cols - 2, 2))
    line = VMEM((channels, rows, depth, width), BF16)
    owed_mid, owed_rim = (VMEM((channels, n, depth, width), BF16) for n in (cols - 2, 2))
    sent = [VMEM(rim_shape, BF16), line, line, owed_mid, owed_mid]
    sent += [VMEM((rows, channels, cols * width), BF16)] * deep_swaps
    early = [("beside", 0)]
    src_w, tgt_w, bias, made_early, mid, rim, col_a, col_b, sum_a, sum_b, *deep = call(
        functools.partial(open_body, early),
        [VMEM(src_w.shape, BF16), VMEM(tgt_w.shape, BF16), VMEM(bias.shape, F32)]
        + operator_shapes(early, channels)
        + [VMEM(mid_shape, BF16)]
        + sent,
        (volume, src_w, tgt_w, bias),
        {n: HBM for n in range(4)},
        scratch=[pltpu.SemaphoreType.DMA((6,))],
    )
    made = {early[0]: made_early}
    made |= build([(kind, 0) for kind in ("middle", "target", "near", "deep")], src_w, tgt_w, sum_a)
    for layer in range(layers):
        inner = swaps(sum_a, sum_b, "srow", "scol")
        beside = swaps(col_a, col_b, "scol", "trow")
        if deep_swaps == 1:
            deeper = [lax.ppermute(deep[0], "trow", [(0, 1), (1, 0)])]
        else:
            deeper = swaps(*deep, "trow", "scol")
        operator = {kind: made[kind, layer] for kind in ("middle", "beside", "target", "near", "deep")}

        def own(after):
            return call(
                functools.partial(own_body, layer),
                [VMEM(mid_shape, F32), VMEM(rim_shape, F32)],
                (mid, rim, *(operator[kind] for kind in ("middle", "beside", "target", "near")), bias, after),
                {7: pl.ANY},
                scratch=[VMEM((depth // BAND, 3, channels * BAND, cols * width), BF16)],
            )

        accs = own(sum_a) if layer else None
        a, b, side = call(
            edge_body,
            [owed_rim, owed_rim, VMEM((2, *line.shape), BF16)],
            (mid, rim, *beside, operator["beside"], accs[0] if layer else operator["middle"]),
            {5: pl.ANY},
        )
        outer = swaps(a, b, "srow", "scol")
        accs = accs or own(a)
        acc_mid, acc_rim = call(
            rest_body,
            [VMEM(mid_shape, F32), VMEM(rim_shape, F32)],
            (mid, rim, side, *(operator[kind] for kind in ("middle", "beside", "deep")), *accs, *deeper),
            aliases={6: 0, 7: 1},
        )
        (mid,) = call(mid_body, [VMEM(mid_shape, BF16)], (mid, acc_mid, *inner))
        if layer < layers - 1:
            later = [(kind, layer + 1) for kind in operator]
            made |= build(later, src_w, tgt_w, mid)
            rim, col_a, col_b, sum_a, sum_b, *deep = call(
                next_body, sent, (mid, rim, acc_rim, *outer, made["beside", layer + 1])
            )
        else:
            (state,) = call(
                last_body,
                [jax.ShapeDtypeStruct(volume.shape, BF16)],
                (mid, rim, acc_rim, *outer),
                out_place=HBM,
                scratch=[VMEM(rim_shape, BF16), pltpu.SemaphoreType.DMA((1 + rows * 2,))],
            )
    return state


def solution(mesh):
    return jax.shard_map(
        shards,
        mesh=mesh,
        in_specs=(P(None, "srow", "scol", "trow", None), P(), P(), P()),
        out_specs=P(None, "srow", "scol", "trow", None),
        check_vma=False,
    )
```

time: 44.3 us -> 38.1 us (0.86)
  waiting for transfers between devices: 11 us -> 5.12 us
  starting transfers between devices: 13.3 us -> 18.7 us
  Pallas kernels: 18.9 us -> 14 us
  local copies, waits for them, and re-layouts: 0.77 us -> 0 us
    ppermute x6, waiting for transfers between devices: 7.63 us -> 0.78 us  [swaps(): return (got_a, lax.ppermute(b, (axis, other), pairs))]
    ppermute x6, starting transfers between devices: 5.8 us -> 11.2 us  [swaps(): got_a = lax.ppermute(a, axis, [(n, n ^ 1) for n in range(count)])]
    pallas_call x10 -> x13, Pallas kernels: 18.9 us -> 14 us  [call(): pl.pallas_call(body, out_shape=tuple(outs), in_specs=[pl.BlockSpec(memory...]
    ppermute x6, waiting for transfers between devices: 0.02 us -> 2.11 us  [swaps(): got_a = lax.ppermute(a, axis, [(n, n ^ 1) for n in range(count)])]
    ppermute x2, waiting for transfers between devices: 3.32 us -> 2.23 us  [shards(): deeper = [lax.ppermute(deep[0], 'trow', [(0, 1), (1, 0)])]]
    unnamed x6 -> x0, local copies, waits for them, and re-layouts: 0.69 us -> none
  transfers between devices with their start and end apart: 14 -> 14, of which waited for: 4 -> 5; matrix products, arithmetic and copies ran while one was open for 0% -> 0% of each run, Pallas kernels for 31% -> 27%
where the time goes in v1:
time: 38.1 us; the launch traced here: 38 us
  starting transfers between devices  18.7 us (49%)
  Pallas kernels  14 us (37%)
  waiting for transfers between devices  5.12 us (13%)
    pallas_call x13, Pallas kernels, call(): pl.pallas_call(body, out_shape=tuple(outs), in_specs=[pl.BlockSpec(memory...  14 us
    ppermute x6, starting transfers between devices, swaps(): got_a = lax.ppermute(a, axis, [(n, n ^ 1) for n in range(count)])  11.2 us
    ppermute x6, starting transfers between devices, swaps(): return (got_a, lax.ppermute(b, (axis, other), pairs))  4.42 us
    ppermute x2, starting transfers between devices, shards(): deeper = [lax.ppermute(deep[0], 'trow', [(0, 1), (1, 0)])]  3.02 us
    ppermute x2, waiting for transfers between devices, shards(): deeper = [lax.ppermute(deep[0], 'trow', [(0, 1), (1, 0)])]  2.23 us
    ppermute x6, waiting for transfers between devices, swaps(): got_a = lax.ppermute(a, axis, [(n, n ^ 1) for n in range(count)])  2.11 us
    ppermute x6, waiting for transfers between devices, swaps(): return (got_a, lax.ppermute(b, (axis, other), pairs))  0.78 us
  transfers between devices with their start and end apart: 14, of which 5 were waited for; matrix products, arithmetic and copies ran while one was open for 0% of the time, Pallas kernels for 27%

profile of v1, /device:TPU:0, one launch (start us, length us, event | category | flops | bytes accessed | tf_op | source)
XLA Modules:
  0.0 38.0 jit_solution(1121999249507942622)
XLA Ops:
  0.0 1.9 %shard_map.46 = (bf16[2,8,8,9]{3,2,1,0:T(8,128)(2,1)S(1)}, bf16[2,8,8,9]{3,2,1,0:T(8,128)(2,1)S(1)}, f32[2,8]{1,0:T(2,128)S(1)}, bf16[2,256,768]{2,1,0:T(8,128)(...) custom-call(bf16[8,2,4,64,128]{4,3,2,1,0:T(8,128)(2,1)} %x_ref.1, ...), custom_call_target="tpu_custom_call" | custom-call | flops 1000000 | bytes 10000 | tf_op jit(solution)/shard_map/pallas_call | solution.py:29
  1.9 0.5 %collective-permute-start = (bf16[8,2,64,128]{3,2,1,0:T(8,128)(2,1)S(1)}, bf16[8,2,64,128]{3,2,1,0:T(8,128)(2,1)S(1)}, u32[]{:S(2)}, u32[]{:S(2)}) collective-permute-start(bf16[8,2,64,128]{3,2,1,0:T(8,128)(2,1)S(1)} %get-tuple-element.47), channel_id=1, source_target_pairs={{0,2},{2,0},{4,6},{6,4},{1,3},{3,1},{5,7},{7,5},{8,10},{10,8},{12,... | collective-permute-start | bytes 786440 | tf_op jit(solution)/shard_map/ppermute | solution.py:366
  2.5 2.6 %collective-permute-start.1 = (bf16[8,2,64,128]{3,2,1,0:T(8,128)(2,1)S(1)}, bf16[8,2,64,128]{3,2,1,0:T(8,128)(2,1)S(1)}, u32[]{:S(2)}, u32[]{:S(2)}) collective-permute-start(bf16[8,2,64,128]{3,2,1,0:T(8,128)(2,1)S(1)} %get-tuple-element.48), channel_id=1, source_target_pairs={{0,1},{1,0},{2,4},{3,5},{4,2},{5,3},{6,7},{7,6},{8,9},{9,8},{10,12... | collective-permute-start | bytes 786440 | tf_op jit(solution)/shard_map/ppermute | solution.py:367
  5.0 0.1 collective-permute-start.4
  5.1 3.1 %collective-permute-start.3 = (bf16[8,2,64,128]{3,2,1,0:T(8,128)(2,1)S(1)}, bf16[8,2,64,128]{3,2,1,0:T(8,128)(2,1)S(1)}, u32[]{:S(2)}, u32[]{:S(2)}) collective-permute-start(bf16[8,2,64,128]{3,2,1,0:T(8,128)(2,1)S(1)} %get-tuple-element.52.after_ref), channel_id=1, source_target_pairs={{0,8},{8,0},{16,24},{24,16},{1,9},{9,1},{17,25},{25,17},{2,10},{10... | collective-permute-start | bytes 786440 | tf_op jit(solution)/shard_map/ppermute | solution.py:366
  8.2 0.5 %shard_map.47 = (bf16[256,768]{1,0:T(8,128)(2,1)S(1)}, bf16[256,768]{1,0:T(8,128)(2,1)S(1)}, bf16[2,256,384]{2,1,0:T(8,128)(2,1)S(1)}, bf16[2,256,24]{2,1,0:T(8,128)(2,1)S(1)}) custom-call(bf16[2,8,8,9]{3,2,1,0:T(8,128)(2,1)S(1)} %get-tuple-element.50.src_w_ref, bf16[2,8,8,9]{3,2,1,0:T(8,128)(2,1)S(1)} %get-tuple-element.51.tgt_w_ref, ...), custom_call_target="tpu_custom_call" | custom-call | flops 1000000 | bytes 10000 | tf_op jit(solution)/shard_map/pallas_call | solution.py:29
  8.7 0.0 collective-permute-done.cola_ref
  8.7 0.7 %collective-permute-done.1.colb_ref = bf16[8,2,64,128]{3,2,1,0:T(8,128)(2,1)S(1)} collective-permute-done((bf16[8,2,64,128]{3,2,1,0:T(8,128)(2,1)S(1)}, bf16[8,2,64,128]{3,2,1,0:T(8,128)(2,1)S(1)}, u32[]{:S(2)}, u32[]{:S(2)}) %collective-permute-start.1) | collective-permute-done | bytes 262176 | tf_op jit(solution)/shard_map/ppermute | solution.py:367
  9.4 0.7 %shard_map.48 = (bf16[8,2,64,128]{3,2,1,0:T(8,128)(2,1)S(1)}, bf16[8,2,64,128]{3,2,1,0:T(8,128)(2,1)S(1)}, bf16[2,8,2,64,128]{4,3,2,1,0:T(8,128)(2,1)S(1)}) custom-call(bf16[8,2,2,64,128]{4,3,2,1,0:T(8,128)(2,1)S(1)} %get-tuple-element.45.mid_ref.x_ref, bf16[8,2,2,64,128]{4,3,2,1,0:T(8,128)(2,1)S(1)} %get-tuple-element.46.rim_ref, ...), custom_call_target="tpu_custom_call" | custom-call | flops 1000000 | bytes 10000 | tf_op jit(solution)/shard_map/pallas_call | solution.py:29
  10.1 0.1 collective-permute-start.6
  10.2 3.6 %collective-permute-start.5 = (bf16[8,2,64,128]{3,2,1,0:T(8,128)(2,1)S(1)}, bf16[8,2,64,128]{3,2,1,0:T(8,128)(2,1)S(1)}, u32[]{:S(2)}, u32[]{:S(2)}) collective-permute-start(bf16[8,2,64,128]{3,2,1,0:T(8,128)(2,1)S(1)} %get-tuple-element.59.after_ref), channel_id=1, source_target_pairs={{0,8},{8,0},{16,24},{24,16},{1,9},{9,1},{17,25},{25,17},{2,10},{10... | collective-permute-start | bytes 786440 | tf_op jit(solution)/shard_map/ppermute | solution.py:366
  13.8 1.5 %collective-permute-start.2 = (bf16[2,8,512]{2,1,0:T(8,128)(2,1)S(1)}, bf16[2,8,512]{2,1,0:T(8,128)(2,1)S(1)}, u32[]{:S(2)}, u32[]{:S(2)}) collective-permute-start(bf16[2,8,512]{2,1,0:T(8,128)(2,1)S(1)} %get-tuple-element.62), channel_id=1, source_target_pairs={{0,1},{1,0},{2,3},{3,2},{4,5},{5,4},{6,7},{7,6},{8,9},{9,8},{10,11... | collective-permute-start | bytes 49160 | tf_op jit(solution)/shard_map/ppermute | solution.py:401
  15.3 2.5 %shard_map.49 = (f32[8,2,2,64,128]{4,3,2,1,0:T(8,128)S(1)}, f32[8,2,2,64,128]{4,3,2,1,0:T(8,128)S(1)}) custom-call(bf16[8,2,2,64,128]{4,3,2,1,0:T(8,128)(2,1)S(1)} %get-tuple-element.45.mid_ref.x_ref, bf16[8,2,2,64,128]{4,3,2,1,0:T(8,128)(2,1)S(1)} %get-tuple-element.46.rim_ref, bf16[256,768]{1,0:T(8,128)(2,1)S(1)} %get-tuple-element.53.after_ref.middle_ref, ...), custom_call_target="tpu_custom_call" | custom-call | flops 1000000 | bytes 10000 | tf_op jit(solution)/shard_map/pallas_call | solution.py:29
  17.8 0.0 collective-permute-done.2.rest_0_
  17.8 1.1 %shard_map.50 = (f32[8,2,2,64,128]{4,3,2,1,0:T(8,128)S(1)}, f32[8,2,2,64,128]{4,3,2,1,0:T(8,128)S(1)}) custom-call(bf16[8,2,2,64,128]{4,3,2,1,0:T(8,128)(2,1)S(1)} %get-tuple-element.45.mid_ref.x_ref, bf16[8,2,2,64,128]{4,3,2,1,0:T(8,128)(2,1)S(1)} %get-tuple-element.46.rim_ref, ...), custom_call_target="tpu_custom_call", output_to_operand_aliasing={{0}: (6, {}), {1}: (7, {})} | custom-call | flops 1000000 | bytes 10000 | tf_op jit(solution)/shard_map/pallas_call | solution.py:29
  19.0 0.0 collective-permute-done.4.b_ref
  19.0 0.0 collective-permute-done.3.a_ref
  19.0 0.2 shard_map.51.after_ref.mid_ref.x_ref
  19.2 0.6 %shard_map.52 = (bf16[256,768]{1,0:T(8,128)(2,1)S(1)}, bf16[2,256,768]{2,1,0:T(8,128)(2,1)S(1)}, bf16[256,768]{1,0:T(8,128)(2,1)S(1)}, bf16[2,256,384]{2,1,0:T(8,128)(2,1)S(1)}, bf16[2,256,24]{2,1,0:T(8,128)(2,1)S(1)}) custom-call(bf16[2,8,8,9]{3,2,1,0:T(8,128)(2,1)S(1)} %get-tuple-element.50.src_w_ref, ...), custom_call_target="tpu_custom_call" | custom-call | flops 1000000 | bytes 10000 | tf_op jit(solution)/shard_map/pallas_call | solution.py:29
  19.9 0.0 collective-permute-done.6.outb_ref
  19.9 0.2 collective-permute-done.5.outa_ref
  20.1 0.9 %shard_map.53 = (bf16[8,2,2,64,128]{4,3,2,1,0:T(8,128)(2,1)S(1)}, bf16[8,2,64,128]{3,2,1,0:T(8,128)(2,1)S(1)}, bf16[8,2,64,128]{3,2,1,0:T(8,128)(2,1)S(1)}, bf16...) custom-call(bf16[8,2,2,64,128]{4,3,2,1,0:T(8,128)(2,1)S(1)} %shard_map.51.after_, ...), custom_call_target="tpu_custom_call" | custom-call | flops 1000000 | bytes 10000 | tf_op jit(solution)/shard_map/pallas_call | solution.py:29
  21.0 0.1 collective-permute-start.7
  21.0 1.6 %collective-permute-start.8 = (bf16[8,2,64,128]{3,2,1,0:T(8,128)(2,1)S(1)}, bf16[8,2,64,128]{3,2,1,0:T(8,128)(2,1)S(1)}, u32[]{:S(2)}, u32[]{:S(2)}) collective-permute-start(bf16[8,2,64,128]{3,2,1,0:T(8,128)(2,1)S(1)} %get-tuple-element.70), channel_id=1, source_target_pairs={{0,1},{1,0},{2,4},{3,5},{4,2},{5,3},{6,7},{7,6},{8,9},{9,8},{10,12... | collective-permute-start | bytes 786440 | tf_op jit(solution)/shard_map/ppermute | solution.py:367
  22.6 0.0 collective-permute-start.11
  22.6 2.2 %collective-permute-start.10 = (bf16[8,2,64,128]{3,2,1,0:T(8,128)(2,1)S(1)}, bf16[8,2,64,128]{3,2,1,0:T(8,128)(2,1)S(1)}, u32[]{:S(2)}, u32[]{:S(2)}) collective-permute-start(bf16[8,2,64,128]{3,2,1,0:T(8,128)(2,1)S(1)} %get-tuple-element.74.after_ref), channel_id=1, source_target_pairs={{0,8},{8,0},{16,24},{24,16},{1,9},{9,1},{17,25},{25,17},{2,10},{10... | collective-permute-start | bytes 786440 | tf_op jit(solution)/shard_map/ppermute | solution.py:366
  24.8 2.5 %shard_map.54 = (f32[8,2,2,64,128]{4,3,2,1,0:T(8,128)S(1)}, f32[8,2,2,64,128]{4,3,2,1,0:T(8,128)S(1)}) custom-call(bf16[8,2,2,64,128]{4,3,2,1,0:T(8,128)(2,1)S(1)} %shard_map.51.after_ref.mid_ref.x_ref, bf16[8,2,2,64,128]{4,3,2,1,0:T(8,128)(2,1)S(1)} %get-tuple-element.68.rim_ref, bf16[256,768]{1,0:T(8,128)(2,1)S(1)} %get-tuple-element.71.middle_ref, ...), custom_call_target="tpu_custom_call" | custom-call | flops 1000000 | bytes 10000 | tf_op jit(solution)/shard_map/pallas_call | solution.py:29
  27.4 0.0 collective-permute-done.7.cola_ref
  27.4 0.1 collective-permute-done.8.colb_ref
  27.5 0.7 %shard_map.55 = (bf16[8,2,64,128]{3,2,1,0:T(8,128)(2,1)S(1)}, bf16[8,2,64,128]{3,2,1,0:T(8,128)(2,1)S(1)}, bf16[2,8,2,64,128]{4,3,2,1,0:T(8,128)(2,1)S(1)}) custom-call(bf16[8,2,2,64,128]{4,3,2,1,0:T(8,128)(2,1)S(1)} %shard_map.51.after_ref.mid_ref.x_ref, bf16[8,2,2,64,128]{4,3,2,1,0:T(8,128)(2,1)S(1)} %get-tuple-element.68.rim_ref, ...), custom_call_target="tpu_custom_call" | custom-call | flops 1000000 | bytes 10000 | tf_op jit(solution)/shard_map/pallas_call | solution.py:29
  28.1 1.8 %collective-permute-start.12 = (bf16[8,2,64,128]{3,2,1,0:T(8,128)(2,1)S(1)}, bf16[8,2,64,128]{3,2,1,0:T(8,128)(2,1)S(1)}, u32[]{:S(2)}, u32[]{:S(2)}) collective-permute-start(bf16[8,2,64,128]{3,2,1,0:T(8,128)(2,1)S(1)} %get-tuple-element.83), channel_id=1, source_target_pairs={{0,8},{8,0},{16,24},{24,16},{1,9},{9,1},{17,25},{25,17},{2,10},{10... | collective-permute-start | bytes 786440 | tf_op jit(solution)/shard_map/ppermute | solution.py:366
  29.9 0.0 collective-permute-start.13
  29.9 1.5 %collective-permute-start.9 = (bf16[2,8,512]{2,1,0:T(8,128)(2,1)S(1)}, bf16[2,8,512]{2,1,0:T(8,128)(2,1)S(1)}, u32[]{:S(2)}, u32[]{:S(2)}) collective-permute-start(bf16[2,8,512]{2,1,0:T(8,128)(2,1)S(1)} %get-tuple-element.79), channel_id=1, source_target_pairs={{0,1},{1,0},{2,3},{3,2},{4,5},{5,4},{6,7},{7,6},{8,9},{9,8},{10,11... | collective-permute-start | bytes 49160 | tf_op jit(solution)/shard_map/ppermute | solution.py:401
  31.5 2.2 %collective-permute-done.9.rest_0_ = bf16[2,8,512]{2,1,0:T(8,128)(2,1)S(1)} collective-permute-done((bf16[2,8,512]{2,1,0:T(8,128)(2,1)S(1)}, bf16[2,8,512]{2,1,0:T(8,128)(2,1)S(1)}, u32[]{:S(2)}, u32[]{:S(2)}) %collective-permute-start.9) | collective-permute-done | bytes 16416 | tf_op jit(solution)/shard_map/ppermute | solution.py:401
  33.7 1.1 %shard_map.56 = (f32[8,2,2,64,128]{4,3,2,1,0:T(8,128)S(1)}, f32[8,2,2,64,128]{4,3,2,1,0:T(8,128)S(1)}) custom-call(bf16[8,2,2,64,128]{4,3,2,1,0:T(8,128)(2,1)S(1)} %shard_map.51.after_ref.mid_ref.x_ref, bf16[8,2,2,64,128]{4,3,2,1,0:T(8,128)(2,1)S(1)} %get-tuple-element.68.rim_ref, ...), custom_call_target="tpu_custom_call", output_to_operand_aliasing={{0}: (6, {}), {1}: (7, {})} | custom-call | flops 1000000 | bytes 10000 | tf_op jit(solution)/shard_map/pallas_call | solution.py:29
  34.8 0.0 collective-permute-done.11.b_ref
  34.8 0.0 collective-permute-done.10.a_ref
  34.9 0.2 shard_map.57.mid_ref
  35.1 1.9 %collective-permute-done.12.a_ref = bf16[8,2,64,128]{3,2,1,0:T(8,128)(2,1)S(1)} collective-permute-done((bf16[8,2,64,128]{3,2,1,0:T(8,128)(2,1)S(1)}, bf16[8,2,64,128]{3,2,1,0:T(8,128)(2,1)S(1)}, u32[]{:S(2)}, u32[]{:S(2)}) %collective-permute-start.12) | collective-permute-done | bytes 262176 | tf_op jit(solution)/shard_map/ppermute | solution.py:366
  37.0 0.0 collective-permute-done.13.b_ref
  37.0 1.0 %shard_map.58 = bf16[8,2,4,64,128]{4,3,2,1,0:T(8,128)(2,1)} custom-call(bf16[8,2,2,64,128]{4,3,2,1,0:T(8,128)(2,1)S(1)} %shard_map.57.mid_ref, bf16[8,2,2,64,128]{4,3,2,1,0:T(8,128)(2,1)S(1)} %get-tuple-element.68.rim_ref, f32[8,2,2,64,128]{4,3,2,1,0:T(8,128)S(1)} %get-tuple-element.82.acc_ref, bf16[8,2,64,128]{3,2,1,0:T(8,128)(2,1)S(1)} %collective-permute-done.12.a_ref, ...), custom_call_target="tpu_custom_call" | custom-call | flops 1000000 | bytes 10000 | tf_op jit(solution)/shard_map/pallas_call | solution.py:29
Async XLA Ops:
  1.9 6.8 %collective-permute-start = (bf16[8,2,64,128]{3,2,1,0:T(8,128)(2,1)S(1)}, bf16[8,2,64,128]{3,2,1,0:T(8,128)(2,1)S(1)}, u32[]{:S(2)}, u32[]{:S(2)}) collective-permute-start(bf16[8,2,64,128]{3,2,1,0:T(8,128)(2,1)S(1)} %get-tuple-element.47), channel_id=1, source_target_pairs={{0,2},{2,0},{4,6},{6,4},{1,3},{3,1},{5,7},{7,5},{8,10},{10,8},{12,... | collective-permute-start | bytes 786440 | tf_op jit(solution)/shard_map/ppermute | solution.py:366
  2.5 6.9 %collective-permute-start.1 = (bf16[8,2,64,128]{3,2,1,0:T(8,128)(2,1)S(1)}, bf16[8,2,64,128]{3,2,1,0:T(8,128)(2,1)S(1)}, u32[]{:S(2)}, u32[]{:S(2)}) collective-permute-start(bf16[8,2,64,128]{3,2,1,0:T(8,128)(2,1)S(1)} %get-tuple-element.48), channel_id=1, source_target_pairs={{0,1},{1,0},{2,4},{3,5},{4,2},{5,3},{6,7},{7,6},{8,9},{9,8},{10,12... | collective-permute-start | bytes 786440 | tf_op jit(solution)/shard_map/ppermute | solution.py:367
  5.0 13.9 %collective-permute-start.4 = (bf16[8,2,64,128]{3,2,1,0:T(8,128)(2,1)S(1)}, bf16[8,2,64,128]{3,2,1,0:T(8,128)(2,1)S(1)}, u32[]{:S(2)}, u32[]{:S(2)}) collective-permute-start(bf16[8,2,64,128]{3,2,1,0:T(8,128)(2,1)S(1)} %get-tuple-element.64), channel_id=1, source_target_pairs={{0,2},{2,0},{4,6},{6,4},{8,16},{10,18},{12,20},{14,22},{16,8},{18,... | collective-permute-start | bytes 786440 | tf_op jit(solution)/shard_map/ppermute | solution.py:367
  5.1 13.9 %collective-permute-start.3 = (bf16[8,2,64,128]{3,2,1,0:T(8,128)(2,1)S(1)}, bf16[8,2,64,128]{3,2,1,0:T(8,128)(2,1)S(1)}, u32[]{:S(2)}, u32[]{:S(2)}) collective-permute-start(bf16[8,2,64,128]{3,2,1,0:T(8,128)(2,1)S(1)} %get-tuple-element.52.after_ref), channel_id=1, source_target_pairs={{0,8},{8,0},{16,24},{24,16},{1,9},{9,1},{17,25},{25,17},{2,10},{10... | collective-permute-start | bytes 786440 | tf_op jit(solution)/shard_map/ppermute | solution.py:366
  10.1 9.8 %collective-permute-start.6 = (bf16[8,2,64,128]{3,2,1,0:T(8,128)(2,1)S(1)}, bf16[8,2,64,128]{3,2,1,0:T(8,128)(2,1)S(1)}, u32[]{:S(2)}, u32[]{:S(2)}) collective-permute-start(bf16[8,2,64,128]{3,2,1,0:T(8,128)(2,1)S(1)} %get-tuple-element.66), channel_id=1, source_target_pairs={{0,2},{2,0},{4,6},{6,4},{8,16},{10,18},{12,20},{14,22},{16,8},{18,... | collective-permute-start | bytes 786440 | tf_op jit(solution)/shard_map/ppermute | solution.py:367
  10.2 9.9 %collective-permute-start.5 = (bf16[8,2,64,128]{3,2,1,0:T(8,128)(2,1)S(1)}, bf16[8,2,64,128]{3,2,1,0:T(8,128)(2,1)S(1)}, u32[]{:S(2)}, u32[]{:S(2)}) collective-permute-start(bf16[8,2,64,128]{3,2,1,0:T(8,128)(2,1)S(1)} %get-tuple-element.59.after_ref), channel_id=1, source_target_pairs={{0,8},{8,0},{16,24},{24,16},{1,9},{9,1},{17,25},{25,17},{2,10},{10... | collective-permute-start | bytes 786440 | tf_op jit(solution)/shard_map/ppermute | solution.py:366
  13.8 4.0 %collective-permute-start.2 = (bf16[2,8,512]{2,1,0:T(8,128)(2,1)S(1)}, bf16[2,8,512]{2,1,0:T(8,128)(2,1)S(1)}, u32[]{:S(2)}, u32[]{:S(2)}) collective-permute-start(bf16[2,8,512]{2,1,0:T(8,128)(2,1)S(1)} %get-tuple-element.62), channel_id=1, source_target_pairs={{0,1},{1,0},{2,3},{3,2},{4,5},{5,4},{6,7},{7,6},{8,9},{9,8},{10,11... | collective-permute-start | bytes 49160 | tf_op jit(solution)/shard_map/ppermute | solution.py:401
  21.0 6.4 %collective-permute-start.7 = (bf16[8,2,64,128]{3,2,1,0:T(8,128)(2,1)S(1)}, bf16[8,2,64,128]{3,2,1,0:T(8,128)(2,1)S(1)}, u32[]{:S(2)}, u32[]{:S(2)}) collective-permute-start(bf16[8,2,64,128]{3,2,1,0:T(8,128)(2,1)S(1)} %get-tuple-element.69), channel_id=1, source_target_pairs={{0,2},{2,0},{4,6},{6,4},{1,3},{3,1},{5,7},{7,5},{8,10},{10,8},{12,... | collective-permute-start | bytes 786440 | tf_op jit(solution)/shard_map/ppermute | solution.py:366
  21.0 6.4 %collective-permute-start.8 = (bf16[8,2,64,128]{3,2,1,0:T(8,128)(2,1)S(1)}, bf16[8,2,64,128]{3,2,1,0:T(8,128)(2,1)S(1)}, u32[]{:S(2)}, u32[]{:S(2)}) collective-permute-start(bf16[8,2,64,128]{3,2,1,0:T(8,128)(2,1)S(1)} %get-tuple-element.70), channel_id=1, source_target_pairs={{0,1},{1,0},{2,4},{3,5},{4,2},{5,3},{6,7},{7,6},{8,9},{9,8},{10,12... | collective-permute-start | bytes 786440 | tf_op jit(solution)/shard_map/ppermute | solution.py:367
  22.6 12.2 %collective-permute-start.11 = (bf16[8,2,64,128]{3,2,1,0:T(8,128)(2,1)S(1)}, bf16[8,2,64,128]{3,2,1,0:T(8,128)(2,1)S(1)}, u32[]{:S(2)}, u32[]{:S(2)}) collective-permute-start(bf16[8,2,64,128]{3,2,1,0:T(8,128)(2,1)S(1)} %get-tuple-element.81), channel_id=1, source_target_pairs={{0,2},{2,0},{4,6},{6,4},{8,16},{10,18},{12,20},{14,22},{16,8},{18,... | collective-permute-start | bytes 786440 | tf_op jit(solution)/shard_map/ppermute | solution.py:367
  22.6 12.2 %collective-permute-start.10 = (bf16[8,2,64,128]{3,2,1,0:T(8,128)(2,1)S(1)}, bf16[8,2,64,128]{3,2,1,0:T(8,128)(2,1)S(1)}, u32[]{:S(2)}, u32[]{:S(2)}) collective-permute-start(bf16[8,2,64,128]{3,2,1,0:T(8,128)(2,1)S(1)} %get-tuple-element.74.after_ref), channel_id=1, source_target_pairs={{0,8},{8,0},{16,24},{24,16},{1,9},{9,1},{17,25},{25,17},{2,10},{10... | collective-permute-start | bytes 786440 | tf_op jit(solution)/shard_map/ppermute | solution.py:366
  28.1 8.8 %collective-permute-start.12 = (bf16[8,2,64,128]{3,2,1,0:T(8,128)(2,1)S(1)}, bf16[8,2,64,128]{3,2,1,0:T(8,128)(2,1)S(1)}, u32[]{:S(2)}, u32[]{:S(2)}) collective-permute-start(bf16[8,2,64,128]{3,2,1,0:T(8,128)(2,1)S(1)} %get-tuple-element.83), channel_id=1, source_target_pairs={{0,8},{8,0},{16,24},{24,16},{1,9},{9,1},{17,25},{25,17},{2,10},{10... | collective-permute-start | bytes 786440 | tf_op jit(solution)/shard_map/ppermute | solution.py:366
  29.9 7.0 %collective-permute-start.13 = (bf16[8,2,64,128]{3,2,1,0:T(8,128)(2,1)S(1)}, bf16[8,2,64,128]{3,2,1,0:T(8,128)(2,1)S(1)}, u32[]{:S(2)}, u32[]{:S(2)}) collective-permute-start(bf16[8,2,64,128]{3,2,1,0:T(8,128)(2,1)S(1)} %get-tuple-element.84), channel_id=1, source_target_pairs={{0,2},{2,0},{4,6},{6,4},{8,16},{10,18},{12,20},{14,22},{16,8},{18,... | collective-permute-start | bytes 786440 | tf_op jit(solution)/shard_map/ppermute | solution.py:367
  29.9 3.7 %collective-permute-start.9 = (bf16[2,8,512]{2,1,0:T(8,128)(2,1)S(1)}, bf16[2,8,512]{2,1,0:T(8,128)(2,1)S(1)}, u32[]{:S(2)}, u32[]{:S(2)}) collective-permute-start(bf16[2,8,512]{2,1,0:T(8,128)(2,1)S(1)} %get-tuple-element.79), channel_id=1, source_target_pairs={{0,1},{1,0},{2,3},{3,2},{4,5},{5,4},{6,7},{7,6},{8,9},{9,8},{10,11... | collective-permute-start | bytes 49160 | tf_op jit(solution)/shard_map/ppermute | solution.py:401

commit v2 on v1

--- a/solution.py
+++ b/solution.py
@@ -158,7 +158,7 @@
         )
 
 
-def edge_body(mid_ref, rim_ref, cola_ref, colb_ref, beside_ref, after_ref, a_ref, b_ref, side_ref):
+def edge_body(mid_ref, rim_ref, cola_ref, colb_ref, beside_ref, after_ref, a_ref, b_ref, side_ref, *deep_refs):
     rows, cols = mid_ref.shape[1], mid_ref.shape[2] + 2
     odd, paired = parity("scol"), has_second("scol")
     side_ref[1 - odd] = cola_ref[...]
@@ -178,6 +178,7 @@
 
     for (i, side), out_ref in zip(sent_rows(rows), (a_ref, b_ref)):
         owed_sums(beside_ref[side], lambda cut, b: [around(i, j + b - 1, cut) for j in (0, cols - 1)], out_ref)
+    sent_depths(mid_ref, rim_ref, deep_refs)
 
 
 def shifted(tile, step):
@@ -193,7 +194,7 @@
 
 
 def own_body(
-    layer, mid_ref, rim_ref, middle_ref, beside_ref, target_ref, near_ref, bias_ref, after_ref, accmid_ref, accrim_ref, lane_ref
+    layer, mid_ref, rim_ref, middle_ref, beside_ref, target_ref, near_ref, bias_ref, accmid_ref, accrim_ref, lane_ref
 ):
     channels, rows, mids, depth, width = mid_ref.shape
     cols = mids + 2
@@ -307,11 +308,10 @@
     finished(x_ref, acc_ref, (a_ref, b_ref), store)
 
 
-def next_body(mid_ref, rim_ref, acc_ref, outa_ref, outb_ref, beside_ref, out_ref, cola_ref, colb_ref, a_ref, b_ref, *deep_refs):
+def next_body(mid_ref, rim_ref, acc_ref, outa_ref, outb_ref, beside_ref, out_ref, cola_ref, colb_ref, a_ref, b_ref):
     mid_body(rim_ref, acc_ref, outa_ref, outb_ref, out_ref)
     sent_columns(out_ref, (cola_ref, colb_ref))
     inner_sums(mid_ref, out_ref, beside_ref, (a_ref, b_ref))
-    sent_depths(mid_ref, out_ref, deep_refs)
 
 
 def last_body(mid_ref, rim_ref, acc_ref, a_ref, b_ref, out_ref, hold_ref, sems):
@@ -331,7 +331,7 @@
 
 
 def open_body(parts, x_ref, src_w_ref, tgt_w_ref, bias_ref, *rest):
-    src_ref, tgt_ref, held_ref, beside_ref, mid_ref, rim_ref, cola_ref, colb_ref, a_ref, b_ref, *deep_refs, sems = rest
+    src_ref, tgt_ref, held_ref, beside_ref, mid_ref, rim_ref, cola_ref, colb_ref, a_ref, b_ref, sems = rest
     last = x_ref.shape[2] - 1
     pairs = (
         (src_w_ref, src_ref),
@@ -350,7 +350,6 @@
         copy.wait()
     sent_columns(rim_ref, (cola_ref, colb_ref))
     inner_sums(mid_ref, rim_ref, beside_ref, (a_ref, b_ref))
-    sent_depths(mid_ref, rim_ref, deep_refs)
 
 
 def swaps(a, b, axis, other):
@@ -380,9 +379,8 @@
     line = VMEM((channels, rows, depth, width), BF16)
     owed_mid, owed_rim = (VMEM((channels, n, depth, width), BF16) for n in (cols - 2, 2))
     sent = [VMEM(rim_shape, BF16), line, line, owed_mid, owed_mid]
-    sent += [VMEM((rows, channels, cols * width), BF16)] * deep_swaps
     early = [("beside", 0)]
-    src_w, tgt_w, bias, made_early, mid, rim, col_a, col_b, sum_a, sum_b, *deep = call(
+    src_w, tgt_w, bias, made_early, mid, rim, col_a, col_b, sum_a, sum_b = call(
         functools.partial(open_body, early),
         [VMEM(src_w.shape, BF16), VMEM(tgt_w.shape, BF16), VMEM(bias.shape, F32)]
         + operator_shapes(early, channels)
@@ -393,34 +391,28 @@
         scratch=[pltpu.SemaphoreType.DMA((6,))],
     )
     made = {early[0]: made_early}
-    made |= build([(kind, 0) for kind in ("middle", "target", "near", "deep")], src_w, tgt_w, sum_a)
+    made |= build([(kind, 0) for kind in ("middle", "target", "near", "deep")], src_w, tgt_w, col_b)
     for layer in range(layers):
         inner = swaps(sum_a, sum_b, "srow", "scol")
         beside = swaps(col_a, col_b, "scol", "trow")
+        operator = {kind: made[kind, layer] for kind in ("middle", "beside", "target", "near", "deep")}
+        accs = call(
+            functools.partial(own_body, layer),
+            [VMEM(mid_shape, F32), VMEM(rim_shape, F32)],
+            (mid, rim, *(operator[kind] for kind in ("middle", "beside", "target", "near")), bias),
+            scratch=[VMEM((depth // BAND, 3, channels * BAND, cols * width), BF16)],
+        )
+        a, b, side, *deep = call(
+            edge_body,
+            [owed_rim, owed_rim, VMEM((2, *line.shape), BF16)] + [VMEM((rows, channels, cols * width), BF16)] * deep_swaps,
+            (mid, rim, *beside, operator["beside"], accs[0]),
+            {5: pl.ANY},
+        )
+        outer = swaps(a, b, "srow", "scol")
         if deep_swaps == 1:
             deeper = [lax.ppermute(deep[0], "trow", [(0, 1), (1, 0)])]
         else:
             deeper = swaps(*deep, "trow", "scol")
-        operator = {kind: made[kind, layer] for kind in ("middle", "beside", "target", "near", "deep")}
-
-        def own(after):
-            return call(
-                functools.partial(own_body, layer),
-                [VMEM(mid_shape, F32), VMEM(rim_shape, F32)],
-                (mid, rim, *(operator[kind] for kind in ("middle", "beside", "target", "near")), bias, after),
-                {7: pl.ANY},
-                scratch=[VMEM((depth // BAND, 3, channels * BAND, cols * width), BF16)],
-            )
-
-        accs = own(sum_a) if layer else None
-        a, b, side = call(
-            edge_body,
-            [owed_rim, owed_rim, VMEM((2, *line.shape), BF16)],
-            (mid, rim, *beside, operator["beside"], accs[0] if layer else operator["middle"]),
-            {5: pl.ANY},
-        )
-        outer = swaps(a, b, "srow", "scol")
-        accs = accs or own(a)
         acc_mid, acc_rim = call(
             rest_body,
             [VMEM(mid_shape, F32), VMEM(rim_shape, F32)],
@@ -431,7 +423,7 @@
         if layer < layers - 1:
             later = [(kind, layer + 1) for kind in operator]
             made |= build(later, src_w, tgt_w, mid)
-            rim, col_a, col_b, sum_a, sum_b, *deep = call(
+            rim, col_a, col_b, sum_a, sum_b = call(
                 next_body, sent, (mid, rim, acc_rim, *outer, made["beside", layer + 1])
             )
         else:

time: 38.1 us -> 37.5 us (0.984)
  starting transfers between devices: 18.7 us -> 16.1 us
  waiting for transfers between devices: 5.12 us -> 7.11 us
    ppermute x2, waiting for transfers between devices: 2.23 us -> 5.22 us  [shards(): deeper = [lax.ppermute(deep[0], 'trow', [(0, 1), (1, 0)])]]
    ppermute x6, starting transfers between devices: 11.2 us -> 9.63 us  [swaps(): got_a = lax.ppermute(a, axis, [(n, n ^ 1) for n in range(count)])]
    ppermute x2, starting transfers between devices: 3.02 us -> 2.25 us  [shards(): deeper = [lax.ppermute(deep[0], 'trow', [(0, 1), (1, 0)])]]
    ppermute x6, waiting for transfers between devices: 0.78 us -> 0.22 us  [swaps(): return (got_a, lax.ppermute(b, (axis, other), pairs))]
    ppermute x6, waiting for transfers between devices: 2.11 us -> 1.67 us  [swaps(): got_a = lax.ppermute(a, axis, [(n, n ^ 1) for n in range(count)])]
  transfers between devices with their start and end apart: 14 -> 14, of which waited for: 5 -> 5; matrix products, arithmetic and copies ran while one was open for 0% -> 0% of each run, Pallas kernels for 27% -> 28%
where the time goes in v2:
time: 37.5 us; the launch traced here: 37.4 us
  starting transfers between devices  16.1 us (43%)
  Pallas kernels  14 us (37%)
  waiting for transfers between devices  7.11 us (19%)
    pallas_call x13, Pallas kernels, call(): pl.pallas_call(body, out_shape=tuple(outs), in_specs=[pl.BlockSpec(memory...  14 us
    ppermute x6, starting transfers between devices, swaps(): got_a = lax.ppermute(a, axis, [(n, n ^ 1) for n in range(count)])  9.63 us
    ppermute x2, waiting for transfers between devices, shards(): deeper = [lax.ppermute(deep[0], 'trow', [(0, 1), (1, 0)])]  5.22 us
    ppermute x6, starting transfers between devices, swaps(): return (got_a, lax.ppermute(b, (axis, other), pairs))  4.18 us
    ppermute x2, starting transfers between devices, shards(): deeper = [lax.ppermute(deep[0], 'trow', [(0, 1), (1, 0)])]  2.25 us
    ppermute x6, waiting for transfers between devices, swaps(): got_a = lax.ppermute(a, axis, [(n, n ^ 1) for n in range(count)])  1.67 us
  transfers between devices with their start and end apart: 14, of which 5 were waited for; matrix products, arithmetic and copies ran while one was open for 0% of the time, Pallas kernels for 28%

profile of v2, /device:TPU:0, one launch (start us, length us, event | category | flops | bytes accessed | tf_op | source)
XLA Modules:
  0.0 37.4 jit_solution(17331137598510159502)
XLA Ops:
  0.0 1.9 %shard_map.46 = (bf16[2,8,8,9]{3,2,1,0:T(8,128)(2,1)S(1)}, bf16[2,8,8,9]{3,2,1,0:T(8,128)(2,1)S(1)}, f32[2,8]{1,0:T(2,128)S(1)}, bf16[2,256,768]{2,1,0:T(8,128)(...) custom-call(bf16[8,2,4,64,128]{4,3,2,1,0:T(8,128)(2,1)} %x_ref.1, ...), custom_call_target="tpu_custom_call" | custom-call | flops 1000000 | bytes 10000 | tf_op jit(solution)/shard_map/pallas_call | solution.py:29
  1.9 0.5 %collective-permute-start = (bf16[8,2,64,128]{3,2,1,0:T(8,128)(2,1)S(1)}, bf16[8,2,64,128]{3,2,1,0:T(8,128)(2,1)S(1)}, u32[]{:S(2)}, u32[]{:S(2)}) collective-permute-start(bf16[8,2,64,128]{3,2,1,0:T(8,128)(2,1)S(1)} %get-tuple-element.47), channel_id=1, source_target_pairs={{0,2},{2,0},{4,6},{6,4},{1,3},{3,1},{5,7},{7,5},{8,10},{10,8},{12,... | collective-permute-start | bytes 786440 | tf_op jit(solution)/shard_map/ppermute | solution.py:365
  2.4 2.6 %collective-permute-start.1 = (bf16[8,2,64,128]{3,2,1,0:T(8,128)(2,1)S(1)}, bf16[8,2,64,128]{3,2,1,0:T(8,128)(2,1)S(1)}, u32[]{:S(2)}, u32[]{:S(2)}) collective-permute-start(bf16[8,2,64,128]{3,2,1,0:T(8,128)(2,1)S(1)} %get-tuple-element.48.after_ref), channel_id=1, source_target_pairs={{0,1},{1,0},{2,4},{3,5},{4,2},{5,3},{6,7},{7,6},{8,9},{9,8},{10,12... | collective-permute-start | bytes 786440 | tf_op jit(solution)/shard_map/ppermute | solution.py:366
  5.0 1.6 %collective-permute-start.3 = (bf16[8,2,64,128]{3,2,1,0:T(8,128)(2,1)S(1)}, bf16[8,2,64,128]{3,2,1,0:T(8,128)(2,1)S(1)}, u32[]{:S(2)}, u32[]{:S(2)}) collective-permute-start(bf16[8,2,64,128]{3,2,1,0:T(8,128)(2,1)S(1)} %get-tuple-element.62), channel_id=1, source_target_pairs={{0,8},{8,0},{16,24},{24,16},{1,9},{9,1},{17,25},{25,17},{2,10},{10... | collective-permute-start | bytes 786440 | tf_op jit(solution)/shard_map/ppermute | solution.py:365
  6.6 0.0 collective-permute-start.4
  6.6 0.5 %shard_map.47 = (bf16[256,768]{1,0:T(8,128)(2,1)S(1)}, bf16[256,768]{1,0:T(8,128)(2,1)S(1)}, bf16[2,256,384]{2,1,0:T(8,128)(2,1)S(1)}, bf16[2,256,24]{2,1,0:T(8,128)(2,1)S(1)}) custom-call(bf16[2,8,8,9]{3,2,1,0:T(8,128)(2,1)S(1)} %get-tuple-element.50.src_w_ref, bf16[2,8,8,9]{3,2,1,0:T(8,128)(2,1)S(1)} %get-tuple-element.51.tgt_w_ref, ...), custom_call_target="tpu_custom_call" | custom-call | flops 1000000 | bytes 10000 | tf_op jit(solution)/shard_map/pallas_call | solution.py:29
  7.1 2.5 %shard_map.48 = (f32[8,2,2,64,128]{4,3,2,1,0:T(8,128)S(1)}, f32[8,2,2,64,128]{4,3,2,1,0:T(8,128)S(1)}) custom-call(bf16[8,2,2,64,128]{4,3,2,1,0:T(8,128)(2,1)S(1)} %get-tuple-element.45.mid_ref.x_ref, bf16[8,2,2,64,128]{4,3,2,1,0:T(8,128)(2,1)S(1)} %get-tuple-element.46.rim_ref, bf16[256,768]{1,0:T(8,128)(2,1)S(1)} %get-tuple-element.52.middle_ref, ...), custom_call_target="tpu_custom_call" | custom-call | flops 1000000 | bytes 10000 | tf_op jit(solution)/shard_map/pallas_call | solution.py:29
  9.6 0.0 collective-permute-done.cola_ref
  9.6 0.0 collective-permute-done.1.colb_ref
  9.7 0.7 %shard_map.49 = (bf16[8,2,64,128]{3,2,1,0:T(8,128)(2,1)S(1)}, bf16[8,2,64,128]{3,2,1,0:T(8,128)(2,1)S(1)}, bf16[2,8,2,64,128]{4,3,2,1,0:T(8,128)(2,1)S(1)}, bf16[2,8,512]{2,1,0:T(8,128)(2,1)S(1)}) custom-call(bf16[8,2,2,64,128]{4,3,2,1,0:T(8,128)(2,1)S(1)} %get-tuple-element.45.mid_ref.x_ref, bf16[8,2,2,64,128]{4,3,2,1,0:T(8,128)(2,1)S(1)} %get-tuple-element.46.rim_ref, ...), custom_call_target="tpu_custom_call" | custom-call | flops 1000000 | bytes 10000 | tf_op jit(solution)/shard_map/pallas_call | solution.py:29
  10.4 3.2 %collective-permute-start.5 = (bf16[8,2,64,128]{3,2,1,0:T(8,128)(2,1)S(1)}, bf16[8,2,64,128]{3,2,1,0:T(8,128)(2,1)S(1)}, u32[]{:S(2)}, u32[]{:S(2)}) collective-permute-start(bf16[8,2,64,128]{3,2,1,0:T(8,128)(2,1)S(1)} %get-tuple-element.65), channel_id=1, source_target_pairs={{0,8},{8,0},{16,24},{24,16},{1,9},{9,1},{17,25},{25,17},{2,10},{10... | collective-permute-start | bytes 786440 | tf_op jit(solution)/shard_map/ppermute | solution.py:365
  13.5 0.0 collective-permute-start.6
  13.6 0.7 %collective-permute-start.2 = (bf16[2,8,512]{2,1,0:T(8,128)(2,1)S(1)}, bf16[2,8,512]{2,1,0:T(8,128)(2,1)S(1)}, u32[]{:S(2)}, u32[]{:S(2)}) collective-permute-start(bf16[2,8,512]{2,1,0:T(8,128)(2,1)S(1)} %get-tuple-element.60), channel_id=1, source_target_pairs={{0,1},{1,0},{2,3},{3,2},{4,5},{5,4},{6,7},{7,6},{8,9},{9,8},{10,11... | collective-permute-start | bytes 49160 | tf_op jit(solution)/shard_map/ppermute | solution.py:413
  14.3 3.0 %collective-permute-done.2.rest_0_ = bf16[2,8,512]{2,1,0:T(8,128)(2,1)S(1)} collective-permute-done((bf16[2,8,512]{2,1,0:T(8,128)(2,1)S(1)}, bf16[2,8,512]{2,1,0:T(8,128)(2,1)S(1)}, u32[]{:S(2)}, u32[]{:S(2)}) %collective-permute-start.2) | collective-permute-done | bytes 16416 | tf_op jit(solution)/shard_map/ppermute | solution.py:413
  17.3 1.1 %shard_map.50 = (f32[8,2,2,64,128]{4,3,2,1,0:T(8,128)S(1)}, f32[8,2,2,64,128]{4,3,2,1,0:T(8,128)S(1)}) custom-call(bf16[8,2,2,64,128]{4,3,2,1,0:T(8,128)(2,1)S(1)} %get-tuple-element.45.mid_ref.x_ref, bf16[8,2,2,64,128]{4,3,2,1,0:T(8,128)(2,1)S(1)} %get-tuple-element.46.rim_ref, ...), custom_call_target="tpu_custom_call", output_to_operand_aliasing={{0}: (6, {}), {1}: (7, {})} | custom-call | flops 1000000 | bytes 10000 | tf_op jit(solution)/shard_map/pallas_call | solution.py:29
  18.4 0.0 collective-permute-done.3.a_ref
  18.4 0.0 collective-permute-done.4.b_ref
  18.5 0.2 shard_map.51.after_ref.mid_ref.x_ref
  18.7 0.6 %shard_map.52 = (bf16[256,768]{1,0:T(8,128)(2,1)S(1)}, bf16[2,256,768]{2,1,0:T(8,128)(2,1)S(1)}, bf16[256,768]{1,0:T(8,128)(2,1)S(1)}, bf16[2,256,384]{2,1,0:T(8,128)(2,1)S(1)}, bf16[2,256,24]{2,1,0:T(8,128)(2,1)S(1)}) custom-call(bf16[2,8,8,9]{3,2,1,0:T(8,128)(2,1)S(1)} %get-tuple-element.50.src_w_ref, ...), custom_call_target="tpu_custom_call" | custom-call | flops 1000000 | bytes 10000 | tf_op jit(solution)/shard_map/pallas_call | solution.py:29
  19.3 0.2 collective-permute-done.5.outa_ref
  19.5 0.0 collective-permute-done.6.outb_ref
  19.5 0.8 %shard_map.53 = (bf16[8,2,2,64,128]{4,3,2,1,0:T(8,128)(2,1)S(1)}, bf16[8,2,64,128]{3,2,1,0:T(8,128)(2,1)S(1)}, bf16[8,2,64,128]{3,2,1,0:T(8,128)(2,1)S(1)}, bf16...) custom-call(bf16[8,2,2,64,128]{4,3,2,1,0:T(8,128)(2,1)S(1)} %shard_map.51.after_ref.mid_ref.x_ref, ...), custom_call_target="tpu_custom_call" | custom-call | flops 1000000 | bytes 10000 | tf_op jit(solution)/shard_map/pallas_call | solution.py:29
  20.4 0.1 collective-permute-start.7
  20.5 1.6 %collective-permute-start.8 = (bf16[8,2,64,128]{3,2,1,0:T(8,128)(2,1)S(1)}, bf16[8,2,64,128]{3,2,1,0:T(8,128)(2,1)S(1)}, u32[]{:S(2)}, u32[]{:S(2)}) collective-permute-start(bf16[8,2,64,128]{3,2,1,0:T(8,128)(2,1)S(1)} %get-tuple-element.70), channel_id=1, source_target_pairs={{0,1},{1,0},{2,4},{3,5},{4,2},{5,3},{6,7},{7,6},{8,9},{9,8},{10,12... | collective-permute-start | bytes 786440 | tf_op jit(solution)/shard_map/ppermute | solution.py:366
  22.0 2.1 %collective-permute-start.10 = (bf16[8,2,64,128]{3,2,1,0:T(8,128)(2,1)S(1)}, bf16[8,2,64,128]{3,2,1,0:T(8,128)(2,1)S(1)}, u32[]{:S(2)}, u32[]{:S(2)}) collective-permute-start(bf16[8,2,64,128]{3,2,1,0:T(8,128)(2,1)S(1)} %get-tuple-element.80), channel_id=1, source_target_pairs={{0,8},{8,0},{16,24},{24,16},{1,9},{9,1},{17,25},{25,17},{2,10},{10... | collective-permute-start | bytes 786440 | tf_op jit(solution)/shard_map/ppermute | solution.py:365
  24.2 0.0 collective-permute-start.11
  24.2 2.5 %shard_map.54 = (f32[8,2,2,64,128]{4,3,2,1,0:T(8,128)S(1)}, f32[8,2,2,64,128]{4,3,2,1,0:T(8,128)S(1)}) custom-call(bf16[8,2,2,64,128]{4,3,2,1,0:T(8,128)(2,1)S(1)} %shard_map.51.after_ref.mid_ref.x_ref, bf16[8,2,2,64,128]{4,3,2,1,0:T(8,128)(2,1)S(1)} %get-tuple-element.68.rim_ref, bf16[256,768]{1,0:T(8,128)(2,1)S(1)} %get-tuple-element.71.middle_ref, ...), custom_call_target="tpu_custom_call" | custom-call | flops 1000000 | bytes 10000 | tf_op jit(solution)/shard_map/pallas_call | solution.py:29
  26.7 0.0 collective-permute-done.7.cola_ref
  26.7 0.2 collective-permute-done.8.colb_ref
  26.9 0.7 %shard_map.55 = (bf16[8,2,64,128]{3,2,1,0:T(8,128)(2,1)S(1)}, bf16[8,2,64,128]{3,2,1,0:T(8,128)(2,1)S(1)}, bf16[2,8,2,64,128]{4,3,2,1,0:T(8,128)(2,1)S(1)}, bf16[2,8,512]{2,1,0:T(8,128)(2,1)S(1)}) custom-call(bf16[8,2,2,64,128]{4,3,2,1,0:T(8,128)(2,1)S(1)} %shard_map.51.after_ref.mid_ref.x_ref, bf16[8,2,2,64,128]{4,3,2,1,0:T(8,128)(2,1)S(1)} %get-tuple-element.68.rim_ref, ...), custom_call_target="tpu_custom_call" | custom-call | flops 1000000 | bytes 10000 | tf_op jit(solution)/shard_map/pallas_call | solution.py:29
  27.6 2.2 %collective-permute-start.12 = (bf16[8,2,64,128]{3,2,1,0:T(8,128)(2,1)S(1)}, bf16[8,2,64,128]{3,2,1,0:T(8,128)(2,1)S(1)}, u32[]{:S(2)}, u32[]{:S(2)}) collective-permute-start(bf16[8,2,64,128]{3,2,1,0:T(8,128)(2,1)S(1)} %get-tuple-element.83), channel_id=1, source_target_pairs={{0,8},{8,0},{16,24},{24,16},{1,9},{9,1},{17,25},{25,17},{2,10},{10... | collective-permute-start | bytes 786440 | tf_op jit(solution)/shard_map/ppermute | solution.py:365
  29.7 0.0 collective-permute-start.13
  29.7 1.5 %collective-permute-start.9 = (bf16[2,8,512]{2,1,0:T(8,128)(2,1)S(1)}, bf16[2,8,512]{2,1,0:T(8,128)(2,1)S(1)}, u32[]{:S(2)}, u32[]{:S(2)}) collective-permute-start(bf16[2,8,512]{2,1,0:T(8,128)(2,1)S(1)} %get-tuple-element.78), channel_id=1, source_target_pairs={{0,1},{1,0},{2,3},{3,2},{4,5},{5,4},{6,7},{7,6},{8,9},{9,8},{10,11... | collective-permute-start | bytes 49160 | tf_op jit(solution)/shard_map/ppermute | solution.py:413
  31.3 2.2 %collective-permute-done.9.rest_0_ = bf16[2,8,512]{2,1,0:T(8,128)(2,1)S(1)} collective-permute-done((bf16[2,8,512]{2,1,0:T(8,128)(2,1)S(1)}, bf16[2,8,512]{2,1,0:T(8,128)(2,1)S(1)}, u32[]{:S(2)}, u32[]{:S(2)}) %collective-permute-start.9) | collective-permute-done | bytes 16416 | tf_op jit(solution)/shard_map/ppermute | solution.py:413
  33.5 1.1 %shard_map.56 = (f32[8,2,2,64,128]{4,3,2,1,0:T(8,128)S(1)}, f32[8,2,2,64,128]{4,3,2,1,0:T(8,128)S(1)}) custom-call(bf16[8,2,2,64,128]{4,3,2,1,0:T(8,128)(2,1)S(1)} %shard_map.51.after_ref.mid_ref.x_ref, bf16[8,2,2,64,128]{4,3,2,1,0:T(8,128)(2,1)S(1)} %get-tuple-element.68.rim_ref, ...), custom_call_target="tpu_custom_call", output_to_operand_aliasing={{0}: (6, {}), {1}: (7, {})} | custom-call | flops 1000000 | bytes 10000 | tf_op jit(solution)/shard_map/pallas_call | solution.py:29
  34.6 0.0 collective-permute-done.10.a_ref
  34.6 0.0 collective-permute-done.11.b_ref
  34.7 0.2 shard_map.57.mid_ref
  34.9 1.5 %collective-permute-done.12.a_ref = bf16[8,2,64,128]{3,2,1,0:T(8,128)(2,1)S(1)} collective-permute-done((bf16[8,2,64,128]{3,2,1,0:T(8,128)(2,1)S(1)}, bf16[8,2,64,128]{3,2,1,0:T(8,128)(2,1)S(1)}, u32[]{:S(2)}, u32[]{:S(2)}) %collective-permute-start.12) | collective-permute-done | bytes 262176 | tf_op jit(solution)/shard_map/ppermute | solution.py:365
  36.4 0.0 collective-permute-done.13.b_ref
  36.4 1.0 %shard_map.58 = bf16[8,2,4,64,128]{4,3,2,1,0:T(8,128)(2,1)} custom-call(bf16[8,2,2,64,128]{4,3,2,1,0:T(8,128)(2,1)S(1)} %shard_map.57.mid_ref, bf16[8,2,2,64,128]{4,3,2,1,0:T(8,128)(2,1)S(1)} %get-tuple-element.68.rim_ref, f32[8,2,2,64,128]{4,3,2,1,0:T(8,128)S(1)} %get-tuple-element.82.acc_ref, bf16[8,2,64,128]{3,2,1,0:T(8,128)(2,1)S(1)} %collective-permute-done.12.a_ref, ...), custom_call_target="tpu_custom_call" | custom-call | flops 1000000 | bytes 10000 | tf_op jit(solution)/shard_map/pallas_call | solution.py:29
Async XLA Ops:
  1.9 7.7 %collective-permute-start = (bf16[8,2,64,128]{3,2,1,0:T(8,128)(2,1)S(1)}, bf16[8,2,64,128]{3,2,1,0:T(8,128)(2,1)S(1)}, u32[]{:S(2)}, u32[]{:S(2)}) collective-permute-start(bf16[8,2,64,128]{3,2,1,0:T(8,128)(2,1)S(1)} %get-tuple-element.47), channel_id=1, source_target_pairs={{0,2},{2,0},{4,6},{6,4},{1,3},{3,1},{5,7},{7,5},{8,10},{10,8},{12,... | collective-permute-start | bytes 786440 | tf_op jit(solution)/shard_map/ppermute | solution.py:365
  2.4 7.2 %collective-permute-start.1 = (bf16[8,2,64,128]{3,2,1,0:T(8,128)(2,1)S(1)}, bf16[8,2,64,128]{3,2,1,0:T(8,128)(2,1)S(1)}, u32[]{:S(2)}, u32[]{:S(2)}) collective-permute-start(bf16[8,2,64,128]{3,2,1,0:T(8,128)(2,1)S(1)} %get-tuple-element.48.after_ref), channel_id=1, source_target_pairs={{0,1},{1,0},{2,4},{3,5},{4,2},{5,3},{6,7},{7,6},{8,9},{9,8},{10,12... | collective-permute-start | bytes 786440 | tf_op jit(solution)/shard_map/ppermute | solution.py:366
  5.0 13.4 %collective-permute-start.3 = (bf16[8,2,64,128]{3,2,1,0:T(8,128)(2,1)S(1)}, bf16[8,2,64,128]{3,2,1,0:T(8,128)(2,1)S(1)}, u32[]{:S(2)}, u32[]{:S(2)}) collective-permute-start(bf16[8,2,64,128]{3,2,1,0:T(8,128)(2,1)S(1)} %get-tuple-element.62), channel_id=1, source_target_pairs={{0,8},{8,0},{16,24},{24,16},{1,9},{9,1},{17,25},{25,17},{2,10},{10... | collective-permute-start | bytes 786440 | tf_op jit(solution)/shard_map/ppermute | solution.py:365
  6.6 11.9 %collective-permute-start.4 = (bf16[8,2,64,128]{3,2,1,0:T(8,128)(2,1)S(1)}, bf16[8,2,64,128]{3,2,1,0:T(8,128)(2,1)S(1)}, u32[]{:S(2)}, u32[]{:S(2)}) collective-permute-start(bf16[8,2,64,128]{3,2,1,0:T(8,128)(2,1)S(1)} %get-tuple-element.63), channel_id=1, source_target_pairs={{0,2},{2,0},{4,6},{6,4},{8,16},{10,18},{12,20},{14,22},{16,8},{18,... | collective-permute-start | bytes 786440 | tf_op jit(solution)/shard_map/ppermute | solution.py:366
  10.4 9.2 %collective-permute-start.5 = (bf16[8,2,64,128]{3,2,1,0:T(8,128)(2,1)S(1)}, bf16[8,2,64,128]{3,2,1,0:T(8,128)(2,1)S(1)}, u32[]{:S(2)}, u32[]{:S(2)}) collective-permute-start(bf16[8,2,64,128]{3,2,1,0:T(8,128)(2,1)S(1)} %get-tuple-element.65), channel_id=1, source_target_pairs={{0,8},{8,0},{16,24},{24,16},{1,9},{9,1},{17,25},{25,17},{2,10},{10... | collective-permute-start | bytes 786440 | tf_op jit(solution)/shard_map/ppermute | solution.py:365
  13.5 6.0 %collective-permute-start.6 = (bf16[8,2,64,128]{3,2,1,0:T(8,128)(2,1)S(1)}, bf16[8,2,64,128]{3,2,1,0:T(8,128)(2,1)S(1)}, u32[]{:S(2)}, u32[]{:S(2)}) collective-permute-start(bf16[8,2,64,128]{3,2,1,0:T(8,128)(2,1)S(1)} %get-tuple-element.66), channel_id=1, source_target_pairs={{0,2},{2,0},{4,6},{6,4},{8,16},{10,18},{12,20},{14,22},{16,8},{18,... | collective-permute-start | bytes 786440 | tf_op jit(solution)/shard_map/ppermute | solution.py:366
  13.6 3.7 %collective-permute-start.2 = (bf16[2,8,512]{2,1,0:T(8,128)(2,1)S(1)}, bf16[2,8,512]{2,1,0:T(8,128)(2,1)S(1)}, u32[]{:S(2)}, u32[]{:S(2)}) collective-permute-start(bf16[2,8,512]{2,1,0:T(8,128)(2,1)S(1)} %get-tuple-element.60), channel_id=1, source_target_pairs={{0,1},{1,0},{2,3},{3,2},{4,5},{5,4},{6,7},{7,6},{8,9},{9,8},{10,11... | collective-permute-start | bytes 49160 | tf_op jit(solution)/shard_map/ppermute | solution.py:413
  20.4 6.3 %collective-permute-start.7 = (bf16[8,2,64,128]{3,2,1,0:T(8,128)(2,1)S(1)}, bf16[8,2,64,128]{3,2,1,0:T(8,128)(2,1)S(1)}, u32[]{:S(2)}, u32[]{:S(2)}) collective-permute-start(bf16[8,2,64,128]{3,2,1,0:T(8,128)(2,1)S(1)} %get-tuple-element.69), channel_id=1, source_target_pairs={{0,2},{2,0},{4,6},{6,4},{1,3},{3,1},{5,7},{7,5},{8,10},{10,8},{12,... | collective-permute-start | bytes 786440 | tf_op jit(solution)/shard_map/ppermute | solution.py:365
  20.5 6.4 %collective-permute-start.8 = (bf16[8,2,64,128]{3,2,1,0:T(8,128)(2,1)S(1)}, bf16[8,2,64,128]{3,2,1,0:T(8,128)(2,1)S(1)}, u32[]{:S(2)}, u32[]{:S(2)}) collective-permute-start(bf16[8,2,64,128]{3,2,1,0:T(8,128)(2,1)S(1)} %get-tuple-element.70), channel_id=1, source_target_pairs={{0,1},{1,0},{2,4},{3,5},{4,2},{5,3},{6,7},{7,6},{8,9},{9,8},{10,12... | collective-permute-start | bytes 786440 | tf_op jit(solution)/shard_map/ppermute | solution.py:366
  22.0 12.6 %collective-permute-start.10 = (bf16[8,2,64,128]{3,2,1,0:T(8,128)(2,1)S(1)}, bf16[8,2,64,128]{3,2,1,0:T(8,128)(2,1)S(1)}, u32[]{:S(2)}, u32[]{:S(2)}) collective-permute-start(bf16[8,2,64,128]{3,2,1,0:T(8,128)(2,1)S(1)} %get-tuple-element.80), channel_id=1, source_target_pairs={{0,8},{8,0},{16,24},{24,16},{1,9},{9,1},{17,25},{25,17},{2,10},{10... | collective-permute-start | bytes 786440 | tf_op jit(solution)/shard_map/ppermute | solution.py:365
  24.2 10.5 %collective-permute-start.11 = (bf16[8,2,64,128]{3,2,1,0:T(8,128)(2,1)S(1)}, bf16[8,2,64,128]{3,2,1,0:T(8,128)(2,1)S(1)}, u32[]{:S(2)}, u32[]{:S(2)}) collective-permute-start(bf16[8,2,64,128]{3,2,1,0:T(8,128)(2,1)S(1)} %get-tuple-element.81), channel_id=1, source_target_pairs={{0,2},{2,0},{4,6},{6,4},{8,16},{10,18},{12,20},{14,22},{16,8},{18,... | collective-permute-start | bytes 786440 | tf_op jit(solution)/shard_map/ppermute | solution.py:366
  27.6 8.8 %collective-permute-start.12 = (bf16[8,2,64,128]{3,2,1,0:T(8,128)(2,1)S(1)}, bf16[8,2,64,128]{3,2,1,0:T(8,128)(2,1)S(1)}, u32[]{:S(2)}, u32[]{:S(2)}) collective-permute-start(bf16[8,2,64,128]{3,2,1,0:T(8,128)(2,1)S(1)} %get-tuple-element.83), channel_id=1, source_target_pairs={{0,8},{8,0},{16,24},{24,16},{1,9},{9,1},{17,25},{25,17},{2,10},{10... | collective-permute-start | bytes 786440 | tf_op jit(solution)/shard_map/ppermute | solution.py:365
  29.7 6.6 %collective-permute-start.13 = (bf16[8,2,64,128]{3,2,1,0:T(8,128)(2,1)S(1)}, bf16[8,2,64,128]{3,2,1,0:T(8,128)(2,1)S(1)}, u32[]{:S(2)}, u32[]{:S(2)}) collective-permute-start(bf16[8,2,64,128]{3,2,1,0:T(8,128)(2,1)S(1)} %get-tuple-element.84), channel_id=1, source_target_pairs={{0,2},{2,0},{4,6},{6,4},{8,16},{10,18},{12,20},{14,22},{16,8},{18,... | collective-permute-start | bytes 786440 | tf_op jit(solution)/shard_map/ppermute | solution.py:366
  29.7 3.7 %collective-permute-start.9 = (bf16[2,8,512]{2,1,0:T(8,128)(2,1)S(1)}, bf16[2,8,512]{2,1,0:T(8,128)(2,1)S(1)}, u32[]{:S(2)}, u32[]{:S(2)}) collective-permute-start(bf16[2,8,512]{2,1,0:T(8,128)(2,1)S(1)} %get-tuple-element.78), channel_id=1, source_target_pairs={{0,1},{1,0},{2,3},{3,2},{4,5},{5,4},{6,7},{7,6},{8,9},{9,8},{10,11... | collective-permute-start | bytes 49160 | tf_op jit(solution)/shard_map/ppermute | solution.py:413

commit v3 on v1

--- a/solution.py
+++ b/solution.py
@@ -150,7 +150,7 @@
             out_ref[:, j, cut] = unband(got[:, at : at + width], channels)
 
 
-def inner_sums(mid_ref, rim_ref, beside_ref, out_refs):
+def inner_body(mid_ref, rim_ref, beside_ref, *out_refs):
     rows, cols = mid_ref.shape[1:3]
     for (i, side), out_ref in zip(sent_rows(rows), out_refs):
         owed_sums(
@@ -286,7 +286,7 @@
         ref[...] = rim_ref[:, :, n]
 
 
-def sent_depths(mid_ref, rim_ref, deep_refs):
+def depth_body(mid_ref, rim_ref, after_ref, *deep_refs):
     channels, rows, mids, depth, _ = mid_ref.shape
     odd = parity("trow")
     shape = (channels, channels * BAND)
@@ -307,17 +307,19 @@
     finished(x_ref, acc_ref, (a_ref, b_ref), store)
 
 
-def next_body(mid_ref, rim_ref, acc_ref, outa_ref, outb_ref, beside_ref, out_ref, cola_ref, colb_ref, a_ref, b_ref, *deep_refs):
-    mid_body(rim_ref, acc_ref, outa_ref, outb_ref, out_ref)
+def next_body(x_ref, acc_ref, a_ref, b_ref, after_ref, out_ref, cola_ref, colb_ref):
+    mid_body(x_ref, acc_ref, a_ref, b_ref, out_ref)
     sent_columns(out_ref, (cola_ref, colb_ref))
-    inner_sums(mid_ref, out_ref, beside_ref, (a_ref, b_ref))
-    sent_depths(mid_ref, out_ref, deep_refs)
 
 
 def last_body(mid_ref, rim_ref, acc_ref, a_ref, b_ref, out_ref, hold_ref, sems):
     rows, mids = mid_ref.shape[1:3]
-    copies = [pltpu.make_async_copy(mid_ref, out_ref.at[:, :, 1 : mids + 1], sems.at[0])]
-    copies[0].start()
+    copies = []
+    for i in range(rows):
+        for j in range(mids):
+            copy = pltpu.make_async_copy(mid_ref.at[:, i, j], out_ref.at[:, i, j + 1], sems.at[len(copies)])
+            copy.start()
+            copies.append(copy)
 
     def store(i, j, value):
         hold_ref[:, i, j] = value
@@ -331,26 +333,22 @@
 
 
 def open_body(parts, x_ref, src_w_ref, tgt_w_ref, bias_ref, *rest):
-    src_ref, tgt_ref, held_ref, beside_ref, mid_ref, rim_ref, cola_ref, colb_ref, a_ref, b_ref, *deep_refs, sems = rest
-    last = x_ref.shape[2] - 1
-    pairs = (
-        (src_w_ref, src_ref),
-        (x_ref.at[:, :, 0], rim_ref.at[:, :, 0]),
-        (x_ref.at[:, :, last], rim_ref.at[:, :, 1]),
-        (x_ref.at[:, :, 1:last], mid_ref),
-        (tgt_w_ref, tgt_ref),
-        (bias_ref, held_ref),
-    )
+    src_ref, tgt_ref, held_ref, beside_ref, mid_ref, rim_ref, cola_ref, colb_ref, sems = rest
+    rows, last = x_ref.shape[1], x_ref.shape[2] - 1
+    pairs = [(src_w_ref, src_ref)]
+    pairs += [(x_ref.at[:, i, n * last], rim_ref.at[:, i, n]) for i in range(rows) for n in range(2)]
+    pairs += [(x_ref.at[:, i, j], mid_ref.at[:, i, j - 1]) for i in range(rows) for j in range(1, last)]
+    pairs += [(tgt_w_ref, tgt_ref), (bias_ref, held_ref)]
     copies = [pltpu.make_async_copy(a, b, sems.at[n]) for n, (a, b) in enumerate(pairs)]
     for copy in copies:
         copy.start()
     copies[0].wait()
     operators(parts, src_ref, None, (beside_ref,))
-    for copy in copies[1:]:
+    for copy in copies[1 : 1 + 2 * rows]:
         copy.wait()
     sent_columns(rim_ref, (cola_ref, colb_ref))
-    inner_sums(mid_ref, rim_ref, beside_ref, (a_ref, b_ref))
-    sent_depths(mid_ref, rim_ref, deep_refs)
+    for copy in copies[1 + 2 * rows :]:
+        copy.wait()
 
 
 def swaps(a, b, axis, other):
@@ -379,10 +377,9 @@
     mid_shape, rim_shape = ((channels, rows, n, depth, width) for n in (cols - 2, 2))
     line = VMEM((channels, rows, depth, width), BF16)
     owed_mid, owed_rim = (VMEM((channels, n, depth, width), BF16) for n in (cols - 2, 2))
-    sent = [VMEM(rim_shape, BF16), line, line, owed_mid, owed_mid]
-    sent += [VMEM((rows, channels, cols * width), BF16)] * deep_swaps
+    sent = [VMEM(rim_shape, BF16), line, line]
     early = [("beside", 0)]
-    src_w, tgt_w, bias, made_early, mid, rim, col_a, col_b, sum_a, sum_b, *deep = call(
+    src_w, tgt_w, bias, beside_0, mid, rim, col_a, col_b = call(
         functools.partial(open_body, early),
         [VMEM(src_w.shape, BF16), VMEM(tgt_w.shape, BF16), VMEM(bias.shape, F32)]
         + operator_shapes(early, channels)
@@ -390,18 +387,18 @@
         + sent,
         (volume, src_w, tgt_w, bias),
         {n: HBM for n in range(4)},
-        scratch=[pltpu.SemaphoreType.DMA((6,))],
+        scratch=[pltpu.SemaphoreType.DMA((3 + rows * cols,))],
     )
-    made = {early[0]: made_early}
-    made |= build([(kind, 0) for kind in ("middle", "target", "near", "deep")], src_w, tgt_w, sum_a)
+    made = {early[0]: beside_0}
+    kinds = ("middle", "beside", "target", "near", "deep")
     for layer in range(layers):
+        beside = swaps(col_a, col_b, "scol", "trow")
+        sum_a, sum_b = call(inner_body, [owed_mid, owed_mid], (mid, rim, made["beside", layer]))
         inner = swaps(sum_a, sum_b, "srow", "scol")
-        beside = swaps(col_a, col_b, "scol", "trow")
-        if deep_swaps == 1:
-            deeper = [lax.ppermute(deep[0], "trow", [(0, 1), (1, 0)])]
-        else:
-            deeper = swaps(*deep, "trow", "scol")
-        operator = {kind: made[kind, layer] for kind in ("middle", "beside", "target", "near", "deep")}
+        if layer == 0:
+            late = [(kind, n) for n in range(layers) for kind in kinds]
+            made |= build([part for part in late if part not in early], src_w, tgt_w, sum_b)
+        operator = {kind: made[kind, layer] for kind in kinds}
 
         def own(after):
             return call(
@@ -412,7 +409,7 @@
                 scratch=[VMEM((depth // BAND, 3, channels * BAND, cols * width), BF16)],
             )
 
-        accs = own(sum_a) if layer else None
+        accs = own(sum_b) if layer else None
         a, b, side = call(
             edge_body,
             [owed_rim, owed_rim, VMEM((2, *line.shape), BF16)],
@@ -420,7 +417,14 @@
             {5: pl.ANY},
         )
         outer = swaps(a, b, "srow", "scol")
-        accs = accs or own(a)
+        deep = call(
+            depth_body, [VMEM((rows, channels, cols * width), BF16)] * deep_swaps, (mid, rim, b), {2: pl.ANY}
+        )
+        if deep_swaps == 1:
+            deeper = [lax.ppermute(deep[0], "trow", [(0, 1), (1, 0)])]
+        else:
+            deeper = swaps(*deep, "trow", "scol")
+        accs = accs or own(b)
         acc_mid, acc_rim = call(
             rest_body,
             [VMEM(mid_shape, F32), VMEM(rim_shape, F32)],
@@ -429,18 +433,14 @@
         )
         (mid,) = call(mid_body, [VMEM(mid_shape, BF16)], (mid, acc_mid, *inner))
         if layer < layers - 1:
-            later = [(kind, layer + 1) for kind in operator]
-            made |= build(later, src_w, tgt_w, mid)
-            rim, col_a, col_b, sum_a, sum_b, *deep = call(
-                next_body, sent, (mid, rim, acc_rim, *outer, made["beside", layer + 1])
-            )
+            rim, col_a, col_b = call(next_body, sent, (rim, acc_rim, *outer, mid), {4: pl.ANY})
         else:
             (state,) = call(
                 last_body,
                 [jax.ShapeDtypeStruct(volume.shape, BF16)],
                 (mid, rim, acc_rim, *outer),
                 out_place=HBM,
-                scratch=[VMEM(rim_shape, BF16), pltpu.SemaphoreType.DMA((1 + rows * 2,))],
+                scratch=[VMEM(rim_shape, BF16), pltpu.SemaphoreType.DMA((rows * cols,))],
             )
     return state
 

time: 38.1 us -> 37.6 us (0.987)
  starting transfers between devices: 18.7 us -> 16 us
  waiting for transfers between devices: 5.12 us -> 6.89 us
  Pallas kernels: 14 us -> 14.4 us
    ppermute x6, starting transfers between devices: 11.2 us -> 9.77 us  [swaps(): got_a = lax.ppermute(a, axis, [(n, n ^ 1) for n in range(count)])]
    ppermute x6, waiting for transfers between devices: 2.11 us -> 3.3 us  [swaps(): got_a = lax.ppermute(a, axis, [(n, n ^ 1) for n in range(count)])]
    ppermute x6, starting transfers between devices: 4.42 us -> 3.61 us  [swaps(): return (got_a, lax.ppermute(b, (axis, other), pairs))]
    pallas_call x13 -> x16, Pallas kernels: 14 us -> 14.4 us  [call(): pl.pallas_call(body, out_shape=tuple(outs), in_specs=[pl.BlockSpec(memory...]
    ppermute x2, starting transfers between devices: 3.02 us -> 2.6 us  [shards(): deeper = [lax.ppermute(deep[0], 'trow', [(0, 1), (1, 0)])]]
  transfers between devices with their start and end apart: 14 -> 14, of which waited for: 5 -> 4; matrix products, arithmetic and copies ran while one was open for 0% -> 0% of each run, Pallas kernels for 27% -> 31%
where the time goes in v3:
time: 37.6 us; the launch traced here: 37.5 us
  starting transfers between devices  16 us (43%)
  Pallas kernels  14.4 us (38%)
  waiting for transfers between devices  6.89 us (18%)
    pallas_call x16, Pallas kernels, call(): pl.pallas_call(body, out_shape=tuple(outs), in_specs=[pl.BlockSpec(memory...  14.4 us
    ppermute x6, starting transfers between devices, swaps(): got_a = lax.ppermute(a, axis, [(n, n ^ 1) for n in range(count)])  9.77 us
    ppermute x6, starting transfers between devices, swaps(): return (got_a, lax.ppermute(b, (axis, other), pairs))  3.61 us
    ppermute x6, waiting for transfers between devices, swaps(): got_a = lax.ppermute(a, axis, [(n, n ^ 1) for n in range(count)])  3.3 us
    ppermute x2, starting transfers between devices, shards(): deeper = [lax.ppermute(deep[0], 'trow', [(0, 1), (1, 0)])]  2.6 us
    ppermute x2, waiting for transfers between devices, shards(): deeper = [lax.ppermute(deep[0], 'trow', [(0, 1), (1, 0)])]  2.59 us
    ppermute x6, waiting for transfers between devices, swaps(): return (got_a, lax.ppermute(b, (axis, other), pairs))  1.01 us
  transfers between devices with their start and end apart: 14, of which 4 were waited for; matrix products, arithmetic and copies ran while one was open for 0% of the time, Pallas kernels for 31%

profile of v3, /device:TPU:0, one launch (start us, length us, event | category | flops | bytes accessed | tf_op | source)
XLA Modules:
  0.0 37.5 jit_solution(3854287160933418167)
XLA Ops:
  0.0 1.4 %shard_map.46 = (bf16[2,8,8,9]{3,2,1,0:T(8,128)(2,1)S(1)}, bf16[2,8,8,9]{3,2,1,0:T(8,128)(2,1)S(1)}, f32[2,8]{1,0:T(2,128)S(1)}, bf16[2,256,768]{2,1,0:T(8,128)(...) custom-call(bf16[8,2,4,64,128]{4,3,2,1,0:T(8,128)(2,1)} %x_ref.1, ...), custom_call_target="tpu_custom_call" | custom-call | flops 1000000 | bytes 10000 | tf_op jit(solution)/shard_map/pallas_call | solution.py:29
  1.4 0.5 %collective-permute-start = (bf16[8,2,64,128]{3,2,1,0:T(8,128)(2,1)S(1)}, bf16[8,2,64,128]{3,2,1,0:T(8,128)(2,1)S(1)}, u32[]{:S(2)}, u32[]{:S(2)}) collective-permute-start(bf16[8,2,64,128]{3,2,1,0:T(8,128)(2,1)S(1)} %get-tuple-element.45), channel_id=1, source_target_pairs={{0,2},{2,0},{4,6},{6,4},{1,3},{3,1},{5,7},{7,5},{8,10},{10,8},{12,... | collective-permute-start | bytes 786440 | tf_op jit(solution)/shard_map/ppermute | solution.py:364
  1.9 2.6 %collective-permute-start.1 = (bf16[8,2,64,128]{3,2,1,0:T(8,128)(2,1)S(1)}, bf16[8,2,64,128]{3,2,1,0:T(8,128)(2,1)S(1)}, u32[]{:S(2)}, u32[]{:S(2)}) collective-permute-start(bf16[8,2,64,128]{3,2,1,0:T(8,128)(2,1)S(1)} %get-tuple-element.46), channel_id=1, source_target_pairs={{0,1},{1,0},{2,4},{3,5},{4,2},{5,3},{6,7},{7,6},{8,9},{9,8},{10,12... | collective-permute-start | bytes 786440 | tf_op jit(solution)/shard_map/ppermute | solution.py:365
  4.5 0.6 %shard_map.47 = (bf16[8,2,64,128]{3,2,1,0:T(8,128)(2,1)S(1)}, bf16[8,2,64,128]{3,2,1,0:T(8,128)(2,1)S(1)}) custom-call(bf16[8,2,2,64,128]{4,3,2,1,0:T(8,128)(2,1)S(1)} %get-tuple-element.43.mid_ref.x_ref, bf16[8,2,2,64,128]{4,3,2,1,0:T(8,128)(2,1)S(1)} %get-tuple-element.44.rim_ref.x_ref, bf16[2,256,768]{2,1,0:T(8,128)(2,1)S(1)} %get-tuple-element.47.beside_ref), custom_call_target="tpu_custom_call" | custom-call | flops 1000000 | bytes 10000 | tf_op jit(solution)/shard_map/pallas_call | solution.py:29
  5.1 1.6 %collective-permute-start.3 = (bf16[8,2,64,128]{3,2,1,0:T(8,128)(2,1)S(1)}, bf16[8,2,64,128]{3,2,1,0:T(8,128)(2,1)S(1)}, u32[]{:S(2)}, u32[]{:S(2)}) collective-permute-start(bf16[8,2,64,128]{3,2,1,0:T(8,128)(2,1)S(1)} %get-tuple-element.61), channel_id=1, source_target_pairs={{0,8},{8,0},{16,24},{24,16},{1,9},{9,1},{17,25},{25,17},{2,10},{10... | collective-permute-start | bytes 786440 | tf_op jit(solution)/shard_map/ppermute | solution.py:364
  6.7 0.0 collective-permute-start.4
  6.7 1.1 %shard_map.48 = (bf16[256,768]{1,0:T(8,128)(2,1)S(1)}, bf16[256,768]{1,0:T(8,128)(2,1)S(1)}, bf16[2,256,384]{2,1,0:T(8,128)(2,1)S(1)}, bf16[2,256,24]{2,1,0:T(8,...) custom-call(bf16[2,8,8,9]{3,2,1,0:T(8,128)(2,1)S(1)} %get-tuple-elem, ...), custom_call_target="tpu_custom_call" | custom-call | flops 1000000 | bytes 10000 | tf_op jit(solution)/shard_map/pallas_call | solution.py:29
  7.9 0.0 collective-permute-done.cola_ref
  7.9 1.0 %collective-permute-done.1.colb_ref = bf16[8,2,64,128]{3,2,1,0:T(8,128)(2,1)S(1)} collective-permute-done((bf16[8,2,64,128]{3,2,1,0:T(8,128)(2,1)S(1)}, bf16[8,2,64,128]{3,2,1,0:T(8,128)(2,1)S(1)}, u32[]{:S(2)}, u32[]{:S(2)}) %collective-permute-start.1) | collective-permute-done | bytes 262176 | tf_op jit(solution)/shard_map/ppermute | solution.py:365
  8.9 0.7 %shard_map.49 = (bf16[8,2,64,128]{3,2,1,0:T(8,128)(2,1)S(1)}, bf16[8,2,64,128]{3,2,1,0:T(8,128)(2,1)S(1)}, bf16[2,8,2,64,128]{4,3,2,1,0:T(8,128)(2,1)S(1)}) custom-call(bf16[8,2,2,64,128]{4,3,2,1,0:T(8,128)(2,1)S(1)} %get-tuple-element.43.mid_ref.x_ref, bf16[8,2,2,64,128]{4,3,2,1,0:T(8,128)(2,1)S(1)} %get-tuple-element.44.rim_ref.x_ref, ...), custom_call_target="tpu_custom_call" | custom-call | flops 1000000 | bytes 10000 | tf_op jit(solution)/shard_map/pallas_call | solution.py:29
  9.5 2.2 %collective-permute-start.5 = (bf16[8,2,64,128]{3,2,1,0:T(8,128)(2,1)S(1)}, bf16[8,2,64,128]{3,2,1,0:T(8,128)(2,1)S(1)}, u32[]{:S(2)}, u32[]{:S(2)}) collective-permute-start(bf16[8,2,64,128]{3,2,1,0:T(8,128)(2,1)S(1)} %get-tuple-element.63), channel_id=1, source_target_pairs={{0,8},{8,0},{16,24},{24,16},{1,9},{9,1},{17,25},{25,17},{2,10},{10... | collective-permute-start | bytes 786440 | tf_op jit(solution)/shard_map/ppermute | solution.py:364
  11.8 0.0 collective-permute-start.6
  11.8 0.2 shard_map.51
  11.9 1.4 %collective-permute-start.2 = (bf16[2,8,512]{2,1,0:T(8,128)(2,1)S(1)}, bf16[2,8,512]{2,1,0:T(8,128)(2,1)S(1)}, u32[]{:S(2)}, u32[]{:S(2)}) collective-permute-start(bf16[2,8,512]{2,1,0:T(8,128)(2,1)S(1)} %shard_map.51), channel_id=1, source_target_pairs={{0,1},{1,0},{2,3},{3,2},{4,5},{5,4},{6,7},{7,6},{8,9},{9,8},{10,11... | collective-permute-start | bytes 49160 | tf_op jit(solution)/shard_map/ppermute | solution.py:424
  13.4 2.5 %shard_map.50 = (f32[8,2,2,64,128]{4,3,2,1,0:T(8,128)S(1)}, f32[8,2,2,64,128]{4,3,2,1,0:T(8,128)S(1)}) custom-call(bf16[8,2,2,64,128]{4,3,2,1,0:T(8,128)(2,1)S(1)} %get-tuple-element.43.mid_ref.x_ref, bf16[8,2,2,64,128]{4,3,2,1,0:T(8,128)(2,1)S(1)} %get-tuple-element.44.rim_ref.x_ref, bf16[256,768]{1,0:T(8,128)(2,1)S(1)} %get-tuple-element.51.after_ref.middle_ref, ...), custom_call_target="tpu_custom_call" | custom-call | flops 1000000 | bytes 10000 | tf_op jit(solution)/shard_map/pallas_call | solution.py:29
  15.9 0.0 collective-permute-done.2.rest_0_
  15.9 1.2 %shard_map.52 = (f32[8,2,2,64,128]{4,3,2,1,0:T(8,128)S(1)}, f32[8,2,2,64,128]{4,3,2,1,0:T(8,128)S(1)}) custom-call(bf16[8,2,2,64,128]{4,3,2,1,0:T(8,128)(2,1)S(1)} %get-tuple-element.43.mid_ref.x_ref, bf16[8,2,2,64,128]{4,3,2,1,0:T(8,128)(2,1)S(1)} %get-tuple-element.44.rim_ref.x_ref, ...), custom_call_target="tpu_custom_call", output_to_operand_aliasing={{0}: (6, {}), {1}: (7, {})} | custom-call | flops 1000000 | bytes 10000 | tf_op jit(solution)/shard_map/pallas_call | solution.py:29
  17.1 0.0 collective-permute-done.3.a_ref
  17.1 0.0 collective-permute-done.4.b_ref
  17.1 0.2 shard_map.53.after_ref.mid_ref.x_ref
  17.3 1.7 %collective-permute-done.5.a_ref = bf16[8,2,64,128]{3,2,1,0:T(8,128)(2,1)S(1)} collective-permute-done((bf16[8,2,64,128]{3,2,1,0:T(8,128)(2,1)S(1)}, bf16[8,2,64,128]{3,2,1,0:T(8,128)(2,1)S(1)}, u32[]{:S(2)}, u32[]{:S(2)}) %collective-permute-start.5) | collective-permute-done | bytes 262176 | tf_op jit(solution)/shard_map/ppermute | solution.py:364
  19.1 0.0 collective-permute-done.6.b_ref
  19.1 0.3 shard_map.54
  19.4 0.1 collective-permute-start.7
  19.5 1.0 %collective-permute-start.8 = (bf16[8,2,64,128]{3,2,1,0:T(8,128)(2,1)S(1)}, bf16[8,2,64,128]{3,2,1,0:T(8,128)(2,1)S(1)}, u32[]{:S(2)}, u32[]{:S(2)}) collective-permute-start(bf16[8,2,64,128]{3,2,1,0:T(8,128)(2,1)S(1)} %get-tuple-element.66), channel_id=1, source_target_pairs={{0,1},{1,0},{2,4},{3,5},{4,2},{5,3},{6,7},{7,6},{8,9},{9,8},{10,12... | collective-permute-start | bytes 786440 | tf_op jit(solution)/shard_map/ppermute | solution.py:365
  20.5 0.6 %shard_map.55 = (bf16[8,2,64,128]{3,2,1,0:T(8,128)(2,1)S(1)}, bf16[8,2,64,128]{3,2,1,0:T(8,128)(2,1)S(1)}) custom-call(bf16[8,2,2,64,128]{4,3,2,1,0:T(8,128)(2,1)S(1)} %shard_map.53.after_ref.mid_ref.x_ref, bf16[8,2,2,64,128]{4,3,2,1,0:T(8,128)(2,1)S(1)} %get-tuple-element.64.rim_ref, bf16[2,256,768]{2,1,0:T(8,128)(2,1)S(1)} %get-tuple-element.67.beside_ref), custom_call_target="tpu_custom_call" | custom-call | flops 1000000 | bytes 10000 | tf_op jit(solution)/shard_map/pallas_call | solution.py:29
  21.1 3.2 %collective-permute-start.10 = (bf16[8,2,64,128]{3,2,1,0:T(8,128)(2,1)S(1)}, bf16[8,2,64,128]{3,2,1,0:T(8,128)(2,1)S(1)}, u32[]{:S(2)}, u32[]{:S(2)}) collective-permute-start(bf16[8,2,64,128]{3,2,1,0:T(8,128)(2,1)S(1)} %get-tuple-element.78), channel_id=1, source_target_pairs={{0,8},{8,0},{16,24},{24,16},{1,9},{9,1},{17,25},{25,17},{2,10},{10... | collective-permute-start | bytes 786440 | tf_op jit(solution)/shard_map/ppermute | solution.py:364
  24.3 0.0 collective-permute-start.11
  24.3 2.5 %shard_map.56 = (f32[8,2,2,64,128]{4,3,2,1,0:T(8,128)S(1)}, f32[8,2,2,64,128]{4,3,2,1,0:T(8,128)S(1)}) custom-call(bf16[8,2,2,64,128]{4,3,2,1,0:T(8,128)(2,1)S(1)} %shard_map.53.after_ref.mid_ref.x_ref, bf16[8,2,2,64,128]{4,3,2,1,0:T(8,128)(2,1)S(1)} %get-tuple-element.64.rim_ref, bf16[256,768]{1,0:T(8,128)(2,1)S(1)} %get-tuple-element.68.middle_ref, ...), custom_call_target="tpu_custom_call" | custom-call | flops 1000000 | bytes 10000 | tf_op jit(solution)/shard_map/pallas_call | solution.py:29
  26.8 0.0 collective-permute-done.7.cola_ref
  26.8 0.0 collective-permute-done.8.colb_ref
  26.8 0.6 %shard_map.57 = (bf16[8,2,64,128]{3,2,1,0:T(8,128)(2,1)S(1)}, bf16[8,2,64,128]{3,2,1,0:T(8,128)(2,1)S(1)}, bf16[2,8,2,64,128]{4,3,2,1,0:T(8,128)(2,1)S(1)}) custom-call(bf16[8,2,2,64,128]{4,3,2,1,0:T(8,128)(2,1)S(1)} %shard_map.53.after_ref.mid_ref.x_ref, bf16[8,2,2,64,128]{4,3,2,1,0:T(8,128)(2,1)S(1)} %get-tuple-element.64.rim_ref, ...), custom_call_target="tpu_custom_call" | custom-call | flops 1000000 | bytes 10000 | tf_op jit(solution)/shard_map/pallas_call | solution.py:29
  27.5 2.1 %collective-permute-start.12 = (bf16[8,2,64,128]{3,2,1,0:T(8,128)(2,1)S(1)}, bf16[8,2,64,128]{3,2,1,0:T(8,128)(2,1)S(1)}, u32[]{:S(2)}, u32[]{:S(2)}) collective-permute-start(bf16[8,2,64,128]{3,2,1,0:T(8,128)(2,1)S(1)} %get-tuple-element.80), channel_id=1, source_target_pairs={{0,8},{8,0},{16,24},{24,16},{1,9},{9,1},{17,25},{25,17},{2,10},{10... | collective-permute-start | bytes 786440 | tf_op jit(solution)/shard_map/ppermute | solution.py:364
  29.6 0.0 collective-permute-start.13
  29.6 0.2 shard_map.58
  29.8 1.2 %collective-permute-start.9 = (bf16[2,8,512]{2,1,0:T(8,128)(2,1)S(1)}, bf16[2,8,512]{2,1,0:T(8,128)(2,1)S(1)}, u32[]{:S(2)}, u32[]{:S(2)}) collective-permute-start(bf16[2,8,512]{2,1,0:T(8,128)(2,1)S(1)} %shard_map.58), channel_id=1, source_target_pairs={{0,1},{1,0},{2,3},{3,2},{4,5},{5,4},{6,7},{7,6},{8,9},{9,8},{10,11... | collective-permute-start | bytes 49160 | tf_op jit(solution)/shard_map/ppermute | solution.py:424
  30.9 2.6 %collective-permute-done.9.rest_0_ = bf16[2,8,512]{2,1,0:T(8,128)(2,1)S(1)} collective-permute-done((bf16[2,8,512]{2,1,0:T(8,128)(2,1)S(1)}, bf16[2,8,512]{2,1,0:T(8,128)(2,1)S(1)}, u32[]{:S(2)}, u32[]{:S(2)}) %collective-permute-start.9) | collective-permute-done | bytes 16416 | tf_op jit(solution)/shard_map/ppermute | solution.py:424
  33.5 1.1 %shard_map.59 = (f32[8,2,2,64,128]{4,3,2,1,0:T(8,128)S(1)}, f32[8,2,2,64,128]{4,3,2,1,0:T(8,128)S(1)}) custom-call(bf16[8,2,2,64,128]{4,3,2,1,0:T(8,128)(2,1)S(1)} %shard_map.53.after_ref.mid_ref.x_ref, bf16[8,2,2,64,128]{4,3,2,1,0:T(8,128)(2,1)S(1)} %get-tuple-element.64.rim_ref, ...), custom_call_target="tpu_custom_call", output_to_operand_aliasing={{0}: (6, {}), {1}: (7, {})} | custom-call | flops 1000000 | bytes 10000 | tf_op jit(solution)/shard_map/pallas_call | solution.py:29
  34.6 0.0 collective-permute-done.10.a_ref
  34.7 0.0 collective-permute-done.11.b_ref
  34.7 0.2 shard_map.60.mid_ref
  34.9 1.5 %collective-permute-done.12.a_ref = bf16[8,2,64,128]{3,2,1,0:T(8,128)(2,1)S(1)} collective-permute-done((bf16[8,2,64,128]{3,2,1,0:T(8,128)(2,1)S(1)}, bf16[8,2,64,128]{3,2,1,0:T(8,128)(2,1)S(1)}, u32[]{:S(2)}, u32[]{:S(2)}) %collective-permute-start.12) | collective-permute-done | bytes 262176 | tf_op jit(solution)/shard_map/ppermute | solution.py:364
  36.5 0.0 collective-permute-done.13.b_ref
  36.5 1.0 %shard_map.61 = bf16[8,2,4,64,128]{4,3,2,1,0:T(8,128)(2,1)} custom-call(bf16[8,2,2,64,128]{4,3,2,1,0:T(8,128)(2,1)S(1)} %shard_map.60.mid_ref, bf16[8,2,2,64,128]{4,3,2,1,0:T(8,128)(2,1)S(1)} %get-tuple-element.64.rim_ref, f32[8,2,2,64,128]{4,3,2,1,0:T(8,128)S(1)} %get-tuple-element.79.acc_ref, bf16[8,2,64,128]{3,2,1,0:T(8,128)(2,1)S(1)} %collective-permute-done.12.a_ref, ...), custom_call_target="tpu_custom_call" | custom-call | flops 1000000 | bytes 10000 | tf_op jit(solution)/shard_map/pallas_call | solution.py:29
Async XLA Ops:
  1.4 6.5 %collective-permute-start = (bf16[8,2,64,128]{3,2,1,0:T(8,128)(2,1)S(1)}, bf16[8,2,64,128]{3,2,1,0:T(8,128)(2,1)S(1)}, u32[]{:S(2)}, u32[]{:S(2)}) collective-permute-start(bf16[8,2,64,128]{3,2,1,0:T(8,128)(2,1)S(1)} %get-tuple-element.45), channel_id=1, source_target_pairs={{0,2},{2,0},{4,6},{6,4},{1,3},{3,1},{5,7},{7,5},{8,10},{10,8},{12,... | collective-permute-start | bytes 786440 | tf_op jit(solution)/shard_map/ppermute | solution.py:364
  1.9 6.9 %collective-permute-start.1 = (bf16[8,2,64,128]{3,2,1,0:T(8,128)(2,1)S(1)}, bf16[8,2,64,128]{3,2,1,0:T(8,128)(2,1)S(1)}, u32[]{:S(2)}, u32[]{:S(2)}) collective-permute-start(bf16[8,2,64,128]{3,2,1,0:T(8,128)(2,1)S(1)} %get-tuple-element.46), channel_id=1, source_target_pairs={{0,1},{1,0},{2,4},{3,5},{4,2},{5,3},{6,7},{7,6},{8,9},{9,8},{10,12... | collective-permute-start | bytes 786440 | tf_op jit(solution)/shard_map/ppermute | solution.py:365
  5.1 12.0 %collective-permute-start.3 = (bf16[8,2,64,128]{3,2,1,0:T(8,128)(2,1)S(1)}, bf16[8,2,64,128]{3,2,1,0:T(8,128)(2,1)S(1)}, u32[]{:S(2)}, u32[]{:S(2)}) collective-permute-start(bf16[8,2,64,128]{3,2,1,0:T(8,128)(2,1)S(1)} %get-tuple-element.61), channel_id=1, source_target_pairs={{0,8},{8,0},{16,24},{24,16},{1,9},{9,1},{17,25},{25,17},{2,10},{10... | collective-permute-start | bytes 786440 | tf_op jit(solution)/shard_map/ppermute | solution.py:364
  6.7 10.4 %collective-permute-start.4 = (bf16[8,2,64,128]{3,2,1,0:T(8,128)(2,1)S(1)}, bf16[8,2,64,128]{3,2,1,0:T(8,128)(2,1)S(1)}, u32[]{:S(2)}, u32[]{:S(2)}) collective-permute-start(bf16[8,2,64,128]{3,2,1,0:T(8,128)(2,1)S(1)} %get-tuple-element.50.after_ref), channel_id=1, source_target_pairs={{0,2},{2,0},{4,6},{6,4},{8,16},{10,18},{12,20},{14,22},{16,8},{18,... | collective-permute-start | bytes 786440 | tf_op jit(solution)/shard_map/ppermute | solution.py:365
  9.5 9.5 %collective-permute-start.5 = (bf16[8,2,64,128]{3,2,1,0:T(8,128)(2,1)S(1)}, bf16[8,2,64,128]{3,2,1,0:T(8,128)(2,1)S(1)}, u32[]{:S(2)}, u32[]{:S(2)}) collective-permute-start(bf16[8,2,64,128]{3,2,1,0:T(8,128)(2,1)S(1)} %get-tuple-element.63), channel_id=1, source_target_pairs={{0,8},{8,0},{16,24},{24,16},{1,9},{9,1},{17,25},{25,17},{2,10},{10... | collective-permute-start | bytes 786440 | tf_op jit(solution)/shard_map/ppermute | solution.py:364
  11.8 7.3 %collective-permute-start.6 = (bf16[8,2,64,128]{3,2,1,0:T(8,128)(2,1)S(1)}, bf16[8,2,64,128]{3,2,1,0:T(8,128)(2,1)S(1)}, u32[]{:S(2)}, u32[]{:S(2)}) collective-permute-start(bf16[8,2,64,128]{3,2,1,0:T(8,128)(2,1)S(1)} %get-tuple-element.57.after_ref), channel_id=1, source_target_pairs={{0,2},{2,0},{4,6},{6,4},{8,16},{10,18},{12,20},{14,22},{16,8},{18,... | collective-permute-start | bytes 786440 | tf_op jit(solution)/shard_map/ppermute | solution.py:365
  11.9 4.0 %collective-permute-start.2 = (bf16[2,8,512]{2,1,0:T(8,128)(2,1)S(1)}, bf16[2,8,512]{2,1,0:T(8,128)(2,1)S(1)}, u32[]{:S(2)}, u32[]{:S(2)}) collective-permute-start(bf16[2,8,512]{2,1,0:T(8,128)(2,1)S(1)} %shard_map.51), channel_id=1, source_target_pairs={{0,1},{1,0},{2,3},{3,2},{4,5},{5,4},{6,7},{7,6},{8,9},{9,8},{10,11... | collective-permute-start | bytes 49160 | tf_op jit(solution)/shard_map/ppermute | solution.py:424
  19.4 7.4 %collective-permute-start.7 = (bf16[8,2,64,128]{3,2,1,0:T(8,128)(2,1)S(1)}, bf16[8,2,64,128]{3,2,1,0:T(8,128)(2,1)S(1)}, u32[]{:S(2)}, u32[]{:S(2)}) collective-permute-start(bf16[8,2,64,128]{3,2,1,0:T(8,128)(2,1)S(1)} %get-tuple-element.65), channel_id=1, source_target_pairs={{0,2},{2,0},{4,6},{6,4},{1,3},{3,1},{5,7},{7,5},{8,10},{10,8},{12,... | collective-permute-start | bytes 786440 | tf_op jit(solution)/shard_map/ppermute | solution.py:364
  19.5 7.3 %collective-permute-start.8 = (bf16[8,2,64,128]{3,2,1,0:T(8,128)(2,1)S(1)}, bf16[8,2,64,128]{3,2,1,0:T(8,128)(2,1)S(1)}, u32[]{:S(2)}, u32[]{:S(2)}) collective-permute-start(bf16[8,2,64,128]{3,2,1,0:T(8,128)(2,1)S(1)} %get-tuple-element.66), channel_id=1, source_target_pairs={{0,1},{1,0},{2,4},{3,5},{4,2},{5,3},{6,7},{7,6},{8,9},{9,8},{10,12... | collective-permute-start | bytes 786440 | tf_op jit(solution)/shard_map/ppermute | solution.py:365
  21.1 13.6 %collective-permute-start.10 = (bf16[8,2,64,128]{3,2,1,0:T(8,128)(2,1)S(1)}, bf16[8,2,64,128]{3,2,1,0:T(8,128)(2,1)S(1)}, u32[]{:S(2)}, u32[]{:S(2)}) collective-permute-start(bf16[8,2,64,128]{3,2,1,0:T(8,128)(2,1)S(1)} %get-tuple-element.78), channel_id=1, source_target_pairs={{0,8},{8,0},{16,24},{24,16},{1,9},{9,1},{17,25},{25,17},{2,10},{10... | collective-permute-start | bytes 786440 | tf_op jit(solution)/shard_map/ppermute | solution.py:364
  24.3 10.4 %collective-permute-start.11 = (bf16[8,2,64,128]{3,2,1,0:T(8,128)(2,1)S(1)}, bf16[8,2,64,128]{3,2,1,0:T(8,128)(2,1)S(1)}, u32[]{:S(2)}, u32[]{:S(2)}) collective-permute-start(bf16[8,2,64,128]{3,2,1,0:T(8,128)(2,1)S(1)} %get-tuple-element.71.after_ref), channel_id=1, source_target_pairs={{0,2},{2,0},{4,6},{6,4},{8,16},{10,18},{12,20},{14,22},{16,8},{18,... | collective-permute-start | bytes 786440 | tf_op jit(solution)/shard_map/ppermute | solution.py:365
  27.5 8.9 %collective-permute-start.12 = (bf16[8,2,64,128]{3,2,1,0:T(8,128)(2,1)S(1)}, bf16[8,2,64,128]{3,2,1,0:T(8,128)(2,1)S(1)}, u32[]{:S(2)}, u32[]{:S(2)}) collective-permute-start(bf16[8,2,64,128]{3,2,1,0:T(8,128)(2,1)S(1)} %get-tuple-element.80), channel_id=1, source_target_pairs={{0,8},{8,0},{16,24},{24,16},{1,9},{9,1},{17,25},{25,17},{2,10},{10... | collective-permute-start | bytes 786440 | tf_op jit(solution)/shard_map/ppermute | solution.py:364
  29.6 6.9 %collective-permute-start.13 = (bf16[8,2,64,128]{3,2,1,0:T(8,128)(2,1)S(1)}, bf16[8,2,64,128]{3,2,1,0:T(8,128)(2,1)S(1)}, u32[]{:S(2)}, u32[]{:S(2)}) collective-permute-start(bf16[8,2,64,128]{3,2,1,0:T(8,128)(2,1)S(1)} %get-tuple-element.76.after_ref), channel_id=1, source_target_pairs={{0,2},{2,0},{4,6},{6,4},{8,16},{10,18},{12,20},{14,22},{16,8},{18,... | collective-permute-start | bytes 786440 | tf_op jit(solution)/shard_map/ppermute | solution.py:365
  29.8 3.7 %collective-permute-start.9 = (bf16[2,8,512]{2,1,0:T(8,128)(2,1)S(1)}, bf16[2,8,512]{2,1,0:T(8,128)(2,1)S(1)}, u32[]{:S(2)}, u32[]{:S(2)}) collective-permute-start(bf16[2,8,512]{2,1,0:T(8,128)(2,1)S(1)} %shard_map.58), channel_id=1, source_target_pairs={{0,1},{1,0},{2,3},{3,2},{4,5},{5,4},{6,7},{7,6},{8,9},{9,8},{10,11... | collective-permute-start | bytes 49160 | tf_op jit(solution)/shard_map/ppermute | solution.py:424

commit v4 on v3

--- a/solution.py
+++ b/solution.py
@@ -397,7 +397,7 @@
         inner = swaps(sum_a, sum_b, "srow", "scol")
         if layer == 0:
             late = [(kind, n) for n in range(layers) for kind in kinds]
-            made |= build([part for part in late if part not in early], src_w, tgt_w, sum_b)
+            made |= build([part for part in late if part not in early], src_w, tgt_w, sum_a)
         operator = {kind: made[kind, layer] for kind in kinds}
 
         def own(after):
@@ -409,7 +409,7 @@
                 scratch=[VMEM((depth // BAND, 3, channels * BAND, cols * width), BF16)],
             )
 
-        accs = own(sum_b) if layer else None
+        accs = own(sum_a) if layer else None
         a, b, side = call(
             edge_body,
             [owed_rim, owed_rim, VMEM((2, *line.shape), BF16)],
@@ -418,13 +418,13 @@
         )
         outer = swaps(a, b, "srow", "scol")
         deep = call(
-            depth_body, [VMEM((rows, channels, cols * width), BF16)] * deep_swaps, (mid, rim, b), {2: pl.ANY}
+            depth_body, [VMEM((rows, channels, cols * width), BF16)] * deep_swaps, (mid, rim, a), {2: pl.ANY}
         )
         if deep_swaps == 1:
             deeper = [lax.ppermute(deep[0], "trow", [(0, 1), (1, 0)])]
         else:
             deeper = swaps(*deep, "trow", "scol")
-        accs = accs or own(b)
+        accs = accs or own(a)
         acc_mid, acc_rim = call(
             rest_body,
             [VMEM(mid_shape, F32), VMEM(rim_shape, F32)],

time: 37.6 us -> 38.3 us (1.019)
  starting transfers between devices: 16 us -> 18.1 us
  waiting for transfers between devices: 6.89 us -> 5.33 us
    ppermute x6, waiting for transfers between devices: 1.01 us -> 0.02 us  [swaps(): return (got_a, lax.ppermute(b, (axis, other), pairs))]
    ppermute x6, starting transfers between devices: 9.77 us -> 10.7 us  [swaps(): got_a = lax.ppermute(a, axis, [(n, n ^ 1) for n in range(count)])]
    ppermute x6, starting transfers between devices: 3.61 us -> 4.46 us  [swaps(): return (got_a, lax.ppermute(b, (axis, other), pairs))]
  transfers between devices with their start and end apart: 14 -> 14, of which waited for: 4 -> 3; matrix products, arithmetic and copies ran while one was open for 0% -> 0% of each run, Pallas kernels for 31% -> 31%
where the time goes in v4:
time: 38.3 us; the launch traced here: 38.1 us
  starting transfers between devices  18.1 us (47%)
  Pallas kernels  14.4 us (38%)
  waiting for transfers between devices  5.33 us (14%)
    pallas_call x16, Pallas kernels, call(): pl.pallas_call(body, out_shape=tuple(outs), in_specs=[pl.BlockSpec(memory...  14.4 us
    ppermute x6, starting transfers between devices, swaps(): got_a = lax.ppermute(a, axis, [(n, n ^ 1) for n in range(count)])  10.7 us
    ppermute x6, starting transfers between devices, swaps(): return (got_a, lax.ppermute(b, (axis, other), pairs))  4.46 us
    ppermute x6, waiting for transfers between devices, swaps(): got_a = lax.ppermute(a, axis, [(n, n ^ 1) for n in range(count)])  3 us
    ppermute x2, starting transfers between devices, shards(): deeper = [lax.ppermute(deep[0], 'trow', [(0, 1), (1, 0)])]  2.97 us
    ppermute x2, waiting for transfers between devices, shards(): deeper = [lax.ppermute(deep[0], 'trow', [(0, 1), (1, 0)])]  2.31 us
  transfers between devices with their start and end apart: 14, of which 3 were waited for; matrix products, arithmetic and copies ran while one was open for 0% of the time, Pallas kernels for 31%

profile of v4, /device:TPU:0, one launch (start us, length us, event | category | flops | bytes accessed | tf_op | source)
XLA Modules:
  0.0 38.1 jit_solution(5186643103364856229)
XLA Ops:
  0.0 1.4 %shard_map.46 = (bf16[2,8,8,9]{3,2,1,0:T(8,128)(2,1)S(1)}, bf16[2,8,8,9]{3,2,1,0:T(8,128)(2,1)S(1)}, f32[2,8]{1,0:T(2,128)S(1)}, bf16[2,256,768]{2,1,0:T(8,128)(...) custom-call(bf16[8,2,4,64,128]{4,3,2,1,0:T(8,128)(2,1)} %x_ref.1, ...), custom_call_target="tpu_custom_call" | custom-call | flops 1000000 | bytes 10000 | tf_op jit(solution)/shard_map/pallas_call | solution.py:29
  1.4 0.5 %collective-permute-start = (bf16[8,2,64,128]{3,2,1,0:T(8,128)(2,1)S(1)}, bf16[8,2,64,128]{3,2,1,0:T(8,128)(2,1)S(1)}, u32[]{:S(2)}, u32[]{:S(2)}) collective-permute-start(bf16[8,2,64,128]{3,2,1,0:T(8,128)(2,1)S(1)} %get-tuple-element.45), channel_id=1, source_target_pairs={{0,2},{2,0},{4,6},{6,4},{1,3},{3,1},{5,7},{7,5},{8,10},{10,8},{12,... | collective-permute-start | bytes 786440 | tf_op jit(solution)/shard_map/ppermute | solution.py:364
  1.9 2.6 %collective-permute-start.1 = (bf16[8,2,64,128]{3,2,1,0:T(8,128)(2,1)S(1)}, bf16[8,2,64,128]{3,2,1,0:T(8,128)(2,1)S(1)}, u32[]{:S(2)}, u32[]{:S(2)}) collective-permute-start(bf16[8,2,64,128]{3,2,1,0:T(8,128)(2,1)S(1)} %get-tuple-element.46), channel_id=1, source_target_pairs={{0,1},{1,0},{2,4},{3,5},{4,2},{5,3},{6,7},{7,6},{8,9},{9,8},{10,12... | collective-permute-start | bytes 786440 | tf_op jit(solution)/shard_map/ppermute | solution.py:365
  4.5 0.6 %shard_map.47 = (bf16[8,2,64,128]{3,2,1,0:T(8,128)(2,1)S(1)}, bf16[8,2,64,128]{3,2,1,0:T(8,128)(2,1)S(1)}) custom-call(bf16[8,2,2,64,128]{4,3,2,1,0:T(8,128)(2,1)S(1)} %get-tuple-element.43.mid_ref.x_ref, bf16[8,2,2,64,128]{4,3,2,1,0:T(8,128)(2,1)S(1)} %get-tuple-element.44.rim_ref.x_ref, bf16[2,256,768]{2,1,0:T(8,128)(2,1)S(1)} %get-tuple-element.47.beside_ref), custom_call_target="tpu_custom_call" | custom-call | flops 1000000 | bytes 10000 | tf_op jit(solution)/shard_map/pallas_call | solution.py:29
  5.1 0.2 collective-permute-start.4
  5.2 3.1 %collective-permute-start.3 = (bf16[8,2,64,128]{3,2,1,0:T(8,128)(2,1)S(1)}, bf16[8,2,64,128]{3,2,1,0:T(8,128)(2,1)S(1)}, u32[]{:S(2)}, u32[]{:S(2)}) collective-permute-start(bf16[8,2,64,128]{3,2,1,0:T(8,128)(2,1)S(1)} %get-tuple-element.50.after_ref), channel_id=1, source_target_pairs={{0,8},{8,0},{16,24},{24,16},{1,9},{9,1},{17,25},{25,17},{2,10},{10... | collective-permute-start | bytes 786440 | tf_op jit(solution)/shard_map/ppermute | solution.py:364
  8.3 1.1 %shard_map.48 = (bf16[256,768]{1,0:T(8,128)(2,1)S(1)}, bf16[256,768]{1,0:T(8,128)(2,1)S(1)}, bf16[2,256,384]{2,1,0:T(8,128)(2,1)S(1)}, bf16[2,256,24]{2,1,0:T(8,...) custom-call(bf16[2,8,8,9]{3,2,1,0:T(8,128)(2,1)S(1)} %get-tuple-elem, ...), custom_call_target="tpu_custom_call" | custom-call | flops 1000000 | bytes 10000 | tf_op jit(solution)/shard_map/pallas_call | solution.py:29
  9.4 0.0 collective-permute-done.cola_ref
  9.4 0.0 collective-permute-done.1.colb_ref
  9.5 0.7 %shard_map.49 = (bf16[8,2,64,128]{3,2,1,0:T(8,128)(2,1)S(1)}, bf16[8,2,64,128]{3,2,1,0:T(8,128)(2,1)S(1)}, bf16[2,8,2,64,128]{4,3,2,1,0:T(8,128)(2,1)S(1)}) custom-call(bf16[8,2,2,64,128]{4,3,2,1,0:T(8,128)(2,1)S(1)} %get-tuple-element.43.mid_ref.x_ref, bf16[8,2,2,64,128]{4,3,2,1,0:T(8,128)(2,1)S(1)} %get-tuple-element.44.rim_ref.x_ref, ...), custom_call_target="tpu_custom_call" | custom-call | flops 1000000 | bytes 10000 | tf_op jit(solution)/shard_map/pallas_call | solution.py:29
  10.1 0.1 collective-permute-start.6
  10.2 3.0 %collective-permute-start.5 = (bf16[8,2,64,128]{3,2,1,0:T(8,128)(2,1)S(1)}, bf16[8,2,64,128]{3,2,1,0:T(8,128)(2,1)S(1)}, u32[]{:S(2)}, u32[]{:S(2)}) collective-permute-start(bf16[8,2,64,128]{3,2,1,0:T(8,128)(2,1)S(1)} %get-tuple-element.57.after_ref), channel_id=1, source_target_pairs={{0,8},{8,0},{16,24},{24,16},{1,9},{9,1},{17,25},{25,17},{2,10},{10... | collective-permute-start | bytes 786440 | tf_op jit(solution)/shard_map/ppermute | solution.py:364
  13.3 0.2 shard_map.51
  13.4 1.5 %collective-permute-start.2 = (bf16[2,8,512]{2,1,0:T(8,128)(2,1)S(1)}, bf16[2,8,512]{2,1,0:T(8,128)(2,1)S(1)}, u32[]{:S(2)}, u32[]{:S(2)}) collective-permute-start(bf16[2,8,512]{2,1,0:T(8,128)(2,1)S(1)} %shard_map.51), channel_id=1, source_target_pairs={{0,1},{1,0},{2,3},{3,2},{4,5},{5,4},{6,7},{7,6},{8,9},{9,8},{10,11... | collective-permute-start | bytes 49160 | tf_op jit(solution)/shard_map/ppermute | solution.py:424
  15.0 2.5 %shard_map.50 = (f32[8,2,2,64,128]{4,3,2,1,0:T(8,128)S(1)}, f32[8,2,2,64,128]{4,3,2,1,0:T(8,128)S(1)}) custom-call(bf16[8,2,2,64,128]{4,3,2,1,0:T(8,128)(2,1)S(1)} %get-tuple-element.43.mid_ref.x_ref, bf16[8,2,2,64,128]{4,3,2,1,0:T(8,128)(2,1)S(1)} %get-tuple-element.44.rim_ref.x_ref, bf16[256,768]{1,0:T(8,128)(2,1)S(1)} %get-tuple-element.51.after_ref.middle_ref, ...), custom_call_target="tpu_custom_call" | custom-call | flops 1000000 | bytes 10000 | tf_op jit(solution)/shard_map/pallas_call | solution.py:29
  17.5 0.0 collective-permute-done.2.rest_0_
  17.5 1.2 %shard_map.52 = (f32[8,2,2,64,128]{4,3,2,1,0:T(8,128)S(1)}, f32[8,2,2,64,128]{4,3,2,1,0:T(8,128)S(1)}) custom-call(bf16[8,2,2,64,128]{4,3,2,1,0:T(8,128)(2,1)S(1)} %get-tuple-element.43.mid_ref.x_ref, bf16[8,2,2,64,128]{4,3,2,1,0:T(8,128)(2,1)S(1)} %get-tuple-element.44.rim_ref.x_ref, ...), custom_call_target="tpu_custom_call", output_to_operand_aliasing={{0}: (6, {}), {1}: (7, {})} | custom-call | flops 1000000 | bytes 10000 | tf_op jit(solution)/shard_map/pallas_call | solution.py:29
  18.7 0.0 collective-permute-done.4.b_ref
  18.7 0.0 collective-permute-done.3.a_ref
  18.7 0.2 shard_map.53.after_ref.mid_ref.x_ref
  18.9 0.0 collective-permute-done.6.b_ref
  18.9 1.3 %collective-permute-done.5.a_ref = bf16[8,2,64,128]{3,2,1,0:T(8,128)(2,1)S(1)} collective-permute-done((bf16[8,2,64,128]{3,2,1,0:T(8,128)(2,1)S(1)}, bf16[8,2,64,128]{3,2,1,0:T(8,128)(2,1)S(1)}, u32[]{:S(2)}, u32[]{:S(2)}) %collective-permute-start.5) | collective-permute-done | bytes 262176 | tf_op jit(solution)/shard_map/ppermute | solution.py:364
  20.2 0.3 shard_map.54
  20.6 0.1 collective-permute-start.7
  20.6 1.5 %collective-permute-start.8 = (bf16[8,2,64,128]{3,2,1,0:T(8,128)(2,1)S(1)}, bf16[8,2,64,128]{3,2,1,0:T(8,128)(2,1)S(1)}, u32[]{:S(2)}, u32[]{:S(2)}) collective-permute-start(bf16[8,2,64,128]{3,2,1,0:T(8,128)(2,1)S(1)} %get-tuple-element.66), channel_id=1, source_target_pairs={{0,1},{1,0},{2,4},{3,5},{4,2},{5,3},{6,7},{7,6},{8,9},{9,8},{10,12... | collective-permute-start | bytes 786440 | tf_op jit(solution)/shard_map/ppermute | solution.py:365
  22.1 0.6 %shard_map.55 = (bf16[8,2,64,128]{3,2,1,0:T(8,128)(2,1)S(1)}, bf16[8,2,64,128]{3,2,1,0:T(8,128)(2,1)S(1)}) custom-call(bf16[8,2,2,64,128]{4,3,2,1,0:T(8,128)(2,1)S(1)} %shard_map.53.after_ref.mid_ref.x_ref, bf16[8,2,2,64,128]{4,3,2,1,0:T(8,128)(2,1)S(1)} %get-tuple-element.64.rim_ref, bf16[2,256,768]{2,1,0:T(8,128)(2,1)S(1)} %get-tuple-element.67.beside_ref), custom_call_target="tpu_custom_call" | custom-call | flops 1000000 | bytes 10000 | tf_op jit(solution)/shard_map/pallas_call | solution.py:29
  22.7 0.1 collective-permute-start.11
  22.8 2.3 %collective-permute-start.10 = (bf16[8,2,64,128]{3,2,1,0:T(8,128)(2,1)S(1)}, bf16[8,2,64,128]{3,2,1,0:T(8,128)(2,1)S(1)}, u32[]{:S(2)}, u32[]{:S(2)}) collective-permute-start(bf16[8,2,64,128]{3,2,1,0:T(8,128)(2,1)S(1)} %get-tuple-element.71.after_ref), channel_id=1, source_target_pairs={{0,8},{8,0},{16,24},{24,16},{1,9},{9,1},{17,25},{25,17},{2,10},{10... | collective-permute-start | bytes 786440 | tf_op jit(solution)/shard_map/ppermute | solution.py:364
  25.1 2.5 %shard_map.56 = (f32[8,2,2,64,128]{4,3,2,1,0:T(8,128)S(1)}, f32[8,2,2,64,128]{4,3,2,1,0:T(8,128)S(1)}) custom-call(bf16[8,2,2,64,128]{4,3,2,1,0:T(8,128)(2,1)S(1)} %shard_map.53.after_ref.mid_ref.x_ref, bf16[8,2,2,64,128]{4,3,2,1,0:T(8,128)(2,1)S(1)} %get-tuple-element.64.rim_ref, bf16[256,768]{1,0:T(8,128)(2,1)S(1)} %get-tuple-element.68.middle_ref, ...), custom_call_target="tpu_custom_call" | custom-call | flops 1000000 | bytes 10000 | tf_op jit(solution)/shard_map/pallas_call | solution.py:29
  27.6 0.0 collective-permute-done.7.cola_ref
  27.6 0.0 collective-permute-done.8.colb_ref
  27.6 0.6 %shard_map.57 = (bf16[8,2,64,128]{3,2,1,0:T(8,128)(2,1)S(1)}, bf16[8,2,64,128]{3,2,1,0:T(8,128)(2,1)S(1)}, bf16[2,8,2,64,128]{4,3,2,1,0:T(8,128)(2,1)S(1)}) custom-call(bf16[8,2,2,64,128]{4,3,2,1,0:T(8,128)(2,1)S(1)} %shard_map.53.after_ref.mid_ref.x_ref, bf16[8,2,2,64,128]{4,3,2,1,0:T(8,128)(2,1)S(1)} %get-tuple-element.64.rim_ref, ...), custom_call_target="tpu_custom_call" | custom-call | flops 1000000 | bytes 10000 | tf_op jit(solution)/shard_map/pallas_call | solution.py:29
  28.2 0.1 collective-permute-start.13
  28.3 1.7 %collective-permute-start.12 = (bf16[8,2,64,128]{3,2,1,0:T(8,128)(2,1)S(1)}, bf16[8,2,64,128]{3,2,1,0:T(8,128)(2,1)S(1)}, u32[]{:S(2)}, u32[]{:S(2)}) collective-permute-start(bf16[8,2,64,128]{3,2,1,0:T(8,128)(2,1)S(1)} %get-tuple-element.76.after_ref), channel_id=1, source_target_pairs={{0,8},{8,0},{16,24},{24,16},{1,9},{9,1},{17,25},{25,17},{2,10},{10... | collective-permute-start | bytes 786440 | tf_op jit(solution)/shard_map/ppermute | solution.py:364
  30.1 0.2 shard_map.58
  30.2 1.4 %collective-permute-start.9 = (bf16[2,8,512]{2,1,0:T(8,128)(2,1)S(1)}, bf16[2,8,512]{2,1,0:T(8,128)(2,1)S(1)}, u32[]{:S(2)}, u32[]{:S(2)}) collective-permute-start(bf16[2,8,512]{2,1,0:T(8,128)(2,1)S(1)} %shard_map.58), channel_id=1, source_target_pairs={{0,1},{1,0},{2,3},{3,2},{4,5},{5,4},{6,7},{7,6},{8,9},{9,8},{10,11... | collective-permute-start | bytes 49160 | tf_op jit(solution)/shard_map/ppermute | solution.py:424
  31.7 2.3 %collective-permute-done.9.rest_0_ = bf16[2,8,512]{2,1,0:T(8,128)(2,1)S(1)} collective-permute-done((bf16[2,8,512]{2,1,0:T(8,128)(2,1)S(1)}, bf16[2,8,512]{2,1,0:T(8,128)(2,1)S(1)}, u32[]{:S(2)}, u32[]{:S(2)}) %collective-permute-start.9) | collective-permute-done | bytes 16416 | tf_op jit(solution)/shard_map/ppermute | solution.py:424
  34.0 1.1 %shard_map.59 = (f32[8,2,2,64,128]{4,3,2,1,0:T(8,128)S(1)}, f32[8,2,2,64,128]{4,3,2,1,0:T(8,128)S(1)}) custom-call(bf16[8,2,2,64,128]{4,3,2,1,0:T(8,128)(2,1)S(1)} %shard_map.53.after_ref.mid_ref.x_ref, bf16[8,2,2,64,128]{4,3,2,1,0:T(8,128)(2,1)S(1)} %get-tuple-element.64.rim_ref, ...), custom_call_target="tpu_custom_call", output_to_operand_aliasing={{0}: (6, {}), {1}: (7, {})} | custom-call | flops 1000000 | bytes 10000 | tf_op jit(solution)/shard_map/pallas_call | solution.py:29
  35.1 0.0 collective-permute-done.11.b_ref
  35.1 0.0 collective-permute-done.10.a_ref
  35.1 0.2 shard_map.60.mid_ref
  35.4 0.0 collective-permute-done.13.b_ref
  35.4 1.7 %collective-permute-done.12.a_ref = bf16[8,2,64,128]{3,2,1,0:T(8,128)(2,1)S(1)} collective-permute-done((bf16[8,2,64,128]{3,2,1,0:T(8,128)(2,1)S(1)}, bf16[8,2,64,128]{3,2,1,0:T(8,128)(2,1)S(1)}, u32[]{:S(2)}, u32[]{:S(2)}) %collective-permute-start.12) | collective-permute-done | bytes 262176 | tf_op jit(solution)/shard_map/ppermute | solution.py:364
  37.1 1.0 %shard_map.61 = bf16[8,2,4,64,128]{4,3,2,1,0:T(8,128)(2,1)} custom-call(bf16[8,2,2,64,128]{4,3,2,1,0:T(8,128)(2,1)S(1)} %shard_map.60.mid_ref, bf16[8,2,2,64,128]{4,3,2,1,0:T(8,128)(2,1)S(1)} %get-tuple-element.64.rim_ref, f32[8,2,2,64,128]{4,3,2,1,0:T(8,128)S(1)} %get-tuple-element.79.acc_ref, bf16[8,2,64,128]{3,2,1,0:T(8,128)(2,1)S(1)} %collective-permute-done.12.a_ref, ...), custom_call_target="tpu_custom_call" | custom-call | flops 1000000 | bytes 10000 | tf_op jit(solution)/shard_map/pallas_call | solution.py:29
Async XLA Ops:
  1.4 8.0 %collective-permute-start = (bf16[8,2,64,128]{3,2,1,0:T(8,128)(2,1)S(1)}, bf16[8,2,64,128]{3,2,1,0:T(8,128)(2,1)S(1)}, u32[]{:S(2)}, u32[]{:S(2)}) collective-permute-start(bf16[8,2,64,128]{3,2,1,0:T(8,128)(2,1)S(1)} %get-tuple-element.45), channel_id=1, source_target_pairs={{0,2},{2,0},{4,6},{6,4},{1,3},{3,1},{5,7},{7,5},{8,10},{10,8},{12,... | collective-permute-start | bytes 786440 | tf_op jit(solution)/shard_map/ppermute | solution.py:364
  1.9 7.5 %collective-permute-start.1 = (bf16[8,2,64,128]{3,2,1,0:T(8,128)(2,1)S(1)}, bf16[8,2,64,128]{3,2,1,0:T(8,128)(2,1)S(1)}, u32[]{:S(2)}, u32[]{:S(2)}) collective-permute-start(bf16[8,2,64,128]{3,2,1,0:T(8,128)(2,1)S(1)} %get-tuple-element.46), channel_id=1, source_target_pairs={{0,1},{1,0},{2,4},{3,5},{4,2},{5,3},{6,7},{7,6},{8,9},{9,8},{10,12... | collective-permute-start | bytes 786440 | tf_op jit(solution)/shard_map/ppermute | solution.py:365
  5.1 13.6 %collective-permute-start.4 = (bf16[8,2,64,128]{3,2,1,0:T(8,128)(2,1)S(1)}, bf16[8,2,64,128]{3,2,1,0:T(8,128)(2,1)S(1)}, u32[]{:S(2)}, u32[]{:S(2)}) collective-permute-start(bf16[8,2,64,128]{3,2,1,0:T(8,128)(2,1)S(1)} %get-tuple-element.61), channel_id=1, source_target_pairs={{0,2},{2,0},{4,6},{6,4},{8,16},{10,18},{12,20},{14,22},{16,8},{18,... | collective-permute-start | bytes 786440 | tf_op jit(solution)/shard_map/ppermute | solution.py:365
  5.2 13.4 %collective-permute-start.3 = (bf16[8,2,64,128]{3,2,1,0:T(8,128)(2,1)S(1)}, bf16[8,2,64,128]{3,2,1,0:T(8,128)(2,1)S(1)}, u32[]{:S(2)}, u32[]{:S(2)}) collective-permute-start(bf16[8,2,64,128]{3,2,1,0:T(8,128)(2,1)S(1)} %get-tuple-element.50.after_ref), channel_id=1, source_target_pairs={{0,8},{8,0},{16,24},{24,16},{1,9},{9,1},{17,25},{25,17},{2,10},{10... | collective-permute-start | bytes 786440 | tf_op jit(solution)/shard_map/ppermute | solution.py:364
  10.1 8.8 %collective-permute-start.6 = (bf16[8,2,64,128]{3,2,1,0:T(8,128)(2,1)S(1)}, bf16[8,2,64,128]{3,2,1,0:T(8,128)(2,1)S(1)}, u32[]{:S(2)}, u32[]{:S(2)}) collective-permute-start(bf16[8,2,64,128]{3,2,1,0:T(8,128)(2,1)S(1)} %get-tuple-element.63), channel_id=1, source_target_pairs={{0,2},{2,0},{4,6},{6,4},{8,16},{10,18},{12,20},{14,22},{16,8},{18,... | collective-permute-start | bytes 786440 | tf_op jit(solution)/shard_map/ppermute | solution.py:365
  10.2 10.0 %collective-permute-start.5 = (bf16[8,2,64,128]{3,2,1,0:T(8,128)(2,1)S(1)}, bf16[8,2,64,128]{3,2,1,0:T(8,128)(2,1)S(1)}, u32[]{:S(2)}, u32[]{:S(2)}) collective-permute-start(bf16[8,2,64,128]{3,2,1,0:T(8,128)(2,1)S(1)} %get-tuple-element.57.after_ref), channel_id=1, source_target_pairs={{0,8},{8,0},{16,24},{24,16},{1,9},{9,1},{17,25},{25,17},{2,10},{10... | collective-permute-start | bytes 786440 | tf_op jit(solution)/shard_map/ppermute | solution.py:364
  13.4 4.1 %collective-permute-start.2 = (bf16[2,8,512]{2,1,0:T(8,128)(2,1)S(1)}, bf16[2,8,512]{2,1,0:T(8,128)(2,1)S(1)}, u32[]{:S(2)}, u32[]{:S(2)}) collective-permute-start(bf16[2,8,512]{2,1,0:T(8,128)(2,1)S(1)} %shard_map.51), channel_id=1, source_target_pairs={{0,1},{1,0},{2,3},{3,2},{4,5},{5,4},{6,7},{7,6},{8,9},{9,8},{10,11... | collective-permute-start | bytes 49160 | tf_op jit(solution)/shard_map/ppermute | solution.py:424
  20.6 7.0 %collective-permute-start.7 = (bf16[8,2,64,128]{3,2,1,0:T(8,128)(2,1)S(1)}, bf16[8,2,64,128]{3,2,1,0:T(8,128)(2,1)S(1)}, u32[]{:S(2)}, u32[]{:S(2)}) collective-permute-start(bf16[8,2,64,128]{3,2,1,0:T(8,128)(2,1)S(1)} %get-tuple-element.65), channel_id=1, source_target_pairs={{0,2},{2,0},{4,6},{6,4},{1,3},{3,1},{5,7},{7,5},{8,10},{10,8},{12,... | collective-permute-start | bytes 786440 | tf_op jit(solution)/shard_map/ppermute | solution.py:364
  20.6 7.0 %collective-permute-start.8 = (bf16[8,2,64,128]{3,2,1,0:T(8,128)(2,1)S(1)}, bf16[8,2,64,128]{3,2,1,0:T(8,128)(2,1)S(1)}, u32[]{:S(2)}, u32[]{:S(2)}) collective-permute-start(bf16[8,2,64,128]{3,2,1,0:T(8,128)(2,1)S(1)} %get-tuple-element.66), channel_id=1, source_target_pairs={{0,1},{1,0},{2,4},{3,5},{4,2},{5,3},{6,7},{7,6},{8,9},{9,8},{10,12... | collective-permute-start | bytes 786440 | tf_op jit(solution)/shard_map/ppermute | solution.py:365
  22.7 12.5 %collective-permute-start.11 = (bf16[8,2,64,128]{3,2,1,0:T(8,128)(2,1)S(1)}, bf16[8,2,64,128]{3,2,1,0:T(8,128)(2,1)S(1)}, u32[]{:S(2)}, u32[]{:S(2)}) collective-permute-start(bf16[8,2,64,128]{3,2,1,0:T(8,128)(2,1)S(1)} %get-tuple-element.78), channel_id=1, source_target_pairs={{0,2},{2,0},{4,6},{6,4},{8,16},{10,18},{12,20},{14,22},{16,8},{18,... | collective-permute-start | bytes 786440 | tf_op jit(solution)/shard_map/ppermute | solution.py:365
  22.8 12.3 %collective-permute-start.10 = (bf16[8,2,64,128]{3,2,1,0:T(8,128)(2,1)S(1)}, bf16[8,2,64,128]{3,2,1,0:T(8,128)(2,1)S(1)}, u32[]{:S(2)}, u32[]{:S(2)}) collective-permute-start(bf16[8,2,64,128]{3,2,1,0:T(8,128)(2,1)S(1)} %get-tuple-element.71.after_ref), channel_id=1, source_target_pairs={{0,8},{8,0},{16,24},{24,16},{1,9},{9,1},{17,25},{25,17},{2,10},{10... | collective-permute-start | bytes 786440 | tf_op jit(solution)/shard_map/ppermute | solution.py:364
  28.2 7.1 %collective-permute-start.13 = (bf16[8,2,64,128]{3,2,1,0:T(8,128)(2,1)S(1)}, bf16[8,2,64,128]{3,2,1,0:T(8,128)(2,1)S(1)}, u32[]{:S(2)}, u32[]{:S(2)}) collective-permute-start(bf16[8,2,64,128]{3,2,1,0:T(8,128)(2,1)S(1)} %get-tuple-element.80), channel_id=1, source_target_pairs={{0,2},{2,0},{4,6},{6,4},{8,16},{10,18},{12,20},{14,22},{16,8},{18,... | collective-permute-start | bytes 786440 | tf_op jit(solution)/shard_map/ppermute | solution.py:365
  28.3 8.8 %collective-permute-start.12 = (bf16[8,2,64,128]{3,2,1,0:T(8,128)(2,1)S(1)}, bf16[8,2,64,128]{3,2,1,0:T(8,128)(2,1)S(1)}, u32[]{:S(2)}, u32[]{:S(2)}) collective-permute-start(bf16[8,2,64,128]{3,2,1,0:T(8,128)(2,1)S(1)} %get-tuple-element.76.after_ref), channel_id=1, source_target_pairs={{0,8},{8,0},{16,24},{24,16},{1,9},{9,1},{17,25},{25,17},{2,10},{10... | collective-permute-start | bytes 786440 | tf_op jit(solution)/shard_map/ppermute | solution.py:364
  30.2 3.7 %collective-permute-start.9 = (bf16[2,8,512]{2,1,0:T(8,128)(2,1)S(1)}, bf16[2,8,512]{2,1,0:T(8,128)(2,1)S(1)}, u32[]{:S(2)}, u32[]{:S(2)}) collective-permute-start(bf16[2,8,512]{2,1,0:T(8,128)(2,1)S(1)} %shard_map.58), channel_id=1, source_target_pairs={{0,1},{1,0},{2,3},{3,2},{4,5},{5,4},{6,7},{7,6},{8,9},{9,8},{10,11... | collective-permute-start | bytes 49160 | tf_op jit(solution)/shard_map/ppermute | solution.py:424

commit v5 on v3

--- a/solution.py
+++ b/solution.py
@@ -150,16 +150,28 @@
             out_ref[:, j, cut] = unband(got[:, at : at + width], channels)
 
 
-def inner_body(mid_ref, rim_ref, beside_ref, *out_refs):
+def inner_body(which, mid_ref, rim_ref, beside_ref, *out_refs):
     rows, cols = mid_ref.shape[1:3]
-    for (i, side), out_ref in zip(sent_rows(rows), out_refs):
+    for n, out_ref in zip(which, out_refs):
+        i, side = sent_rows(rows)[n]
         owed_sums(
             beside_ref[side], lambda cut, b: [column(mid_ref, rim_ref, i, j + b, cut) for j in range(cols)], out_ref
         )
 
 
-def edge_body(mid_ref, rim_ref, cola_ref, colb_ref, beside_ref, after_ref, a_ref, b_ref, side_ref):
+def part_body(mid_ref, rim_ref, beside_ref, after_ref, *part_refs):
     rows, cols = mid_ref.shape[1], mid_ref.shape[2] + 2
+    cuts = bands_of(mid_ref.shape[3])
+    for (i, side), part_ref in zip(sent_rows(rows), part_refs):
+        span = part_ref.shape[1]
+        for n, (first, j) in enumerate(((1, 0), (0, cols - 2))):
+            tiles = [jnp.concatenate([column(mid_ref, rim_ref, i, j + b, cut) for cut in cuts], axis=1) for b in range(2)]
+            operator = beside_ref[side, :, first * span : (first + 2) * span]
+            part_ref[n] = dot(operator, jnp.concatenate(tiles, axis=0))
+
+
+def edge_body(cola_ref, colb_ref, beside_ref, parta_ref, partb_ref, after_ref, a_ref, b_ref, side_ref):
+    channels, rows, depth, width = cola_ref.shape
     odd, paired = parity("scol"), has_second("scol")
     side_ref[1 - odd] = cola_ref[...]
 
@@ -171,13 +183,14 @@
     def _():
         side_ref[odd] = jnp.zeros_like(colb_ref)
 
-    def around(i, j, cut):
-        if j in (-1, cols):
-            return band(side_ref[0 if j < 0 else 1, :, i, cut])
-        return column(mid_ref, rim_ref, i, j, cut)
-
-    for (i, side), out_ref in zip(sent_rows(rows), (a_ref, b_ref)):
-        owed_sums(beside_ref[side], lambda cut, b: [around(i, j + b - 1, cut) for j in (0, cols - 1)], out_ref)
+    cuts = bands_of(depth)
+    for (i, side), part_ref, out_ref in zip(sent_rows(rows), (parta_ref, partb_ref), (a_ref, b_ref)):
+        span = part_ref.shape[1]
+        for n, tap in enumerate((0, 2)):
+            halo = jnp.concatenate([band(side_ref[n, :, i, cut]) for cut in cuts], axis=1)
+            got = (part_ref[n] + dot(beside_ref[side, :, tap * span : (tap + 1) * span], halo)).astype(BF16)
+            for q, cut in enumerate(cuts):
+                out_ref[:, n, cut] = unband(got[:, q * width : (q + 1) * width], channels)
 
 
 def shifted(tile, step):
@@ -272,6 +285,8 @@
     odd = parity("srow")
     paired = has_second("srow").astype(F32)
     for n, i in enumerate([(rows - 1) * (1 - odd), (rows - 1) * odd, *range(1, rows - 1)]):
+        if n < 2 and owed_refs[n] is None:
+            continue
         for j in range(cols):
             total = acc_ref[:, i, j]
             if n < 2:
@@ -307,8 +322,12 @@
     finished(x_ref, acc_ref, (a_ref, b_ref), store)
 
 
-def next_body(x_ref, acc_ref, a_ref, b_ref, after_ref, out_ref, cola_ref, colb_ref):
-    mid_body(x_ref, acc_ref, a_ref, b_ref, out_ref)
+def begin_body(x_ref, acc_ref, a_ref, after_ref, out_ref):
+    mid_body(x_ref, acc_ref, a_ref, None, out_ref)
+
+
+def next_body(x_ref, acc_ref, b_ref, begun_ref, after_ref, out_ref, cola_ref, colb_ref):
+    mid_body(x_ref, acc_ref, None, b_ref, out_ref)
     sent_columns(out_ref, (cola_ref, colb_ref))
 
 
@@ -351,7 +370,11 @@
         copy.wait()
 
 
-def swaps(a, b, axis, other):
+def swap_first(value, axis):
+    return lax.ppermute(value, axis, [(n, n ^ 1) for n in range(lax.axis_size(axis))])
+
+
+def swap_second(value, axis, other):
     count, across = lax.axis_size(axis), lax.axis_size(other)
     pairs = []
     for n in range(count):
@@ -361,8 +384,7 @@
             else:
                 target = (n, m ^ 1)
             pairs.append((n * across + m, target[0] * across + target[1]))
-    got_a = lax.ppermute(a, axis, [(n, n ^ 1) for n in range(count)])
-    return got_a, lax.ppermute(b, (axis, other), pairs)
+    return lax.ppermute(value, (axis, other), pairs)
 
 
 def shards(volume, src_weight, tgt_weight, bias):
@@ -376,7 +398,7 @@
     deep_swaps = 1 if counts[2] == 2 else 2
     mid_shape, rim_shape = ((channels, rows, n, depth, width) for n in (cols - 2, 2))
     line = VMEM((channels, rows, depth, width), BF16)
-    owed_mid, owed_rim = (VMEM((channels, n, depth, width), BF16) for n in (cols - 2, 2))
+    owed_rim = VMEM((channels, 2, depth, width), BF16)
     sent = [VMEM(rim_shape, BF16), line, line]
     early = [("beside", 0)]
     src_w, tgt_w, bias, beside_0, mid, rim, col_a, col_b = call(
@@ -391,10 +413,14 @@
     )
     made = {early[0]: beside_0}
     kinds = ("middle", "beside", "target", "near", "deep")
+    owed_inner = [VMEM((channels, cols - 2, depth, width), BF16)]
+    sum_a = None
     for layer in range(layers):
-        beside = swaps(col_a, col_b, "scol", "trow")
-        sum_a, sum_b = call(inner_body, [owed_mid, owed_mid], (mid, rim, made["beside", layer]))
-        inner = swaps(sum_a, sum_b, "srow", "scol")
+        beside = swap_first(col_a, "scol"), swap_second(col_b, "scol", "trow")
+        which = (0, 1) if sum_a is None else (1,)
+        sums = call(functools.partial(inner_body, which), owed_inner * len(which), (mid, rim, made["beside", layer]))
+        sum_b = sums[-1]
+        inner = swap_first(sums[0], "srow") if sum_a is None else got_a, swap_second(sum_b, "srow", "scol")
         if layer == 0:
             late = [(kind, n) for n in range(layers) for kind in kinds]
             made |= build([part for part in late if part not in early], src_w, tgt_w, sum_b)
@@ -409,21 +435,26 @@
                 scratch=[VMEM((depth // BAND, 3, channels * BAND, cols * width), BF16)],
             )
 
+        parts = call(
+            part_body,
+            [VMEM((2, channels * BAND, depth // BAND * width), F32)] * 2,
+            (mid, rim, operator["beside"], sum_b),
+            {3: pl.ANY},
+        )
         accs = own(sum_b) if layer else None
         a, b, side = call(
             edge_body,
             [owed_rim, owed_rim, VMEM((2, *line.shape), BF16)],
-            (mid, rim, *beside, operator["beside"], accs[0] if layer else operator["middle"]),
+            (*beside, operator["beside"], *parts, accs[0] if layer else operator["middle"]),
             {5: pl.ANY},
         )
-        outer = swaps(a, b, "srow", "scol")
+        outer = swap_first(a, "srow"), swap_second(b, "srow", "scol")
         deep = call(
             depth_body, [VMEM((rows, channels, cols * width), BF16)] * deep_swaps, (mid, rim, b), {2: pl.ANY}
         )
-        if deep_swaps == 1:
-            deeper = [lax.ppermute(deep[0], "trow", [(0, 1), (1, 0)])]
-        else:
-            deeper = swaps(*deep, "trow", "scol")
+        deeper = [swap_first(deep[0], "trow")]
+        if deep_swaps == 2:
+            deeper.append(swap_second(deep[1], "trow", "scol"))
         accs = accs or own(b)
         acc_mid, acc_rim = call(
             rest_body,
@@ -433,7 +464,12 @@
         )
         (mid,) = call(mid_body, [VMEM(mid_shape, BF16)], (mid, acc_mid, *inner))
         if layer < layers - 1:
-            rim, col_a, col_b = call(next_body, sent, (rim, acc_rim, *outer, mid), {4: pl.ANY})
+            begun, *_ = call(begin_body, sent[:1], (rim, acc_rim, outer[0], mid), {3: pl.ANY})
+            (sum_a,) = call(functools.partial(inner_body, (0,)), owed_inner, (mid, begun, made["beside", layer + 1]))
+            got_a = swap_first(sum_a, "srow")
+            rim, col_a, col_b = call(
+                next_body, sent, (rim, acc_rim, outer[1], begun, sum_a), {4: pl.ANY}, aliases={3: 0}
+            )
         else:
             (state,) = call(
                 last_body,

time: 37.6 us -> 37.3 us (level)
  starting transfers between devices: 16 us -> 15.4 us
  Pallas kernels: 14.4 us -> 14.9 us
    ppermute x14, starting transfers between devices: 16 us -> 15.4 us  [the longest x8 11.8 us: swap_first(): lax.ppermute(value, axis, [(n, n ^ 1) for n in range(lax.axis_size(axis))])]
    pallas_call x16 -> x20, Pallas kernels: 14.4 us -> 14.9 us  [call(): pl.pallas_call(body, out_shape=tuple(outs), in_specs=[pl.BlockSpec(memory...]
  transfers between devices with their start and end apart: 14 -> 14, of which waited for: 4 -> 5; matrix products, arithmetic and copies ran while one was open for 0% -> 0% of each run, Pallas kernels for 31% -> 33%
where the time goes in v5:
time: 37.3 us; the launch traced here: 37.2 us
  starting transfers between devices  15.4 us (41%)
  Pallas kernels  14.9 us (40%)
  waiting for transfers between devices  6.59 us (18%)
    pallas_call x20, Pallas kernels, call(): pl.pallas_call(body, out_shape=tuple(outs), in_specs=[pl.BlockSpec(memory...  14.9 us
    ppermute x8, starting transfers between devices, swap_first(): lax.ppermute(value, axis, [(n, n ^ 1) for n in range(lax.axis_size(axis))])  11.8 us
    ppermute x8, waiting for transfers between devices, swap_first(): lax.ppermute(value, axis, [(n, n ^ 1) for n in range(lax.axis_size(axis))])  6.02 us
    ppermute x6, starting transfers between devices, swap_second(): return lax.ppermute(value, (axis, other), pairs)  3.68 us
  transfers between devices with their start and end apart: 14, of which 5 were waited for; matrix products, arithmetic and copies ran while one was open for 0% of the time, Pallas kernels for 33%

profile of v5, /device:TPU:0, one launch (start us, length us, event | category | flops | bytes accessed | tf_op | source)
XLA Modules:
  0.0 37.2 jit_solution(4005443291422814142)
XLA Ops:
  0.0 1.4 %shard_map.46 = (bf16[2,8,8,9]{3,2,1,0:T(8,128)(2,1)S(1)}, bf16[2,8,8,9]{3,2,1,0:T(8,128)(2,1)S(1)}, f32[2,8]{1,0:T(2,128)S(1)}, bf16[2,256,768]{2,1,0:T(8,128)(...) custom-call(bf16[8,2,4,64,128]{4,3,2,1,0:T(8,128)(2,1)} %x_ref.1, ...), custom_call_target="tpu_custom_call" | custom-call | flops 1000000 | bytes 10000 | tf_op jit(solution)/shard_map/pallas_call | solution.py:29
  1.4 0.5 %collective-permute-start = (bf16[8,2,64,128]{3,2,1,0:T(8,128)(2,1)S(1)}, bf16[8,2,64,128]{3,2,1,0:T(8,128)(2,1)S(1)}, u32[]{:S(2)}, u32[]{:S(2)}) collective-permute-start(bf16[8,2,64,128]{3,2,1,0:T(8,128)(2,1)S(1)} %get-tuple-element.47), channel_id=1, source_target_pairs={{0,2},{2,0},{4,6},{6,4},{1,3},{3,1},{5,7},{7,5},{8,10},{10,8},{12,... | collective-permute-start | bytes 786440 | tf_op jit(solution)/shard_map/ppermute | solution.py:374
  1.9 2.6 %collective-permute-start.1 = (bf16[8,2,64,128]{3,2,1,0:T(8,128)(2,1)S(1)}, bf16[8,2,64,128]{3,2,1,0:T(8,128)(2,1)S(1)}, u32[]{:S(2)}, u32[]{:S(2)}) collective-permute-start(bf16[8,2,64,128]{3,2,1,0:T(8,128)(2,1)S(1)} %get-tuple-element.48), channel_id=1, source_target_pairs={{0,1},{1,0},{2,4},{3,5},{4,2},{5,3},{6,7},{7,6},{8,9},{9,8},{10,12... | collective-permute-start | bytes 786440 | tf_op jit(solution)/shard_map/ppermute | solution.py:387
  4.5 0.6 %shard_map.47 = (bf16[8,2,64,128]{3,2,1,0:T(8,128)(2,1)S(1)}, bf16[8,2,64,128]{3,2,1,0:T(8,128)(2,1)S(1)}) custom-call(bf16[8,2,2,64,128]{4,3,2,1,0:T(8,128)(2,1)S(1)} %get-tuple-element.45.mid_ref.x_ref, bf16[8,2,2,64,128]{4,3,2,1,0:T(8,128)(2,1)S(1)} %get-tuple-element.46.rim_ref.x_ref, bf16[2,256,768]{2,1,0:T(8,128)(2,1)S(1)} %get-tuple-element.49.beside_ref), custom_call_target="tpu_custom_call" | custom-call | flops 1000000 | bytes 10000 | tf_op jit(solution)/shard_map/pallas_call | solution.py:29
  5.1 1.6 %collective-permute-start.3 = (bf16[8,2,64,128]{3,2,1,0:T(8,128)(2,1)S(1)}, bf16[8,2,64,128]{3,2,1,0:T(8,128)(2,1)S(1)}, u32[]{:S(2)}, u32[]{:S(2)}) collective-permute-start(bf16[8,2,64,128]{3,2,1,0:T(8,128)(2,1)S(1)} %get-tuple-element.65), channel_id=1, source_target_pairs={{0,8},{8,0},{16,24},{24,16},{1,9},{9,1},{17,25},{25,17},{2,10},{10... | collective-permute-start | bytes 786440 | tf_op jit(solution)/shard_map/ppermute | solution.py:374
  6.7 0.0 collective-permute-start.4
  6.7 0.4 %shard_map.48 = (f32[2,256,256]{2,1,0:T(8,128)S(1)}, f32[2,256,256]{2,1,0:T(8,128)S(1)}) custom-call(bf16[8,2,2,64,128]{4,3,2,1,0:T(8,128)(2,1)S(1)} %get-tuple-element.45.mid_ref.x_ref, bf16[8,2,2,64,128]{4,3,2,1,0:T(8,128)(2,1)S(1)} %get-tuple-element.46.rim_ref.x_ref, bf16[2,256,768]{2,1,0:T(8,128)(2,1)S(1)} %get-tuple-element.49.beside_ref, ...), custom_call_target="tpu_custom_call" | custom-call | flops 1000000 | bytes 10000 | tf_op jit(solution)/shard_map/pallas_call | solution.py:29
  7.2 1.1 %shard_map.49 = (bf16[256,768]{1,0:T(8,128)(2,1)S(1)}, bf16[256,768]{1,0:T(8,128)(2,1)S(1)}, bf16[2,256,384]{2,1,0:T(8,128)(2,1)S(1)}, bf16[2,256,24]{2,1,0:T(8,...) custom-call(bf16[2,8,8,9]{3,2,1,0:T(8,128)(2,1)S(1)} %get-tuple-elem, ...), custom_call_target="tpu_custom_call" | custom-call | flops 1000000 | bytes 10000 | tf_op jit(solution)/shard_map/pallas_call | solution.py:29
  8.3 0.0 collective-permute-done.cola_ref
  8.3 0.6 %collective-permute-done.1.colb_ref = bf16[8,2,64,128]{3,2,1,0:T(8,128)(2,1)S(1)} collective-permute-done((bf16[8,2,64,128]{3,2,1,0:T(8,128)(2,1)S(1)}, bf16[8,2,64,128]{3,2,1,0:T(8,128)(2,1)S(1)}, u32[]{:S(2)}, u32[]{:S(2)}) %collective-permute-start.1) | collective-permute-done | bytes 262176 | tf_op jit(solution)/shard_map/ppermute | solution.py:387
  8.9 0.4 %shard_map.50 = (bf16[8,2,64,128]{3,2,1,0:T(8,128)(2,1)S(1)}, bf16[8,2,64,128]{3,2,1,0:T(8,128)(2,1)S(1)}, bf16[2,8,2,64,128]{4,3,2,1,0:T(8,128)(2,1)S(1)}) custom-call(bf16[8,2,64,128]{3,2,1,0:T(8,128)(2,1)S(1)} %collective-permute-done.cola_ref, bf16[8,2,64,128]{3,2,1,0:T(8,128)(2,1)S(1)} %collective-permute-done.1.colb_ref, ...), custom_call_target="tpu_custom_call" | custom-call | flops 1000000 | bytes 10000 | tf_op jit(solution)/shard_map/pallas_call | solution.py:29
  9.2 2.7 %collective-permute-start.6 = (bf16[8,2,64,128]{3,2,1,0:T(8,128)(2,1)S(1)}, bf16[8,2,64,128]{3,2,1,0:T(8,128)(2,1)S(1)}, u32[]{:S(2)}, u32[]{:S(2)}) collective-permute-start(bf16[8,2,64,128]{3,2,1,0:T(8,128)(2,1)S(1)} %get-tuple-element.67), channel_id=1, source_target_pairs={{0,8},{8,0},{16,24},{24,16},{1,9},{9,1},{17,25},{25,17},{2,10},{10... | collective-permute-start | bytes 786440 | tf_op jit(solution)/shard_map/ppermute | solution.py:374
  11.9 0.0 collective-permute-start.5
  11.9 0.2 shard_map.52
  12.1 1.0 %collective-permute-start.2 = (bf16[2,8,512]{2,1,0:T(8,128)(2,1)S(1)}, bf16[2,8,512]{2,1,0:T(8,128)(2,1)S(1)}, u32[]{:S(2)}, u32[]{:S(2)}) collective-permute-start(bf16[2,8,512]{2,1,0:T(8,128)(2,1)S(1)} %shard_map.52), channel_id=1, source_target_pairs={{0,1},{1,0},{2,3},{3,2},{4,5},{5,4},{6,7},{7,6},{8,9},{9,8},{10,11... | collective-permute-start | bytes 49160 | tf_op jit(solution)/shard_map/ppermute | solution.py:374
  13.1 2.5 %shard_map.51 = (f32[8,2,2,64,128]{4,3,2,1,0:T(8,128)S(1)}, f32[8,2,2,64,128]{4,3,2,1,0:T(8,128)S(1)}) custom-call(bf16[8,2,2,64,128]{4,3,2,1,0:T(8,128)(2,1)S(1)} %get-tuple-element.45.mid_ref.x_ref, bf16[8,2,2,64,128]{4,3,2,1,0:T(8,128)(2,1)S(1)} %get-tuple-element.46.rim_ref.x_ref, bf16[256,768]{1,0:T(8,128)(2,1)S(1)} %get-tuple-element.55.after_ref.middle_ref, ...), custom_call_target="tpu_custom_call" | custom-call | flops 1000000 | bytes 10000 | tf_op jit(solution)/shard_map/pallas_call | solution.py:29
  15.6 0.2 collective-permute-done.2.rest_0_
  15.9 1.1 %shard_map.53 = (f32[8,2,2,64,128]{4,3,2,1,0:T(8,128)S(1)}, f32[8,2,2,64,128]{4,3,2,1,0:T(8,128)S(1)}) custom-call(bf16[8,2,2,64,128]{4,3,2,1,0:T(8,128)(2,1)S(1)} %get-tuple-element.45.mid_ref.x_ref, bf16[8,2,2,64,128]{4,3,2,1,0:T(8,128)(2,1)S(1)} %get-tuple-element.46.rim_ref.x_ref, ...), custom_call_target="tpu_custom_call", output_to_operand_aliasing={{0}: (6, {}), {1}: (7, {})} | custom-call | flops 1000000 | bytes 10000 | tf_op jit(solution)/shard_map/pallas_call | solution.py:29
  17.0 0.0 collective-permute-done.3.a_ref
  17.0 0.0 collective-permute-done.4.b_ref
  17.0 0.2 shard_map.54.after_ref.mid_ref.x_ref
  17.2 1.8 %collective-permute-done.6.a_ref = bf16[8,2,64,128]{3,2,1,0:T(8,128)(2,1)S(1)} collective-permute-done((bf16[8,2,64,128]{3,2,1,0:T(8,128)(2,1)S(1)}, bf16[8,2,64,128]{3,2,1,0:T(8,128)(2,1)S(1)}, u32[]{:S(2)}, u32[]{:S(2)}) %collective-permute-start.6) | collective-permute-done | bytes 262176 | tf_op jit(solution)/shard_map/ppermute | solution.py:374
  19.1 0.1 shard_map.55.rim_ref.begun_ref
  19.2 0.4 %shard_map.56.after_ref = bf16[8,2,64,128]{3,2,1,0:T(8,128)(2,1)S(1)} custom-call(bf16[8,2,2,64,128]{4,3,2,1,0:T(8,128)(2,1)S(1)} %shard_map.54.after_ref.mid_ref.x_ref, bf16[8,2,2,64,128]{4,3,2,1,0:T(8,128)(2,1)S(1)} %shard_map.55.rim_ref.begun_ref, bf16[2,256,768]{2,1,0:T(8,128)(2,1)S(1)} %get-tuple-element.68.beside_ref), custom_call_target="tpu_custom_call" | custom-call | flops 1000000 | bytes 10000 | tf_op jit(solution)/shard_map/pallas_call | solution.py:29
  19.6 0.0 collective-permute-done.5.b_ref
  19.6 0.2 shard_map.57
  19.8 0.1 collective-permute-start.7
  19.9 1.0 %collective-permute-start.8 = (bf16[8,2,64,128]{3,2,1,0:T(8,128)(2,1)S(1)}, bf16[8,2,64,128]{3,2,1,0:T(8,128)(2,1)S(1)}, u32[]{:S(2)}, u32[]{:S(2)}) collective-permute-start(bf16[8,2,64,128]{3,2,1,0:T(8,128)(2,1)S(1)} %get-tuple-element.71), channel_id=1, source_target_pairs={{0,1},{1,0},{2,4},{3,5},{4,2},{5,3},{6,7},{7,6},{8,9},{9,8},{10,12... | collective-permute-start | bytes 786440 | tf_op jit(solution)/shard_map/ppermute | solution.py:387
  20.9 2.6 %collective-permute-start.10 = (bf16[8,2,64,128]{3,2,1,0:T(8,128)(2,1)S(1)}, bf16[8,2,64,128]{3,2,1,0:T(8,128)(2,1)S(1)}, u32[]{:S(2)}, u32[]{:S(2)}) collective-permute-start(bf16[8,2,64,128]{3,2,1,0:T(8,128)(2,1)S(1)} %shard_map.56.after_ref), channel_id=1, source_target_pairs={{0,8},{8,0},{16,24},{24,16},{1,9},{9,1},{17,25},{25,17},{2,10},{10... | collective-permute-start | bytes 786440 | tf_op jit(solution)/shard_map/ppermute | solution.py:374
  23.5 0.4 shard_map.58.after_ref
  23.9 0.1 collective-permute-start.11
  24.0 0.5 %shard_map.59 = (f32[2,256,256]{2,1,0:T(8,128)S(1)}, f32[2,256,256]{2,1,0:T(8,128)S(1)}) custom-call(bf16[8,2,2,64,128]{4,3,2,1,0:T(8,128)(2,1)S(1)} %shard_map.54.after_ref.mid_ref.x_ref, bf16[8,2,2,64,128]{4,3,2,1,0:T(8,128)(2,1)S(1)} %get-tuple-element.69.rim_ref, bf16[2,256,768]{2,1,0:T(8,128)(2,1)S(1)} %get-tuple-element.68.beside_ref, ...), custom_call_target="tpu_custom_call" | custom-call | flops 1000000 | bytes 10000 | tf_op jit(solution)/shard_map/pallas_call | solution.py:29
  24.4 2.5 %shard_map.60 = (f32[8,2,2,64,128]{4,3,2,1,0:T(8,128)S(1)}, f32[8,2,2,64,128]{4,3,2,1,0:T(8,128)S(1)}) custom-call(bf16[8,2,2,64,128]{4,3,2,1,0:T(8,128)(2,1)S(1)} %shard_map.54.after_ref.mid_ref.x_ref, bf16[8,2,2,64,128]{4,3,2,1,0:T(8,128)(2,1)S(1)} %get-tuple-element.69.rim_ref, bf16[256,768]{1,0:T(8,128)(2,1)S(1)} %get-tuple-element.74.middle_ref, ...), custom_call_target="tpu_custom_call" | custom-call | flops 1000000 | bytes 10000 | tf_op jit(solution)/shard_map/pallas_call | solution.py:29
  27.0 0.0 collective-permute-done.7.cola_ref
  27.0 0.0 collective-permute-done.8.colb_ref
  27.0 0.4 %shard_map.61 = (bf16[8,2,64,128]{3,2,1,0:T(8,128)(2,1)S(1)}, bf16[8,2,64,128]{3,2,1,0:T(8,128)(2,1)S(1)}, bf16[2,8,2,64,128]{4,3,2,1,0:T(8,128)(2,1)S(1)}) custom-call(bf16[8,2,64,128]{3,2,1,0:T(8,128)(2,1)S(1)} %collective-permute-done.7.cola_ref, bf16[8,2,64,128]{3,2,1,0:T(8,128)(2,1)S(1)} %collective-permute-done.8.colb_ref, ...), custom_call_target="tpu_custom_call" | custom-call | flops 1000000 | bytes 10000 | tf_op jit(solution)/shard_map/pallas_call | solution.py:29
  27.4 2.6 %collective-permute-start.12 = (bf16[8,2,64,128]{3,2,1,0:T(8,128)(2,1)S(1)}, bf16[8,2,64,128]{3,2,1,0:T(8,128)(2,1)S(1)}, u32[]{:S(2)}, u32[]{:S(2)}) collective-permute-start(bf16[8,2,64,128]{3,2,1,0:T(8,128)(2,1)S(1)} %get-tuple-element.84), channel_id=1, source_target_pairs={{0,8},{8,0},{16,24},{24,16},{1,9},{9,1},{17,25},{25,17},{2,10},{10... | collective-permute-start | bytes 786440 | tf_op jit(solution)/shard_map/ppermute | solution.py:374
  30.0 0.0 collective-permute-start.13
  30.0 0.2 shard_map.62
  30.1 0.6 %collective-permute-start.9 = (bf16[2,8,512]{2,1,0:T(8,128)(2,1)S(1)}, bf16[2,8,512]{2,1,0:T(8,128)(2,1)S(1)}, u32[]{:S(2)}, u32[]{:S(2)}) collective-permute-start(bf16[2,8,512]{2,1,0:T(8,128)(2,1)S(1)} %shard_map.62), channel_id=1, source_target_pairs={{0,1},{1,0},{2,3},{3,2},{4,5},{5,4},{6,7},{7,6},{8,9},{9,8},{10,11... | collective-permute-start | bytes 49160 | tf_op jit(solution)/shard_map/ppermute | solution.py:374
  30.8 3.1 %collective-permute-done.9.rest_0_ = bf16[2,8,512]{2,1,0:T(8,128)(2,1)S(1)} collective-permute-done((bf16[2,8,512]{2,1,0:T(8,128)(2,1)S(1)}, bf16[2,8,512]{2,1,0:T(8,128)(2,1)S(1)}, u32[]{:S(2)}, u32[]{:S(2)}) %collective-permute-start.9) | collective-permute-done | bytes 16416 | tf_op jit(solution)/shard_map/ppermute | solution.py:374
  33.9 1.1 %shard_map.63 = (f32[8,2,2,64,128]{4,3,2,1,0:T(8,128)S(1)}, f32[8,2,2,64,128]{4,3,2,1,0:T(8,128)S(1)}) custom-call(bf16[8,2,2,64,128]{4,3,2,1,0:T(8,128)(2,1)S(1)} %shard_map.54.after_ref.mid_ref.x_ref, bf16[8,2,2,64,128]{4,3,2,1,0:T(8,128)(2,1)S(1)} %get-tuple-element.69.rim_ref, ...), custom_call_target="tpu_custom_call", output_to_operand_aliasing={{0}: (6, {}), {1}: (7, {})} | custom-call | flops 1000000 | bytes 10000 | tf_op jit(solution)/shard_map/pallas_call | solution.py:29
  35.0 0.0 collective-permute-done.11.b_ref
  35.0 0.0 collective-permute-done.10.a_ref
  35.0 0.2 shard_map.64.mid_ref
  35.3 0.8 %collective-permute-done.12.a_ref = bf16[8,2,64,128]{3,2,1,0:T(8,128)(2,1)S(1)} collective-permute-done((bf16[8,2,64,128]{3,2,1,0:T(8,128)(2,1)S(1)}, bf16[8,2,64,128]{3,2,1,0:T(8,128)(2,1)S(1)}, u32[]{:S(2)}, u32[]{:S(2)}) %collective-permute-start.12) | collective-permute-done | bytes 262176 | tf_op jit(solution)/shard_map/ppermute | solution.py:374
  36.1 0.0 collective-permute-done.13.b_ref
  36.1 1.0 %shard_map.65 = bf16[8,2,4,64,128]{4,3,2,1,0:T(8,128)(2,1)} custom-call(bf16[8,2,2,64,128]{4,3,2,1,0:T(8,128)(2,1)S(1)} %shard_map.64.mid_ref, bf16[8,2,2,64,128]{4,3,2,1,0:T(8,128)(2,1)S(1)} %get-tuple-element.69.rim_ref, f32[8,2,2,64,128]{4,3,2,1,0:T(8,128)S(1)} %get-tuple-element.83.acc_ref, bf16[8,2,64,128]{3,2,1,0:T(8,128)(2,1)S(1)} %collective-permute-done.12.a_ref, ...), custom_call_target="tpu_custom_call" | custom-call | flops 1000000 | bytes 10000 | tf_op jit(solution)/shard_map/pallas_call | solution.py:29
Async XLA Ops:
  1.4 6.9 %collective-permute-start = (bf16[8,2,64,128]{3,2,1,0:T(8,128)(2,1)S(1)}, bf16[8,2,64,128]{3,2,1,0:T(8,128)(2,1)S(1)}, u32[]{:S(2)}, u32[]{:S(2)}) collective-permute-start(bf16[8,2,64,128]{3,2,1,0:T(8,128)(2,1)S(1)} %get-tuple-element.47), channel_id=1, source_target_pairs={{0,2},{2,0},{4,6},{6,4},{1,3},{3,1},{5,7},{7,5},{8,10},{10,8},{12,... | collective-permute-start | bytes 786440 | tf_op jit(solution)/shard_map/ppermute | solution.py:374
  1.9 6.9 %collective-permute-start.1 = (bf16[8,2,64,128]{3,2,1,0:T(8,128)(2,1)S(1)}, bf16[8,2,64,128]{3,2,1,0:T(8,128)(2,1)S(1)}, u32[]{:S(2)}, u32[]{:S(2)}) collective-permute-start(bf16[8,2,64,128]{3,2,1,0:T(8,128)(2,1)S(1)} %get-tuple-element.48), channel_id=1, source_target_pairs={{0,1},{1,0},{2,4},{3,5},{4,2},{5,3},{6,7},{7,6},{8,9},{9,8},{10,12... | collective-permute-start | bytes 786440 | tf_op jit(solution)/shard_map/ppermute | solution.py:387
  5.1 11.9 %collective-permute-start.3 = (bf16[8,2,64,128]{3,2,1,0:T(8,128)(2,1)S(1)}, bf16[8,2,64,128]{3,2,1,0:T(8,128)(2,1)S(1)}, u32[]{:S(2)}, u32[]{:S(2)}) collective-permute-start(bf16[8,2,64,128]{3,2,1,0:T(8,128)(2,1)S(1)} %get-tuple-element.65), channel_id=1, source_target_pairs={{0,8},{8,0},{16,24},{24,16},{1,9},{9,1},{17,25},{25,17},{2,10},{10... | collective-permute-start | bytes 786440 | tf_op jit(solution)/shard_map/ppermute | solution.py:374
  6.7 10.3 %collective-permute-start.4 = (bf16[8,2,64,128]{3,2,1,0:T(8,128)(2,1)S(1)}, bf16[8,2,64,128]{3,2,1,0:T(8,128)(2,1)S(1)}, u32[]{:S(2)}, u32[]{:S(2)}) collective-permute-start(bf16[8,2,64,128]{3,2,1,0:T(8,128)(2,1)S(1)} %get-tuple-element.50.after_ref), channel_id=1, source_target_pairs={{0,2},{2,0},{4,6},{6,4},{8,16},{10,18},{12,20},{14,22},{16,8},{18,... | collective-permute-start | bytes 786440 | tf_op jit(solution)/shard_map/ppermute | solution.py:387
  9.2 9.8 %collective-permute-start.6 = (bf16[8,2,64,128]{3,2,1,0:T(8,128)(2,1)S(1)}, bf16[8,2,64,128]{3,2,1,0:T(8,128)(2,1)S(1)}, u32[]{:S(2)}, u32[]{:S(2)}) collective-permute-start(bf16[8,2,64,128]{3,2,1,0:T(8,128)(2,1)S(1)} %get-tuple-element.67), channel_id=1, source_target_pairs={{0,8},{8,0},{16,24},{24,16},{1,9},{9,1},{17,25},{25,17},{2,10},{10... | collective-permute-start | bytes 786440 | tf_op jit(solution)/shard_map/ppermute | solution.py:374
  11.9 7.7 %collective-permute-start.5 = (bf16[8,2,64,128]{3,2,1,0:T(8,128)(2,1)S(1)}, bf16[8,2,64,128]{3,2,1,0:T(8,128)(2,1)S(1)}, u32[]{:S(2)}, u32[]{:S(2)}) collective-permute-start(bf16[8,2,64,128]{3,2,1,0:T(8,128)(2,1)S(1)} %get-tuple-element.61.after_ref), channel_id=1, source_target_pairs={{0,2},{2,0},{4,6},{6,4},{8,16},{10,18},{12,20},{14,22},{16,8},{18,... | collective-permute-start | bytes 786440 | tf_op jit(solution)/shard_map/ppermute | solution.py:387
  12.1 3.7 %collective-permute-start.2 = (bf16[2,8,512]{2,1,0:T(8,128)(2,1)S(1)}, bf16[2,8,512]{2,1,0:T(8,128)(2,1)S(1)}, u32[]{:S(2)}, u32[]{:S(2)}) collective-permute-start(bf16[2,8,512]{2,1,0:T(8,128)(2,1)S(1)} %shard_map.52), channel_id=1, source_target_pairs={{0,1},{1,0},{2,3},{3,2},{4,5},{5,4},{6,7},{7,6},{8,9},{9,8},{10,11... | collective-permute-start | bytes 49160 | tf_op jit(solution)/shard_map/ppermute | solution.py:374
  19.8 7.2 %collective-permute-start.7 = (bf16[8,2,64,128]{3,2,1,0:T(8,128)(2,1)S(1)}, bf16[8,2,64,128]{3,2,1,0:T(8,128)(2,1)S(1)}, u32[]{:S(2)}, u32[]{:S(2)}) collective-permute-start(bf16[8,2,64,128]{3,2,1,0:T(8,128)(2,1)S(1)} %get-tuple-element.70), channel_id=1, source_target_pairs={{0,2},{2,0},{4,6},{6,4},{1,3},{3,1},{5,7},{7,5},{8,10},{10,8},{12,... | collective-permute-start | bytes 786440 | tf_op jit(solution)/shard_map/ppermute | solution.py:374
  19.9 7.1 %collective-permute-start.8 = (bf16[8,2,64,128]{3,2,1,0:T(8,128)(2,1)S(1)}, bf16[8,2,64,128]{3,2,1,0:T(8,128)(2,1)S(1)}, u32[]{:S(2)}, u32[]{:S(2)}) collective-permute-start(bf16[8,2,64,128]{3,2,1,0:T(8,128)(2,1)S(1)} %get-tuple-element.71), channel_id=1, source_target_pairs={{0,1},{1,0},{2,4},{3,5},{4,2},{5,3},{6,7},{7,6},{8,9},{9,8},{10,12... | collective-permute-start | bytes 786440 | tf_op jit(solution)/shard_map/ppermute | solution.py:387
  20.9 14.1 %collective-permute-start.10 = (bf16[8,2,64,128]{3,2,1,0:T(8,128)(2,1)S(1)}, bf16[8,2,64,128]{3,2,1,0:T(8,128)(2,1)S(1)}, u32[]{:S(2)}, u32[]{:S(2)}) collective-permute-start(bf16[8,2,64,128]{3,2,1,0:T(8,128)(2,1)S(1)} %shard_map.56.after_ref), channel_id=1, source_target_pairs={{0,8},{8,0},{16,24},{24,16},{1,9},{9,1},{17,25},{25,17},{2,10},{10... | collective-permute-start | bytes 786440 | tf_op jit(solution)/shard_map/ppermute | solution.py:374
  23.9 11.1 %collective-permute-start.11 = (bf16[8,2,64,128]{3,2,1,0:T(8,128)(2,1)S(1)}, bf16[8,2,64,128]{3,2,1,0:T(8,128)(2,1)S(1)}, u32[]{:S(2)}, u32[]{:S(2)}) collective-permute-start(bf16[8,2,64,128]{3,2,1,0:T(8,128)(2,1)S(1)} %shard_map.58.after_ref), channel_id=1, source_target_pairs={{0,2},{2,0},{4,6},{6,4},{8,16},{10,18},{12,20},{14,22},{16,8},{18,... | collective-permute-start | bytes 786440 | tf_op jit(solution)/shard_map/ppermute | solution.py:387
  27.4 8.7 %collective-permute-start.12 = (bf16[8,2,64,128]{3,2,1,0:T(8,128)(2,1)S(1)}, bf16[8,2,64,128]{3,2,1,0:T(8,128)(2,1)S(1)}, u32[]{:S(2)}, u32[]{:S(2)}) collective-permute-start(bf16[8,2,64,128]{3,2,1,0:T(8,128)(2,1)S(1)} %get-tuple-element.84), channel_id=1, source_target_pairs={{0,8},{8,0},{16,24},{24,16},{1,9},{9,1},{17,25},{25,17},{2,10},{10... | collective-permute-start | bytes 786440 | tf_op jit(solution)/shard_map/ppermute | solution.py:374
  30.0 6.2 %collective-permute-start.13 = (bf16[8,2,64,128]{3,2,1,0:T(8,128)(2,1)S(1)}, bf16[8,2,64,128]{3,2,1,0:T(8,128)(2,1)S(1)}, u32[]{:S(2)}, u32[]{:S(2)}) collective-permute-start(bf16[8,2,64,128]{3,2,1,0:T(8,128)(2,1)S(1)} %get-tuple-element.81.after_ref), channel_id=1, source_target_pairs={{0,2},{2,0},{4,6},{6,4},{8,16},{10,18},{12,20},{14,22},{16,8},{18,... | collective-permute-start | bytes 786440 | tf_op jit(solution)/shard_map/ppermute | solution.py:387
  30.1 3.7 %collective-permute-start.9 = (bf16[2,8,512]{2,1,0:T(8,128)(2,1)S(1)}, bf16[2,8,512]{2,1,0:T(8,128)(2,1)S(1)}, u32[]{:S(2)}, u32[]{:S(2)}) collective-permute-start(bf16[2,8,512]{2,1,0:T(8,128)(2,1)S(1)} %shard_map.62), channel_id=1, source_target_pairs={{0,1},{1,0},{2,3},{3,2},{4,5},{5,4},{6,7},{7,6},{8,9},{9,8},{10,11... | collective-permute-start | bytes 49160 | tf_op jit(solution)/shard_map/ppermute | solution.py:374

commit v6 on v5

--- a/solution.py
+++ b/solution.py
@@ -426,26 +426,16 @@
             made |= build([part for part in late if part not in early], src_w, tgt_w, sum_b)
         operator = {kind: made[kind, layer] for kind in kinds}
 
-        def own(after):
-            return call(
-                functools.partial(own_body, layer),
-                [VMEM(mid_shape, F32), VMEM(rim_shape, F32)],
-                (mid, rim, *(operator[kind] for kind in ("middle", "beside", "target", "near")), bias, after),
-                {7: pl.ANY},
-                scratch=[VMEM((depth // BAND, 3, channels * BAND, cols * width), BF16)],
-            )
-
         parts = call(
             part_body,
             [VMEM((2, channels * BAND, depth // BAND * width), F32)] * 2,
             (mid, rim, operator["beside"], sum_b),
             {3: pl.ANY},
         )
-        accs = own(sum_b) if layer else None
         a, b, side = call(
             edge_body,
             [owed_rim, owed_rim, VMEM((2, *line.shape), BF16)],
-            (*beside, operator["beside"], *parts, accs[0] if layer else operator["middle"]),
+            (*beside, operator["beside"], *parts, operator["middle"]),
             {5: pl.ANY},
         )
         outer = swap_first(a, "srow"), swap_second(b, "srow", "scol")
@@ -455,7 +445,13 @@
         deeper = [swap_first(deep[0], "trow")]
         if deep_swaps == 2:
             deeper.append(swap_second(deep[1], "trow", "scol"))
-        accs = accs or own(b)
+        accs = call(
+            functools.partial(own_body, layer),
+            [VMEM(mid_shape, F32), VMEM(rim_shape, F32)],
+            (mid, rim, *(operator[kind] for kind in ("middle", "beside", "target", "near")), bias, b),
+            {7: pl.ANY},
+            scratch=[VMEM((depth // BAND, 3, channels * BAND, cols * width), BF16)],
+        )
         acc_mid, acc_rim = call(
             rest_body,
             [VMEM(mid_shape, F32), VMEM(rim_shape, F32)],

time: 37.3 us -> 36.9 us (0.989)
  waiting for transfers between devices: 6.59 us -> 5.74 us
  starting transfers between devices: 15.4 us -> 15.9 us
    ppermute x8, waiting for transfers between devices: 6.02 us -> 3.3 us  [swap_first(): lax.ppermute(value, axis, [(n, n ^ 1) for n in range(lax.axis_size(axis))])]
    ppermute x6, waiting for transfers between devices: 0.57 us -> 2.44 us  [swap_second(): return lax.ppermute(value, (axis, other), pairs)]
    ppermute x8, starting transfers between devices: 11.8 us -> 12.2 us  [swap_first(): lax.ppermute(value, axis, [(n, n ^ 1) for n in range(lax.axis_size(axis))])]
where the time goes in v6:
time: 36.9 us; the launch traced here: 36.7 us
  starting transfers between devices  15.9 us (43%)
  Pallas kernels  14.9 us (40%)
  waiting for transfers between devices  5.74 us (16%)
    pallas_call x20, Pallas kernels, call(): pl.pallas_call(body, out_shape=tuple(outs), in_specs=[pl.BlockSpec(memory...  14.9 us
    ppermute x8, starting transfers between devices, swap_first(): lax.ppermute(value, axis, [(n, n ^ 1) for n in range(lax.axis_size(axis))])  12.2 us
    ppermute x6, starting transfers between devices, swap_second(): return lax.ppermute(value, (axis, other), pairs)  3.68 us
    ppermute x8, waiting for transfers between devices, swap_first(): lax.ppermute(value, axis, [(n, n ^ 1) for n in range(lax.axis_size(axis))])  3.3 us
    ppermute x6, waiting for transfers between devices, swap_second(): return lax.ppermute(value, (axis, other), pairs)  2.44 us
  transfers between devices with their start and end apart: 14, of which 5 were waited for; matrix products, arithmetic and copies ran while one was open for 0% of the time, Pallas kernels for 33%

profile of v6, /device:TPU:0, one launch (start us, length us, event | category | flops | bytes accessed | tf_op | source)
XLA Modules:
  0.0 36.7 jit_solution(5052807194371459884)
XLA Ops:
  0.0 1.4 %shard_map.46 = (bf16[2,8,8,9]{3,2,1,0:T(8,128)(2,1)S(1)}, bf16[2,8,8,9]{3,2,1,0:T(8,128)(2,1)S(1)}, f32[2,8]{1,0:T(2,128)S(1)}, bf16[2,256,768]{2,1,0:T(8,128)(...) custom-call(bf16[8,2,4,64,128]{4,3,2,1,0:T(8,128)(2,1)} %x_ref.1, ...), custom_call_target="tpu_custom_call" | custom-call | flops 1000000 | bytes 10000 | tf_op jit(solution)/shard_map/pallas_call | solution.py:29
  1.4 0.5 %collective-permute-start = (bf16[8,2,64,128]{3,2,1,0:T(8,128)(2,1)S(1)}, bf16[8,2,64,128]{3,2,1,0:T(8,128)(2,1)S(1)}, u32[]{:S(2)}, u32[]{:S(2)}) collective-permute-start(bf16[8,2,64,128]{3,2,1,0:T(8,128)(2,1)S(1)} %get-tuple-element.47), channel_id=1, source_target_pairs={{0,2},{2,0},{4,6},{6,4},{1,3},{3,1},{5,7},{7,5},{8,10},{10,8},{12,... | collective-permute-start | bytes 786440 | tf_op jit(solution)/shard_map/ppermute | solution.py:374
  1.9 2.6 %collective-permute-start.1 = (bf16[8,2,64,128]{3,2,1,0:T(8,128)(2,1)S(1)}, bf16[8,2,64,128]{3,2,1,0:T(8,128)(2,1)S(1)}, u32[]{:S(2)}, u32[]{:S(2)}) collective-permute-start(bf16[8,2,64,128]{3,2,1,0:T(8,128)(2,1)S(1)} %get-tuple-element.48), channel_id=1, source_target_pairs={{0,1},{1,0},{2,4},{3,5},{4,2},{5,3},{6,7},{7,6},{8,9},{9,8},{10,12... | collective-permute-start | bytes 786440 | tf_op jit(solution)/shard_map/ppermute | solution.py:387
  4.5 0.6 %shard_map.47 = (bf16[8,2,64,128]{3,2,1,0:T(8,128)(2,1)S(1)}, bf16[8,2,64,128]{3,2,1,0:T(8,128)(2,1)S(1)}) custom-call(bf16[8,2,2,64,128]{4,3,2,1,0:T(8,128)(2,1)S(1)} %get-tuple-element.45.mid_ref.x_ref, bf16[8,2,2,64,128]{4,3,2,1,0:T(8,128)(2,1)S(1)} %get-tuple-element.46.rim_ref.x_ref, bf16[2,256,768]{2,1,0:T(8,128)(2,1)S(1)} %get-tuple-element.49.beside_ref), custom_call_target="tpu_custom_call" | custom-call | flops 1000000 | bytes 10000 | tf_op jit(solution)/shard_map/pallas_call | solution.py:29
  5.1 1.6 %collective-permute-start.3 = (bf16[8,2,64,128]{3,2,1,0:T(8,128)(2,1)S(1)}, bf16[8,2,64,128]{3,2,1,0:T(8,128)(2,1)S(1)}, u32[]{:S(2)}, u32[]{:S(2)}) collective-permute-start(bf16[8,2,64,128]{3,2,1,0:T(8,128)(2,1)S(1)} %get-tuple-element.65), channel_id=1, source_target_pairs={{0,8},{8,0},{16,24},{24,16},{1,9},{9,1},{17,25},{25,17},{2,10},{10... | collective-permute-start | bytes 786440 | tf_op jit(solution)/shard_map/ppermute | solution.py:374
  6.7 0.0 collective-permute-start.4
  6.7 0.4 %shard_map.48 = (f32[2,256,256]{2,1,0:T(8,128)S(1)}, f32[2,256,256]{2,1,0:T(8,128)S(1)}) custom-call(bf16[8,2,2,64,128]{4,3,2,1,0:T(8,128)(2,1)S(1)} %get-tuple-element.45.mid_ref.x_ref, bf16[8,2,2,64,128]{4,3,2,1,0:T(8,128)(2,1)S(1)} %get-tuple-element.46.rim_ref.x_ref, bf16[2,256,768]{2,1,0:T(8,128)(2,1)S(1)} %get-tuple-element.49.beside_ref, ...), custom_call_target="tpu_custom_call" | custom-call | flops 1000000 | bytes 10000 | tf_op jit(solution)/shard_map/pallas_call | solution.py:29
  7.2 1.1 %shard_map.49 = (bf16[256,768]{1,0:T(8,128)(2,1)S(1)}, bf16[256,768]{1,0:T(8,128)(2,1)S(1)}, bf16[2,256,384]{2,1,0:T(8,128)(2,1)S(1)}, bf16[2,256,24]{2,1,0:T(8,...) custom-call(bf16[2,8,8,9]{3,2,1,0:T(8,128)(2,1)S(1)} %get-tuple-elem, ...), custom_call_target="tpu_custom_call" | custom-call | flops 1000000 | bytes 10000 | tf_op jit(solution)/shard_map/pallas_call | solution.py:29
  8.3 0.0 collective-permute-done.cola_ref
  8.3 0.6 %collective-permute-done.1.colb_ref = bf16[8,2,64,128]{3,2,1,0:T(8,128)(2,1)S(1)} collective-permute-done((bf16[8,2,64,128]{3,2,1,0:T(8,128)(2,1)S(1)}, bf16[8,2,64,128]{3,2,1,0:T(8,128)(2,1)S(1)}, u32[]{:S(2)}, u32[]{:S(2)}) %collective-permute-start.1) | collective-permute-done | bytes 262176 | tf_op jit(solution)/shard_map/ppermute | solution.py:387
  8.9 0.4 %shard_map.50 = (bf16[8,2,64,128]{3,2,1,0:T(8,128)(2,1)S(1)}, bf16[8,2,64,128]{3,2,1,0:T(8,128)(2,1)S(1)}, bf16[2,8,2,64,128]{4,3,2,1,0:T(8,128)(2,1)S(1)}) custom-call(bf16[8,2,64,128]{3,2,1,0:T(8,128)(2,1)S(1)} %collective-permute-done.cola_ref, bf16[8,2,64,128]{3,2,1,0:T(8,128)(2,1)S(1)} %collective-permute-done.1.colb_ref, ...), custom_call_target="tpu_custom_call" | custom-call | flops 1000000 | bytes 10000 | tf_op jit(solution)/shard_map/pallas_call | solution.py:29
  9.3 2.7 %collective-permute-start.6 = (bf16[8,2,64,128]{3,2,1,0:T(8,128)(2,1)S(1)}, bf16[8,2,64,128]{3,2,1,0:T(8,128)(2,1)S(1)}, u32[]{:S(2)}, u32[]{:S(2)}) collective-permute-start(bf16[8,2,64,128]{3,2,1,0:T(8,128)(2,1)S(1)} %get-tuple-element.67), channel_id=1, source_target_pairs={{0,8},{8,0},{16,24},{24,16},{1,9},{9,1},{17,25},{25,17},{2,10},{10... | collective-permute-start | bytes 786440 | tf_op jit(solution)/shard_map/ppermute | solution.py:374
  11.9 0.0 collective-permute-start.5
  11.9 0.2 shard_map.52
  12.1 1.0 %collective-permute-start.2 = (bf16[2,8,512]{2,1,0:T(8,128)(2,1)S(1)}, bf16[2,8,512]{2,1,0:T(8,128)(2,1)S(1)}, u32[]{:S(2)}, u32[]{:S(2)}) collective-permute-start(bf16[2,8,512]{2,1,0:T(8,128)(2,1)S(1)} %shard_map.52), channel_id=1, source_target_pairs={{0,1},{1,0},{2,3},{3,2},{4,5},{5,4},{6,7},{7,6},{8,9},{9,8},{10,11... | collective-permute-start | bytes 49160 | tf_op jit(solution)/shard_map/ppermute | solution.py:374
  13.1 2.5 %shard_map.51 = (f32[8,2,2,64,128]{4,3,2,1,0:T(8,128)S(1)}, f32[8,2,2,64,128]{4,3,2,1,0:T(8,128)S(1)}) custom-call(bf16[8,2,2,64,128]{4,3,2,1,0:T(8,128)(2,1)S(1)} %get-tuple-element.45.mid_ref.x_ref, bf16[8,2,2,64,128]{4,3,2,1,0:T(8,128)(2,1)S(1)} %get-tuple-element.46.rim_ref.x_ref, bf16[256,768]{1,0:T(8,128)(2,1)S(1)} %get-tuple-element.55.after_ref.middle_ref, ...), custom_call_target="tpu_custom_call" | custom-call | flops 1000000 | bytes 10000 | tf_op jit(solution)/shard_map/pallas_call | solution.py:29
  15.6 0.2 collective-permute-done.2.rest_0_
  15.9 1.1 %shard_map.53 = (f32[8,2,2,64,128]{4,3,2,1,0:T(8,128)S(1)}, f32[8,2,2,64,128]{4,3,2,1,0:T(8,128)S(1)}) custom-call(bf16[8,2,2,64,128]{4,3,2,1,0:T(8,128)(2,1)S(1)} %get-tuple-element.45.mid_ref.x_ref, bf16[8,2,2,64,128]{4,3,2,1,0:T(8,128)(2,1)S(1)} %get-tuple-element.46.rim_ref.x_ref, ...), custom_call_target="tpu_custom_call", output_to_operand_aliasing={{0}: (6, {}), {1}: (7, {})} | custom-call | flops 1000000 | bytes 10000 | tf_op jit(solution)/shard_map/pallas_call | solution.py:29
  17.0 0.0 collective-permute-done.3.a_ref
  17.0 0.0 collective-permute-done.4.b_ref
  17.0 0.2 shard_map.54.after_ref.mid_ref.x_ref
  17.2 1.8 %collective-permute-done.6.a_ref = bf16[8,2,64,128]{3,2,1,0:T(8,128)(2,1)S(1)} collective-permute-done((bf16[8,2,64,128]{3,2,1,0:T(8,128)(2,1)S(1)}, bf16[8,2,64,128]{3,2,1,0:T(8,128)(2,1)S(1)}, u32[]{:S(2)}, u32[]{:S(2)}) %collective-permute-start.6) | collective-permute-done | bytes 262176 | tf_op jit(solution)/shard_map/ppermute | solution.py:374
  19.1 0.1 shard_map.55.rim_ref.begun_ref
  19.2 0.4 %shard_map.56.after_ref = bf16[8,2,64,128]{3,2,1,0:T(8,128)(2,1)S(1)} custom-call(bf16[8,2,2,64,128]{4,3,2,1,0:T(8,128)(2,1)S(1)} %shard_map.54.after_ref.mid_ref.x_ref, bf16[8,2,2,64,128]{4,3,2,1,0:T(8,128)(2,1)S(1)} %shard_map.55.rim_ref.begun_ref, bf16[2,256,768]{2,1,0:T(8,128)(2,1)S(1)} %get-tuple-element.68.beside_ref), custom_call_target="tpu_custom_call" | custom-call | flops 1000000 | bytes 10000 | tf_op jit(solution)/shard_map/pallas_call | solution.py:29
  19.6 0.0 collective-permute-done.5.b_ref
  19.6 0.2 shard_map.57
  19.8 0.1 collective-permute-start.7
  19.9 1.0 %collective-permute-start.8 = (bf16[8,2,64,128]{3,2,1,0:T(8,128)(2,1)S(1)}, bf16[8,2,64,128]{3,2,1,0:T(8,128)(2,1)S(1)}, u32[]{:S(2)}, u32[]{:S(2)}) collective-permute-start(bf16[8,2,64,128]{3,2,1,0:T(8,128)(2,1)S(1)} %get-tuple-element.71), channel_id=1, source_target_pairs={{0,1},{1,0},{2,4},{3,5},{4,2},{5,3},{6,7},{7,6},{8,9},{9,8},{10,12... | collective-permute-start | bytes 786440 | tf_op jit(solution)/shard_map/ppermute | solution.py:387
  20.9 2.6 %collective-permute-start.10 = (bf16[8,2,64,128]{3,2,1,0:T(8,128)(2,1)S(1)}, bf16[8,2,64,128]{3,2,1,0:T(8,128)(2,1)S(1)}, u32[]{:S(2)}, u32[]{:S(2)}) collective-permute-start(bf16[8,2,64,128]{3,2,1,0:T(8,128)(2,1)S(1)} %shard_map.56.after_ref), channel_id=1, source_target_pairs={{0,8},{8,0},{16,24},{24,16},{1,9},{9,1},{17,25},{25,17},{2,10},{10... | collective-permute-start | bytes 786440 | tf_op jit(solution)/shard_map/ppermute | solution.py:374
  23.5 0.4 shard_map.58.after_ref
  23.9 0.1 collective-permute-start.11
  24.0 0.5 %shard_map.59 = (f32[2,256,256]{2,1,0:T(8,128)S(1)}, f32[2,256,256]{2,1,0:T(8,128)S(1)}) custom-call(bf16[8,2,2,64,128]{4,3,2,1,0:T(8,128)(2,1)S(1)} %shard_map.54.after_ref.mid_ref.x_ref, bf16[8,2,2,64,128]{4,3,2,1,0:T(8,128)(2,1)S(1)} %get-tuple-element.69.rim_ref, bf16[2,256,768]{2,1,0:T(8,128)(2,1)S(1)} %get-tuple-element.68.beside_ref, ...), custom_call_target="tpu_custom_call" | custom-call | flops 1000000 | bytes 10000 | tf_op jit(solution)/shard_map/pallas_call | solution.py:29
  24.4 0.0 collective-permute-done.7.cola_ref
  24.5 1.9 %collective-permute-done.8.colb_ref = bf16[8,2,64,128]{3,2,1,0:T(8,128)(2,1)S(1)} collective-permute-done((bf16[8,2,64,128]{3,2,1,0:T(8,128)(2,1)S(1)}, bf16[8,2,64,128]{3,2,1,0:T(8,128)(2,1)S(1)}, u32[]{:S(2)}, u32[]{:S(2)}) %collective-permute-start.8) | collective-permute-done | bytes 262176 | tf_op jit(solution)/shard_map/ppermute | solution.py:387
  26.3 0.4 %shard_map.60 = (bf16[8,2,64,128]{3,2,1,0:T(8,128)(2,1)S(1)}, bf16[8,2,64,128]{3,2,1,0:T(8,128)(2,1)S(1)}, bf16[2,8,2,64,128]{4,3,2,1,0:T(8,128)(2,1)S(1)}) custom-call(bf16[8,2,64,128]{3,2,1,0:T(8,128)(2,1)S(1)} %collective-permute-done.7.cola_ref, bf16[8,2,64,128]{3,2,1,0:T(8,128)(2,1)S(1)} %collective-permute-done.8.colb_ref, ...), custom_call_target="tpu_custom_call" | custom-call | flops 1000000 | bytes 10000 | tf_op jit(solution)/shard_map/pallas_call | solution.py:29
  26.7 2.3 %collective-permute-start.12 = (bf16[8,2,64,128]{3,2,1,0:T(8,128)(2,1)S(1)}, bf16[8,2,64,128]{3,2,1,0:T(8,128)(2,1)S(1)}, u32[]{:S(2)}, u32[]{:S(2)}) collective-permute-start(bf16[8,2,64,128]{3,2,1,0:T(8,128)(2,1)S(1)} %get-tuple-element.84), channel_id=1, source_target_pairs={{0,8},{8,0},{16,24},{24,16},{1,9},{9,1},{17,25},{25,17},{2,10},{10... | collective-permute-start | bytes 786440 | tf_op jit(solution)/shard_map/ppermute | solution.py:374
  29.0 0.0 collective-permute-start.13
  29.0 0.2 shard_map.62
  29.1 1.4 %collective-permute-start.9 = (bf16[2,8,512]{2,1,0:T(8,128)(2,1)S(1)}, bf16[2,8,512]{2,1,0:T(8,128)(2,1)S(1)}, u32[]{:S(2)}, u32[]{:S(2)}) collective-permute-start(bf16[2,8,512]{2,1,0:T(8,128)(2,1)S(1)} %shard_map.62), channel_id=1, source_target_pairs={{0,1},{1,0},{2,3},{3,2},{4,5},{5,4},{6,7},{7,6},{8,9},{9,8},{10,11... | collective-permute-start | bytes 49160 | tf_op jit(solution)/shard_map/ppermute | solution.py:374
  30.5 2.5 %shard_map.61 = (f32[8,2,2,64,128]{4,3,2,1,0:T(8,128)S(1)}, f32[8,2,2,64,128]{4,3,2,1,0:T(8,128)S(1)}) custom-call(bf16[8,2,2,64,128]{4,3,2,1,0:T(8,128)(2,1)S(1)} %shard_map.54.after_ref.mid_ref.x_ref, bf16[8,2,2,64,128]{4,3,2,1,0:T(8,128)(2,1)S(1)} %get-tuple-element.69.rim_ref, bf16[256,768]{1,0:T(8,128)(2,1)S(1)} %get-tuple-element.74.after_ref.middle_ref, ...), custom_call_target="tpu_custom_call" | custom-call | flops 1000000 | bytes 10000 | tf_op jit(solution)/shard_map/pallas_call | solution.py:29
  33.1 0.0 collective-permute-done.9.rest_0_
  33.1 1.1 %shard_map.63 = (f32[8,2,2,64,128]{4,3,2,1,0:T(8,128)S(1)}, f32[8,2,2,64,128]{4,3,2,1,0:T(8,128)S(1)}) custom-call(bf16[8,2,2,64,128]{4,3,2,1,0:T(8,128)(2,1)S(1)} %shard_map.54.after_ref.mid_ref.x_ref, bf16[8,2,2,64,128]{4,3,2,1,0:T(8,128)(2,1)S(1)} %get-tuple-element.69.rim_ref, ...), custom_call_target="tpu_custom_call", output_to_operand_aliasing={{0}: (6, {}), {1}: (7, {})} | custom-call | flops 1000000 | bytes 10000 | tf_op jit(solution)/shard_map/pallas_call | solution.py:29
  34.2 0.0 collective-permute-done.11.b_ref
  34.2 0.0 collective-permute-done.10.a_ref
  34.2 0.2 shard_map.64.mid_ref
  34.4 1.2 %collective-permute-done.12.a_ref = bf16[8,2,64,128]{3,2,1,0:T(8,128)(2,1)S(1)} collective-permute-done((bf16[8,2,64,128]{3,2,1,0:T(8,128)(2,1)S(1)}, bf16[8,2,64,128]{3,2,1,0:T(8,128)(2,1)S(1)}, u32[]{:S(2)}, u32[]{:S(2)}) %collective-permute-start.12) | collective-permute-done | bytes 262176 | tf_op jit(solution)/shard_map/ppermute | solution.py:374
  35.7 0.0 collective-permute-done.13.b_ref
  35.7 1.0 %shard_map.65 = bf16[8,2,4,64,128]{4,3,2,1,0:T(8,128)(2,1)} custom-call(bf16[8,2,2,64,128]{4,3,2,1,0:T(8,128)(2,1)S(1)} %shard_map.64.mid_ref, bf16[8,2,2,64,128]{4,3,2,1,0:T(8,128)(2,1)S(1)} %get-tuple-element.69.rim_ref, f32[8,2,2,64,128]{4,3,2,1,0:T(8,128)S(1)} %get-tuple-element.83.acc_ref, bf16[8,2,64,128]{3,2,1,0:T(8,128)(2,1)S(1)} %collective-permute-done.12.a_ref, ...), custom_call_target="tpu_custom_call" | custom-call | flops 1000000 | bytes 10000 | tf_op jit(solution)/shard_map/pallas_call | solution.py:29
Async XLA Ops:
  1.4 6.9 %collective-permute-start = (bf16[8,2,64,128]{3,2,1,0:T(8,128)(2,1)S(1)}, bf16[8,2,64,128]{3,2,1,0:T(8,128)(2,1)S(1)}, u32[]{:S(2)}, u32[]{:S(2)}) collective-permute-start(bf16[8,2,64,128]{3,2,1,0:T(8,128)(2,1)S(1)} %get-tuple-element.47), channel_id=1, source_target_pairs={{0,2},{2,0},{4,6},{6,4},{1,3},{3,1},{5,7},{7,5},{8,10},{10,8},{12,... | collective-permute-start | bytes 786440 | tf_op jit(solution)/shard_map/ppermute | solution.py:374
  1.9 6.9 %collective-permute-start.1 = (bf16[8,2,64,128]{3,2,1,0:T(8,128)(2,1)S(1)}, bf16[8,2,64,128]{3,2,1,0:T(8,128)(2,1)S(1)}, u32[]{:S(2)}, u32[]{:S(2)}) collective-permute-start(bf16[8,2,64,128]{3,2,1,0:T(8,128)(2,1)S(1)} %get-tuple-element.48), channel_id=1, source_target_pairs={{0,1},{1,0},{2,4},{3,5},{4,2},{5,3},{6,7},{7,6},{8,9},{9,8},{10,12... | collective-permute-start | bytes 786440 | tf_op jit(solution)/shard_map/ppermute | solution.py:387
  5.1 11.9 %collective-permute-start.3 = (bf16[8,2,64,128]{3,2,1,0:T(8,128)(2,1)S(1)}, bf16[8,2,64,128]{3,2,1,0:T(8,128)(2,1)S(1)}, u32[]{:S(2)}, u32[]{:S(2)}) collective-permute-start(bf16[8,2,64,128]{3,2,1,0:T(8,128)(2,1)S(1)} %get-tuple-element.65), channel_id=1, source_target_pairs={{0,8},{8,0},{16,24},{24,16},{1,9},{9,1},{17,25},{25,17},{2,10},{10... | collective-permute-start | bytes 786440 | tf_op jit(solution)/shard_map/ppermute | solution.py:374
  6.7 10.3 %collective-permute-start.4 = (bf16[8,2,64,128]{3,2,1,0:T(8,128)(2,1)S(1)}, bf16[8,2,64,128]{3,2,1,0:T(8,128)(2,1)S(1)}, u32[]{:S(2)}, u32[]{:S(2)}) collective-permute-start(bf16[8,2,64,128]{3,2,1,0:T(8,128)(2,1)S(1)} %get-tuple-element.50.after_ref), channel_id=1, source_target_pairs={{0,2},{2,0},{4,6},{6,4},{8,16},{10,18},{12,20},{14,22},{16,8},{18,... | collective-permute-start | bytes 786440 | tf_op jit(solution)/shard_map/ppermute | solution.py:387
  9.3 9.8 %collective-permute-start.6 = (bf16[8,2,64,128]{3,2,1,0:T(8,128)(2,1)S(1)}, bf16[8,2,64,128]{3,2,1,0:T(8,128)(2,1)S(1)}, u32[]{:S(2)}, u32[]{:S(2)}) collective-permute-start(bf16[8,2,64,128]{3,2,1,0:T(8,128)(2,1)S(1)} %get-tuple-element.67), channel_id=1, source_target_pairs={{0,8},{8,0},{16,24},{24,16},{1,9},{9,1},{17,25},{25,17},{2,10},{10... | collective-permute-start | bytes 786440 | tf_op jit(solution)/shard_map/ppermute | solution.py:374
  11.9 7.6 %collective-permute-start.5 = (bf16[8,2,64,128]{3,2,1,0:T(8,128)(2,1)S(1)}, bf16[8,2,64,128]{3,2,1,0:T(8,128)(2,1)S(1)}, u32[]{:S(2)}, u32[]{:S(2)}) collective-permute-start(bf16[8,2,64,128]{3,2,1,0:T(8,128)(2,1)S(1)} %get-tuple-element.61.after_ref), channel_id=1, source_target_pairs={{0,2},{2,0},{4,6},{6,4},{8,16},{10,18},{12,20},{14,22},{16,8},{18,... | collective-permute-start | bytes 786440 | tf_op jit(solution)/shard_map/ppermute | solution.py:387
  12.1 3.7 %collective-permute-start.2 = (bf16[2,8,512]{2,1,0:T(8,128)(2,1)S(1)}, bf16[2,8,512]{2,1,0:T(8,128)(2,1)S(1)}, u32[]{:S(2)}, u32[]{:S(2)}) collective-permute-start(bf16[2,8,512]{2,1,0:T(8,128)(2,1)S(1)} %shard_map.52), channel_id=1, source_target_pairs={{0,1},{1,0},{2,3},{3,2},{4,5},{5,4},{6,7},{7,6},{8,9},{9,8},{10,11... | collective-permute-start | bytes 49160 | tf_op jit(solution)/shard_map/ppermute | solution.py:374
  19.8 4.6 %collective-permute-start.7 = (bf16[8,2,64,128]{3,2,1,0:T(8,128)(2,1)S(1)}, bf16[8,2,64,128]{3,2,1,0:T(8,128)(2,1)S(1)}, u32[]{:S(2)}, u32[]{:S(2)}) collective-permute-start(bf16[8,2,64,128]{3,2,1,0:T(8,128)(2,1)S(1)} %get-tuple-element.70), channel_id=1, source_target_pairs={{0,2},{2,0},{4,6},{6,4},{1,3},{3,1},{5,7},{7,5},{8,10},{10,8},{12,... | collective-permute-start | bytes 786440 | tf_op jit(solution)/shard_map/ppermute | solution.py:374
  19.9 6.4 %collective-permute-start.8 = (bf16[8,2,64,128]{3,2,1,0:T(8,128)(2,1)S(1)}, bf16[8,2,64,128]{3,2,1,0:T(8,128)(2,1)S(1)}, u32[]{:S(2)}, u32[]{:S(2)}) collective-permute-start(bf16[8,2,64,128]{3,2,1,0:T(8,128)(2,1)S(1)} %get-tuple-element.71), channel_id=1, source_target_pairs={{0,1},{1,0},{2,4},{3,5},{4,2},{5,3},{6,7},{7,6},{8,9},{9,8},{10,12... | collective-permute-start | bytes 786440 | tf_op jit(solution)/shard_map/ppermute | solution.py:387
  20.9 13.3 %collective-permute-start.10 = (bf16[8,2,64,128]{3,2,1,0:T(8,128)(2,1)S(1)}, bf16[8,2,64,128]{3,2,1,0:T(8,128)(2,1)S(1)}, u32[]{:S(2)}, u32[]{:S(2)}) collective-permute-start(bf16[8,2,64,128]{3,2,1,0:T(8,128)(2,1)S(1)} %shard_map.56.after_ref), channel_id=1, source_target_pairs={{0,8},{8,0},{16,24},{24,16},{1,9},{9,1},{17,25},{25,17},{2,10},{10... | collective-permute-start | bytes 786440 | tf_op jit(solution)/shard_map/ppermute | solution.py:374
  23.9 10.3 %collective-permute-start.11 = (bf16[8,2,64,128]{3,2,1,0:T(8,128)(2,1)S(1)}, bf16[8,2,64,128]{3,2,1,0:T(8,128)(2,1)S(1)}, u32[]{:S(2)}, u32[]{:S(2)}) collective-permute-start(bf16[8,2,64,128]{3,2,1,0:T(8,128)(2,1)S(1)} %shard_map.58.after_ref), channel_id=1, source_target_pairs={{0,2},{2,0},{4,6},{6,4},{8,16},{10,18},{12,20},{14,22},{16,8},{18,... | collective-permute-start | bytes 786440 | tf_op jit(solution)/shard_map/ppermute | solution.py:387
  26.7 9.0 %collective-permute-start.12 = (bf16[8,2,64,128]{3,2,1,0:T(8,128)(2,1)S(1)}, bf16[8,2,64,128]{3,2,1,0:T(8,128)(2,1)S(1)}, u32[]{:S(2)}, u32[]{:S(2)}) collective-permute-start(bf16[8,2,64,128]{3,2,1,0:T(8,128)(2,1)S(1)} %get-tuple-element.84), channel_id=1, source_target_pairs={{0,8},{8,0},{16,24},{24,16},{1,9},{9,1},{17,25},{25,17},{2,10},{10... | collective-permute-start | bytes 786440 | tf_op jit(solution)/shard_map/ppermute | solution.py:374
  29.0 6.7 %collective-permute-start.13 = (bf16[8,2,64,128]{3,2,1,0:T(8,128)(2,1)S(1)}, bf16[8,2,64,128]{3,2,1,0:T(8,128)(2,1)S(1)}, u32[]{:S(2)}, u32[]{:S(2)}) collective-permute-start(bf16[8,2,64,128]{3,2,1,0:T(8,128)(2,1)S(1)} %get-tuple-element.79.after_ref), channel_id=1, source_target_pairs={{0,2},{2,0},{4,6},{6,4},{8,16},{10,18},{12,20},{14,22},{16,8},{18,... | collective-permute-start | bytes 786440 | tf_op jit(solution)/shard_map/ppermute | solution.py:387
  29.1 3.9 %collective-permute-start.9 = (bf16[2,8,512]{2,1,0:T(8,128)(2,1)S(1)}, bf16[2,8,512]{2,1,0:T(8,128)(2,1)S(1)}, u32[]{:S(2)}, u32[]{:S(2)}) collective-permute-start(bf16[2,8,512]{2,1,0:T(8,128)(2,1)S(1)} %shard_map.62), channel_id=1, source_target_pairs={{0,1},{1,0},{2,3},{3,2},{4,5},{5,4},{6,7},{7,6},{8,9},{9,8},{10,11... | collective-permute-start | bytes 49160 | tf_op jit(solution)/shard_map/ppermute | solution.py:374

commit v7 on v6

--- a/solution.py
+++ b/solution.py
@@ -429,7 +429,7 @@
         parts = call(
             part_body,
             [VMEM((2, channels * BAND, depth // BAND * width), F32)] * 2,
-            (mid, rim, operator["beside"], sum_b),
+            (mid, rim, operator["beside"], inner[0] if layer else sum_b),
             {3: pl.ANY},
         )
         a, b, side = call(

time: 36.9 us -> 37.9 us (1.027)
  waiting for transfers between devices: 5.74 us -> 7.61 us
  starting transfers between devices: 15.9 us -> 15.1 us
    ppermute x8, waiting for transfers between devices: 3.3 us -> 6.64 us  [swap_first(): lax.ppermute(value, axis, [(n, n ^ 1) for n in range(lax.axis_size(axis))])]
    ppermute x6, waiting for transfers between devices: 2.44 us -> 0.97 us  [swap_second(): return lax.ppermute(value, (axis, other), pairs)]
    ppermute x8, starting transfers between devices: 12.2 us -> 10.9 us  [swap_first(): lax.ppermute(value, axis, [(n, n ^ 1) for n in range(lax.axis_size(axis))])]
    ppermute x6, starting transfers between devices: 3.68 us -> 4.14 us  [swap_second(): return lax.ppermute(value, (axis, other), pairs)]
  transfers between devices with their start and end apart: 14 -> 14, of which waited for: 5 -> 6; matrix products, arithmetic and copies ran while one was open for 0% -> 0% of each run, Pallas kernels for 33% -> 33%
where the time goes in v7:
time: 37.9 us; the launch traced here: 37.8 us
  starting transfers between devices  15.1 us (40%)
  Pallas kernels  14.9 us (39%)
  waiting for transfers between devices  7.61 us (20%)
    pallas_call x20, Pallas kernels, call(): pl.pallas_call(body, out_shape=tuple(outs), in_specs=[pl.BlockSpec(memory...  14.9 us
    ppermute x8, starting transfers between devices, swap_first(): lax.ppermute(value, axis, [(n, n ^ 1) for n in range(lax.axis_size(axis))])  10.9 us
    ppermute x8, waiting for transfers between devices, swap_first(): lax.ppermute(value, axis, [(n, n ^ 1) for n in range(lax.axis_size(axis))])  6.64 us
    ppermute x6, starting transfers between devices, swap_second(): return lax.ppermute(value, (axis, other), pairs)  4.14 us
    ppermute x6, waiting for transfers between devices, swap_second(): return lax.ppermute(value, (axis, other), pairs)  0.97 us
  transfers between devices with their start and end apart: 14, of which 6 were waited for; matrix products, arithmetic and copies ran while one was open for 0% of the time, Pallas kernels for 33%

profile of v7, /device:TPU:0, one launch (start us, length us, event | category | flops | bytes accessed | tf_op | source)
XLA Modules:
  0.0 37.8 jit_solution(3728867952412074448)
XLA Ops:
  0.0 1.4 %shard_map.46 = (bf16[2,8,8,9]{3,2,1,0:T(8,128)(2,1)S(1)}, bf16[2,8,8,9]{3,2,1,0:T(8,128)(2,1)S(1)}, f32[2,8]{1,0:T(2,128)S(1)}, bf16[2,256,768]{2,1,0:T(8,128)(...) custom-call(bf16[8,2,4,64,128]{4,3,2,1,0:T(8,128)(2,1)} %x_ref.1, ...), custom_call_target="tpu_custom_call" | custom-call | flops 1000000 | bytes 10000 | tf_op jit(solution)/shard_map/pallas_call | solution.py:29
  1.4 0.5 %collective-permute-start = (bf16[8,2,64,128]{3,2,1,0:T(8,128)(2,1)S(1)}, bf16[8,2,64,128]{3,2,1,0:T(8,128)(2,1)S(1)}, u32[]{:S(2)}, u32[]{:S(2)}) collective-permute-start(bf16[8,2,64,128]{3,2,1,0:T(8,128)(2,1)S(1)} %get-tuple-element.47), channel_id=1, source_target_pairs={{0,2},{2,0},{4,6},{6,4},{1,3},{3,1},{5,7},{7,5},{8,10},{10,8},{12,... | collective-permute-start | bytes 786440 | tf_op jit(solution)/shard_map/ppermute | solution.py:374
  1.9 2.6 %collective-permute-start.1 = (bf16[8,2,64,128]{3,2,1,0:T(8,128)(2,1)S(1)}, bf16[8,2,64,128]{3,2,1,0:T(8,128)(2,1)S(1)}, u32[]{:S(2)}, u32[]{:S(2)}) collective-permute-start(bf16[8,2,64,128]{3,2,1,0:T(8,128)(2,1)S(1)} %get-tuple-element.48), channel_id=1, source_target_pairs={{0,1},{1,0},{2,4},{3,5},{4,2},{5,3},{6,7},{7,6},{8,9},{9,8},{10,12... | collective-permute-start | bytes 786440 | tf_op jit(solution)/shard_map/ppermute | solution.py:387
  4.5 0.6 %shard_map.47 = (bf16[8,2,64,128]{3,2,1,0:T(8,128)(2,1)S(1)}, bf16[8,2,64,128]{3,2,1,0:T(8,128)(2,1)S(1)}) custom-call(bf16[8,2,2,64,128]{4,3,2,1,0:T(8,128)(2,1)S(1)} %get-tuple-element.45.mid_ref.x_ref, bf16[8,2,2,64,128]{4,3,2,1,0:T(8,128)(2,1)S(1)} %get-tuple-element.46.rim_ref.x_ref, bf16[2,256,768]{2,1,0:T(8,128)(2,1)S(1)} %get-tuple-element.49.beside_ref), custom_call_target="tpu_custom_call" | custom-call | flops 1000000 | bytes 10000 | tf_op jit(solution)/shard_map/pallas_call | solution.py:29
  5.1 1.6 %collective-permute-start.3 = (bf16[8,2,64,128]{3,2,1,0:T(8,128)(2,1)S(1)}, bf16[8,2,64,128]{3,2,1,0:T(8,128)(2,1)S(1)}, u32[]{:S(2)}, u32[]{:S(2)}) collective-permute-start(bf16[8,2,64,128]{3,2,1,0:T(8,128)(2,1)S(1)} %get-tuple-element.65), channel_id=1, source_target_pairs={{0,8},{8,0},{16,24},{24,16},{1,9},{9,1},{17,25},{25,17},{2,10},{10... | collective-permute-start | bytes 786440 | tf_op jit(solution)/shard_map/ppermute | solution.py:374
  6.7 0.0 collective-permute-start.4
  6.7 0.4 %shard_map.48 = (f32[2,256,256]{2,1,0:T(8,128)S(1)}, f32[2,256,256]{2,1,0:T(8,128)S(1)}) custom-call(bf16[8,2,2,64,128]{4,3,2,1,0:T(8,128)(2,1)S(1)} %get-tuple-element.45.mid_ref.x_ref, bf16[8,2,2,64,128]{4,3,2,1,0:T(8,128)(2,1)S(1)} %get-tuple-element.46.rim_ref.x_ref, bf16[2,256,768]{2,1,0:T(8,128)(2,1)S(1)} %get-tuple-element.49.beside_ref, ...), custom_call_target="tpu_custom_call" | custom-call | flops 1000000 | bytes 10000 | tf_op jit(solution)/shard_map/pallas_call | solution.py:29
  7.2 1.1 %shard_map.49 = (bf16[256,768]{1,0:T(8,128)(2,1)S(1)}, bf16[256,768]{1,0:T(8,128)(2,1)S(1)}, bf16[2,256,384]{2,1,0:T(8,128)(2,1)S(1)}, bf16[2,256,24]{2,1,0:T(8,...) custom-call(bf16[2,8,8,9]{3,2,1,0:T(8,128)(2,1)S(1)} %get-tuple-elem, ...), custom_call_target="tpu_custom_call" | custom-call | flops 1000000 | bytes 10000 | tf_op jit(solution)/shard_map/pallas_call | solution.py:29
  8.3 0.0 collective-permute-done.cola_ref
  8.3 0.6 %collective-permute-done.1.colb_ref = bf16[8,2,64,128]{3,2,1,0:T(8,128)(2,1)S(1)} collective-permute-done((bf16[8,2,64,128]{3,2,1,0:T(8,128)(2,1)S(1)}, bf16[8,2,64,128]{3,2,1,0:T(8,128)(2,1)S(1)}, u32[]{:S(2)}, u32[]{:S(2)}) %collective-permute-start.1) | collective-permute-done | bytes 262176 | tf_op jit(solution)/shard_map/ppermute | solution.py:387
  8.9 0.4 shard_map.50
  9.3 2.7 %collective-permute-start.6 = (bf16[8,2,64,128]{3,2,1,0:T(8,128)(2,1)S(1)}, bf16[8,2,64,128]{3,2,1,0:T(8,128)(2,1)S(1)}, u32[]{:S(2)}, u32[]{:S(2)}) collective-permute-start(bf16[8,2,64,128]{3,2,1,0:T(8,128)(2,1)S(1)} %get-tuple-element.67), channel_id=1, source_target_pairs={{0,8},{8,0},{16,24},{24,16},{1,9},{9,1},{17,25},{25,17},{2,10},{10... | collective-permute-start | bytes 786440 | tf_op jit(solution)/shard_map/ppermute | solution.py:374
  11.9 0.0 collective-permute-start.5
  11.9 0.2 shard_map.52
  12.1 1.0 %collective-permute-start.2 = (bf16[2,8,512]{2,1,0:T(8,128)(2,1)S(1)}, bf16[2,8,512]{2,1,0:T(8,128)(2,1)S(1)}, u32[]{:S(2)}, u32[]{:S(2)}) collective-permute-start(bf16[2,8,512]{2,1,0:T(8,128)(2,1)S(1)} %shard_map.52), channel_id=1, source_target_pairs={{0,1},{1,0},{2,3},{3,2},{4,5},{5,4},{6,7},{7,6},{8,9},{9,8},{10,11... | collective-permute-start | bytes 49160 | tf_op jit(solution)/shard_map/ppermute | solution.py:374
  13.1 2.5 %shard_map.51 = (f32[8,2,2,64,128]{4,3,2,1,0:T(8,128)S(1)}, f32[8,2,2,64,128]{4,3,2,1,0:T(8,128)S(1)}) custom-call(bf16[8,2,2,64,128]{4,3,2,1,0:T(8,128)(2,1)S(1)} %get-tuple-element.45.mid_ref.x_ref, bf16[8,2,2,64,128]{4,3,2,1,0:T(8,128)(2,1)S(1)} %get-tuple-element.46.rim_ref.x_ref, bf16[256,768]{1,0:T(8,128)(2,1)S(1)} %get-tuple-element.55.after_ref.middle_ref, ...), custom_call_target="tpu_custom_call" | custom-call | flops 1000000 | bytes 10000 | tf_op jit(solution)/shard_map/pallas_call | solution.py:29
  15.6 0.2 collective-permute-done.2.rest_0_
  15.9 1.1 %shard_map.53 = (f32[8,2,2,64,128]{4,3,2,1,0:T(8,128)S(1)}, f32[8,2,2,64,128]{4,3,2,1,0:T(8,128)S(1)}) custom-call(bf16[8,2,2,64,128]{4,3,2,1,0:T(8,128)(2,1)S(1)} %get-tuple-element.45.mid_ref.x_ref, bf16[8,2,2,64,128]{4,3,2,1,0:T(8,128)(2,1)S(1)} %get-tuple-element.46.rim_ref.x_ref, ...), custom_call_target="tpu_custom_call", output_to_operand_aliasing={{0}: (6, {}), {1}: (7, {})} | custom-call | flops 1000000 | bytes 10000 | tf_op jit(solution)/shard_map/pallas_call | solution.py:29
  17.0 0.0 collective-permute-done.3.a_ref
  17.0 0.0 collective-permute-done.4.b_ref
  17.0 0.2 shard_map.54.after_ref.mid_ref.x_ref
  17.2 1.8 %collective-permute-done.6.a_ref = bf16[8,2,64,128]{3,2,1,0:T(8,128)(2,1)S(1)} collective-permute-done((bf16[8,2,64,128]{3,2,1,0:T(8,128)(2,1)S(1)}, bf16[8,2,64,128]{3,2,1,0:T(8,128)(2,1)S(1)}, u32[]{:S(2)}, u32[]{:S(2)}) %collective-permute-start.6) | collective-permute-done | bytes 262176 | tf_op jit(solution)/shard_map/ppermute | solution.py:374
  19.1 0.1 shard_map.55.rim_ref.begun_ref
  19.2 0.4 %shard_map.56.after_ref = bf16[8,2,64,128]{3,2,1,0:T(8,128)(2,1)S(1)} custom-call(bf16[8,2,2,64,128]{4,3,2,1,0:T(8,128)(2,1)S(1)} %shard_map.54.after_ref.mid_ref.x_ref, bf16[8,2,2,64,128]{4,3,2,1,0:T(8,128)(2,1)S(1)} %shard_map.55.rim_ref.begun_ref, bf16[2,256,768]{2,1,0:T(8,128)(2,1)S(1)} %get-tuple-element.68.beside_ref), custom_call_target="tpu_custom_call" | custom-call | flops 1000000 | bytes 10000 | tf_op jit(solution)/shard_map/pallas_call | solution.py:29
  19.6 1.6 %collective-permute-start.9 = (bf16[8,2,64,128]{3,2,1,0:T(8,128)(2,1)S(1)}, bf16[8,2,64,128]{3,2,1,0:T(8,128)(2,1)S(1)}, u32[]{:S(2)}, u32[]{:S(2)}) collective-permute-start(bf16[8,2,64,128]{3,2,1,0:T(8,128)(2,1)S(1)} %shard_map.56.after_ref), channel_id=1, source_target_pairs={{0,8},{8,0},{16,24},{24,16},{1,9},{9,1},{17,25},{25,17},{2,10},{10... | collective-permute-start | bytes 786440 | tf_op jit(solution)/shard_map/ppermute | solution.py:374
  21.2 0.0 collective-permute-done.5.b_ref
  21.2 0.2 shard_map.57
  21.4 0.1 collective-permute-start.7
  21.5 1.5 %collective-permute-start.8 = (bf16[8,2,64,128]{3,2,1,0:T(8,128)(2,1)S(1)}, bf16[8,2,64,128]{3,2,1,0:T(8,128)(2,1)S(1)}, u32[]{:S(2)}, u32[]{:S(2)}) collective-permute-start(bf16[8,2,64,128]{3,2,1,0:T(8,128)(2,1)S(1)} %get-tuple-element.71), channel_id=1, source_target_pairs={{0,1},{1,0},{2,4},{3,5},{4,2},{5,3},{6,7},{7,6},{8,9},{9,8},{10,12... | collective-permute-start | bytes 786440 | tf_op jit(solution)/shard_map/ppermute | solution.py:387
  23.0 0.4 shard_map.63
  23.3 0.1 collective-permute-start.11
  23.4 3.7 %collective-permute-done.9.after_ref.a_ref = bf16[8,2,64,128]{3,2,1,0:T(8,128)(2,1)S(1)} collective-permute-done((bf16[8,2,64,128]{3,2,1,0:T(8,128)(2,1)S(1)}, bf16[8,2,64,128]{3,2,1,0:T(8,128)(2,1)S(1)}, u32[]{:S(2)}, u32[]{:S(2)}) %collective-permute-start.9) | collective-permute-done | bytes 262176 | tf_op jit(solution)/shard_map/ppermute | solution.py:374
  27.1 0.4 %shard_map.58 = (f32[2,256,256]{2,1,0:T(8,128)S(1)}, f32[2,256,256]{2,1,0:T(8,128)S(1)}) custom-call(bf16[8,2,2,64,128]{4,3,2,1,0:T(8,128)(2,1)S(1)} %shard_map.54.after_ref.mid_ref.x_ref, bf16[8,2,2,64,128]{4,3,2,1,0:T(8,128)(2,1)S(1)} %get-tuple-element.69.rim_ref, bf16[2,256,768]{2,1,0:T(8,128)(2,1)S(1)} %get-tuple-element.68.beside_ref, ...), custom_call_target="tpu_custom_call" | custom-call | flops 1000000 | bytes 10000 | tf_op jit(solution)/shard_map/pallas_call | solution.py:29
  27.5 0.0 collective-permute-done.7.cola_ref
  27.6 0.4 %collective-permute-done.8.colb_ref = bf16[8,2,64,128]{3,2,1,0:T(8,128)(2,1)S(1)} collective-permute-done((bf16[8,2,64,128]{3,2,1,0:T(8,128)(2,1)S(1)}, bf16[8,2,64,128]{3,2,1,0:T(8,128)(2,1)S(1)}, u32[]{:S(2)}, u32[]{:S(2)}) %collective-permute-start.8) | collective-permute-done | bytes 262176 | tf_op jit(solution)/shard_map/ppermute | solution.py:387
  28.0 0.4 shard_map.59
  28.3 1.3 %collective-permute-start.12 = (bf16[8,2,64,128]{3,2,1,0:T(8,128)(2,1)S(1)}, bf16[8,2,64,128]{3,2,1,0:T(8,128)(2,1)S(1)}, u32[]{:S(2)}, u32[]{:S(2)}) collective-permute-start(bf16[8,2,64,128]{3,2,1,0:T(8,128)(2,1)S(1)} %get-tuple-element.84), channel_id=1, source_target_pairs={{0,8},{8,0},{16,24},{24,16},{1,9},{9,1},{17,25},{25,17},{2,10},{10... | collective-permute-start | bytes 786440 | tf_op jit(solution)/shard_map/ppermute | solution.py:374
  29.6 0.0 collective-permute-start.13
  29.6 0.2 shard_map.61
  29.8 2.1 %collective-permute-start.10 = (bf16[2,8,512]{2,1,0:T(8,128)(2,1)S(1)}, bf16[2,8,512]{2,1,0:T(8,128)(2,1)S(1)}, u32[]{:S(2)}, u32[]{:S(2)}) collective-permute-start(bf16[2,8,512]{2,1,0:T(8,128)(2,1)S(1)} %shard_map.61), channel_id=1, source_target_pairs={{0,1},{1,0},{2,3},{3,2},{4,5},{5,4},{6,7},{7,6},{8,9},{9,8},{10,11... | collective-permute-start | bytes 49160 | tf_op jit(solution)/shard_map/ppermute | solution.py:374
  31.9 2.5 %shard_map.60 = (f32[8,2,2,64,128]{4,3,2,1,0:T(8,128)S(1)}, f32[8,2,2,64,128]{4,3,2,1,0:T(8,128)S(1)}) custom-call(bf16[8,2,2,64,128]{4,3,2,1,0:T(8,128)(2,1)S(1)} %shard_map.54.after_ref.mid_ref.x_ref, bf16[8,2,2,64,128]{4,3,2,1,0:T(8,128)(2,1)S(1)} %get-tuple-element.69.rim_ref, bf16[256,768]{1,0:T(8,128)(2,1)S(1)} %get-tuple-element.74.after_ref.middle_ref, ...), custom_call_target="tpu_custom_call" | custom-call | flops 1000000 | bytes 10000 | tf_op jit(solution)/shard_map/pallas_call | solution.py:29
  34.4 0.0 collective-permute-done.10.rest_0_
  34.4 1.1 %shard_map.62 = (f32[8,2,2,64,128]{4,3,2,1,0:T(8,128)S(1)}, f32[8,2,2,64,128]{4,3,2,1,0:T(8,128)S(1)}) custom-call(bf16[8,2,2,64,128]{4,3,2,1,0:T(8,128)(2,1)S(1)} %shard_map.54.after_ref.mid_ref.x_ref, bf16[8,2,2,64,128]{4,3,2,1,0:T(8,128)(2,1)S(1)} %get-tuple-element.69.rim_ref, ...), custom_call_target="tpu_custom_call", output_to_operand_aliasing={{0}: (6, {}), {1}: (7, {})} | custom-call | flops 1000000 | bytes 10000 | tf_op jit(solution)/shard_map/pallas_call | solution.py:29
  35.6 0.0 collective-permute-done.11.b_ref
  35.6 0.2 shard_map.64.mid_ref
  35.8 0.9 %collective-permute-done.12.a_ref = bf16[8,2,64,128]{3,2,1,0:T(8,128)(2,1)S(1)} collective-permute-done((bf16[8,2,64,128]{3,2,1,0:T(8,128)(2,1)S(1)}, bf16[8,2,64,128]{3,2,1,0:T(8,128)(2,1)S(1)}, u32[]{:S(2)}, u32[]{:S(2)}) %collective-permute-start.12) | collective-permute-done | bytes 262176 | tf_op jit(solution)/shard_map/ppermute | solution.py:374
  36.7 0.0 collective-permute-done.13.b_ref
  36.7 1.0 %shard_map.65 = bf16[8,2,4,64,128]{4,3,2,1,0:T(8,128)(2,1)} custom-call(bf16[8,2,2,64,128]{4,3,2,1,0:T(8,128)(2,1)S(1)} %shard_map.64.mid_ref, bf16[8,2,2,64,128]{4,3,2,1,0:T(8,128)(2,1)S(1)} %get-tuple-element.69.rim_ref, f32[8,2,2,64,128]{4,3,2,1,0:T(8,128)S(1)} %get-tuple-element.83.acc_ref, bf16[8,2,64,128]{3,2,1,0:T(8,128)(2,1)S(1)} %collective-permute-done.12.a_ref, ...), custom_call_target="tpu_custom_call" | custom-call | flops 1000000 | bytes 10000 | tf_op jit(solution)/shard_map/pallas_call | solution.py:29
Async XLA Ops:
  1.4 6.9 %collective-permute-start = (bf16[8,2,64,128]{3,2,1,0:T(8,128)(2,1)S(1)}, bf16[8,2,64,128]{3,2,1,0:T(8,128)(2,1)S(1)}, u32[]{:S(2)}, u32[]{:S(2)}) collective-permute-start(bf16[8,2,64,128]{3,2,1,0:T(8,128)(2,1)S(1)} %get-tuple-element.47), channel_id=1, source_target_pairs={{0,2},{2,0},{4,6},{6,4},{1,3},{3,1},{5,7},{7,5},{8,10},{10,8},{12,... | collective-permute-start | bytes 786440 | tf_op jit(solution)/shard_map/ppermute | solution.py:374
  1.9 6.9 %collective-permute-start.1 = (bf16[8,2,64,128]{3,2,1,0:T(8,128)(2,1)S(1)}, bf16[8,2,64,128]{3,2,1,0:T(8,128)(2,1)S(1)}, u32[]{:S(2)}, u32[]{:S(2)}) collective-permute-start(bf16[8,2,64,128]{3,2,1,0:T(8,128)(2,1)S(1)} %get-tuple-element.48), channel_id=1, source_target_pairs={{0,1},{1,0},{2,4},{3,5},{4,2},{5,3},{6,7},{7,6},{8,9},{9,8},{10,12... | collective-permute-start | bytes 786440 | tf_op jit(solution)/shard_map/ppermute | solution.py:387
  5.1 11.9 %collective-permute-start.3 = (bf16[8,2,64,128]{3,2,1,0:T(8,128)(2,1)S(1)}, bf16[8,2,64,128]{3,2,1,0:T(8,128)(2,1)S(1)}, u32[]{:S(2)}, u32[]{:S(2)}) collective-permute-start(bf16[8,2,64,128]{3,2,1,0:T(8,128)(2,1)S(1)} %get-tuple-element.65), channel_id=1, source_target_pairs={{0,8},{8,0},{16,24},{24,16},{1,9},{9,1},{17,25},{25,17},{2,10},{10... | collective-permute-start | bytes 786440 | tf_op jit(solution)/shard_map/ppermute | solution.py:374
  6.7 10.3 %collective-permute-start.4 = (bf16[8,2,64,128]{3,2,1,0:T(8,128)(2,1)S(1)}, bf16[8,2,64,128]{3,2,1,0:T(8,128)(2,1)S(1)}, u32[]{:S(2)}, u32[]{:S(2)}) collective-permute-start(bf16[8,2,64,128]{3,2,1,0:T(8,128)(2,1)S(1)} %get-tuple-element.50.after_ref), channel_id=1, source_target_pairs={{0,2},{2,0},{4,6},{6,4},{8,16},{10,18},{12,20},{14,22},{16,8},{18,... | collective-permute-start | bytes 786440 | tf_op jit(solution)/shard_map/ppermute | solution.py:387
  9.3 9.8 %collective-permute-start.6 = (bf16[8,2,64,128]{3,2,1,0:T(8,128)(2,1)S(1)}, bf16[8,2,64,128]{3,2,1,0:T(8,128)(2,1)S(1)}, u32[]{:S(2)}, u32[]{:S(2)}) collective-permute-start(bf16[8,2,64,128]{3,2,1,0:T(8,128)(2,1)S(1)} %get-tuple-element.67), channel_id=1, source_target_pairs={{0,8},{8,0},{16,24},{24,16},{1,9},{9,1},{17,25},{25,17},{2,10},{10... | collective-permute-start | bytes 786440 | tf_op jit(solution)/shard_map/ppermute | solution.py:374
  11.9 9.3 %collective-permute-start.5 = (bf16[8,2,64,128]{3,2,1,0:T(8,128)(2,1)S(1)}, bf16[8,2,64,128]{3,2,1,0:T(8,128)(2,1)S(1)}, u32[]{:S(2)}, u32[]{:S(2)}) collective-permute-start(bf16[8,2,64,128]{3,2,1,0:T(8,128)(2,1)S(1)} %get-tuple-element.61.after_ref), channel_id=1, source_target_pairs={{0,2},{2,0},{4,6},{6,4},{8,16},{10,18},{12,20},{14,22},{16,8},{18,... | collective-permute-start | bytes 786440 | tf_op jit(solution)/shard_map/ppermute | solution.py:387
  12.1 3.7 %collective-permute-start.2 = (bf16[2,8,512]{2,1,0:T(8,128)(2,1)S(1)}, bf16[2,8,512]{2,1,0:T(8,128)(2,1)S(1)}, u32[]{:S(2)}, u32[]{:S(2)}) collective-permute-start(bf16[2,8,512]{2,1,0:T(8,128)(2,1)S(1)} %shard_map.52), channel_id=1, source_target_pairs={{0,1},{1,0},{2,3},{3,2},{4,5},{5,4},{6,7},{7,6},{8,9},{9,8},{10,11... | collective-permute-start | bytes 49160 | tf_op jit(solution)/shard_map/ppermute | solution.py:374
  19.6 7.5 %collective-permute-start.9 = (bf16[8,2,64,128]{3,2,1,0:T(8,128)(2,1)S(1)}, bf16[8,2,64,128]{3,2,1,0:T(8,128)(2,1)S(1)}, u32[]{:S(2)}, u32[]{:S(2)}) collective-permute-start(bf16[8,2,64,128]{3,2,1,0:T(8,128)(2,1)S(1)} %shard_map.56.after_ref), channel_id=1, source_target_pairs={{0,8},{8,0},{16,24},{24,16},{1,9},{9,1},{17,25},{25,17},{2,10},{10... | collective-permute-start | bytes 786440 | tf_op jit(solution)/shard_map/ppermute | solution.py:374
  21.4 6.1 %collective-permute-start.7 = (bf16[8,2,64,128]{3,2,1,0:T(8,128)(2,1)S(1)}, bf16[8,2,64,128]{3,2,1,0:T(8,128)(2,1)S(1)}, u32[]{:S(2)}, u32[]{:S(2)}) collective-permute-start(bf16[8,2,64,128]{3,2,1,0:T(8,128)(2,1)S(1)} %get-tuple-element.70), channel_id=1, source_target_pairs={{0,2},{2,0},{4,6},{6,4},{1,3},{3,1},{5,7},{7,5},{8,10},{10,8},{12,... | collective-permute-start | bytes 786440 | tf_op jit(solution)/shard_map/ppermute | solution.py:374
  21.5 6.4 %collective-permute-start.8 = (bf16[8,2,64,128]{3,2,1,0:T(8,128)(2,1)S(1)}, bf16[8,2,64,128]{3,2,1,0:T(8,128)(2,1)S(1)}, u32[]{:S(2)}, u32[]{:S(2)}) collective-permute-start(bf16[8,2,64,128]{3,2,1,0:T(8,128)(2,1)S(1)} %get-tuple-element.71), channel_id=1, source_target_pairs={{0,1},{1,0},{2,4},{3,5},{4,2},{5,3},{6,7},{7,6},{8,9},{9,8},{10,12... | collective-permute-start | bytes 786440 | tf_op jit(solution)/shard_map/ppermute | solution.py:387
  23.3 12.2 %collective-permute-start.11 = (bf16[8,2,64,128]{3,2,1,0:T(8,128)(2,1)S(1)}, bf16[8,2,64,128]{3,2,1,0:T(8,128)(2,1)S(1)}, u32[]{:S(2)}, u32[]{:S(2)}) collective-permute-start(bf16[8,2,64,128]{3,2,1,0:T(8,128)(2,1)S(1)} %shard_map.63), channel_id=1, source_target_pairs={{0,2},{2,0},{4,6},{6,4},{8,16},{10,18},{12,20},{14,22},{16,8},{18,... | collective-permute-start | bytes 786440 | tf_op jit(solution)/shard_map/ppermute | solution.py:387
  28.3 8.4 %collective-permute-start.12 = (bf16[8,2,64,128]{3,2,1,0:T(8,128)(2,1)S(1)}, bf16[8,2,64,128]{3,2,1,0:T(8,128)(2,1)S(1)}, u32[]{:S(2)}, u32[]{:S(2)}) collective-permute-start(bf16[8,2,64,128]{3,2,1,0:T(8,128)(2,1)S(1)} %get-tuple-element.84), channel_id=1, source_target_pairs={{0,8},{8,0},{16,24},{24,16},{1,9},{9,1},{17,25},{25,17},{2,10},{10... | collective-permute-start | bytes 786440 | tf_op jit(solution)/shard_map/ppermute | solution.py:374
  29.6 7.1 %collective-permute-start.13 = (bf16[8,2,64,128]{3,2,1,0:T(8,128)(2,1)S(1)}, bf16[8,2,64,128]{3,2,1,0:T(8,128)(2,1)S(1)}, u32[]{:S(2)}, u32[]{:S(2)}) collective-permute-start(bf16[8,2,64,128]{3,2,1,0:T(8,128)(2,1)S(1)} %get-tuple-element.79.after_ref), channel_id=1, source_target_pairs={{0,2},{2,0},{4,6},{6,4},{8,16},{10,18},{12,20},{14,22},{16,8},{18,... | collective-permute-start | bytes 786440 | tf_op jit(solution)/shard_map/ppermute | solution.py:387
  29.8 4.7 %collective-permute-start.10 = (bf16[2,8,512]{2,1,0:T(8,128)(2,1)S(1)}, bf16[2,8,512]{2,1,0:T(8,128)(2,1)S(1)}, u32[]{:S(2)}, u32[]{:S(2)}) collective-permute-start(bf16[2,8,512]{2,1,0:T(8,128)(2,1)S(1)} %shard_map.61), channel_id=1, source_target_pairs={{0,1},{1,0},{2,3},{3,2},{4,5},{5,4},{6,7},{7,6},{8,9},{9,8},{10,11... | collective-permute-start | bytes 49160 | tf_op jit(solution)/shard_map/ppermute | solution.py:374

commit v8 on v7

--- a/solution.py
+++ b/solution.py
@@ -110,6 +110,32 @@
         {2: pl.ANY},
     )
     return dict(zip(parts, got))
+
+
+class View:
+    def __init__(self, ref, columns):
+        self.ref, self.columns = ref, columns
+
+    @property
+    def shape(self):
+        channels, rows, _, depth, width = self.ref.shape
+        return channels, rows, len(self.columns), depth, width
+
+    def __getitem__(self, index):
+        first, i, j, *rest = index
+        return self.ref[(first, i, self.columns[j], *rest)]
+
+
+def middle(x_ref):
+    return View(x_ref, tuple(range(1, x_ref.shape[2] - 1)))
+
+
+def sides(x_ref):
+    return View(x_ref, (0, x_ref.shape[2] - 1))
+
+
+def whole(body, views, x_ref, *refs):
+    body(*(view(x_ref) for view in views), *refs)
 
 
 def band(tile):
@@ -352,21 +378,22 @@
 
 
 def open_body(parts, x_ref, src_w_ref, tgt_w_ref, bias_ref, *rest):
-    src_ref, tgt_ref, held_ref, beside_ref, mid_ref, rim_ref, cola_ref, colb_ref, sems = rest
-    rows, last = x_ref.shape[1], x_ref.shape[2] - 1
-    pairs = [(src_w_ref, src_ref)]
-    pairs += [(x_ref.at[:, i, n * last], rim_ref.at[:, i, n]) for i in range(rows) for n in range(2)]
-    pairs += [(x_ref.at[:, i, j], mid_ref.at[:, i, j - 1]) for i in range(rows) for j in range(1, last)]
-    pairs += [(tgt_w_ref, tgt_ref), (bias_ref, held_ref)]
+    src_ref, tgt_ref, held_ref, beside_ref, cola_ref, colb_ref, sems = rest
+    last = x_ref.shape[2] - 1
+    odd = parity("scol")
+    pairs = (
+        (src_w_ref, src_ref),
+        (x_ref.at[:, :, last * (1 - odd)], cola_ref),
+        (x_ref.at[:, :, last * odd], colb_ref),
+        (tgt_w_ref, tgt_ref),
+        (bias_ref, held_ref),
+    )
     copies = [pltpu.make_async_copy(a, b, sems.at[n]) for n, (a, b) in enumerate(pairs)]
     for copy in copies:
         copy.start()
     copies[0].wait()
     operators(parts, src_ref, None, (beside_ref,))
-    for copy in copies[1 : 1 + 2 * rows]:
-        copy.wait()
-    sent_columns(rim_ref, (cola_ref, colb_ref))
-    for copy in copies[1 + 2 * rows :]:
+    for copy in copies[1:]:
         copy.wait()
 
 
@@ -392,45 +419,46 @@
     channels, rows, cols, depth, width = volume.shape
     axes = ("srow", "scol", "trow")
     counts = [lax.axis_size(n) for n in axes]
-    assert all(count % 2 == 0 for count in counts) and rows > 1 and cols > 2
+    assert all(count % 2 == 0 for count in counts) and rows > 1 and cols > 2 and layers > 1
     src_w = jnp.transpose(src_weight, (0, 2, 3, 1))
     tgt_w = jnp.transpose(tgt_weight, (0, 2, 3, 1))
     deep_swaps = 1 if counts[2] == 2 else 2
     mid_shape, rim_shape = ((channels, rows, n, depth, width) for n in (cols - 2, 2))
     line = VMEM((channels, rows, depth, width), BF16)
     owed_rim = VMEM((channels, 2, depth, width), BF16)
-    sent = [VMEM(rim_shape, BF16), line, line]
     early = [("beside", 0)]
-    src_w, tgt_w, bias, beside_0, mid, rim, col_a, col_b = call(
+    src_w, tgt_w, bias, beside_0, col_a, col_b = call(
         functools.partial(open_body, early),
-        [VMEM(src_w.shape, BF16), VMEM(tgt_w.shape, BF16), VMEM(bias.shape, F32)]
-        + operator_shapes(early, channels)
-        + [VMEM(mid_shape, BF16)]
-        + sent,
+        [VMEM(src_w.shape, BF16), VMEM(tgt_w.shape, BF16), VMEM(bias.shape, F32)] + operator_shapes(early, channels) + [line, line],
         (volume, src_w, tgt_w, bias),
         {n: HBM for n in range(4)},
-        scratch=[pltpu.SemaphoreType.DMA((3 + rows * cols,))],
+        scratch=[pltpu.SemaphoreType.DMA((5,))],
     )
     made = {early[0]: beside_0}
     kinds = ("middle", "beside", "target", "near", "deep")
     owed_inner = [VMEM((channels, cols - 2, depth, width), BF16)]
-    sum_a = None
+    block, sum_a = (volume,), None
     for layer in range(layers):
+
+        def on(body, *views):
+            return functools.partial(whole, body, views) if layer == 0 else body
+
+        both, base = (middle, sides), len(block)
+        mid, rim = block[0], block[-1]
         beside = swap_first(col_a, "scol"), swap_second(col_b, "scol", "trow")
         which = (0, 1) if sum_a is None else (1,)
-        sums = call(functools.partial(inner_body, which), owed_inner * len(which), (mid, rim, made["beside", layer]))
+        sums = call(on(functools.partial(inner_body, which), *both), owed_inner * len(which), (*block, made["beside", layer]))
         sum_b = sums[-1]
         inner = swap_first(sums[0], "srow") if sum_a is None else got_a, swap_second(sum_b, "srow", "scol")
         if layer == 0:
             late = [(kind, n) for n in range(layers) for kind in kinds]
             made |= build([part for part in late if part not in early], src_w, tgt_w, sum_b)
         operator = {kind: made[kind, layer] for kind in kinds}
-
         parts = call(
-            part_body,
+            on(part_body, *both),
             [VMEM((2, channels * BAND, depth // BAND * width), F32)] * 2,
-            (mid, rim, operator["beside"], inner[0] if layer else sum_b),
-            {3: pl.ANY},
+            (*block, operator["beside"], sum_b),
+            {base + 1: pl.ANY},
         )
         a, b, side = call(
             edge_body,
@@ -440,32 +468,41 @@
         )
         outer = swap_first(a, "srow"), swap_second(b, "srow", "scol")
         deep = call(
-            depth_body, [VMEM((rows, channels, cols * width), BF16)] * deep_swaps, (mid, rim, b), {2: pl.ANY}
+            on(depth_body, *both),
+            [VMEM((rows, channels, cols * width), BF16)] * deep_swaps,
+            (*block, b),
+            {base: pl.ANY},
         )
         deeper = [swap_first(deep[0], "trow")]
         if deep_swaps == 2:
             deeper.append(swap_second(deep[1], "trow", "scol"))
         accs = call(
-            functools.partial(own_body, layer),
+            on(functools.partial(own_body, layer), *both),
             [VMEM(mid_shape, F32), VMEM(rim_shape, F32)],
-            (mid, rim, *(operator[kind] for kind in ("middle", "beside", "target", "near")), bias, b),
-            {7: pl.ANY},
+            (*block, *(operator[kind] for kind in ("middle", "beside", "target", "near")), bias, b),
+            {base + 5: pl.ANY},
             scratch=[VMEM((depth // BAND, 3, channels * BAND, cols * width), BF16)],
         )
         acc_mid, acc_rim = call(
-            rest_body,
+            on(rest_body, *both),
             [VMEM(mid_shape, F32), VMEM(rim_shape, F32)],
-            (mid, rim, side, *(operator[kind] for kind in ("middle", "beside", "deep")), *accs, *deeper),
-            aliases={6: 0, 7: 1},
+            (*block, side, *(operator[kind] for kind in ("middle", "beside", "deep")), *accs, *deeper),
+            aliases={base + 4: 0, base + 5: 1},
         )
-        (mid,) = call(mid_body, [VMEM(mid_shape, BF16)], (mid, acc_mid, *inner))
+        (mid,) = call(on(mid_body, middle), [VMEM(mid_shape, BF16)], (mid, acc_mid, *inner))
         if layer < layers - 1:
-            begun, *_ = call(begin_body, sent[:1], (rim, acc_rim, outer[0], mid), {3: pl.ANY})
+            whole_rim = [VMEM(rim_shape, BF16)]
+            (begun,) = call(on(begin_body, sides), whole_rim, (rim, acc_rim, outer[0], mid), {3: pl.ANY})
             (sum_a,) = call(functools.partial(inner_body, (0,)), owed_inner, (mid, begun, made["beside", layer + 1]))
             got_a = swap_first(sum_a, "srow")
             rim, col_a, col_b = call(
-                next_body, sent, (rim, acc_rim, outer[1], begun, sum_a), {4: pl.ANY}, aliases={3: 0}
+                on(next_body, sides),
+                whole_rim + [line, line],
+                (rim, acc_rim, outer[1], begun, sum_a),
+                {4: pl.ANY},
+                aliases={3: 0},
             )
+            block = (mid, rim)
         else:
             (state,) = call(
                 last_body,

time: 37.9 us -> 36.6 us (0.966)
  waiting for transfers between devices: 7.61 us -> 5.72 us
  starting transfers between devices: 15.1 us -> 15.9 us
    ppermute x8, waiting for transfers between devices: 6.64 us -> 3.28 us  [swap_first(): lax.ppermute(value, axis, [(n, n ^ 1) for n in range(lax.axis_size(axis))])]
    ppermute x6, waiting for transfers between devices: 0.97 us -> 2.44 us  [swap_second(): return lax.ppermute(value, (axis, other), pairs)]
    ppermute x8, starting transfers between devices: 10.9 us -> 12.2 us  [swap_first(): lax.ppermute(value, axis, [(n, n ^ 1) for n in range(lax.axis_size(axis))])]
    ppermute x6, starting transfers between devices: 4.14 us -> 3.71 us  [swap_second(): return lax.ppermute(value, (axis, other), pairs)]
  transfers between devices with their start and end apart: 14 -> 14, of which waited for: 6 -> 5; matrix products, arithmetic and copies ran while one was open for 0% -> 0% of each run, Pallas kernels for 33% -> 34%
where the time goes in v8:
time: 36.6 us; the launch traced here: 36.5 us
  starting transfers between devices  15.9 us (43%)
  Pallas kernels  14.7 us (40%)
  waiting for transfers between devices  5.72 us (16%)
    pallas_call x20, Pallas kernels, call(): pl.pallas_call(body, out_shape=tuple(outs), in_specs=[pl.BlockSpec(memory...  14.7 us
    ppermute x8, starting transfers between devices, swap_first(): lax.ppermute(value, axis, [(n, n ^ 1) for n in range(lax.axis_size(axis))])  12.2 us
    ppermute x6, starting transfers between devices, swap_second(): return lax.ppermute(value, (axis, other), pairs)  3.71 us
    ppermute x8, waiting for transfers between devices, swap_first(): lax.ppermute(value, axis, [(n, n ^ 1) for n in range(lax.axis_size(axis))])  3.28 us
    ppermute x6, waiting for transfers between devices, swap_second(): return lax.ppermute(value, (axis, other), pairs)  2.44 us
  transfers between devices with their start and end apart: 14, of which 5 were waited for; matrix products, arithmetic and copies ran while one was open for 0% of the time, Pallas kernels for 34%

profile of v8, /device:TPU:0, one launch (start us, length us, event | category | flops | bytes accessed | tf_op | source)
XLA Modules:
  0.0 36.5 jit_solution(1295819056389030432)
XLA Ops:
  0.0 0.0 copy-start
  0.0 1.2 %shard_map.46 = (bf16[2,8,8,9]{3,2,1,0:T(8,128)(2,1)S(1)}, bf16[2,8,8,9]{3,2,1,0:T(8,128)(2,1)S(1)}, f32[2,8]{1,0:T(2,128)S(1)}, bf16[2,256,768]{2,1,0:T(8,128)(...) custom-call(bf16[8,2,4,64,128]{4,3,2,1,0:T(8,128)(2,1)} %x_ref.17, ...), custom_call_target="tpu_custom_call" | custom-call | flops 1000000 | bytes 10000 | tf_op jit(solution)/shard_map/pallas_call | solution.py:29
  1.2 0.5 %collective-permute-start = (bf16[8,2,64,128]{3,2,1,0:T(8,128)(2,1)S(1)}, bf16[8,2,64,128]{3,2,1,0:T(8,128)(2,1)S(1)}, u32[]{:S(2)}, u32[]{:S(2)}) collective-permute-start(bf16[8,2,64,128]{3,2,1,0:T(8,128)(2,1)S(1)} %get-tuple-element.43), channel_id=1, source_target_pairs={{0,2},{2,0},{4,6},{6,4},{1,3},{3,1},{5,7},{7,5},{8,10},{10,8},{12,... | collective-permute-start | bytes 786440 | tf_op jit(solution)/shard_map/ppermute | solution.py:401
  1.7 2.6 %collective-permute-start.1 = (bf16[8,2,64,128]{3,2,1,0:T(8,128)(2,1)S(1)}, bf16[8,2,64,128]{3,2,1,0:T(8,128)(2,1)S(1)}, u32[]{:S(2)}, u32[]{:S(2)}) collective-permute-start(bf16[8,2,64,128]{3,2,1,0:T(8,128)(2,1)S(1)} %get-tuple-element.44), channel_id=1, source_target_pairs={{0,1},{1,0},{2,4},{3,5},{4,2},{5,3},{6,7},{7,6},{8,9},{9,8},{10,12... | collective-permute-start | bytes 786440 | tf_op jit(solution)/shard_map/ppermute | solution.py:414
  4.3 0.0 copy-done
  4.3 0.6 %shard_map.47 = (bf16[8,2,64,128]{3,2,1,0:T(8,128)(2,1)S(1)}, bf16[8,2,64,128]{3,2,1,0:T(8,128)(2,1)S(1)}) custom-call(bf16[8,2,4,64,128]{4,3,2,1,0:T(8,128)(2,1)S(1)} %copy-done, bf16[2,256,768]{2,1,0:T(8,128)(2,1)S(1)} %get-tuple-element.45.refs_0_.beside_ref.refs_1_.refs_2_), custom_call_target="tpu_custom_call" | custom-call | flops 1000000 | bytes 10000 | tf_op jit(solution)/shard_map/pallas_call | solution.py:29
  4.9 1.6 %collective-permute-start.3 = (bf16[8,2,64,128]{3,2,1,0:T(8,128)(2,1)S(1)}, bf16[8,2,64,128]{3,2,1,0:T(8,128)(2,1)S(1)}, u32[]{:S(2)}, u32[]{:S(2)}) collective-permute-start(bf16[8,2,64,128]{3,2,1,0:T(8,128)(2,1)S(1)} %get-tuple-element.61), channel_id=1, source_target_pairs={{0,8},{8,0},{16,24},{24,16},{1,9},{9,1},{17,25},{25,17},{2,10},{10... | collective-permute-start | bytes 786440 | tf_op jit(solution)/shard_map/ppermute | solution.py:401
  6.5 0.0 collective-permute-start.4
  6.5 0.4 %shard_map.48 = (f32[2,256,256]{2,1,0:T(8,128)S(1)}, f32[2,256,256]{2,1,0:T(8,128)S(1)}) custom-call(bf16[8,2,4,64,128]{4,3,2,1,0:T(8,128)(2,1)S(1)} %copy-done, bf16[2,256,768]{2,1,0:T(8,128)(2,1)S(1)} %get-tuple-element.45.refs_0_.beside_ref.refs_1_.refs_2_, bf16[8,2,64,128]{3,2,1,0:T(8,128)(2,1)S(1)} %get-tuple-element.46.refs_1_.after_ref), custom_call_target="tpu_custom_call" | custom-call | flops 1000000 | bytes 10000 | tf_op jit(solution)/shard_map/pallas_call | solution.py:29
  7.0 1.1 %shard_map.49 = (bf16[256,768]{1,0:T(8,128)(2,1)S(1)}, bf16[256,768]{1,0:T(8,128)(2,1)S(1)}, bf16[2,256,384]{2,1,0:T(8,128)(2,1)S(1)}, bf16[2,256,24]{2,1,0:T(8,...) custom-call(bf16[2,8,8,9]{3,2,1,0:T(8,128)(2,1)S(1)} %get-tuple-elem, ...), custom_call_target="tpu_custom_call" | custom-call | flops 1000000 | bytes 10000 | tf_op jit(solution)/shard_map/pallas_call | solution.py:29
  8.1 0.0 collective-permute-done.cola_ref
  8.1 0.6 %collective-permute-done.1.colb_ref = bf16[8,2,64,128]{3,2,1,0:T(8,128)(2,1)S(1)} collective-permute-done((bf16[8,2,64,128]{3,2,1,0:T(8,128)(2,1)S(1)}, bf16[8,2,64,128]{3,2,1,0:T(8,128)(2,1)S(1)}, u32[]{:S(2)}, u32[]{:S(2)}) %collective-permute-start.1) | collective-permute-done | bytes 262176 | tf_op jit(solution)/shard_map/ppermute | solution.py:414
  8.7 0.4 %shard_map.50 = (bf16[8,2,64,128]{3,2,1,0:T(8,128)(2,1)S(1)}, bf16[8,2,64,128]{3,2,1,0:T(8,128)(2,1)S(1)}, bf16[2,8,2,64,128]{4,3,2,1,0:T(8,128)(2,1)S(1)}) custom-call(bf16[8,2,64,128]{3,2,1,0:T(8,128)(2,1)S(1)} %collective-permute-done.cola_ref, bf16[8,2,64,128]{3,2,1,0:T(8,128)(2,1)S(1)} %collective-permute-done.1.colb_ref, ...), custom_call_target="tpu_custom_call" | custom-call | flops 1000000 | bytes 10000 | tf_op jit(solution)/shard_map/pallas_call | solution.py:29
  9.0 2.7 %collective-permute-start.6 = (bf16[8,2,64,128]{3,2,1,0:T(8,128)(2,1)S(1)}, bf16[8,2,64,128]{3,2,1,0:T(8,128)(2,1)S(1)}, u32[]{:S(2)}, u32[]{:S(2)}) collective-permute-start(bf16[8,2,64,128]{3,2,1,0:T(8,128)(2,1)S(1)} %get-tuple-element.63), channel_id=1, source_target_pairs={{0,8},{8,0},{16,24},{24,16},{1,9},{9,1},{17,25},{25,17},{2,10},{10... | collective-permute-start | bytes 786440 | tf_op jit(solution)/shard_map/ppermute | solution.py:401
  11.7 0.0 collective-permute-start.5
  11.7 0.2 shard_map.52
  11.9 1.0 %collective-permute-start.2 = (bf16[2,8,512]{2,1,0:T(8,128)(2,1)S(1)}, bf16[2,8,512]{2,1,0:T(8,128)(2,1)S(1)}, u32[]{:S(2)}, u32[]{:S(2)}) collective-permute-start(bf16[2,8,512]{2,1,0:T(8,128)(2,1)S(1)} %shard_map.52), channel_id=1, source_target_pairs={{0,1},{1,0},{2,3},{3,2},{4,5},{5,4},{6,7},{7,6},{8,9},{9,8},{10,11... | collective-permute-start | bytes 49160 | tf_op jit(solution)/shard_map/ppermute | solution.py:401
  12.9 2.5 %shard_map.51 = (f32[8,2,2,64,128]{4,3,2,1,0:T(8,128)S(1)}, f32[8,2,2,64,128]{4,3,2,1,0:T(8,128)S(1)}) custom-call(bf16[8,2,4,64,128]{4,3,2,1,0:T(8,128)(2,1)S(1)} %copy-done, bf16[256,768]{1,0:T(8,128)(2,1)S(1)} %get-tuple-element.51.after_ref.refs_0_.refs_1_, bf16[2,256,768]{2,1,0:T(8,128)(2,1)S(1)} %get-tuple-element.45.refs_0_.beside_ref.refs_1_.refs_2_, ...), custom_call_target="tpu_custom_call" | custom-call | flops 1000000 | bytes 10000 | tf_op jit(solution)/shard_map/pallas_call | solution.py:29
  15.4 0.2 collective-permute-done.2.refs_6_
  15.7 1.1 %shard_map.53 = (f32[8,2,2,64,128]{4,3,2,1,0:T(8,128)S(1)}, f32[8,2,2,64,128]{4,3,2,1,0:T(8,128)S(1)}) custom-call(bf16[8,2,4,64,128]{4,3,2,1,0:T(8,128)(2,1)S(1)} %copy-done, bf16[2,8,2,64,128]{4,3,2,1,0:T(8,128)(2,1)S(1)} %get-tuple-element.52.refs_0_, ...), custom_call_target="tpu_custom_call", output_to_operand_aliasing={{0}: (5, {}), {1}: (6, {})} | custom-call | flops 1000000 | bytes 10000 | tf_op jit(solution)/shard_map/pallas_call | solution.py:29
  16.8 0.0 collective-permute-done.3.refs_1_
  16.8 0.0 collective-permute-done.4.refs_2_
  16.8 0.2 shard_map.54.refs_2_.mid_ref.x_ref
  17.0 1.8 %collective-permute-done.6.refs_1_ = bf16[8,2,64,128]{3,2,1,0:T(8,128)(2,1)S(1)} collective-permute-done((bf16[8,2,64,128]{3,2,1,0:T(8,128)(2,1)S(1)}, bf16[8,2,64,128]{3,2,1,0:T(8,128)(2,1)S(1)}, u32[]{:S(2)}, u32[]{:S(2)}) %collective-permute-start.6) | collective-permute-done | bytes 262176 | tf_op jit(solution)/shard_map/ppermute | solution.py:401
  18.9 0.1 shard_map.55.rim_ref.refs_2_
  19.0 0.4 %shard_map.56.refs_3_ = bf16[8,2,64,128]{3,2,1,0:T(8,128)(2,1)S(1)} custom-call(bf16[8,2,2,64,128]{4,3,2,1,0:T(8,128)(2,1)S(1)} %shard_map.54.refs_2_.mid_ref.x_ref, bf16[8,2,2,64,128]{4,3,2,1,0:T(8,128)(2,1)S(1)} %shard_map.55.rim_ref.refs_2_, bf16[2,256,768]{2,1,0:T(8,128)(2,1)S(1)} %get-tuple-element.64.beside_ref), custom_call_target="tpu_custom_call" | custom-call | flops 1000000 | bytes 10000 | tf_op jit(solution)/shard_map/pallas_call | solution.py:29
  19.4 0.0 collective-permute-done.5.refs_1_
  19.4 0.2 shard_map.57
  19.6 0.1 collective-permute-start.7
  19.7 1.0 %collective-permute-start.8 = (bf16[8,2,64,128]{3,2,1,0:T(8,128)(2,1)S(1)}, bf16[8,2,64,128]{3,2,1,0:T(8,128)(2,1)S(1)}, u32[]{:S(2)}, u32[]{:S(2)}) collective-permute-start(bf16[8,2,64,128]{3,2,1,0:T(8,128)(2,1)S(1)} %get-tuple-element.67), channel_id=1, source_target_pairs={{0,1},{1,0},{2,4},{3,5},{4,2},{5,3},{6,7},{7,6},{8,9},{9,8},{10,12... | collective-permute-start | bytes 786440 | tf_op jit(solution)/shard_map/ppermute | solution.py:414
  20.7 2.6 %collective-permute-start.10 = (bf16[8,2,64,128]{3,2,1,0:T(8,128)(2,1)S(1)}, bf16[8,2,64,128]{3,2,1,0:T(8,128)(2,1)S(1)}, u32[]{:S(2)}, u32[]{:S(2)}) collective-permute-start(bf16[8,2,64,128]{3,2,1,0:T(8,128)(2,1)S(1)} %shard_map.56.refs_3_), channel_id=1, source_target_pairs={{0,8},{8,0},{16,24},{24,16},{1,9},{9,1},{17,25},{25,17},{2,10},{10... | collective-permute-start | bytes 786440 | tf_op jit(solution)/shard_map/ppermute | solution.py:401
  23.3 0.4 shard_map.58.after_ref
  23.7 0.1 collective-permute-start.11
  23.8 0.4 %shard_map.59 = (f32[2,256,256]{2,1,0:T(8,128)S(1)}, f32[2,256,256]{2,1,0:T(8,128)S(1)}) custom-call(bf16[8,2,2,64,128]{4,3,2,1,0:T(8,128)(2,1)S(1)} %shard_map.54.refs_2_.mid_ref.x_ref, bf16[8,2,2,64,128]{4,3,2,1,0:T(8,128)(2,1)S(1)} %get-tuple-element.65.rim_ref, bf16[2,256,768]{2,1,0:T(8,128)(2,1)S(1)} %get-tuple-element.64.beside_ref, ...), custom_call_target="tpu_custom_call" | custom-call | flops 1000000 | bytes 10000 | tf_op jit(solution)/shard_map/pallas_call | solution.py:29
  24.2 0.0 collective-permute-done.7.cola_ref
  24.2 1.9 %collective-permute-done.8.colb_ref = bf16[8,2,64,128]{3,2,1,0:T(8,128)(2,1)S(1)} collective-permute-done((bf16[8,2,64,128]{3,2,1,0:T(8,128)(2,1)S(1)}, bf16[8,2,64,128]{3,2,1,0:T(8,128)(2,1)S(1)}, u32[]{:S(2)}, u32[]{:S(2)}) %collective-permute-start.8) | collective-permute-done | bytes 262176 | tf_op jit(solution)/shard_map/ppermute | solution.py:414
  26.1 0.4 %shard_map.60 = (bf16[8,2,64,128]{3,2,1,0:T(8,128)(2,1)S(1)}, bf16[8,2,64,128]{3,2,1,0:T(8,128)(2,1)S(1)}, bf16[2,8,2,64,128]{4,3,2,1,0:T(8,128)(2,1)S(1)}) custom-call(bf16[8,2,64,128]{3,2,1,0:T(8,128)(2,1)S(1)} %collective-permute-done.7.cola_ref, bf16[8,2,64,128]{3,2,1,0:T(8,128)(2,1)S(1)} %collective-permute-done.8.colb_ref, ...), custom_call_target="tpu_custom_call" | custom-call | flops 1000000 | bytes 10000 | tf_op jit(solution)/shard_map/pallas_call | solution.py:29
  26.5 2.3 %collective-permute-start.12 = (bf16[8,2,64,128]{3,2,1,0:T(8,128)(2,1)S(1)}, bf16[8,2,64,128]{3,2,1,0:T(8,128)(2,1)S(1)}, u32[]{:S(2)}, u32[]{:S(2)}) collective-permute-start(bf16[8,2,64,128]{3,2,1,0:T(8,128)(2,1)S(1)} %get-tuple-element.80), channel_id=1, source_target_pairs={{0,8},{8,0},{16,24},{24,16},{1,9},{9,1},{17,25},{25,17},{2,10},{10... | collective-permute-start | bytes 786440 | tf_op jit(solution)/shard_map/ppermute | solution.py:401
  28.7 0.0 collective-permute-start.13
  28.7 0.2 shard_map.62
  28.9 1.4 %collective-permute-start.9 = (bf16[2,8,512]{2,1,0:T(8,128)(2,1)S(1)}, bf16[2,8,512]{2,1,0:T(8,128)(2,1)S(1)}, u32[]{:S(2)}, u32[]{:S(2)}) collective-permute-start(bf16[2,8,512]{2,1,0:T(8,128)(2,1)S(1)} %shard_map.62), channel_id=1, source_target_pairs={{0,1},{1,0},{2,3},{3,2},{4,5},{5,4},{6,7},{7,6},{8,9},{9,8},{10,11... | collective-permute-start | bytes 49160 | tf_op jit(solution)/shard_map/ppermute | solution.py:401
  30.3 2.5 %shard_map.61 = (f32[8,2,2,64,128]{4,3,2,1,0:T(8,128)S(1)}, f32[8,2,2,64,128]{4,3,2,1,0:T(8,128)S(1)}) custom-call(bf16[8,2,2,64,128]{4,3,2,1,0:T(8,128)(2,1)S(1)} %shard_map.54.refs_2_.mid_ref.x_ref, bf16[8,2,2,64,128]{4,3,2,1,0:T(8,128)(2,1)S(1)} %get-tuple-element.65.rim_ref, bf16[256,768]{1,0:T(8,128)(2,1)S(1)} %get-tuple-element.70.after_ref.middle_ref, ...), custom_call_target="tpu_custom_call" | custom-call | flops 1000000 | bytes 10000 | tf_op jit(solution)/shard_map/pallas_call | solution.py:29
  32.8 0.0 collective-permute-done.9.rest_0_
  32.9 1.1 %shard_map.63 = (f32[8,2,2,64,128]{4,3,2,1,0:T(8,128)S(1)}, f32[8,2,2,64,128]{4,3,2,1,0:T(8,128)S(1)}) custom-call(bf16[8,2,2,64,128]{4,3,2,1,0:T(8,128)(2,1)S(1)} %shard_map.54.refs_2_.mid_ref.x_ref, bf16[8,2,2,64,128]{4,3,2,1,0:T(8,128)(2,1)S(1)} %get-tuple-element.65.rim_ref, ...), custom_call_target="tpu_custom_call", output_to_operand_aliasing={{0}: (6, {}), {1}: (7, {})} | custom-call | flops 1000000 | bytes 10000 | tf_op jit(solution)/shard_map/pallas_call | solution.py:29
  34.0 0.0 collective-permute-done.11.b_ref
  34.0 0.0 collective-permute-done.10.a_ref
  34.0 0.2 shard_map.64.mid_ref
  34.3 1.2 %collective-permute-done.12.a_ref = bf16[8,2,64,128]{3,2,1,0:T(8,128)(2,1)S(1)} collective-permute-done((bf16[8,2,64,128]{3,2,1,0:T(8,128)(2,1)S(1)}, bf16[8,2,64,128]{3,2,1,0:T(8,128)(2,1)S(1)}, u32[]{:S(2)}, u32[]{:S(2)}) %collective-permute-start.12) | collective-permute-done | bytes 262176 | tf_op jit(solution)/shard_map/ppermute | solution.py:401
  35.5 0.0 collective-permute-done.13.b_ref
  35.5 1.0 %shard_map.65 = bf16[8,2,4,64,128]{4,3,2,1,0:T(8,128)(2,1)} custom-call(bf16[8,2,2,64,128]{4,3,2,1,0:T(8,128)(2,1)S(1)} %shard_map.64.mid_ref, bf16[8,2,2,64,128]{4,3,2,1,0:T(8,128)(2,1)S(1)} %get-tuple-element.65.rim_ref, f32[8,2,2,64,128]{4,3,2,1,0:T(8,128)S(1)} %get-tuple-element.79.acc_ref, bf16[8,2,64,128]{3,2,1,0:T(8,128)(2,1)S(1)} %collective-permute-done.12.a_ref, ...), custom_call_target="tpu_custom_call" | custom-call | flops 1000000 | bytes 10000 | tf_op jit(solution)/shard_map/pallas_call | solution.py:29
Async XLA Ops:
  0.0 4.3 %copy-start = (bf16[8,2,4,64,128]{4,3,2,1,0:T(8,128)(2,1)S(1)}, bf16[8,2,4,64,128]{4,3,2,1,0:T(8,128)(2,1)}, u32[]{:S(2)}) copy-start(bf16[8,2,4,64,128]{4,3,2,1,0:T(8,128)(2,1)} %x_ref.17) | copy-start | bytes 3145732
  1.2 6.9 %collective-permute-start = (bf16[8,2,64,128]{3,2,1,0:T(8,128)(2,1)S(1)}, bf16[8,2,64,128]{3,2,1,0:T(8,128)(2,1)S(1)}, u32[]{:S(2)}, u32[]{:S(2)}) collective-permute-start(bf16[8,2,64,128]{3,2,1,0:T(8,128)(2,1)S(1)} %get-tuple-element.43), channel_id=1, source_target_pairs={{0,2},{2,0},{4,6},{6,4},{1,3},{3,1},{5,7},{7,5},{8,10},{10,8},{12,... | collective-permute-start | bytes 786440 | tf_op jit(solution)/shard_map/ppermute | solution.py:401
  1.7 6.9 %collective-permute-start.1 = (bf16[8,2,64,128]{3,2,1,0:T(8,128)(2,1)S(1)}, bf16[8,2,64,128]{3,2,1,0:T(8,128)(2,1)S(1)}, u32[]{:S(2)}, u32[]{:S(2)}) collective-permute-start(bf16[8,2,64,128]{3,2,1,0:T(8,128)(2,1)S(1)} %get-tuple-element.44), channel_id=1, source_target_pairs={{0,1},{1,0},{2,4},{3,5},{4,2},{5,3},{6,7},{7,6},{8,9},{9,8},{10,12... | collective-permute-start | bytes 786440 | tf_op jit(solution)/shard_map/ppermute | solution.py:414
  4.9 11.9 %collective-permute-start.3 = (bf16[8,2,64,128]{3,2,1,0:T(8,128)(2,1)S(1)}, bf16[8,2,64,128]{3,2,1,0:T(8,128)(2,1)S(1)}, u32[]{:S(2)}, u32[]{:S(2)}) collective-permute-start(bf16[8,2,64,128]{3,2,1,0:T(8,128)(2,1)S(1)} %get-tuple-element.61), channel_id=1, source_target_pairs={{0,8},{8,0},{16,24},{24,16},{1,9},{9,1},{17,25},{25,17},{2,10},{10... | collective-permute-start | bytes 786440 | tf_op jit(solution)/shard_map/ppermute | solution.py:401
  6.5 10.3 %collective-permute-start.4 = (bf16[8,2,64,128]{3,2,1,0:T(8,128)(2,1)S(1)}, bf16[8,2,64,128]{3,2,1,0:T(8,128)(2,1)S(1)}, u32[]{:S(2)}, u32[]{:S(2)}) collective-permute-start(bf16[8,2,64,128]{3,2,1,0:T(8,128)(2,1)S(1)} %get-tuple-element.46.refs_1_.after_ref), channel_id=1, source_target_pairs={{0,2},{2,0},{4,6},{6,4},{8,16},{10,18},{12,20},{14,22},{16,8},{18,... | collective-permute-start | bytes 786440 | tf_op jit(solution)/shard_map/ppermute | solution.py:414
  9.0 9.8 %collective-permute-start.6 = (bf16[8,2,64,128]{3,2,1,0:T(8,128)(2,1)S(1)}, bf16[8,2,64,128]{3,2,1,0:T(8,128)(2,1)S(1)}, u32[]{:S(2)}, u32[]{:S(2)}) collective-permute-start(bf16[8,2,64,128]{3,2,1,0:T(8,128)(2,1)S(1)} %get-tuple-element.63), channel_id=1, source_target_pairs={{0,8},{8,0},{16,24},{24,16},{1,9},{9,1},{17,25},{25,17},{2,10},{10... | collective-permute-start | bytes 786440 | tf_op jit(solution)/shard_map/ppermute | solution.py:401
  11.7 7.7 %collective-permute-start.5 = (bf16[8,2,64,128]{3,2,1,0:T(8,128)(2,1)S(1)}, bf16[8,2,64,128]{3,2,1,0:T(8,128)(2,1)S(1)}, u32[]{:S(2)}, u32[]{:S(2)}) collective-permute-start(bf16[8,2,64,128]{3,2,1,0:T(8,128)(2,1)S(1)} %get-tuple-element.57.refs_5_.refs_0_), channel_id=1, source_target_pairs={{0,2},{2,0},{4,6},{6,4},{8,16},{10,18},{12,20},{14,22},{16,8},{18,... | collective-permute-start | bytes 786440 | tf_op jit(solution)/shard_map/ppermute | solution.py:414
  11.9 3.7 %collective-permute-start.2 = (bf16[2,8,512]{2,1,0:T(8,128)(2,1)S(1)}, bf16[2,8,512]{2,1,0:T(8,128)(2,1)S(1)}, u32[]{:S(2)}, u32[]{:S(2)}) collective-permute-start(bf16[2,8,512]{2,1,0:T(8,128)(2,1)S(1)} %shard_map.52), channel_id=1, source_target_pairs={{0,1},{1,0},{2,3},{3,2},{4,5},{5,4},{6,7},{7,6},{8,9},{9,8},{10,11... | collective-permute-start | bytes 49160 | tf_op jit(solution)/shard_map/ppermute | solution.py:401
  19.6 4.6 %collective-permute-start.7 = (bf16[8,2,64,128]{3,2,1,0:T(8,128)(2,1)S(1)}, bf16[8,2,64,128]{3,2,1,0:T(8,128)(2,1)S(1)}, u32[]{:S(2)}, u32[]{:S(2)}) collective-permute-start(bf16[8,2,64,128]{3,2,1,0:T(8,128)(2,1)S(1)} %get-tuple-element.66), channel_id=1, source_target_pairs={{0,2},{2,0},{4,6},{6,4},{1,3},{3,1},{5,7},{7,5},{8,10},{10,8},{12,... | collective-permute-start | bytes 786440 | tf_op jit(solution)/shard_map/ppermute | solution.py:401
  19.7 6.4 %collective-permute-start.8 = (bf16[8,2,64,128]{3,2,1,0:T(8,128)(2,1)S(1)}, bf16[8,2,64,128]{3,2,1,0:T(8,128)(2,1)S(1)}, u32[]{:S(2)}, u32[]{:S(2)}) collective-permute-start(bf16[8,2,64,128]{3,2,1,0:T(8,128)(2,1)S(1)} %get-tuple-element.67), channel_id=1, source_target_pairs={{0,1},{1,0},{2,4},{3,5},{4,2},{5,3},{6,7},{7,6},{8,9},{9,8},{10,12... | collective-permute-start | bytes 786440 | tf_op jit(solution)/shard_map/ppermute | solution.py:414
  20.7 13.3 %collective-permute-start.10 = (bf16[8,2,64,128]{3,2,1,0:T(8,128)(2,1)S(1)}, bf16[8,2,64,128]{3,2,1,0:T(8,128)(2,1)S(1)}, u32[]{:S(2)}, u32[]{:S(2)}) collective-permute-start(bf16[8,2,64,128]{3,2,1,0:T(8,128)(2,1)S(1)} %shard_map.56.refs_3_), channel_id=1, source_target_pairs={{0,8},{8,0},{16,24},{24,16},{1,9},{9,1},{17,25},{25,17},{2,10},{10... | collective-permute-start | bytes 786440 | tf_op jit(solution)/shard_map/ppermute | solution.py:401
  23.7 10.3 %collective-permute-start.11 = (bf16[8,2,64,128]{3,2,1,0:T(8,128)(2,1)S(1)}, bf16[8,2,64,128]{3,2,1,0:T(8,128)(2,1)S(1)}, u32[]{:S(2)}, u32[]{:S(2)}) collective-permute-start(bf16[8,2,64,128]{3,2,1,0:T(8,128)(2,1)S(1)} %shard_map.58.after_ref), channel_id=1, source_target_pairs={{0,2},{2,0},{4,6},{6,4},{8,16},{10,18},{12,20},{14,22},{16,8},{18,... | collective-permute-start | bytes 786440 | tf_op jit(solution)/shard_map/ppermute | solution.py:414
  26.5 9.0 %collective-permute-start.12 = (bf16[8,2,64,128]{3,2,1,0:T(8,128)(2,1)S(1)}, bf16[8,2,64,128]{3,2,1,0:T(8,128)(2,1)S(1)}, u32[]{:S(2)}, u32[]{:S(2)}) collective-permute-start(bf16[8,2,64,128]{3,2,1,0:T(8,128)(2,1)S(1)} %get-tuple-element.80), channel_id=1, source_target_pairs={{0,8},{8,0},{16,24},{24,16},{1,9},{9,1},{17,25},{25,17},{2,10},{10... | collective-permute-start | bytes 786440 | tf_op jit(solution)/shard_map/ppermute | solution.py:401
  28.7 6.7 %collective-permute-start.13 = (bf16[8,2,64,128]{3,2,1,0:T(8,128)(2,1)S(1)}, bf16[8,2,64,128]{3,2,1,0:T(8,128)(2,1)S(1)}, u32[]{:S(2)}, u32[]{:S(2)}) collective-permute-start(bf16[8,2,64,128]{3,2,1,0:T(8,128)(2,1)S(1)} %get-tuple-element.75.after_ref), channel_id=1, source_target_pairs={{0,2},{2,0},{4,6},{6,4},{8,16},{10,18},{12,20},{14,22},{16,8},{18,... | collective-permute-start | bytes 786440 | tf_op jit(solution)/shard_map/ppermute | solution.py:414
  28.9 3.9 %collective-permute-start.9 = (bf16[2,8,512]{2,1,0:T(8,128)(2,1)S(1)}, bf16[2,8,512]{2,1,0:T(8,128)(2,1)S(1)}, u32[]{:S(2)}, u32[]{:S(2)}) collective-permute-start(bf16[2,8,512]{2,1,0:T(8,128)(2,1)S(1)} %shard_map.62), channel_id=1, source_target_pairs={{0,1},{1,0},{2,3},{3,2},{4,5},{5,4},{6,7},{7,6},{8,9},{9,8},{10,11... | collective-permute-start | bytes 49160 | tf_op jit(solution)/shard_map/ppermute | solution.py:401

commit v9 on v8

--- a/solution.py
+++ b/solution.py
@@ -401,15 +401,16 @@
     return lax.ppermute(value, axis, [(n, n ^ 1) for n in range(lax.axis_size(axis))])
 
 
-def swap_second(value, axis, other):
-    count, across = lax.axis_size(axis), lax.axis_size(other)
+def swap_second(value, axis, other=None):
+    count = lax.axis_size(axis)
+    inside = {n: n + 1 if n % 2 else n - 1 for n in range(1, count - 1)}
+    if other is None:
+        return lax.ppermute(value, axis, [*inside.items(), (0, count - 1), (count - 1, 0)])
+    across = lax.axis_size(other)
     pairs = []
     for n in range(count):
         for m in range(across):
-            if 0 < n < count - 1:
-                target = (n + 1 if n % 2 else n - 1, m)
-            else:
-                target = (n, m ^ 1)
+            target = (inside[n], m) if n in inside else (n, m ^ 1)
             pairs.append((n * across + m, target[0] * across + target[1]))
     return lax.ppermute(value, (axis, other), pairs)
 
@@ -445,7 +446,7 @@
 
         both, base = (middle, sides), len(block)
         mid, rim = block[0], block[-1]
-        beside = swap_first(col_a, "scol"), swap_second(col_b, "scol", "trow")
+        beside = swap_first(col_a, "scol"), swap_second(col_b, "scol")
         which = (0, 1) if sum_a is None else (1,)
         sums = call(on(functools.partial(inner_body, which), *both), owed_inner * len(which), (*block, made["beside", layer]))
         sum_b = sums[-1]

time: 36.6 us -> 40 us (1.093)
  waiting for transfers between devices: 5.72 us -> 8.26 us
  starting transfers between devices: 15.9 us -> 16.7 us
    ppermute x0 -> x2, waiting for transfers between devices: none -> 5.99 us  [swap_second(): lax.ppermute(value, axis, [*inside.items(), (0, count - 1), (count - 1, 0)])]
    ppermute x0 -> x2, starting transfers between devices: none -> 4.4 us  [swap_second(): lax.ppermute(value, axis, [*inside.items(), (0, count - 1), (count - 1, 0)])]
    ppermute x6 -> x4, starting transfers between devices: 3.71 us -> 0.86 us  [swap_second(): return lax.ppermute(value, (axis, other), pairs)]
    ppermute x6 -> x4, waiting for transfers between devices: 2.44 us -> 0.01 us  [swap_second(): return lax.ppermute(value, (axis, other), pairs)]
    ppermute x8, waiting for transfers between devices: 3.28 us -> 2.25 us  [swap_first(): lax.ppermute(value, axis, [(n, n ^ 1) for n in range(lax.axis_size(axis))])]
    ppermute x8, starting transfers between devices: 12.2 us -> 11.4 us  [swap_first(): lax.ppermute(value, axis, [(n, n ^ 1) for n in range(lax.axis_size(axis))])]
  transfers between devices with their start and end apart: 14 -> 14, of which waited for: 5 -> 4; matrix products, arithmetic and copies ran while one was open for 0% -> 0% of each run, Pallas kernels for 34% -> 31%
where the time goes in v9:
time: 40 us; the launch traced here: 39.9 us
  starting transfers between devices  16.7 us (42%)
  Pallas kernels  14.7 us (37%)
  waiting for transfers between devices  8.26 us (21%)
    pallas_call x20, Pallas kernels, call(): pl.pallas_call(body, out_shape=tuple(outs), in_specs=[pl.BlockSpec(memory...  14.7 us
    ppermute x8, starting transfers between devices, swap_first(): lax.ppermute(value, axis, [(n, n ^ 1) for n in range(lax.axis_size(axis))])  11.4 us
    ppermute x2, waiting for transfers between devices, swap_second(): lax.ppermute(value, axis, [*inside.items(), (0, count - 1), (count - 1, 0)])  5.99 us
    ppermute x2, starting transfers between devices, swap_second(): lax.ppermute(value, axis, [*inside.items(), (0, count - 1), (count - 1, 0)])  4.4 us
    ppermute x8, waiting for transfers between devices, swap_first(): lax.ppermute(value, axis, [(n, n ^ 1) for n in range(lax.axis_size(axis))])  2.25 us
    ppermute x4, starting transfers between devices, swap_second(): return lax.ppermute(value, (axis, other), pairs)  0.86 us
  transfers between devices with their start and end apart: 14, of which 4 were waited for; matrix products, arithmetic and copies ran while one was open for 0% of the time, Pallas kernels for 31%

profile of v9, /device:TPU:0, one launch (start us, length us, event | category | flops | bytes accessed | tf_op | source)
XLA Modules:
  0.0 39.9 jit_solution(7482935313112220446)
XLA Ops:
  0.0 0.0 copy-start
  0.0 1.2 %shard_map.46 = (bf16[2,8,8,9]{3,2,1,0:T(8,128)(2,1)S(1)}, bf16[2,8,8,9]{3,2,1,0:T(8,128)(2,1)S(1)}, f32[2,8]{1,0:T(2,128)S(1)}, bf16[2,256,768]{2,1,0:T(8,128)(...) custom-call(bf16[8,2,4,64,128]{4,3,2,1,0:T(8,128)(2,1)} %x_ref.17, ...), custom_call_target="tpu_custom_call" | custom-call | flops 1000000 | bytes 10000 | tf_op jit(solution)/shard_map/pallas_call | solution.py:29
  1.2 0.5 %collective-permute-start = (bf16[8,2,64,128]{3,2,1,0:T(8,128)(2,1)S(1)}, bf16[8,2,64,128]{3,2,1,0:T(8,128)(2,1)S(1)}, u32[]{:S(2)}, u32[]{:S(2)}) collective-permute-start(bf16[8,2,64,128]{3,2,1,0:T(8,128)(2,1)S(1)} %get-tuple-element.43), channel_id=1, source_target_pairs={{0,2},{2,0},{4,6},{6,4},{1,3},{3,1},{5,7},{7,5},{8,10},{10,8},{12,... | collective-permute-start | bytes 786440 | tf_op jit(solution)/shard_map/ppermute | solution.py:401
  1.7 2.6 %collective-permute-start.1 = (bf16[8,2,64,128]{3,2,1,0:T(8,128)(2,1)S(1)}, bf16[8,2,64,128]{3,2,1,0:T(8,128)(2,1)S(1)}, u32[]{:S(2)}, u32[]{:S(2)}) collective-permute-start(bf16[8,2,64,128]{3,2,1,0:T(8,128)(2,1)S(1)} %get-tuple-element.44), channel_id=1, source_target_pairs={{2,4},{4,2},{0,6},{6,0},{3,5},{5,3},{1,7},{7,1},{10,12},{12,10},{8... | collective-permute-start | bytes 786440 | tf_op jit(solution)/shard_map/ppermute | solution.py:408
  4.3 0.0 copy-done
  4.3 0.6 %shard_map.47 = (bf16[8,2,64,128]{3,2,1,0:T(8,128)(2,1)S(1)}, bf16[8,2,64,128]{3,2,1,0:T(8,128)(2,1)S(1)}) custom-call(bf16[8,2,4,64,128]{4,3,2,1,0:T(8,128)(2,1)S(1)} %copy-done, bf16[2,256,768]{2,1,0:T(8,128)(2,1)S(1)} %get-tuple-element.45.refs_0_.beside_ref.refs_1_.refs_2_), custom_call_target="tpu_custom_call" | custom-call | flops 1000000 | bytes 10000 | tf_op jit(solution)/shard_map/pallas_call | solution.py:29
  4.9 1.6 %collective-permute-start.3 = (bf16[8,2,64,128]{3,2,1,0:T(8,128)(2,1)S(1)}, bf16[8,2,64,128]{3,2,1,0:T(8,128)(2,1)S(1)}, u32[]{:S(2)}, u32[]{:S(2)}) collective-permute-start(bf16[8,2,64,128]{3,2,1,0:T(8,128)(2,1)S(1)} %get-tuple-element.61), channel_id=1, source_target_pairs={{0,8},{8,0},{16,24},{24,16},{1,9},{9,1},{17,25},{25,17},{2,10},{10... | collective-permute-start | bytes 786440 | tf_op jit(solution)/shard_map/ppermute | solution.py:401
  6.5 0.0 collective-permute-start.4
  6.6 0.4 %shard_map.48 = (f32[2,256,256]{2,1,0:T(8,128)S(1)}, f32[2,256,256]{2,1,0:T(8,128)S(1)}) custom-call(bf16[8,2,4,64,128]{4,3,2,1,0:T(8,128)(2,1)S(1)} %copy-done, bf16[2,256,768]{2,1,0:T(8,128)(2,1)S(1)} %get-tuple-element.45.refs_0_.beside_ref.refs_1_.refs_2_, bf16[8,2,64,128]{3,2,1,0:T(8,128)(2,1)S(1)} %get-tuple-element.46.refs_1_.after_ref), custom_call_target="tpu_custom_call" | custom-call | flops 1000000 | bytes 10000 | tf_op jit(solution)/shard_map/pallas_call | solution.py:29
  7.0 1.1 %shard_map.49 = (bf16[256,768]{1,0:T(8,128)(2,1)S(1)}, bf16[256,768]{1,0:T(8,128)(2,1)S(1)}, bf16[2,256,384]{2,1,0:T(8,128)(2,1)S(1)}, bf16[2,256,24]{2,1,0:T(8,...) custom-call(bf16[2,8,8,9]{3,2,1,0:T(8,128)(2,1)S(1)} %get-tuple-elem, ...), custom_call_target="tpu_custom_call" | custom-call | flops 1000000 | bytes 10000 | tf_op jit(solution)/shard_map/pallas_call | solution.py:29
  8.1 0.0 collective-permute-done.cola_ref
  8.1 2.8 %collective-permute-done.1.colb_ref = bf16[8,2,64,128]{3,2,1,0:T(8,128)(2,1)S(1)} collective-permute-done((bf16[8,2,64,128]{3,2,1,0:T(8,128)(2,1)S(1)}, bf16[8,2,64,128]{3,2,1,0:T(8,128)(2,1)S(1)}, u32[]{:S(2)}, u32[]{:S(2)}) %collective-permute-start.1) | collective-permute-done | bytes 262176 | tf_op jit(solution)/shard_map/ppermute | solution.py:408
  10.9 0.4 shard_map.50
  11.3 1.6 %collective-permute-start.6 = (bf16[8,2,64,128]{3,2,1,0:T(8,128)(2,1)S(1)}, bf16[8,2,64,128]{3,2,1,0:T(8,128)(2,1)S(1)}, u32[]{:S(2)}, u32[]{:S(2)}) collective-permute-start(bf16[8,2,64,128]{3,2,1,0:T(8,128)(2,1)S(1)} %get-tuple-element.63), channel_id=1, source_target_pairs={{0,8},{8,0},{16,24},{24,16},{1,9},{9,1},{17,25},{25,17},{2,10},{10... | collective-permute-start | bytes 786440 | tf_op jit(solution)/shard_map/ppermute | solution.py:401
  12.8 0.4 collective-permute-start.5
  13.2 0.2 shard_map.52
  13.4 1.5 %collective-permute-start.2 = (bf16[2,8,512]{2,1,0:T(8,128)(2,1)S(1)}, bf16[2,8,512]{2,1,0:T(8,128)(2,1)S(1)}, u32[]{:S(2)}, u32[]{:S(2)}) collective-permute-start(bf16[2,8,512]{2,1,0:T(8,128)(2,1)S(1)} %shard_map.52), channel_id=1, source_target_pairs={{0,1},{1,0},{2,3},{3,2},{4,5},{5,4},{6,7},{7,6},{8,9},{9,8},{10,11... | collective-permute-start | bytes 49160 | tf_op jit(solution)/shard_map/ppermute | solution.py:401
  14.9 2.5 %shard_map.51 = (f32[8,2,2,64,128]{4,3,2,1,0:T(8,128)S(1)}, f32[8,2,2,64,128]{4,3,2,1,0:T(8,128)S(1)}) custom-call(bf16[8,2,4,64,128]{4,3,2,1,0:T(8,128)(2,1)S(1)} %copy-done, bf16[256,768]{1,0:T(8,128)(2,1)S(1)} %get-tuple-element.51.after_ref.refs_0_.refs_1_, bf16[2,256,768]{2,1,0:T(8,128)(2,1)S(1)} %get-tuple-element.45.refs_0_.beside_ref.refs_1_.refs_2_, ...), custom_call_target="tpu_custom_call" | custom-call | flops 1000000 | bytes 10000 | tf_op jit(solution)/shard_map/pallas_call | solution.py:29
  17.5 0.0 collective-permute-done.2.refs_6_
  17.5 1.1 %shard_map.53 = (f32[8,2,2,64,128]{4,3,2,1,0:T(8,128)S(1)}, f32[8,2,2,64,128]{4,3,2,1,0:T(8,128)S(1)}) custom-call(bf16[8,2,4,64,128]{4,3,2,1,0:T(8,128)(2,1)S(1)} %copy-done, bf16[2,8,2,64,128]{4,3,2,1,0:T(8,128)(2,1)S(1)} %get-tuple-element.52.refs_0_, ...), custom_call_target="tpu_custom_call", output_to_operand_aliasing={{0}: (5, {}), {1}: (6, {})} | custom-call | flops 1000000 | bytes 10000 | tf_op jit(solution)/shard_map/pallas_call | solution.py:29
  18.6 0.0 collective-permute-done.3.refs_1_
  18.6 0.0 collective-permute-done.4.refs_2_
  18.6 0.2 shard_map.54.refs_2_.mid_ref.x_ref
  18.9 1.1 %collective-permute-done.6.refs_1_ = bf16[8,2,64,128]{3,2,1,0:T(8,128)(2,1)S(1)} collective-permute-done((bf16[8,2,64,128]{3,2,1,0:T(8,128)(2,1)S(1)}, bf16[8,2,64,128]{3,2,1,0:T(8,128)(2,1)S(1)}, u32[]{:S(2)}, u32[]{:S(2)}) %collective-permute-start.6) | collective-permute-done | bytes 262176 | tf_op jit(solution)/shard_map/ppermute | solution.py:401
  20.0 0.1 shard_map.55.rim_ref.refs_2_
  20.1 0.4 shard_map.56.refs_3_
  20.5 0.0 collective-permute-done.5.refs_1_
  20.5 0.2 shard_map.57
  20.7 0.1 collective-permute-start.7
  20.8 1.8 %collective-permute-start.8 = (bf16[8,2,64,128]{3,2,1,0:T(8,128)(2,1)S(1)}, bf16[8,2,64,128]{3,2,1,0:T(8,128)(2,1)S(1)}, u32[]{:S(2)}, u32[]{:S(2)}) collective-permute-start(bf16[8,2,64,128]{3,2,1,0:T(8,128)(2,1)S(1)} %get-tuple-element.67), channel_id=1, source_target_pairs={{2,4},{4,2},{0,6},{6,0},{3,5},{5,3},{1,7},{7,1},{10,12},{12,10},{8... | collective-permute-start | bytes 786440 | tf_op jit(solution)/shard_map/ppermute | solution.py:408
  22.6 2.2 %collective-permute-start.10 = (bf16[8,2,64,128]{3,2,1,0:T(8,128)(2,1)S(1)}, bf16[8,2,64,128]{3,2,1,0:T(8,128)(2,1)S(1)}, u32[]{:S(2)}, u32[]{:S(2)}) collective-permute-start(bf16[8,2,64,128]{3,2,1,0:T(8,128)(2,1)S(1)} %shard_map.56.refs_3_), channel_id=1, source_target_pairs={{0,8},{8,0},{16,24},{24,16},{1,9},{9,1},{17,25},{25,17},{2,10},{10... | collective-permute-start | bytes 786440 | tf_op jit(solution)/shard_map/ppermute | solution.py:401
  24.8 0.4 shard_map.58.after_ref
  25.1 0.1 collective-permute-start.11
  25.2 0.5 %shard_map.59 = (f32[2,256,256]{2,1,0:T(8,128)S(1)}, f32[2,256,256]{2,1,0:T(8,128)S(1)}) custom-call(bf16[8,2,2,64,128]{4,3,2,1,0:T(8,128)(2,1)S(1)} %shard_map.54.refs_2_.mid_ref.x_ref, bf16[8,2,2,64,128]{4,3,2,1,0:T(8,128)(2,1)S(1)} %get-tuple-element.65.rim_ref, bf16[2,256,768]{2,1,0:T(8,128)(2,1)S(1)} %get-tuple-element.64.beside_ref, ...), custom_call_target="tpu_custom_call" | custom-call | flops 1000000 | bytes 10000 | tf_op jit(solution)/shard_map/pallas_call | solution.py:29
  25.7 0.0 collective-permute-done.7.cola_ref
  25.7 3.2 %collective-permute-done.8.colb_ref = bf16[8,2,64,128]{3,2,1,0:T(8,128)(2,1)S(1)} collective-permute-done((bf16[8,2,64,128]{3,2,1,0:T(8,128)(2,1)S(1)}, bf16[8,2,64,128]{3,2,1,0:T(8,128)(2,1)S(1)}, u32[]{:S(2)}, u32[]{:S(2)}) %collective-permute-start.8) | collective-permute-done | bytes 262176 | tf_op jit(solution)/shard_map/ppermute | solution.py:408
  28.9 0.4 shard_map.60
  29.3 2.4 %collective-permute-start.12 = (bf16[8,2,64,128]{3,2,1,0:T(8,128)(2,1)S(1)}, bf16[8,2,64,128]{3,2,1,0:T(8,128)(2,1)S(1)}, u32[]{:S(2)}, u32[]{:S(2)}) collective-permute-start(bf16[8,2,64,128]{3,2,1,0:T(8,128)(2,1)S(1)} %get-tuple-element.80), channel_id=1, source_target_pairs={{0,8},{8,0},{16,24},{24,16},{1,9},{9,1},{17,25},{25,17},{2,10},{10... | collective-permute-start | bytes 786440 | tf_op jit(solution)/shard_map/ppermute | solution.py:401
  31.7 0.4 collective-permute-start.13
  32.1 0.2 shard_map.62
  32.3 1.5 %collective-permute-start.9 = (bf16[2,8,512]{2,1,0:T(8,128)(2,1)S(1)}, bf16[2,8,512]{2,1,0:T(8,128)(2,1)S(1)}, u32[]{:S(2)}, u32[]{:S(2)}) collective-permute-start(bf16[2,8,512]{2,1,0:T(8,128)(2,1)S(1)} %shard_map.62), channel_id=1, source_target_pairs={{0,1},{1,0},{2,3},{3,2},{4,5},{5,4},{6,7},{7,6},{8,9},{9,8},{10,11... | collective-permute-start | bytes 49160 | tf_op jit(solution)/shard_map/ppermute | solution.py:401
  33.8 2.5 %shard_map.61 = (f32[8,2,2,64,128]{4,3,2,1,0:T(8,128)S(1)}, f32[8,2,2,64,128]{4,3,2,1,0:T(8,128)S(1)}) custom-call(bf16[8,2,2,64,128]{4,3,2,1,0:T(8,128)(2,1)S(1)} %shard_map.54.refs_2_.mid_ref.x_ref, bf16[8,2,2,64,128]{4,3,2,1,0:T(8,128)(2,1)S(1)} %get-tuple-element.65.rim_ref, bf16[256,768]{1,0:T(8,128)(2,1)S(1)} %get-tuple-element.70.after_ref.middle_ref, ...), custom_call_target="tpu_custom_call" | custom-call | flops 1000000 | bytes 10000 | tf_op jit(solution)/shard_map/pallas_call | solution.py:29
  36.3 0.0 collective-permute-done.9.rest_0_
  36.3 1.1 %shard_map.63 = (f32[8,2,2,64,128]{4,3,2,1,0:T(8,128)S(1)}, f32[8,2,2,64,128]{4,3,2,1,0:T(8,128)S(1)}) custom-call(bf16[8,2,2,64,128]{4,3,2,1,0:T(8,128)(2,1)S(1)} %shard_map.54.refs_2_.mid_ref.x_ref, bf16[8,2,2,64,128]{4,3,2,1,0:T(8,128)(2,1)S(1)} %get-tuple-element.65.rim_ref, ...), custom_call_target="tpu_custom_call", output_to_operand_aliasing={{0}: (6, {}), {1}: (7, {})} | custom-call | flops 1000000 | bytes 10000 | tf_op jit(solution)/shard_map/pallas_call | solution.py:29
  37.5 0.0 collective-permute-done.11.b_ref
  37.5 0.0 collective-permute-done.10.a_ref
  37.5 0.2 shard_map.64.mid_ref
  37.7 1.1 %collective-permute-done.12.a_ref = bf16[8,2,64,128]{3,2,1,0:T(8,128)(2,1)S(1)} collective-permute-done((bf16[8,2,64,128]{3,2,1,0:T(8,128)(2,1)S(1)}, bf16[8,2,64,128]{3,2,1,0:T(8,128)(2,1)S(1)}, u32[]{:S(2)}, u32[]{:S(2)}) %collective-permute-start.12) | collective-permute-done | bytes 262176 | tf_op jit(solution)/shard_map/ppermute | solution.py:401
  38.8 0.0 collective-permute-done.13.b_ref
  38.8 1.0 %shard_map.65 = bf16[8,2,4,64,128]{4,3,2,1,0:T(8,128)(2,1)} custom-call(bf16[8,2,2,64,128]{4,3,2,1,0:T(8,128)(2,1)S(1)} %shard_map.64.mid_ref, bf16[8,2,2,64,128]{4,3,2,1,0:T(8,128)(2,1)S(1)} %get-tuple-element.65.rim_ref, f32[8,2,2,64,128]{4,3,2,1,0:T(8,128)S(1)} %get-tuple-element.79.acc_ref, bf16[8,2,64,128]{3,2,1,0:T(8,128)(2,1)S(1)} %collective-permute-done.12.a_ref, ...), custom_call_target="tpu_custom_call" | custom-call | flops 1000000 | bytes 10000 | tf_op jit(solution)/shard_map/pallas_call | solution.py:29
Async XLA Ops:
  0.0 4.3 %copy-start = (bf16[8,2,4,64,128]{4,3,2,1,0:T(8,128)(2,1)S(1)}, bf16[8,2,4,64,128]{4,3,2,1,0:T(8,128)(2,1)}, u32[]{:S(2)}) copy-start(bf16[8,2,4,64,128]{4,3,2,1,0:T(8,128)(2,1)} %x_ref.17) | copy-start | bytes 3145732
  1.2 6.9 %collective-permute-start = (bf16[8,2,64,128]{3,2,1,0:T(8,128)(2,1)S(1)}, bf16[8,2,64,128]{3,2,1,0:T(8,128)(2,1)S(1)}, u32[]{:S(2)}, u32[]{:S(2)}) collective-permute-start(bf16[8,2,64,128]{3,2,1,0:T(8,128)(2,1)S(1)} %get-tuple-element.43), channel_id=1, source_target_pairs={{0,2},{2,0},{4,6},{6,4},{1,3},{3,1},{5,7},{7,5},{8,10},{10,8},{12,... | collective-permute-start | bytes 786440 | tf_op jit(solution)/shard_map/ppermute | solution.py:401
  1.7 9.2 %collective-permute-start.1 = (bf16[8,2,64,128]{3,2,1,0:T(8,128)(2,1)S(1)}, bf16[8,2,64,128]{3,2,1,0:T(8,128)(2,1)S(1)}, u32[]{:S(2)}, u32[]{:S(2)}) collective-permute-start(bf16[8,2,64,128]{3,2,1,0:T(8,128)(2,1)S(1)} %get-tuple-element.44), channel_id=1, source_target_pairs={{2,4},{4,2},{0,6},{6,0},{3,5},{5,3},{1,7},{7,1},{10,12},{12,10},{8... | collective-permute-start | bytes 786440 | tf_op jit(solution)/shard_map/ppermute | solution.py:408
  4.9 13.7 %collective-permute-start.3 = (bf16[8,2,64,128]{3,2,1,0:T(8,128)(2,1)S(1)}, bf16[8,2,64,128]{3,2,1,0:T(8,128)(2,1)S(1)}, u32[]{:S(2)}, u32[]{:S(2)}) collective-permute-start(bf16[8,2,64,128]{3,2,1,0:T(8,128)(2,1)S(1)} %get-tuple-element.61), channel_id=1, source_target_pairs={{0,8},{8,0},{16,24},{24,16},{1,9},{9,1},{17,25},{25,17},{2,10},{10... | collective-permute-start | bytes 786440 | tf_op jit(solution)/shard_map/ppermute | solution.py:401
  6.5 12.1 %collective-permute-start.4 = (bf16[8,2,64,128]{3,2,1,0:T(8,128)(2,1)S(1)}, bf16[8,2,64,128]{3,2,1,0:T(8,128)(2,1)S(1)}, u32[]{:S(2)}, u32[]{:S(2)}) collective-permute-start(bf16[8,2,64,128]{3,2,1,0:T(8,128)(2,1)S(1)} %get-tuple-element.46.refs_1_.after_ref), channel_id=1, source_target_pairs={{0,2},{2,0},{4,6},{6,4},{8,16},{10,18},{12,20},{14,22},{16,8},{18,... | collective-permute-start | bytes 786440 | tf_op jit(solution)/shard_map/ppermute | solution.py:415
  11.3 8.7 %collective-permute-start.6 = (bf16[8,2,64,128]{3,2,1,0:T(8,128)(2,1)S(1)}, bf16[8,2,64,128]{3,2,1,0:T(8,128)(2,1)S(1)}, u32[]{:S(2)}, u32[]{:S(2)}) collective-permute-start(bf16[8,2,64,128]{3,2,1,0:T(8,128)(2,1)S(1)} %get-tuple-element.63), channel_id=1, source_target_pairs={{0,8},{8,0},{16,24},{24,16},{1,9},{9,1},{17,25},{25,17},{2,10},{10... | collective-permute-start | bytes 786440 | tf_op jit(solution)/shard_map/ppermute | solution.py:401
  12.8 7.6 %collective-permute-start.5 = (bf16[8,2,64,128]{3,2,1,0:T(8,128)(2,1)S(1)}, bf16[8,2,64,128]{3,2,1,0:T(8,128)(2,1)S(1)}, u32[]{:S(2)}, u32[]{:S(2)}) collective-permute-start(bf16[8,2,64,128]{3,2,1,0:T(8,128)(2,1)S(1)} %get-tuple-element.57.refs_5_.refs_0_), channel_id=1, source_target_pairs={{0,2},{2,0},{4,6},{6,4},{8,16},{10,18},{12,20},{14,22},{16,8},{18,... | collective-permute-start | bytes 786440 | tf_op jit(solution)/shard_map/ppermute | solution.py:415
  13.4 4.0 %collective-permute-start.2 = (bf16[2,8,512]{2,1,0:T(8,128)(2,1)S(1)}, bf16[2,8,512]{2,1,0:T(8,128)(2,1)S(1)}, u32[]{:S(2)}, u32[]{:S(2)}) collective-permute-start(bf16[2,8,512]{2,1,0:T(8,128)(2,1)S(1)} %shard_map.52), channel_id=1, source_target_pairs={{0,1},{1,0},{2,3},{3,2},{4,5},{5,4},{6,7},{7,6},{8,9},{9,8},{10,11... | collective-permute-start | bytes 49160 | tf_op jit(solution)/shard_map/ppermute | solution.py:401
  20.7 5.0 %collective-permute-start.7 = (bf16[8,2,64,128]{3,2,1,0:T(8,128)(2,1)S(1)}, bf16[8,2,64,128]{3,2,1,0:T(8,128)(2,1)S(1)}, u32[]{:S(2)}, u32[]{:S(2)}) collective-permute-start(bf16[8,2,64,128]{3,2,1,0:T(8,128)(2,1)S(1)} %get-tuple-element.66), channel_id=1, source_target_pairs={{0,2},{2,0},{4,6},{6,4},{1,3},{3,1},{5,7},{7,5},{8,10},{10,8},{12,... | collective-permute-start | bytes 786440 | tf_op jit(solution)/shard_map/ppermute | solution.py:401
  20.8 8.1 %collective-permute-start.8 = (bf16[8,2,64,128]{3,2,1,0:T(8,128)(2,1)S(1)}, bf16[8,2,64,128]{3,2,1,0:T(8,128)(2,1)S(1)}, u32[]{:S(2)}, u32[]{:S(2)}) collective-permute-start(bf16[8,2,64,128]{3,2,1,0:T(8,128)(2,1)S(1)} %get-tuple-element.67), channel_id=1, source_target_pairs={{2,4},{4,2},{0,6},{6,0},{3,5},{5,3},{1,7},{7,1},{10,12},{12,10},{8... | collective-permute-start | bytes 786440 | tf_op jit(solution)/shard_map/ppermute | solution.py:408
  22.6 14.9 %collective-permute-start.10 = (bf16[8,2,64,128]{3,2,1,0:T(8,128)(2,1)S(1)}, bf16[8,2,64,128]{3,2,1,0:T(8,128)(2,1)S(1)}, u32[]{:S(2)}, u32[]{:S(2)}) collective-permute-start(bf16[8,2,64,128]{3,2,1,0:T(8,128)(2,1)S(1)} %shard_map.56.refs_3_), channel_id=1, source_target_pairs={{0,8},{8,0},{16,24},{24,16},{1,9},{9,1},{17,25},{25,17},{2,10},{10... | collective-permute-start | bytes 786440 | tf_op jit(solution)/shard_map/ppermute | solution.py:401
  25.1 12.3 %collective-permute-start.11 = (bf16[8,2,64,128]{3,2,1,0:T(8,128)(2,1)S(1)}, bf16[8,2,64,128]{3,2,1,0:T(8,128)(2,1)S(1)}, u32[]{:S(2)}, u32[]{:S(2)}) collective-permute-start(bf16[8,2,64,128]{3,2,1,0:T(8,128)(2,1)S(1)} %shard_map.58.after_ref), channel_id=1, source_target_pairs={{0,2},{2,0},{4,6},{6,4},{8,16},{10,18},{12,20},{14,22},{16,8},{18,... | collective-permute-start | bytes 786440 | tf_op jit(solution)/shard_map/ppermute | solution.py:415
  29.3 9.6 %collective-permute-start.12 = (bf16[8,2,64,128]{3,2,1,0:T(8,128)(2,1)S(1)}, bf16[8,2,64,128]{3,2,1,0:T(8,128)(2,1)S(1)}, u32[]{:S(2)}, u32[]{:S(2)}) collective-permute-start(bf16[8,2,64,128]{3,2,1,0:T(8,128)(2,1)S(1)} %get-tuple-element.80), channel_id=1, source_target_pairs={{0,8},{8,0},{16,24},{24,16},{1,9},{9,1},{17,25},{25,17},{2,10},{10... | collective-permute-start | bytes 786440 | tf_op jit(solution)/shard_map/ppermute | solution.py:401
  31.7 7.1 %collective-permute-start.13 = (bf16[8,2,64,128]{3,2,1,0:T(8,128)(2,1)S(1)}, bf16[8,2,64,128]{3,2,1,0:T(8,128)(2,1)S(1)}, u32[]{:S(2)}, u32[]{:S(2)}) collective-permute-start(bf16[8,2,64,128]{3,2,1,0:T(8,128)(2,1)S(1)} %get-tuple-element.75.after_ref), channel_id=1, source_target_pairs={{0,2},{2,0},{4,6},{6,4},{8,16},{10,18},{12,20},{14,22},{16,8},{18,... | collective-permute-start | bytes 786440 | tf_op jit(solution)/shard_map/ppermute | solution.py:415
  32.3 4.0 %collective-permute-start.9 = (bf16[2,8,512]{2,1,0:T(8,128)(2,1)S(1)}, bf16[2,8,512]{2,1,0:T(8,128)(2,1)S(1)}, u32[]{:S(2)}, u32[]{:S(2)}) collective-permute-start(bf16[2,8,512]{2,1,0:T(8,128)(2,1)S(1)} %shard_map.62), channel_id=1, source_target_pairs={{0,1},{1,0},{2,3},{3,2},{4,5},{5,4},{6,7},{7,6},{8,9},{9,8},{10,11... | collective-permute-start | bytes 49160 | tf_op jit(solution)/shard_map/ppermute | solution.py:401

commit v10 on v8

--- a/solution.py
+++ b/solution.py
@@ -113,25 +113,25 @@
 
 
 class View:
-    def __init__(self, ref, columns):
-        self.ref, self.columns = ref, columns
+    def __init__(self, ref, count, at):
+        self.ref, self.count, self.at = ref, count, at
 
     @property
     def shape(self):
         channels, rows, _, depth, width = self.ref.shape
-        return channels, rows, len(self.columns), depth, width
+        return channels, rows, self.count, depth, width
 
     def __getitem__(self, index):
         first, i, j, *rest = index
-        return self.ref[(first, i, self.columns[j], *rest)]
+        return self.ref[(first, i, self.at(j), *rest)]
 
 
 def middle(x_ref):
-    return View(x_ref, tuple(range(1, x_ref.shape[2] - 1)))
+    return View(x_ref, x_ref.shape[2] - 2, lambda j: j + 1)
 
 
 def sides(x_ref):
-    return View(x_ref, (0, x_ref.shape[2] - 1))
+    return View(x_ref, 2, lambda j: j * (x_ref.shape[2] - 1))
 
 
 def whole(body, views, x_ref, *refs):
@@ -185,38 +185,65 @@
         )
 
 
+def side_of(second):
+    odd = parity("scol")
+    return odd if second else 1 - odd
+
+
+def all_bands(read, depth):
+    return jnp.concatenate([band(read(cut)) for cut in bands_of(depth)], axis=1)
+
+
+def own_taps(mid_ref, rim_ref, beside_ref, i, row_side, n):
+    mids, depth = mid_ref.shape[2:4]
+    span = mid_ref.shape[0] * BAND
+    rim = all_bands(lambda cut: rim_ref[:, i, n, cut], depth)
+    mid = all_bands(lambda cut: mid_ref[:, i, n * (mids - 1), cut], depth)
+    inward = pl.multiple_of((2 - 2 * n) * span, span)
+    return dot(beside_ref[row_side, :, span : 2 * span], rim) + dot(beside_ref[row_side, :, pl.ds(inward, span)], mid)
+
+
+def halo_tap(halo_ref, beside_ref, i, row_side, n):
+    span = halo_ref.shape[0] * BAND
+    outward = pl.multiple_of(2 * n * span, span)
+    return dot(beside_ref[row_side, :, pl.ds(outward, span)], all_bands(lambda cut: halo_ref[:, i, cut], halo_ref.shape[2]))
+
+
+def put_sums(got, out_ref):
+    channels, _, depth, width = out_ref.shape
+    got = got.astype(BF16)
+    for q, cut in enumerate(bands_of(depth)):
+        out_ref[:, 0, cut] = unband(got[:, q * width : (q + 1) * width], channels)
+
+
+def near_body(mid_ref, rim_ref, cola_ref, beside_ref, after_ref, a_ref, b_ref):
+    n = side_of(False)
+    for (i, row_side), out_ref in zip(sent_rows(mid_ref.shape[1]), (a_ref, b_ref)):
+        got = own_taps(mid_ref, rim_ref, beside_ref, i, row_side, n) + halo_tap(cola_ref, beside_ref, i, row_side, n)
+        put_sums(got, out_ref)
+
+
 def part_body(mid_ref, rim_ref, beside_ref, after_ref, *part_refs):
-    rows, cols = mid_ref.shape[1], mid_ref.shape[2] + 2
-    cuts = bands_of(mid_ref.shape[3])
-    for (i, side), part_ref in zip(sent_rows(rows), part_refs):
-        span = part_ref.shape[1]
-        for n, (first, j) in enumerate(((1, 0), (0, cols - 2))):
-            tiles = [jnp.concatenate([column(mid_ref, rim_ref, i, j + b, cut) for cut in cuts], axis=1) for b in range(2)]
-            operator = beside_ref[side, :, first * span : (first + 2) * span]
-            part_ref[n] = dot(operator, jnp.concatenate(tiles, axis=0))
-
-
-def edge_body(cola_ref, colb_ref, beside_ref, parta_ref, partb_ref, after_ref, a_ref, b_ref, side_ref):
-    channels, rows, depth, width = cola_ref.shape
-    odd, paired = parity("scol"), has_second("scol")
-    side_ref[1 - odd] = cola_ref[...]
+    for (i, row_side), part_ref in zip(sent_rows(mid_ref.shape[1]), part_refs):
+        part_ref[...] = own_taps(mid_ref, rim_ref, beside_ref, i, row_side, side_of(True))
+
+
+def far_body(cola_ref, colb_ref, beside_ref, parta_ref, partb_ref, *refs):
+    a_ref, b_ref, side_ref = refs[-3:]
+    rows = cola_ref.shape[1]
+    n, paired = side_of(True), has_second("scol")
+    side_ref[side_of(False)] = cola_ref[...]
 
     @pl.when(paired)
     def _():
-        side_ref[odd] = colb_ref[...]
+        side_ref[n] = colb_ref[...]
 
     @pl.when(jnp.logical_not(paired))
     def _():
-        side_ref[odd] = jnp.zeros_like(colb_ref)
-
-    cuts = bands_of(depth)
-    for (i, side), part_ref, out_ref in zip(sent_rows(rows), (parta_ref, partb_ref), (a_ref, b_ref)):
-        span = part_ref.shape[1]
-        for n, tap in enumerate((0, 2)):
-            halo = jnp.concatenate([band(side_ref[n, :, i, cut]) for cut in cuts], axis=1)
-            got = (part_ref[n] + dot(beside_ref[side, :, tap * span : (tap + 1) * span], halo)).astype(BF16)
-            for q, cut in enumerate(cuts):
-                out_ref[:, n, cut] = unband(got[:, q * width : (q + 1) * width], channels)
+        side_ref[n] = jnp.zeros_like(colb_ref)
+
+    for (i, row_side), part_ref, out_ref in zip(sent_rows(rows), (parta_ref, partb_ref), (a_ref, b_ref)):
+        put_sums(part_ref[...] + halo_tap(side_ref.at[n], beside_ref, i, row_side, n), out_ref)
 
 
 def shifted(tile, step):
@@ -274,11 +301,9 @@
             acc_ref[:, i, j, cut] += unband(got[:, at : at + width], channels)
 
 
-def rest_body(
-    mid_ref, rim_ref, side_ref, middle_ref, beside_ref, deep_ref, accmid_ref, accrim_ref, *rest
-):
-    *deep_halos, outmid_ref, outrim_ref = rest
-    channels, rows, mids, depth, width = mid_ref.shape
+def source_body(mid_ref, rim_ref, side_ref, middle_ref, beside_ref, *refs):
+    outrim_ref = refs[-1]
+    rows, mids = mid_ref.shape[1:3]
     cols = mids + 2
 
     def around(r, j, cut):
@@ -292,7 +317,14 @@
             if 0 <= r < rows:
                 operator = middle_ref[...] if a == 1 else beside_ref[a // 2]
                 add_sums(operator, lambda cut, b: [around(r, j + b - 1, cut) for j in (0, cols - 1)], outrim_ref, i)
-        odd = parity("trow")
+
+
+def deep_body(deep_ref, *refs):
+    *deep_halos, _, _, outmid_ref, outrim_ref = refs
+    channels, rows, mids, depth, width = outmid_ref.shape
+    cols = mids + 2
+    odd = parity("trow")
+    for i in range(rows):
         for n, halo_ref in enumerate(deep_halos):
             side = (1 - odd) if n == 0 else odd
             cut = pl.ds(pl.multiple_of(side * (depth - BAND), BAND), BAND)
@@ -306,18 +338,15 @@
                 acc_ref[:, i, at, cut] += unband(got[:, j * width : (j + 1) * width], channels)
 
 
-def finished(x_ref, acc_ref, owed_refs, store):
-    rows, cols = x_ref.shape[1:3]
+def finished(x_ref, acc_ref, swaps, owed, store):
+    rows = x_ref.shape[1]
     odd = parity("srow")
     paired = has_second("srow").astype(F32)
-    for n, i in enumerate([(rows - 1) * (1 - odd), (rows - 1) * odd, *range(1, rows - 1)]):
-        if n < 2 and owed_refs[n] is None:
-            continue
-        for j in range(cols):
-            total = acc_ref[:, i, j]
-            if n < 2:
-                owed = owed_refs[n][:, j].astype(F32)
-                total = total + (owed if n == 0 else owed * paired)
+    for n in swaps:
+        i = (rows - 1) * (odd if n else 1 - odd)
+        for j, brought in owed(n):
+            brought = brought.astype(F32)
+            total = acc_ref[:, i, j] + (brought * paired if n else brought)
             store(i, j, (x_ref[:, i, j].astype(F32) + jnp.maximum(total, 0.0)).astype(BF16))
 
 
@@ -345,36 +374,56 @@
     def store(i, j, value):
         out_ref[:, i, j] = value
 
-    finished(x_ref, acc_ref, (a_ref, b_ref), store)
-
-
-def begin_body(x_ref, acc_ref, a_ref, after_ref, out_ref):
-    mid_body(x_ref, acc_ref, a_ref, None, out_ref)
-
-
-def next_body(x_ref, acc_ref, b_ref, begun_ref, after_ref, out_ref, cola_ref, colb_ref):
-    mid_body(x_ref, acc_ref, None, b_ref, out_ref)
+    finished(x_ref, acc_ref, (0, 1), lambda n: [(j, (a_ref, b_ref)[n][:, j]) for j in range(x_ref.shape[2])], store)
+
+
+def side_columns(near_ref, far_ref):
+    return [(side_of(False), near_ref[:, 0]), (side_of(True), far_ref[:, 0])]
+
+
+def begin_body(x_ref, acc_ref, near_ref, far_ref, after_ref, out_ref):
+    def store(i, j, value):
+        out_ref[:, i, j] = value
+
+    finished(x_ref, acc_ref, (0,), lambda n: side_columns(near_ref, far_ref), store)
+
+
+def next_body(x_ref, acc_ref, near_ref, far_ref, begun_ref, after_ref, out_ref, cola_ref, colb_ref):
+    def store(i, j, value):
+        out_ref[:, i, j] = value
+
+    finished(x_ref, acc_ref, (1,), lambda n: side_columns(near_ref, far_ref), store)
     sent_columns(out_ref, (cola_ref, colb_ref))
 
 
-def last_body(mid_ref, rim_ref, acc_ref, a_ref, b_ref, out_ref, hold_ref, sems):
+def last_body(mid_ref, rim_ref, acc_ref, neara_ref, nearb_ref, fara_ref, farb_ref, out_ref, hold_ref, sems):
     rows, mids = mid_ref.shape[1:3]
     copies = []
+
+    def write(source, i, j):
+        copies.append(pltpu.make_async_copy(source, out_ref.at[:, i, j], sems.at[len(copies)]))
+        copies[-1].start()
+
     for i in range(rows):
         for j in range(mids):
-            copy = pltpu.make_async_copy(mid_ref.at[:, i, j], out_ref.at[:, i, j + 1], sems.at[len(copies)])
-            copy.start()
-            copies.append(copy)
+            write(mid_ref.at[:, i, j], i, j + 1)
 
     def store(i, j, value):
         hold_ref[:, i, j] = value
-        copy = pltpu.make_async_copy(hold_ref.at[:, i, j], out_ref.at[:, i, j * (mids + 1)], sems.at[len(copies)])
-        copy.start()
-        copies.append(copy)
-
-    finished(rim_ref, acc_ref, (a_ref, b_ref), store)
+        write(hold_ref.at[:, i, j], i, j * (mids + 1))
+
+    owed = lambda n: side_columns((neara_ref, nearb_ref)[n], (fara_ref, farb_ref)[n])
+    finished(rim_ref, acc_ref, (0, 1), owed, store)
     for copy in copies:
         copy.wait()
+
+
+def gate_body(*refs):
+    refs[-1][...] = jnp.zeros_like(refs[-1])
+
+
+def pass_body(x_ref, after_ref, out_ref):
+    out_ref[...] = x_ref[...]
 
 
 def open_body(parts, x_ref, src_w_ref, tgt_w_ref, bias_ref, *rest):
@@ -425,7 +474,7 @@
     deep_swaps = 1 if counts[2] == 2 else 2
     mid_shape, rim_shape = ((channels, rows, n, depth, width) for n in (cols - 2, 2))
     line = VMEM((channels, rows, depth, width), BF16)
-    owed_rim = VMEM((channels, 2, depth, width), BF16)
+    owed_side = VMEM((channels, 1, depth, width), BF16)
     early = [("beside", 0)]
     src_w, tgt_w, bias, beside_0, col_a, col_b = call(
         functools.partial(open_body, early),
@@ -445,69 +494,86 @@
 
         both, base = (middle, sides), len(block)
         mid, rim = block[0], block[-1]
-        beside = swap_first(col_a, "scol"), swap_second(col_b, "scol", "trow")
         which = (0, 1) if sum_a is None else (1,)
         sums = call(on(functools.partial(inner_body, which), *both), owed_inner * len(which), (*block, made["beside", layer]))
         sum_b = sums[-1]
+        if layer == 0:
+            (col_b,) = call(pass_body, [line], (col_b, sum_b), {1: pl.ANY})
+        beside = swap_first(col_a, "scol"), swap_second(col_b, "scol", "trow")
         inner = swap_first(sums[0], "srow") if sum_a is None else got_a, swap_second(sum_b, "srow", "scol")
+        def own(after):
+            return call(
+                on(functools.partial(own_body, layer), *both),
+                [VMEM(mid_shape, F32), VMEM(rim_shape, F32)],
+                (*block, *(operator[kind] for kind in ("middle", "beside", "target", "near")), bias, after),
+                {base + 5: pl.ANY},
+                scratch=[VMEM((depth // BAND, 3, channels * BAND, cols * width), BF16)],
+            )
+
+        near = call(on(near_body, *both), [owed_side] * 2, (*block, beside[0], made["beside", layer], sum_b), {base + 2: pl.ANY})
+        near_got = swap_first(near[0], "srow"), swap_second(near[1], "srow", "scol")
         if layer == 0:
-            late = [(kind, n) for n in range(layers) for kind in kinds]
-            made |= build([part for part in late if part not in early], src_w, tgt_w, sum_b)
+            made |= build([(kind, 0) for kind in kinds if kind != "beside"], src_w, tgt_w, near[1])
         operator = {kind: made[kind, layer] for kind in kinds}
         parts = call(
             on(part_body, *both),
-            [VMEM((2, channels * BAND, depth // BAND * width), F32)] * 2,
-            (*block, operator["beside"], sum_b),
+            [VMEM((channels * BAND, depth // BAND * width), F32)] * 2,
+            (*block, operator["beside"], near[1]),
             {base + 1: pl.ANY},
         )
-        a, b, side = call(
-            edge_body,
-            [owed_rim, owed_rim, VMEM((2, *line.shape), BF16)],
-            (*beside, operator["beside"], *parts, operator["middle"]),
-            {5: pl.ANY},
-        )
-        outer = swap_first(a, "srow"), swap_second(b, "srow", "scol")
         deep = call(
             on(depth_body, *both),
             [VMEM((rows, channels, cols * width), BF16)] * deep_swaps,
-            (*block, b),
+            (*block, near[1]),
             {base: pl.ANY},
         )
         deeper = [swap_first(deep[0], "trow")]
         if deep_swaps == 2:
             deeper.append(swap_second(deep[1], "trow", "scol"))
-        accs = call(
-            on(functools.partial(own_body, layer), *both),
-            [VMEM(mid_shape, F32), VMEM(rim_shape, F32)],
-            (*block, *(operator[kind] for kind in ("middle", "beside", "target", "near")), bias, b),
-            {base + 5: pl.ANY},
-            scratch=[VMEM((depth // BAND, 3, channels * BAND, cols * width), BF16)],
+        accs = own(parts[1])
+        waited = (*inner, accs[0])
+        (gate,) = call(gate_body, [VMEM((8, 128), F32)], waited, {n: pl.ANY for n in range(len(waited))})
+        a, b, side = call(
+            far_body,
+            [owed_side, owed_side, VMEM((2, *line.shape), BF16)],
+            (*beside, operator["beside"], *parts, gate),
+            {5: pl.ANY},
+        )
+        far_got = swap_first(a, "srow"), swap_second(b, "srow", "scol")
+        if layer < layers - 1:
+            made |= build([(kind, layer + 1) for kind in kinds], src_w, tgt_w, b)
+        (acc_rim,) = call(
+            on(source_body, *both),
+            [VMEM(rim_shape, F32)],
+            (*block, side, operator["middle"], operator["beside"], *near_got, accs[1]),
+            {base + 3: pl.ANY, base + 4: pl.ANY},
+            aliases={base + 5: 0},
         )
         acc_mid, acc_rim = call(
-            on(rest_body, *both),
+            deep_body,
             [VMEM(mid_shape, F32), VMEM(rim_shape, F32)],
-            (*block, side, *(operator[kind] for kind in ("middle", "beside", "deep")), *accs, *deeper),
-            aliases={base + 4: 0, base + 5: 1},
+            (operator["deep"], *deeper, accs[0], acc_rim),
+            aliases={1 + deep_swaps: 0, 2 + deep_swaps: 1},
         )
         (mid,) = call(on(mid_body, middle), [VMEM(mid_shape, BF16)], (mid, acc_mid, *inner))
         if layer < layers - 1:
             whole_rim = [VMEM(rim_shape, BF16)]
-            (begun,) = call(on(begin_body, sides), whole_rim, (rim, acc_rim, outer[0], mid), {3: pl.ANY})
+            (begun,) = call(on(begin_body, sides), whole_rim, (rim, acc_rim, near_got[0], far_got[0], mid), {4: pl.ANY})
             (sum_a,) = call(functools.partial(inner_body, (0,)), owed_inner, (mid, begun, made["beside", layer + 1]))
             got_a = swap_first(sum_a, "srow")
             rim, col_a, col_b = call(
                 on(next_body, sides),
                 whole_rim + [line, line],
-                (rim, acc_rim, outer[1], begun, sum_a),
-                {4: pl.ANY},
-                aliases={3: 0},
+                (rim, acc_rim, near_got[1], far_got[1], begun, sum_a),
+                {5: pl.ANY},
+                aliases={4: 0},
             )
             block = (mid, rim)
         else:
             (state,) = call(
                 last_body,
                 [jax.ShapeDtypeStruct(volume.shape, BF16)],
-                (mid, rim, acc_rim, *outer),
+                (mid, rim, acc_rim, *near_got, *far_got),
                 out_place=HBM,
                 scratch=[VMEM(rim_shape, BF16), pltpu.SemaphoreType.DMA((rows * cols,))],
             )

time: 36.6 us -> 39.3 us (1.074)
  starting transfers between devices: 15.9 us -> 19.4 us
  waiting for transfers between devices: 5.72 us -> 3.94 us
  Pallas kernels: 14.7 us -> 15.5 us
    ppermute x8 -> x10, starting transfers between devices: 12.2 us -> 15.5 us  [swap_first(): lax.ppermute(value, axis, [(n, n ^ 1) for n in range(lax.axis_size(axis))])]
    ppermute x6 -> x8, waiting for transfers between devices: 2.44 us -> 0.02 us  [swap_second(): return lax.ppermute(value, (axis, other), pairs)]
    pallas_call x20 -> x28, Pallas kernels: 14.7 us -> 15.5 us  [call(): pl.pallas_call(body, out_shape=tuple(outs), in_specs=[pl.BlockSpec(memory...]
    ppermute x8 -> x10, waiting for transfers between devices: 3.28 us -> 3.92 us  [swap_first(): lax.ppermute(value, axis, [(n, n ^ 1) for n in range(lax.axis_size(axis))])]
    ppermute x6 -> x8, starting transfers between devices: 3.71 us -> 3.87 us  [swap_second(): return lax.ppermute(value, (axis, other), pairs)]
  transfers between devices with their start and end apart: 14 -> 18, of which waited for: 5 -> 3; matrix products, arithmetic and copies ran while one was open for 0% -> 0% of each run, Pallas kernels for 34% -> 33%
where the time goes in v10:
time: 39.3 us; the launch traced here: 39.1 us
  starting transfers between devices  19.4 us (49%)
  Pallas kernels  15.5 us (39%)
  waiting for transfers between devices  3.94 us (10%)
    ppermute x10, starting transfers between devices, swap_first(): lax.ppermute(value, axis, [(n, n ^ 1) for n in range(lax.axis_size(axis))])  15.5 us
    pallas_call x28, Pallas kernels, call(): pl.pallas_call(body, out_shape=tuple(outs), in_specs=[pl.BlockSpec(memory...  15.5 us
    ppermute x10, waiting for transfers between devices, swap_first(): lax.ppermute(value, axis, [(n, n ^ 1) for n in range(lax.axis_size(axis))])  3.92 us
    ppermute x8, starting transfers between devices, swap_second(): return lax.ppermute(value, (axis, other), pairs)  3.87 us
  transfers between devices with their start and end apart: 18, of which 3 were waited for; matrix products, arithmetic and copies ran while one was open for 0% of the time, Pallas kernels for 33%

profile of v10, /device:TPU:0, one launch (start us, length us, event | category | flops | bytes accessed | tf_op | source)
XLA Modules:
  0.0 39.1 jit_solution(9350334889132826326)
XLA Ops:
  0.0 0.0 copy-start
  0.0 1.2 %shard_map.46 = (bf16[2,8,8,9]{3,2,1,0:T(8,128)(2,1)S(1)}, bf16[2,8,8,9]{3,2,1,0:T(8,128)(2,1)S(1)}, f32[2,8]{1,0:T(2,128)S(1)}, bf16[2,256,768]{2,1,0:T(8,128)(...) custom-call(bf16[8,2,4,64,128]{4,3,2,1,0:T(8,128)(2,1)} %x_ref.19, ...), custom_call_target="tpu_custom_call" | custom-call | flops 1000000 | bytes 10000 | tf_op jit(solution)/shard_map/pallas_call | solution.py:29
  1.2 0.5 %collective-permute-start = (bf16[8,2,64,128]{3,2,1,0:T(8,128)(2,1)S(1)}, bf16[8,2,64,128]{3,2,1,0:T(8,128)(2,1)S(1)}, u32[]{:S(2)}, u32[]{:S(2)}) collective-permute-start(bf16[8,2,64,128]{3,2,1,0:T(8,128)(2,1)S(1)} %get-tuple-element.49), channel_id=1, source_target_pairs={{0,2},{2,0},{4,6},{6,4},{1,3},{3,1},{5,7},{7,5},{8,10},{10,8},{12,... | collective-permute-start | bytes 786440 | tf_op jit(solution)/shard_map/ppermute | solution.py:450
  1.7 0.0 copy-done
  1.7 0.6 %shard_map.47 = (bf16[8,2,64,128]{3,2,1,0:T(8,128)(2,1)S(1)}, bf16[8,2,64,128]{3,2,1,0:T(8,128)(2,1)S(1)}) custom-call(bf16[8,2,4,64,128]{4,3,2,1,0:T(8,128)(2,1)S(1)} %copy-done, bf16[2,256,768]{2,1,0:T(8,128)(2,1)S(1)} %get-tuple-element.50.refs_0_.refs_1_.beside_ref.refs_2_), custom_call_target="tpu_custom_call" | custom-call | flops 1000000 | bytes 10000 | tf_op jit(solution)/shard_map/pallas_call | solution.py:29
  2.3 2.8 %collective-permute-start.3 = (bf16[8,2,64,128]{3,2,1,0:T(8,128)(2,1)S(1)}, bf16[8,2,64,128]{3,2,1,0:T(8,128)(2,1)S(1)}, u32[]{:S(2)}, u32[]{:S(2)}) collective-permute-start(bf16[8,2,64,128]{3,2,1,0:T(8,128)(2,1)S(1)} %get-tuple-element.62), channel_id=1, source_target_pairs={{0,8},{8,0},{16,24},{24,16},{1,9},{9,1},{17,25},{25,17},{2,10},{10... | collective-permute-start | bytes 786440 | tf_op jit(solution)/shard_map/ppermute | solution.py:450
  5.1 0.1 collective-permute-start.4
  5.2 1.6 %collective-permute-start.2 = (bf16[8,2,64,128]{3,2,1,0:T(8,128)(2,1)S(1)}, bf16[8,2,64,128]{3,2,1,0:T(8,128)(2,1)S(1)}, u32[]{:S(2)}, u32[]{:S(2)}) collective-permute-start(bf16[8,2,64,128]{3,2,1,0:T(8,128)(2,1)S(1)} %shard_map.53), channel_id=1, source_target_pairs={{0,1},{1,0},{2,4},{3,5},{4,2},{5,3},{6,7},{7,6},{8,9},{9,8},{10,12... | collective-permute-start | bytes 786440 | tf_op jit(solution)/shard_map/ppermute | solution.py:463
  6.8 0.0 collective-permute-done.refs_0_.cola_ref
  6.8 0.4 shard_map.48
  7.1 3.2 %collective-permute-start.5 = (bf16[8,1,64,128]{3,2,1,0:T(8,128)(2,1)S(1)}, bf16[8,1,64,128]{3,2,1,0:T(8,128)(2,1)S(1)}, u32[]{:S(2)}, u32[]{:S(2)}) collective-permute-start(bf16[8,1,64,128]{3,2,1,0:T(8,128)(2,1)S(1)} %get-tuple-element.64), channel_id=1, source_target_pairs={{0,8},{8,0},{16,24},{24,16},{1,9},{9,1},{17,25},{25,17},{2,10},{10... | collective-permute-start | bytes 393224 | tf_op jit(solution)/shard_map/ppermute | solution.py:450
  10.3 0.0 collective-permute-start.6
  10.3 0.3 shard_map.51
  10.6 0.5 %shard_map.49 = (bf16[256,768]{1,0:T(8,128)(2,1)S(1)}, bf16[256,768]{1,0:T(8,128)(2,1)S(1)}, bf16[2,256,384]{2,1,0:T(8,128)(2,1)S(1)}, bf16[2,256,24]{2,1,0:T(8,128)(2,1)S(1)}) custom-call(bf16[2,8,8,9]{3,2,1,0:T(8,128)(2,1)S(1)} %get-tuple-element.47.src_w_ref, bf16[2,8,8,9]{3,2,1,0:T(8,128)(2,1)S(1)} %get-tuple-element.48.tgt_w_ref, ...), custom_call_target="tpu_custom_call" | custom-call | flops 1000000 | bytes 10000 | tf_op jit(solution)/shard_map/pallas_call | solution.py:29
  11.1 2.5 %shard_map.52 = (f32[8,2,2,64,128]{4,3,2,1,0:T(8,128)S(1)}, f32[8,2,2,64,128]{4,3,2,1,0:T(8,128)S(1)}) custom-call(bf16[8,2,4,64,128]{4,3,2,1,0:T(8,128)(2,1)S(1)} %copy-done, bf16[256,768]{1,0:T(8,128)(2,1)S(1)} %get-tuple-element.54.refs_0_.refs_1_, bf16[2,256,768]{2,1,0:T(8,128)(2,1)S(1)} %get-tuple-element.50.refs_0_.refs_1_.beside_ref.refs_2_, ...), custom_call_target="tpu_custom_call" | custom-call | flops 1000000 | bytes 10000 | tf_op jit(solution)/shard_map/pallas_call | solution.py:29
  13.7 0.0 collective-permute-done.3.refs_0_.refs_1_
  13.7 0.0 collective-permute-done.4.refs_1_.refs_2_
  13.7 0.0 collective-permute-done.2.colb_ref
  13.7 0.3 shard_map.55
  14.0 1.7 %collective-permute-start.8 = (bf16[8,1,64,128]{3,2,1,0:T(8,128)(2,1)S(1)}, bf16[8,1,64,128]{3,2,1,0:T(8,128)(2,1)S(1)}, u32[]{:S(2)}, u32[]{:S(2)}) collective-permute-start(bf16[8,1,64,128]{3,2,1,0:T(8,128)(2,1)S(1)} %get-tuple-element.70), channel_id=1, source_target_pairs={{0,8},{8,0},{16,24},{24,16},{1,9},{9,1},{17,25},{25,17},{2,10},{10... | collective-permute-start | bytes 393224 | tf_op jit(solution)/shard_map/ppermute | solution.py:450
  15.7 0.0 collective-permute-start.7
  15.7 0.2 shard_map.50
  15.9 1.5 %collective-permute-start.1 = (bf16[2,8,512]{2,1,0:T(8,128)(2,1)S(1)}, bf16[2,8,512]{2,1,0:T(8,128)(2,1)S(1)}, u32[]{:S(2)}, u32[]{:S(2)}) collective-permute-start(bf16[2,8,512]{2,1,0:T(8,128)(2,1)S(1)} %shard_map.50), channel_id=1, source_target_pairs={{0,1},{1,0},{2,3},{3,2},{4,5},{5,4},{6,7},{7,6},{8,9},{9,8},{10,11... | collective-permute-start | bytes 49160 | tf_op jit(solution)/shard_map/ppermute | solution.py:450
  17.4 0.6 %shard_map.59 = (bf16[256,768]{1,0:T(8,128)(2,1)S(1)}, bf16[2,256,768]{2,1,0:T(8,128)(2,1)S(1)}, bf16[256,768]{1,0:T(8,128)(2,1)S(1)}, bf16[2,256,384]{2,1,0:T(8,128)(2,1)S(1)}, bf16[2,256,24]{2,1,0:T(8,128)(2,1)S(1)}) custom-call(bf16[2,8,8,9]{3,2,1,0:T(8,128)(2,1)S(1)} %get-tuple-element.47.src_w_ref, ...), custom_call_target="tpu_custom_call" | custom-call | flops 1000000 | bytes 10000 | tf_op jit(solution)/shard_map/pallas_call | solution.py:29
  18.1 0.0 collective-permute-done.5.refs_3_.refs_1_
  18.1 0.0 collective-permute-done.6.refs_4_.refs_1_
  18.1 1.0 %shard_map.56.refs_2_ = f32[8,2,2,64,128]{4,3,2,1,0:T(8,128)S(1)} custom-call(bf16[8,2,4,64,128]{4,3,2,1,0:T(8,128)(2,1)S(1)} %copy-done, bf16[2,8,2,64,128]{4,3,2,1,0:T(8,128)(2,1)S(1)} %get-tuple-element.63.refs_0_, bf16[256,768]{1,0:T(8,128)(2,1)S(1)} %get-tuple-element.54.refs_0_.refs_1_, ...), custom_call_target="tpu_custom_call", output_to_operand_aliasing={{}: (6, {})} | custom-call | flops 1000000 | bytes 10000 | tf_op jit(solution)/shard_map/pallas_call | solution.py:29
  19.1 0.6 %collective-permute-done.1.refs_0_ = bf16[2,8,512]{2,1,0:T(8,128)(2,1)S(1)} collective-permute-done((bf16[2,8,512]{2,1,0:T(8,128)(2,1)S(1)}, bf16[2,8,512]{2,1,0:T(8,128)(2,1)S(1)}, u32[]{:S(2)}, u32[]{:S(2)}) %collective-permute-start.1) | collective-permute-done | bytes 16416 | tf_op jit(solution)/shard_map/ppermute | solution.py:450
  19.7 0.3 shard_map.57
  20.0 0.2 shard_map.58.refs_3_.mid_ref.x_ref
  20.2 0.0 collective-permute-done.8.refs_2_
  20.2 0.1 shard_map.60.rim_ref.refs_3_
  20.4 0.4 shard_map.61.refs_4_
  20.8 0.0 collective-permute-done.7.refs_2_
  20.8 0.2 shard_map.62
  21.0 0.1 collective-permute-start.9
  21.1 0.4 shard_map.63.after_ref
  21.5 0.5 %collective-permute-start.13 = (bf16[8,2,64,128]{3,2,1,0:T(8,128)(2,1)S(1)}, bf16[8,2,64,128]{3,2,1,0:T(8,128)(2,1)S(1)}, u32[]{:S(2)}, u32[]{:S(2)}) collective-permute-start(bf16[8,2,64,128]{3,2,1,0:T(8,128)(2,1)S(1)} %shard_map.63.after_ref), channel_id=1, source_target_pairs={{0,2},{2,0},{4,6},{6,4},{8,16},{10,18},{12,20},{14,22},{16,8},{18,... | collective-permute-start | bytes 786440 | tf_op jit(solution)/shard_map/ppermute | solution.py:463
  22.0 2.0 %collective-permute-start.12 = (bf16[8,2,64,128]{3,2,1,0:T(8,128)(2,1)S(1)}, bf16[8,2,64,128]{3,2,1,0:T(8,128)(2,1)S(1)}, u32[]{:S(2)}, u32[]{:S(2)}) collective-permute-start(bf16[8,2,64,128]{3,2,1,0:T(8,128)(2,1)S(1)} %shard_map.61.refs_4_), channel_id=1, source_target_pairs={{0,8},{8,0},{16,24},{24,16},{1,9},{9,1},{17,25},{25,17},{2,10},{10... | collective-permute-start | bytes 786440 | tf_op jit(solution)/shard_map/ppermute | solution.py:450
  24.0 1.5 %collective-permute-start.11 = (bf16[8,2,64,128]{3,2,1,0:T(8,128)(2,1)S(1)}, bf16[8,2,64,128]{3,2,1,0:T(8,128)(2,1)S(1)}, u32[]{:S(2)}, u32[]{:S(2)}) collective-permute-start(bf16[8,2,64,128]{3,2,1,0:T(8,128)(2,1)S(1)} %get-tuple-element.80), channel_id=1, source_target_pairs={{0,1},{1,0},{2,4},{3,5},{4,2},{5,3},{6,7},{7,6},{8,9},{9,8},{10,12... | collective-permute-start | bytes 786440 | tf_op jit(solution)/shard_map/ppermute | solution.py:463
  25.6 0.0 collective-permute-done.9.cola_ref
  25.6 0.4 shard_map.64
  25.9 0.1 collective-permute-start.14
  26.0 0.2 collective-permute-start.15
  26.2 0.3 shard_map.66
  26.5 2.5 %shard_map.67 = (f32[8,2,2,64,128]{4,3,2,1,0:T(8,128)S(1)}, f32[8,2,2,64,128]{4,3,2,1,0:T(8,128)S(1)}) custom-call(bf16[8,2,2,64,128]{4,3,2,1,0:T(8,128)(2,1)S(1)} %shard_map.58.refs_3_.mid_ref.x_ref, bf16[8,2,2,64,128]{4,3,2,1,0:T(8,128)(2,1)S(1)} %get-tuple-element.72.rim_ref, bf16[256,768]{1,0:T(8,128)(2,1)S(1)} %get-tuple-element.75.middle_ref, ...), custom_call_target="tpu_custom_call" | custom-call | flops 1000000 | bytes 10000 | tf_op jit(solution)/shard_map/pallas_call | solution.py:29
  29.0 0.0 collective-permute-done.13.refs_1_.b_ref
  29.0 2.1 %collective-permute-done.12.refs_0_.a_ref = bf16[8,2,64,128]{3,2,1,0:T(8,128)(2,1)S(1)} collective-permute-done((bf16[8,2,64,128]{3,2,1,0:T(8,128)(2,1)S(1)}, bf16[8,2,64,128]{3,2,1,0:T(8,128)(2,1)S(1)}, u32[]{:S(2)}, u32[]{:S(2)}) %collective-permute-start.12) | collective-permute-done | bytes 262176 | tf_op jit(solution)/shard_map/ppermute | solution.py:450
  31.1 0.0 collective-permute-done.11.colb_ref
  31.1 0.3 shard_map.69
  31.4 2.1 %collective-permute-start.16 = (bf16[8,1,64,128]{3,2,1,0:T(8,128)(2,1)S(1)}, bf16[8,1,64,128]{3,2,1,0:T(8,128)(2,1)S(1)}, u32[]{:S(2)}, u32[]{:S(2)}) collective-permute-start(bf16[8,1,64,128]{3,2,1,0:T(8,128)(2,1)S(1)} %get-tuple-element.87), channel_id=1, source_target_pairs={{0,8},{8,0},{16,24},{24,16},{1,9},{9,1},{17,25},{25,17},{2,10},{10... | collective-permute-start | bytes 393224 | tf_op jit(solution)/shard_map/ppermute | solution.py:450
  33.6 0.0 collective-permute-start.17
  33.6 0.2 shard_map.65
  33.7 1.5 %collective-permute-start.10 = (bf16[2,8,512]{2,1,0:T(8,128)(2,1)S(1)}, bf16[2,8,512]{2,1,0:T(8,128)(2,1)S(1)}, u32[]{:S(2)}, u32[]{:S(2)}) collective-permute-start(bf16[2,8,512]{2,1,0:T(8,128)(2,1)S(1)} %shard_map.65), channel_id=1, source_target_pairs={{0,1},{1,0},{2,3},{3,2},{4,5},{5,4},{6,7},{7,6},{8,9},{9,8},{10,11... | collective-permute-start | bytes 49160 | tf_op jit(solution)/shard_map/ppermute | solution.py:450
  35.3 0.0 collective-permute-done.14.refs_0_.neara_ref
  35.3 0.0 collective-permute-done.15.refs_1_.nearb_ref
  35.3 1.0 %shard_map.70.refs_2_ = f32[8,2,2,64,128]{4,3,2,1,0:T(8,128)S(1)} custom-call(bf16[8,2,2,64,128]{4,3,2,1,0:T(8,128)(2,1)S(1)} %shard_map.58.refs_3_.mid_ref.x_ref, bf16[8,2,2,64,128]{4,3,2,1,0:T(8,128)(2,1)S(1)} %get-tuple-element.72.rim_ref, bf16[2,8,2,64,128]{4,3,2,1,0:T(8,128)(2,1)S(1)} %get-tuple-element.82.side_ref, ...), custom_call_target="tpu_custom_call", output_to_operand_aliasing={{}: (7, {})} | custom-call | flops 1000000 | bytes 10000 | tf_op jit(solution)/shard_map/pallas_call | solution.py:29
  36.3 1.2 %collective-permute-done.10.refs_0_ = bf16[2,8,512]{2,1,0:T(8,128)(2,1)S(1)} collective-permute-done((bf16[2,8,512]{2,1,0:T(8,128)(2,1)S(1)}, bf16[2,8,512]{2,1,0:T(8,128)(2,1)S(1)}, u32[]{:S(2)}, u32[]{:S(2)}) %collective-permute-start.10) | collective-permute-done | bytes 16416 | tf_op jit(solution)/shard_map/ppermute | solution.py:450
  37.5 0.3 shard_map.71
  37.8 0.2 shard_map.72.mid_ref
  38.1 0.0 collective-permute-done.16.fara_ref
  38.1 0.0 collective-permute-done.17.farb_ref
  38.1 1.0 %shard_map.73 = bf16[8,2,4,64,128]{4,3,2,1,0:T(8,128)(2,1)} custom-call(bf16[8,2,2,64,128]{4,3,2,1,0:T(8,128)(2,1)S(1)} %shard_map.72.mid_ref, bf16[8,2,2,64,128]{4,3,2,1,0:T(8,128)(2,1)S(1)} %get-tuple-element.72.rim_ref, f32[8,2,2,64,128]{4,3,2,1,0:T(8,128)S(1)} %get-tuple-element.86.acc_ref, ...), custom_call_target="tpu_custom_call" | custom-call | flops 1000000 | bytes 10000 | tf_op jit(solution)/shard_map/pallas_call | solution.py:29
  (3 shorter events, 0.0 us)
Async XLA Ops:
  0.0 1.7 %copy-start = (bf16[8,2,4,64,128]{4,3,2,1,0:T(8,128)(2,1)S(1)}, bf16[8,2,4,64,128]{4,3,2,1,0:T(8,128)(2,1)}, u32[]{:S(2)}) copy-start(bf16[8,2,4,64,128]{4,3,2,1,0:T(8,128)(2,1)} %x_ref.19) | copy-start | bytes 3145732
  1.2 5.6 %collective-permute-start = (bf16[8,2,64,128]{3,2,1,0:T(8,128)(2,1)S(1)}, bf16[8,2,64,128]{3,2,1,0:T(8,128)(2,1)S(1)}, u32[]{:S(2)}, u32[]{:S(2)}) collective-permute-start(bf16[8,2,64,128]{3,2,1,0:T(8,128)(2,1)S(1)} %get-tuple-element.49), channel_id=1, source_target_pairs={{0,2},{2,0},{4,6},{6,4},{1,3},{3,1},{5,7},{7,5},{8,10},{10,8},{12,... | collective-permute-start | bytes 786440 | tf_op jit(solution)/shard_map/ppermute | solution.py:450
  2.3 11.4 %collective-permute-start.3 = (bf16[8,2,64,128]{3,2,1,0:T(8,128)(2,1)S(1)}, bf16[8,2,64,128]{3,2,1,0:T(8,128)(2,1)S(1)}, u32[]{:S(2)}, u32[]{:S(2)}) collective-permute-start(bf16[8,2,64,128]{3,2,1,0:T(8,128)(2,1)S(1)} %get-tuple-element.62), channel_id=1, source_target_pairs={{0,8},{8,0},{16,24},{24,16},{1,9},{9,1},{17,25},{25,17},{2,10},{10... | collective-permute-start | bytes 786440 | tf_op jit(solution)/shard_map/ppermute | solution.py:450
  5.1 8.6 %collective-permute-start.4 = (bf16[8,2,64,128]{3,2,1,0:T(8,128)(2,1)S(1)}, bf16[8,2,64,128]{3,2,1,0:T(8,128)(2,1)S(1)}, u32[]{:S(2)}, u32[]{:S(2)}) collective-permute-start(bf16[8,2,64,128]{3,2,1,0:T(8,128)(2,1)S(1)} %get-tuple-element.51.refs_2_.after_ref), channel_id=1, source_target_pairs={{0,2},{2,0},{4,6},{6,4},{8,16},{10,18},{12,20},{14,22},{16,8},{18,... | collective-permute-start | bytes 786440 | tf_op jit(solution)/shard_map/ppermute | solution.py:463
  5.2 8.5 %collective-permute-start.2 = (bf16[8,2,64,128]{3,2,1,0:T(8,128)(2,1)S(1)}, bf16[8,2,64,128]{3,2,1,0:T(8,128)(2,1)S(1)}, u32[]{:S(2)}, u32[]{:S(2)}) collective-permute-start(bf16[8,2,64,128]{3,2,1,0:T(8,128)(2,1)S(1)} %shard_map.53), channel_id=1, source_target_pairs={{0,1},{1,0},{2,4},{3,5},{4,2},{5,3},{6,7},{7,6},{8,9},{9,8},{10,12... | collective-permute-start | bytes 786440 | tf_op jit(solution)/shard_map/ppermute | solution.py:463
  7.1 10.9 %collective-permute-start.5 = (bf16[8,1,64,128]{3,2,1,0:T(8,128)(2,1)S(1)}, bf16[8,1,64,128]{3,2,1,0:T(8,128)(2,1)S(1)}, u32[]{:S(2)}, u32[]{:S(2)}) collective-permute-start(bf16[8,1,64,128]{3,2,1,0:T(8,128)(2,1)S(1)} %get-tuple-element.64), channel_id=1, source_target_pairs={{0,8},{8,0},{16,24},{24,16},{1,9},{9,1},{17,25},{25,17},{2,10},{10... | collective-permute-start | bytes 393224 | tf_op jit(solution)/shard_map/ppermute | solution.py:450
  10.3 7.8 %collective-permute-start.6 = (bf16[8,1,64,128]{3,2,1,0:T(8,128)(2,1)S(1)}, bf16[8,1,64,128]{3,2,1,0:T(8,128)(2,1)S(1)}, u32[]{:S(2)}, u32[]{:S(2)}) collective-permute-start(bf16[8,1,64,128]{3,2,1,0:T(8,128)(2,1)S(1)} %get-tuple-element.52.after_ref.refs_0_.refs_1_), channel_id=1, source_target_pairs={{0,2},{2,0},{4,6},{6,4},{8,16},{10,18},{12,20},{14,22},{16,8},{18,... | collective-permute-start | bytes 393224 | tf_op jit(solution)/shard_map/ppermute | solution.py:463
  14.0 6.2 %collective-permute-start.8 = (bf16[8,1,64,128]{3,2,1,0:T(8,128)(2,1)S(1)}, bf16[8,1,64,128]{3,2,1,0:T(8,128)(2,1)S(1)}, u32[]{:S(2)}, u32[]{:S(2)}) collective-permute-start(bf16[8,1,64,128]{3,2,1,0:T(8,128)(2,1)S(1)} %get-tuple-element.70), channel_id=1, source_target_pairs={{0,8},{8,0},{16,24},{24,16},{1,9},{9,1},{17,25},{25,17},{2,10},{10... | collective-permute-start | bytes 393224 | tf_op jit(solution)/shard_map/ppermute | solution.py:450
  15.7 5.0 %collective-permute-start.7 = (bf16[8,1,64,128]{3,2,1,0:T(8,128)(2,1)S(1)}, bf16[8,1,64,128]{3,2,1,0:T(8,128)(2,1)S(1)}, u32[]{:S(2)}, u32[]{:S(2)}) collective-permute-start(bf16[8,1,64,128]{3,2,1,0:T(8,128)(2,1)S(1)} %get-tuple-element.67.after_ref), channel_id=1, source_target_pairs={{0,2},{2,0},{4,6},{6,4},{8,16},{10,18},{12,20},{14,22},{16,8},{18,... | collective-permute-start | bytes 393224 | tf_op jit(solution)/shard_map/ppermute | solution.py:463
  15.9 3.7 %collective-permute-start.1 = (bf16[2,8,512]{2,1,0:T(8,128)(2,1)S(1)}, bf16[2,8,512]{2,1,0:T(8,128)(2,1)S(1)}, u32[]{:S(2)}, u32[]{:S(2)}) collective-permute-start(bf16[2,8,512]{2,1,0:T(8,128)(2,1)S(1)} %shard_map.50), channel_id=1, source_target_pairs={{0,1},{1,0},{2,3},{3,2},{4,5},{5,4},{6,7},{7,6},{8,9},{9,8},{10,11... | collective-permute-start | bytes 49160 | tf_op jit(solution)/shard_map/ppermute | solution.py:450
  21.0 4.6 %collective-permute-start.9 = (bf16[8,2,64,128]{3,2,1,0:T(8,128)(2,1)S(1)}, bf16[8,2,64,128]{3,2,1,0:T(8,128)(2,1)S(1)}, u32[]{:S(2)}, u32[]{:S(2)}) collective-permute-start(bf16[8,2,64,128]{3,2,1,0:T(8,128)(2,1)S(1)} %get-tuple-element.73), channel_id=1, source_target_pairs={{0,2},{2,0},{4,6},{6,4},{1,3},{3,1},{5,7},{7,5},{8,10},{10,8},{12,... | collective-permute-start | bytes 786440 | tf_op jit(solution)/shard_map/ppermute | solution.py:450
  21.5 7.5 %collective-permute-start.13 = (bf16[8,2,64,128]{3,2,1,0:T(8,128)(2,1)S(1)}, bf16[8,2,64,128]{3,2,1,0:T(8,128)(2,1)S(1)}, u32[]{:S(2)}, u32[]{:S(2)}) collective-permute-start(bf16[8,2,64,128]{3,2,1,0:T(8,128)(2,1)S(1)} %shard_map.63.after_ref), channel_id=1, source_target_pairs={{0,2},{2,0},{4,6},{6,4},{8,16},{10,18},{12,20},{14,22},{16,8},{18,... | collective-permute-start | bytes 786440 | tf_op jit(solution)/shard_map/ppermute | solution.py:463
  22.0 9.1 %collective-permute-start.12 = (bf16[8,2,64,128]{3,2,1,0:T(8,128)(2,1)S(1)}, bf16[8,2,64,128]{3,2,1,0:T(8,128)(2,1)S(1)}, u32[]{:S(2)}, u32[]{:S(2)}) collective-permute-start(bf16[8,2,64,128]{3,2,1,0:T(8,128)(2,1)S(1)} %shard_map.61.refs_4_), channel_id=1, source_target_pairs={{0,8},{8,0},{16,24},{24,16},{1,9},{9,1},{17,25},{25,17},{2,10},{10... | collective-permute-start | bytes 786440 | tf_op jit(solution)/shard_map/ppermute | solution.py:450
  24.0 7.1 %collective-permute-start.11 = (bf16[8,2,64,128]{3,2,1,0:T(8,128)(2,1)S(1)}, bf16[8,2,64,128]{3,2,1,0:T(8,128)(2,1)S(1)}, u32[]{:S(2)}, u32[]{:S(2)}) collective-permute-start(bf16[8,2,64,128]{3,2,1,0:T(8,128)(2,1)S(1)} %get-tuple-element.80), channel_id=1, source_target_pairs={{0,1},{1,0},{2,4},{3,5},{4,2},{5,3},{6,7},{7,6},{8,9},{9,8},{10,12... | collective-permute-start | bytes 786440 | tf_op jit(solution)/shard_map/ppermute | solution.py:463
  25.9 9.3 %collective-permute-start.14 = (bf16[8,1,64,128]{3,2,1,0:T(8,128)(2,1)S(1)}, bf16[8,1,64,128]{3,2,1,0:T(8,128)(2,1)S(1)}, u32[]{:S(2)}, u32[]{:S(2)}) collective-permute-start(bf16[8,1,64,128]{3,2,1,0:T(8,128)(2,1)S(1)} %get-tuple-element.83), channel_id=1, source_target_pairs={{0,8},{8,0},{16,24},{24,16},{1,9},{9,1},{17,25},{25,17},{2,10},{10... | collective-permute-start | bytes 393224 | tf_op jit(solution)/shard_map/ppermute | solution.py:450
  26.0 9.3 %collective-permute-start.15 = (bf16[8,1,64,128]{3,2,1,0:T(8,128)(2,1)S(1)}, bf16[8,1,64,128]{3,2,1,0:T(8,128)(2,1)S(1)}, u32[]{:S(2)}, u32[]{:S(2)}) collective-permute-start(bf16[8,1,64,128]{3,2,1,0:T(8,128)(2,1)S(1)} %get-tuple-element.74.after_ref), channel_id=1, source_target_pairs={{0,2},{2,0},{4,6},{6,4},{8,16},{10,18},{12,20},{14,22},{16,8},{18,... | collective-permute-start | bytes 393224 | tf_op jit(solution)/shard_map/ppermute | solution.py:463
  31.4 6.6 %collective-permute-start.16 = (bf16[8,1,64,128]{3,2,1,0:T(8,128)(2,1)S(1)}, bf16[8,1,64,128]{3,2,1,0:T(8,128)(2,1)S(1)}, u32[]{:S(2)}, u32[]{:S(2)}) collective-permute-start(bf16[8,1,64,128]{3,2,1,0:T(8,128)(2,1)S(1)} %get-tuple-element.87), channel_id=1, source_target_pairs={{0,8},{8,0},{16,24},{24,16},{1,9},{9,1},{17,25},{25,17},{2,10},{10... | collective-permute-start | bytes 393224 | tf_op jit(solution)/shard_map/ppermute | solution.py:450
  33.6 4.5 %collective-permute-start.17 = (bf16[8,1,64,128]{3,2,1,0:T(8,128)(2,1)S(1)}, bf16[8,1,64,128]{3,2,1,0:T(8,128)(2,1)S(1)}, u32[]{:S(2)}, u32[]{:S(2)}) collective-permute-start(bf16[8,1,64,128]{3,2,1,0:T(8,128)(2,1)S(1)} %get-tuple-element.88), channel_id=1, source_target_pairs={{0,2},{2,0},{4,6},{6,4},{8,16},{10,18},{12,20},{14,22},{16,8},{18,... | collective-permute-start | bytes 393224 | tf_op jit(solution)/shard_map/ppermute | solution.py:463
  33.7 3.7 %collective-permute-start.10 = (bf16[2,8,512]{2,1,0:T(8,128)(2,1)S(1)}, bf16[2,8,512]{2,1,0:T(8,128)(2,1)S(1)}, u32[]{:S(2)}, u32[]{:S(2)}) collective-permute-start(bf16[2,8,512]{2,1,0:T(8,128)(2,1)S(1)} %shard_map.65), channel_id=1, source_target_pairs={{0,1},{1,0},{2,3},{3,2},{4,5},{5,4},{6,7},{7,6},{8,9},{9,8},{10,11... | collective-permute-start | bytes 49160 | tf_op jit(solution)/shard_map/ppermute | solution.py:450

commit v11 on v10

--- a/solution.py
+++ b/solution.py
@@ -22,7 +22,7 @@
     return (at > 0) & (at < lax.axis_size(axis) - 1)
 
 
-def call(body, outs, args, places=None, out_place=VMEM, scratch=(), aliases=None):
+def call(body, outs, args, places=None, out_place=VMEM, scratch=(), aliases=None, flops=10**6):
     places = places or {}
     spaces = [places.get(n, VMEM) for n in range(len(args))]
     held = [pltpu.with_memory_space_constraint(a, m) if m in (VMEM, HBM) else a for a, m in zip(args, spaces)]
@@ -34,7 +34,7 @@
         scratch_shapes=list(scratch),
         input_output_aliases=aliases or {},
         compiler_params=pltpu.CompilerParams(vmem_limit_bytes=SCOPED),
-        cost_estimate=pl.CostEstimate(flops=10**6, bytes_accessed=10**4, transcendentals=0),
+        cost_estimate=pl.CostEstimate(flops=flops, bytes_accessed=10**4, transcendentals=0),
     )(*held)
 
 
@@ -165,8 +165,8 @@
     return [slice(start, start + BAND) for start in range(0, depth, BAND)]
 
 
-def owed_sums(operator, tiles, out_ref):
-    channels, cols, depth, width = out_ref.shape
+def owed_sums(operator, tiles, cols, out_ref):
+    channels, _, depth, width = out_ref.shape
     cuts = bands_of(depth)
     operand = jnp.concatenate([jnp.concatenate([t for cut in cuts for t in tiles(cut, b)], axis=1) for b in range(3)], axis=0)
     got = dot(operator, operand).astype(BF16)
@@ -181,7 +181,7 @@
     for n, out_ref in zip(which, out_refs):
         i, side = sent_rows(rows)[n]
         owed_sums(
-            beside_ref[side], lambda cut, b: [column(mid_ref, rim_ref, i, j + b, cut) for j in range(cols)], out_ref
+            beside_ref[side], lambda cut, b: [column(mid_ref, rim_ref, i, j + b, cut) for j in range(cols)], cols, out_ref
         )
 
 
@@ -209,18 +209,18 @@
     return dot(beside_ref[row_side, :, pl.ds(outward, span)], all_bands(lambda cut: halo_ref[:, i, cut], halo_ref.shape[2]))
 
 
-def put_sums(got, out_ref):
+def put_sums(got, out_ref, j=0):
     channels, _, depth, width = out_ref.shape
     got = got.astype(BF16)
     for q, cut in enumerate(bands_of(depth)):
-        out_ref[:, 0, cut] = unband(got[:, q * width : (q + 1) * width], channels)
-
-
-def near_body(mid_ref, rim_ref, cola_ref, beside_ref, after_ref, a_ref, b_ref):
-    n = side_of(False)
-    for (i, row_side), out_ref in zip(sent_rows(mid_ref.shape[1]), (a_ref, b_ref)):
+        out_ref[:, j, cut] = unband(got[:, q * width : (q + 1) * width], channels)
+
+
+def near_body(mid_ref, rim_ref, cola_ref, beside_ref, *refs):
+    n, mids = side_of(False), mid_ref.shape[2]
+    for (i, row_side), out_ref in zip(sent_rows(mid_ref.shape[1]), refs[-2:]):
         got = own_taps(mid_ref, rim_ref, beside_ref, i, row_side, n) + halo_tap(cola_ref, beside_ref, i, row_side, n)
-        put_sums(got, out_ref)
+        put_sums(got, out_ref, mids)
 
 
 def part_body(mid_ref, rim_ref, beside_ref, after_ref, *part_refs):
@@ -378,7 +378,7 @@
 
 
 def side_columns(near_ref, far_ref):
-    return [(side_of(False), near_ref[:, 0]), (side_of(True), far_ref[:, 0])]
+    return [(side_of(False), near_ref[:, near_ref.shape[1] - 1]), (side_of(True), far_ref[:, 0])]
 
 
 def begin_body(x_ref, acc_ref, near_ref, far_ref, after_ref, out_ref):
@@ -418,11 +418,7 @@
         copy.wait()
 
 
-def gate_body(*refs):
-    refs[-1][...] = jnp.zeros_like(refs[-1])
-
-
-def pass_body(x_ref, after_ref, out_ref):
+def pass_body(x_ref, after_ref, also_ref, out_ref):
     out_ref[...] = x_ref[...]
 
 
@@ -485,7 +481,7 @@
     )
     made = {early[0]: beside_0}
     kinds = ("middle", "beside", "target", "near", "deep")
-    owed_inner = [VMEM((channels, cols - 2, depth, width), BF16)]
+    owed_inner = [VMEM((channels, cols - 1, depth, width), BF16)]
     block, sum_a = (volume,), None
     for layer in range(layers):
 
@@ -496,29 +492,24 @@
         mid, rim = block[0], block[-1]
         which = (0, 1) if sum_a is None else (1,)
         sums = call(on(functools.partial(inner_body, which), *both), owed_inner * len(which), (*block, made["beside", layer]))
-        sum_b = sums[-1]
+        sum_a, sum_b = sums if sum_a is None else (sum_a, *sums)
+        got_col_a = swap_first(col_a, "scol")
+        near = call(
+            on(near_body, *both),
+            owed_inner * 2,
+            (*block, got_col_a, made["beside", layer], sum_a, sum_b),
+            aliases={base + 2: 0, base + 3: 1},
+        )
+        near_got = swap_first(near[0], "srow"), swap_second(near[1], "srow", "scol")
+        (col_b,) = call(pass_body, [line], (col_b, *near), {1: pl.ANY, 2: pl.ANY})
+        beside = got_col_a, swap_second(col_b, "scol", "trow")
         if layer == 0:
-            (col_b,) = call(pass_body, [line], (col_b, sum_b), {1: pl.ANY})
-        beside = swap_first(col_a, "scol"), swap_second(col_b, "scol", "trow")
-        inner = swap_first(sums[0], "srow") if sum_a is None else got_a, swap_second(sum_b, "srow", "scol")
-        def own(after):
-            return call(
-                on(functools.partial(own_body, layer), *both),
-                [VMEM(mid_shape, F32), VMEM(rim_shape, F32)],
-                (*block, *(operator[kind] for kind in ("middle", "beside", "target", "near")), bias, after),
-                {base + 5: pl.ANY},
-                scratch=[VMEM((depth // BAND, 3, channels * BAND, cols * width), BF16)],
-            )
-
-        near = call(on(near_body, *both), [owed_side] * 2, (*block, beside[0], made["beside", layer], sum_b), {base + 2: pl.ANY})
-        near_got = swap_first(near[0], "srow"), swap_second(near[1], "srow", "scol")
-        if layer == 0:
-            made |= build([(kind, 0) for kind in kinds if kind != "beside"], src_w, tgt_w, near[1])
+            made |= build([(kind, 0) for kind in kinds if kind != "beside"], src_w, tgt_w, sum_b)
         operator = {kind: made[kind, layer] for kind in kinds}
         parts = call(
             on(part_body, *both),
             [VMEM((channels * BAND, depth // BAND * width), F32)] * 2,
-            (*block, operator["beside"], near[1]),
+            (*block, operator["beside"], sum_b),
             {base + 1: pl.ANY},
         )
         deep = call(
@@ -530,13 +521,18 @@
         deeper = [swap_first(deep[0], "trow")]
         if deep_swaps == 2:
             deeper.append(swap_second(deep[1], "trow", "scol"))
-        accs = own(parts[1])
-        waited = (*inner, accs[0])
-        (gate,) = call(gate_body, [VMEM((8, 128), F32)], waited, {n: pl.ANY for n in range(len(waited))})
+        accs = call(
+            on(functools.partial(own_body, layer), *both),
+            [VMEM(mid_shape, F32), VMEM(rim_shape, F32)],
+            (*block, *(operator[kind] for kind in ("middle", "beside", "target", "near")), bias, parts[1]),
+            {base + 5: pl.ANY},
+            scratch=[VMEM((depth // BAND, 3, channels * BAND, cols * width), BF16)],
+            flops=10**10,
+        )
         a, b, side = call(
             far_body,
             [owed_side, owed_side, VMEM((2, *line.shape), BF16)],
-            (*beside, operator["beside"], *parts, gate),
+            (*beside, operator["beside"], *parts, accs[0]),
             {5: pl.ANY},
         )
         far_got = swap_first(a, "srow"), swap_second(b, "srow", "scol")
@@ -545,9 +541,8 @@
         (acc_rim,) = call(
             on(source_body, *both),
             [VMEM(rim_shape, F32)],
-            (*block, side, operator["middle"], operator["beside"], *near_got, accs[1]),
-            {base + 3: pl.ANY, base + 4: pl.ANY},
-            aliases={base + 5: 0},
+            (*block, side, operator["middle"], operator["beside"], accs[1]),
+            aliases={base + 3: 0},
         )
         acc_mid, acc_rim = call(
             deep_body,
@@ -555,12 +550,11 @@
             (operator["deep"], *deeper, accs[0], acc_rim),
             aliases={1 + deep_swaps: 0, 2 + deep_swaps: 1},
         )
-        (mid,) = call(on(mid_body, middle), [VMEM(mid_shape, BF16)], (mid, acc_mid, *inner))
+        (mid,) = call(on(mid_body, middle), [VMEM(mid_shape, BF16)], (mid, acc_mid, *near_got))
         if layer < layers - 1:
             whole_rim = [VMEM(rim_shape, BF16)]
             (begun,) = call(on(begin_body, sides), whole_rim, (rim, acc_rim, near_got[0], far_got[0], mid), {4: pl.ANY})
             (sum_a,) = call(functools.partial(inner_body, (0,)), owed_inner, (mid, begun, made["beside", layer + 1]))
-            got_a = swap_first(sum_a, "srow")
             rim, col_a, col_b = call(
                 on(next_body, sides),
                 whole_rim + [line, line],

time: 39.3 us -> 39.2 us (level)
  starting transfers between devices: 19.4 us -> 15.2 us
  waiting for transfers between devices: 3.94 us -> 7.95 us
    ppermute x8 -> x6, waiting for transfers between devices: 0.02 us -> 4.67 us  [swap_second(): return lax.ppermute(value, (axis, other), pairs)]
    ppermute x10 -> x8, starting transfers between devices: 15.5 us -> 11.8 us  [swap_first(): lax.ppermute(value, axis, [(n, n ^ 1) for n in range(lax.axis_size(axis))])]
    ppermute x10 -> x8, waiting for transfers between devices: 3.92 us -> 3.28 us  [swap_first(): lax.ppermute(value, axis, [(n, n ^ 1) for n in range(lax.axis_size(axis))])]
    ppermute x8 -> x6, starting transfers between devices: 3.87 us -> 3.48 us  [swap_second(): return lax.ppermute(value, (axis, other), pairs)]
    pallas_call x28 -> x27, Pallas kernels: 15.5 us -> 15.6 us  [call(): pl.pallas_call(body, out_shape=tuple(outs), in_specs=[pl.BlockSpec(memory...]
  transfers between devices with their start and end apart: 18 -> 14, of which waited for: 3 -> 6; matrix products, arithmetic and copies ran while one was open for 0% -> 0% of each run, Pallas kernels for 33% -> 32%
where the time goes in v11:
time: 39.2 us; the launch traced here: 39 us
  Pallas kernels  15.6 us (40%)
  starting transfers between devices  15.2 us (39%)
  waiting for transfers between devices  7.95 us (20%)
    pallas_call x27, Pallas kernels, call(): pl.pallas_call(body, out_shape=tuple(outs), in_specs=[pl.BlockSpec(memory...  15.6 us
    ppermute x8, starting transfers between devices, swap_first(): lax.ppermute(value, axis, [(n, n ^ 1) for n in range(lax.axis_size(axis))])  11.8 us
    ppermute x6, waiting for transfers between devices, swap_second(): return lax.ppermute(value, (axis, other), pairs)  4.67 us
    ppermute x6, starting transfers between devices, swap_second(): return lax.ppermute(value, (axis, other), pairs)  3.48 us
    ppermute x8, waiting for transfers between devices, swap_first(): lax.ppermute(value, axis, [(n, n ^ 1) for n in range(lax.axis_size(axis))])  3.28 us
  transfers between devices with their start and end apart: 14, of which 6 were waited for; matrix products, arithmetic and copies ran while one was open for 0% of the time, Pallas kernels for 32%

profile of v11, /device:TPU:0, one launch (start us, length us, event | category | flops | bytes accessed | tf_op | source)
XLA Modules:
  0.0 39.0 jit_solution(1782606224163900295)
XLA Ops:
  0.0 0.0 copy-start
  0.0 1.2 %shard_map.46 = (bf16[2,8,8,9]{3,2,1,0:T(8,128)(2,1)S(1)}, bf16[2,8,8,9]{3,2,1,0:T(8,128)(2,1)S(1)}, f32[2,8]{1,0:T(2,128)S(1)}, bf16[2,256,768]{2,1,0:T(8,128)(...) custom-call(bf16[8,2,4,64,128]{4,3,2,1,0:T(8,128)(2,1)} %x_ref.19, ...), custom_call_target="tpu_custom_call" | custom-call | flops 1000000 | bytes 10000 | tf_op jit(solution)/shard_map/pallas_call | solution.py:29
  1.2 0.5 %collective-permute-start = (bf16[8,2,64,128]{3,2,1,0:T(8,128)(2,1)S(1)}, bf16[8,2,64,128]{3,2,1,0:T(8,128)(2,1)S(1)}, u32[]{:S(2)}, u32[]{:S(2)}) collective-permute-start(bf16[8,2,64,128]{3,2,1,0:T(8,128)(2,1)S(1)} %get-tuple-element.52), channel_id=1, source_target_pairs={{0,2},{2,0},{4,6},{6,4},{1,3},{3,1},{5,7},{7,5},{8,10},{10,8},{12,... | collective-permute-start | bytes 786440 | tf_op jit(solution)/shard_map/ppermute | solution.py:446
  1.7 0.0 copy-done
  1.7 0.6 %shard_map.47 = (bf16[8,3,64,128]{3,2,1,0:T(8,128)(2,1)S(1)}, bf16[8,3,64,128]{3,2,1,0:T(8,128)(2,1)S(1)}) custom-call(bf16[8,2,4,64,128]{4,3,2,1,0:T(8,128)(2,1)S(1)} %copy-done, bf16[2,256,768]{2,1,0:T(8,128)(2,1)S(1)} %get-tuple-element.49.refs_0_.refs_1_.beside_ref.refs_2_), custom_call_target="tpu_custom_call" | custom-call | flops 1000000 | bytes 10000 | tf_op jit(solution)/shard_map/pallas_call | solution.py:29
  2.3 0.3 shard_map.51
  2.6 0.5 %shard_map.48 = (bf16[256,768]{1,0:T(8,128)(2,1)S(1)}, bf16[256,768]{1,0:T(8,128)(2,1)S(1)}, bf16[2,256,384]{2,1,0:T(8,128)(2,1)S(1)}, bf16[2,256,24]{2,1,0:T(8,128)(2,1)S(1)}) custom-call(bf16[2,8,8,9]{3,2,1,0:T(8,128)(2,1)S(1)} %get-tuple-element.47.src_w_ref, bf16[2,8,8,9]{3,2,1,0:T(8,128)(2,1)S(1)} %get-tuple-element.48.tgt_w_ref, ...), custom_call_target="tpu_custom_call" | custom-call | flops 1000000 | bytes 10000 | tf_op jit(solution)/shard_map/pallas_call | solution.py:29
  3.2 0.0 collective-permute-done.refs_0_.cola_ref
  3.2 0.4 shard_map.49
  3.6 0.2 collective-permute-start.4
  3.8 4.1 %collective-permute-start.3 = (bf16[8,3,64,128]{3,2,1,0:T(8,128)(2,1)S(1)}, bf16[8,3,64,128]{3,2,1,0:T(8,128)(2,1)S(1)}, u32[]{:S(2)}, u32[]{:S(2)}) collective-permute-start(bf16[8,3,64,128]{3,2,1,0:T(8,128)(2,1)S(1)} %get-tuple-element.62.after_ref), channel_id=1, source_target_pairs={{0,8},{8,0},{16,24},{24,16},{1,9},{9,1},{17,25},{25,17},{2,10},{10... | collective-permute-start | bytes 1179656 | tf_op jit(solution)/shard_map/ppermute | solution.py:446
  8.0 1.6 %collective-permute-start.2 = (bf16[8,2,64,128]{3,2,1,0:T(8,128)(2,1)S(1)}, bf16[8,2,64,128]{3,2,1,0:T(8,128)(2,1)S(1)}, u32[]{:S(2)}, u32[]{:S(2)}) collective-permute-start(bf16[8,2,64,128]{3,2,1,0:T(8,128)(2,1)S(1)} %shard_map.53), channel_id=1, source_target_pairs={{0,1},{1,0},{2,4},{3,5},{4,2},{5,3},{6,7},{7,6},{8,9},{9,8},{10,12... | collective-permute-start | bytes 786440 | tf_op jit(solution)/shard_map/ppermute | solution.py:459
  9.5 2.5 %shard_map.52 = (f32[8,2,2,64,128]{4,3,2,1,0:T(8,128)S(1)}, f32[8,2,2,64,128]{4,3,2,1,0:T(8,128)S(1)}) custom-call(bf16[8,2,4,64,128]{4,3,2,1,0:T(8,128)(2,1)S(1)} %copy-done, bf16[256,768]{1,0:T(8,128)(2,1)S(1)} %get-tuple-element.55.refs_0_.refs_1_, bf16[2,256,768]{2,1,0:T(8,128)(2,1)S(1)} %get-tuple-element.49.refs_0_.refs_1_.beside_ref.refs_2_, ...), custom_call_target="tpu_custom_call" | custom-call | flops 10000000000 | bytes 10000 | tf_op jit(solution)/shard_map/pallas_call | solution.py:29
  12.1 2.3 %collective-permute-done.2.colb_ref = bf16[8,2,64,128]{3,2,1,0:T(8,128)(2,1)S(1)} collective-permute-done((bf16[8,2,64,128]{3,2,1,0:T(8,128)(2,1)S(1)}, bf16[8,2,64,128]{3,2,1,0:T(8,128)(2,1)S(1)}, u32[]{:S(2)}, u32[]{:S(2)}) %collective-permute-start.2) | collective-permute-done | bytes 262176 | tf_op jit(solution)/shard_map/ppermute | solution.py:459
  14.4 0.3 shard_map.54
  14.7 0.1 collective-permute-start.6
  14.8 0.1 collective-permute-start.5
  14.9 0.2 shard_map.50
  15.1 1.5 %collective-permute-start.1 = (bf16[2,8,512]{2,1,0:T(8,128)(2,1)S(1)}, bf16[2,8,512]{2,1,0:T(8,128)(2,1)S(1)}, u32[]{:S(2)}, u32[]{:S(2)}) collective-permute-start(bf16[2,8,512]{2,1,0:T(8,128)(2,1)S(1)} %shard_map.50), channel_id=1, source_target_pairs={{0,1},{1,0},{2,3},{3,2},{4,5},{5,4},{6,7},{7,6},{8,9},{9,8},{10,11... | collective-permute-start | bytes 49160 | tf_op jit(solution)/shard_map/ppermute | solution.py:446
  16.6 0.6 %shard_map.58 = (bf16[256,768]{1,0:T(8,128)(2,1)S(1)}, bf16[2,256,768]{2,1,0:T(8,128)(2,1)S(1)}, bf16[256,768]{1,0:T(8,128)(2,1)S(1)}, bf16[2,256,384]{2,1,0:T(8,128)(2,1)S(1)}, bf16[2,256,24]{2,1,0:T(8,128)(2,1)S(1)}) custom-call(bf16[2,8,8,9]{3,2,1,0:T(8,128)(2,1)S(1)} %get-tuple-element.47.src_w_ref, ...), custom_call_target="tpu_custom_call" | custom-call | flops 1000000 | bytes 10000 | tf_op jit(solution)/shard_map/pallas_call | solution.py:29
  17.2 1.0 %shard_map.55.refs_2_ = f32[8,2,2,64,128]{4,3,2,1,0:T(8,128)S(1)} custom-call(bf16[8,2,4,64,128]{4,3,2,1,0:T(8,128)(2,1)S(1)} %copy-done, bf16[2,8,2,64,128]{4,3,2,1,0:T(8,128)(2,1)S(1)} %get-tuple-element.64.refs_0_, bf16[256,768]{1,0:T(8,128)(2,1)S(1)} %get-tuple-element.55.refs_0_.refs_1_, ...), custom_call_target="tpu_custom_call", output_to_operand_aliasing={{}: (4, {})} | custom-call | flops 1000000 | bytes 10000 | tf_op jit(solution)/shard_map/pallas_call | solution.py:29
  18.2 0.6 %collective-permute-done.1.refs_0_ = bf16[2,8,512]{2,1,0:T(8,128)(2,1)S(1)} collective-permute-done((bf16[2,8,512]{2,1,0:T(8,128)(2,1)S(1)}, bf16[2,8,512]{2,1,0:T(8,128)(2,1)S(1)}, u32[]{:S(2)}, u32[]{:S(2)}) %collective-permute-start.1) | collective-permute-done | bytes 16416 | tf_op jit(solution)/shard_map/ppermute | solution.py:446
  18.8 0.3 shard_map.56
  19.1 0.0 collective-permute-done.4.refs_2_.refs_1_
  19.2 0.0 collective-permute-done.3.refs_1_
  19.2 0.2 shard_map.57.refs_3_.mid_ref.x_ref
  19.4 0.7 %collective-permute-done.6.refs_2_ = bf16[8,1,64,128]{3,2,1,0:T(8,128)(2,1)S(1)} collective-permute-done((bf16[8,1,64,128]{3,2,1,0:T(8,128)(2,1)S(1)}, bf16[8,1,64,128]{3,2,1,0:T(8,128)(2,1)S(1)}, u32[]{:S(2)}, u32[]{:S(2)}) %collective-permute-start.6) | collective-permute-done | bytes 131104 | tf_op jit(solution)/shard_map/ppermute | solution.py:446
  20.1 0.1 shard_map.59.rim_ref.refs_3_
  20.2 0.4 shard_map.60.refs_4_.refs_0_
  20.6 0.0 collective-permute-done.5.refs_2_
  20.6 0.2 shard_map.61
  20.8 0.1 collective-permute-start.7
  20.9 0.4 shard_map.62.refs_1_.after_ref
  21.3 0.3 shard_map.65
  21.6 0.8 %collective-permute-done.7.cola_ref = bf16[8,2,64,128]{3,2,1,0:T(8,128)(2,1)S(1)} collective-permute-done((bf16[8,2,64,128]{3,2,1,0:T(8,128)(2,1)S(1)}, bf16[8,2,64,128]{3,2,1,0:T(8,128)(2,1)S(1)}, u32[]{:S(2)}, u32[]{:S(2)}) %collective-permute-start.7) | collective-permute-done | bytes 262176 | tf_op jit(solution)/shard_map/ppermute | solution.py:446
  22.4 0.4 shard_map.63
  22.8 1.8 %collective-permute-start.10 = (bf16[8,3,64,128]{3,2,1,0:T(8,128)(2,1)S(1)}, bf16[8,3,64,128]{3,2,1,0:T(8,128)(2,1)S(1)}, u32[]{:S(2)}, u32[]{:S(2)}) collective-permute-start(bf16[8,3,64,128]{3,2,1,0:T(8,128)(2,1)S(1)} %get-tuple-element.81.after_ref), channel_id=1, source_target_pairs={{0,8},{8,0},{16,24},{24,16},{1,9},{9,1},{17,25},{25,17},{2,10},{10... | collective-permute-start | bytes 1179656 | tf_op jit(solution)/shard_map/ppermute | solution.py:446
  24.6 0.0 collective-permute-start.11
  24.6 1.6 %collective-permute-start.9 = (bf16[8,2,64,128]{3,2,1,0:T(8,128)(2,1)S(1)}, bf16[8,2,64,128]{3,2,1,0:T(8,128)(2,1)S(1)}, u32[]{:S(2)}, u32[]{:S(2)}) collective-permute-start(bf16[8,2,64,128]{3,2,1,0:T(8,128)(2,1)S(1)} %shard_map.67), channel_id=1, source_target_pairs={{0,1},{1,0},{2,4},{3,5},{4,2},{5,3},{6,7},{7,6},{8,9},{9,8},{10,12... | collective-permute-start | bytes 786440 | tf_op jit(solution)/shard_map/ppermute | solution.py:459
  26.2 2.5 %shard_map.66 = (f32[8,2,2,64,128]{4,3,2,1,0:T(8,128)S(1)}, f32[8,2,2,64,128]{4,3,2,1,0:T(8,128)S(1)}) custom-call(bf16[8,2,2,64,128]{4,3,2,1,0:T(8,128)(2,1)S(1)} %shard_map.57.refs_3_.mid_ref.x_ref, bf16[8,2,2,64,128]{4,3,2,1,0:T(8,128)(2,1)S(1)} %get-tuple-element.72.rim_ref, bf16[256,768]{1,0:T(8,128)(2,1)S(1)} %get-tuple-element.75.middle_ref, ...), custom_call_target="tpu_custom_call" | custom-call | flops 10000000000 | bytes 10000 | tf_op jit(solution)/shard_map/pallas_call | solution.py:29
  28.7 2.3 %collective-permute-done.9.colb_ref = bf16[8,2,64,128]{3,2,1,0:T(8,128)(2,1)S(1)} collective-permute-done((bf16[8,2,64,128]{3,2,1,0:T(8,128)(2,1)S(1)}, bf16[8,2,64,128]{3,2,1,0:T(8,128)(2,1)S(1)}, u32[]{:S(2)}, u32[]{:S(2)}) %collective-permute-start.9) | collective-permute-done | bytes 262176 | tf_op jit(solution)/shard_map/ppermute | solution.py:459
  31.1 0.3 shard_map.68
  31.4 2.1 %collective-permute-start.12 = (bf16[8,1,64,128]{3,2,1,0:T(8,128)(2,1)S(1)}, bf16[8,1,64,128]{3,2,1,0:T(8,128)(2,1)S(1)}, u32[]{:S(2)}, u32[]{:S(2)}) collective-permute-start(bf16[8,1,64,128]{3,2,1,0:T(8,128)(2,1)S(1)} %get-tuple-element.87), channel_id=1, source_target_pairs={{0,8},{8,0},{16,24},{24,16},{1,9},{9,1},{17,25},{25,17},{2,10},{10... | collective-permute-start | bytes 393224 | tf_op jit(solution)/shard_map/ppermute | solution.py:446
  33.5 0.0 collective-permute-start.13
  33.5 0.2 shard_map.64
  33.6 1.5 %collective-permute-start.8 = (bf16[2,8,512]{2,1,0:T(8,128)(2,1)S(1)}, bf16[2,8,512]{2,1,0:T(8,128)(2,1)S(1)}, u32[]{:S(2)}, u32[]{:S(2)}) collective-permute-start(bf16[2,8,512]{2,1,0:T(8,128)(2,1)S(1)} %shard_map.64), channel_id=1, source_target_pairs={{0,1},{1,0},{2,3},{3,2},{4,5},{5,4},{6,7},{7,6},{8,9},{9,8},{10,11... | collective-permute-start | bytes 49160 | tf_op jit(solution)/shard_map/ppermute | solution.py:446
  35.2 1.0 %shard_map.69.refs_2_ = f32[8,2,2,64,128]{4,3,2,1,0:T(8,128)S(1)} custom-call(bf16[8,2,2,64,128]{4,3,2,1,0:T(8,128)(2,1)S(1)} %shard_map.57.refs_3_.mid_ref.x_ref, bf16[8,2,2,64,128]{4,3,2,1,0:T(8,128)(2,1)S(1)} %get-tuple-element.72.rim_ref, bf16[2,8,2,64,128]{4,3,2,1,0:T(8,128)(2,1)S(1)} %get-tuple-element.83.side_ref, ...), custom_call_target="tpu_custom_call", output_to_operand_aliasing={{}: (5, {})} | custom-call | flops 1000000 | bytes 10000 | tf_op jit(solution)/shard_map/pallas_call | solution.py:29
  36.2 1.2 %collective-permute-done.8.refs_0_ = bf16[2,8,512]{2,1,0:T(8,128)(2,1)S(1)} collective-permute-done((bf16[2,8,512]{2,1,0:T(8,128)(2,1)S(1)}, bf16[2,8,512]{2,1,0:T(8,128)(2,1)S(1)}, u32[]{:S(2)}, u32[]{:S(2)}) %collective-permute-start.8) | collective-permute-done | bytes 16416 | tf_op jit(solution)/shard_map/ppermute | solution.py:446
  37.4 0.3 shard_map.70
  37.7 0.0 collective-permute-done.10.a_ref.neara_ref
  37.7 0.0 collective-permute-done.11.b_ref.nearb_ref
  37.8 0.2 shard_map.71.mid_ref
  38.0 0.0 collective-permute-done.12.fara_ref
  38.0 0.0 collective-permute-done.13.farb_ref
  38.0 1.0 %shard_map.72 = bf16[8,2,4,64,128]{4,3,2,1,0:T(8,128)(2,1)} custom-call(bf16[8,2,2,64,128]{4,3,2,1,0:T(8,128)(2,1)S(1)} %shard_map.71.mid_ref, bf16[8,2,2,64,128]{4,3,2,1,0:T(8,128)(2,1)S(1)} %get-tuple-element.72.rim_ref, f32[8,2,2,64,128]{4,3,2,1,0:T(8,128)S(1)} %get-tuple-element.86.acc_ref, ...), custom_call_target="tpu_custom_call" | custom-call | flops 1000000 | bytes 10000 | tf_op jit(solution)/shard_map/pallas_call | solution.py:29
  (2 shorter events, 0.0 us)
Async XLA Ops:
  0.0 1.7 %copy-start = (bf16[8,2,4,64,128]{4,3,2,1,0:T(8,128)(2,1)S(1)}, bf16[8,2,4,64,128]{4,3,2,1,0:T(8,128)(2,1)}, u32[]{:S(2)}) copy-start(bf16[8,2,4,64,128]{4,3,2,1,0:T(8,128)(2,1)} %x_ref.19) | copy-start | bytes 3145732
  1.2 2.0 %collective-permute-start = (bf16[8,2,64,128]{3,2,1,0:T(8,128)(2,1)S(1)}, bf16[8,2,64,128]{3,2,1,0:T(8,128)(2,1)S(1)}, u32[]{:S(2)}, u32[]{:S(2)}) collective-permute-start(bf16[8,2,64,128]{3,2,1,0:T(8,128)(2,1)S(1)} %get-tuple-element.52), channel_id=1, source_target_pairs={{0,2},{2,0},{4,6},{6,4},{1,3},{3,1},{5,7},{7,5},{8,10},{10,8},{12,... | collective-permute-start | bytes 786440 | tf_op jit(solution)/shard_map/ppermute | solution.py:446
  3.6 15.6 %collective-permute-start.4 = (bf16[8,3,64,128]{3,2,1,0:T(8,128)(2,1)S(1)}, bf16[8,3,64,128]{3,2,1,0:T(8,128)(2,1)S(1)}, u32[]{:S(2)}, u32[]{:S(2)}) collective-permute-start(bf16[8,3,64,128]{3,2,1,0:T(8,128)(2,1)S(1)} %get-tuple-element.54.refs_0_.also_ref), channel_id=1, source_target_pairs={{0,2},{2,0},{4,6},{6,4},{8,16},{10,18},{12,20},{14,22},{16,8},{18,... | collective-permute-start | bytes 1179656 | tf_op jit(solution)/shard_map/ppermute | solution.py:459
  3.8 15.4 %collective-permute-start.3 = (bf16[8,3,64,128]{3,2,1,0:T(8,128)(2,1)S(1)}, bf16[8,3,64,128]{3,2,1,0:T(8,128)(2,1)S(1)}, u32[]{:S(2)}, u32[]{:S(2)}) collective-permute-start(bf16[8,3,64,128]{3,2,1,0:T(8,128)(2,1)S(1)} %get-tuple-element.62.after_ref), channel_id=1, source_target_pairs={{0,8},{8,0},{16,24},{24,16},{1,9},{9,1},{17,25},{25,17},{2,10},{10... | collective-permute-start | bytes 1179656 | tf_op jit(solution)/shard_map/ppermute | solution.py:446
  8.0 6.4 %collective-permute-start.2 = (bf16[8,2,64,128]{3,2,1,0:T(8,128)(2,1)S(1)}, bf16[8,2,64,128]{3,2,1,0:T(8,128)(2,1)S(1)}, u32[]{:S(2)}, u32[]{:S(2)}) collective-permute-start(bf16[8,2,64,128]{3,2,1,0:T(8,128)(2,1)S(1)} %shard_map.53), channel_id=1, source_target_pairs={{0,1},{1,0},{2,4},{3,5},{4,2},{5,3},{6,7},{7,6},{8,9},{9,8},{10,12... | collective-permute-start | bytes 786440 | tf_op jit(solution)/shard_map/ppermute | solution.py:459
  14.7 5.4 %collective-permute-start.6 = (bf16[8,1,64,128]{3,2,1,0:T(8,128)(2,1)S(1)}, bf16[8,1,64,128]{3,2,1,0:T(8,128)(2,1)S(1)}, u32[]{:S(2)}, u32[]{:S(2)}) collective-permute-start(bf16[8,1,64,128]{3,2,1,0:T(8,128)(2,1)S(1)} %get-tuple-element.70), channel_id=1, source_target_pairs={{0,8},{8,0},{16,24},{24,16},{1,9},{9,1},{17,25},{25,17},{2,10},{10... | collective-permute-start | bytes 393224 | tf_op jit(solution)/shard_map/ppermute | solution.py:446
  14.8 5.8 %collective-permute-start.5 = (bf16[8,1,64,128]{3,2,1,0:T(8,128)(2,1)S(1)}, bf16[8,1,64,128]{3,2,1,0:T(8,128)(2,1)S(1)}, u32[]{:S(2)}, u32[]{:S(2)}) collective-permute-start(bf16[8,1,64,128]{3,2,1,0:T(8,128)(2,1)S(1)} %get-tuple-element.67.after_ref), channel_id=1, source_target_pairs={{0,2},{2,0},{4,6},{6,4},{8,16},{10,18},{12,20},{14,22},{16,8},{18,... | collective-permute-start | bytes 393224 | tf_op jit(solution)/shard_map/ppermute | solution.py:459
  15.1 3.7 %collective-permute-start.1 = (bf16[2,8,512]{2,1,0:T(8,128)(2,1)S(1)}, bf16[2,8,512]{2,1,0:T(8,128)(2,1)S(1)}, u32[]{:S(2)}, u32[]{:S(2)}) collective-permute-start(bf16[2,8,512]{2,1,0:T(8,128)(2,1)S(1)} %shard_map.50), channel_id=1, source_target_pairs={{0,1},{1,0},{2,3},{3,2},{4,5},{5,4},{6,7},{7,6},{8,9},{9,8},{10,11... | collective-permute-start | bytes 49160 | tf_op jit(solution)/shard_map/ppermute | solution.py:446
  20.8 1.6 %collective-permute-start.7 = (bf16[8,2,64,128]{3,2,1,0:T(8,128)(2,1)S(1)}, bf16[8,2,64,128]{3,2,1,0:T(8,128)(2,1)S(1)}, u32[]{:S(2)}, u32[]{:S(2)}) collective-permute-start(bf16[8,2,64,128]{3,2,1,0:T(8,128)(2,1)S(1)} %get-tuple-element.73), channel_id=1, source_target_pairs={{0,2},{2,0},{4,6},{6,4},{1,3},{3,1},{5,7},{7,5},{8,10},{10,8},{12,... | collective-permute-start | bytes 786440 | tf_op jit(solution)/shard_map/ppermute | solution.py:446
  22.8 14.9 %collective-permute-start.10 = (bf16[8,3,64,128]{3,2,1,0:T(8,128)(2,1)S(1)}, bf16[8,3,64,128]{3,2,1,0:T(8,128)(2,1)S(1)}, u32[]{:S(2)}, u32[]{:S(2)}) collective-permute-start(bf16[8,3,64,128]{3,2,1,0:T(8,128)(2,1)S(1)} %get-tuple-element.81.after_ref), channel_id=1, source_target_pairs={{0,8},{8,0},{16,24},{24,16},{1,9},{9,1},{17,25},{25,17},{2,10},{10... | collective-permute-start | bytes 1179656 | tf_op jit(solution)/shard_map/ppermute | solution.py:446
  24.6 13.1 %collective-permute-start.11 = (bf16[8,3,64,128]{3,2,1,0:T(8,128)(2,1)S(1)}, bf16[8,3,64,128]{3,2,1,0:T(8,128)(2,1)S(1)}, u32[]{:S(2)}, u32[]{:S(2)}) collective-permute-start(bf16[8,3,64,128]{3,2,1,0:T(8,128)(2,1)S(1)} %get-tuple-element.74.after_ref.also_ref), channel_id=1, source_target_pairs={{0,2},{2,0},{4,6},{6,4},{8,16},{10,18},{12,20},{14,22},{16,8},{18,... | collective-permute-start | bytes 1179656 | tf_op jit(solution)/shard_map/ppermute | solution.py:459
  24.6 6.4 %collective-permute-start.9 = (bf16[8,2,64,128]{3,2,1,0:T(8,128)(2,1)S(1)}, bf16[8,2,64,128]{3,2,1,0:T(8,128)(2,1)S(1)}, u32[]{:S(2)}, u32[]{:S(2)}) collective-permute-start(bf16[8,2,64,128]{3,2,1,0:T(8,128)(2,1)S(1)} %shard_map.67), channel_id=1, source_target_pairs={{0,1},{1,0},{2,4},{3,5},{4,2},{5,3},{6,7},{7,6},{8,9},{9,8},{10,12... | collective-permute-start | bytes 786440 | tf_op jit(solution)/shard_map/ppermute | solution.py:459
  31.4 6.6 %collective-permute-start.12 = (bf16[8,1,64,128]{3,2,1,0:T(8,128)(2,1)S(1)}, bf16[8,1,64,128]{3,2,1,0:T(8,128)(2,1)S(1)}, u32[]{:S(2)}, u32[]{:S(2)}) collective-permute-start(bf16[8,1,64,128]{3,2,1,0:T(8,128)(2,1)S(1)} %get-tuple-element.87), channel_id=1, source_target_pairs={{0,8},{8,0},{16,24},{24,16},{1,9},{9,1},{17,25},{25,17},{2,10},{10... | collective-permute-start | bytes 393224 | tf_op jit(solution)/shard_map/ppermute | solution.py:446
  33.5 4.5 %collective-permute-start.13 = (bf16[8,1,64,128]{3,2,1,0:T(8,128)(2,1)S(1)}, bf16[8,1,64,128]{3,2,1,0:T(8,128)(2,1)S(1)}, u32[]{:S(2)}, u32[]{:S(2)}) collective-permute-start(bf16[8,1,64,128]{3,2,1,0:T(8,128)(2,1)S(1)} %get-tuple-element.88), channel_id=1, source_target_pairs={{0,2},{2,0},{4,6},{6,4},{8,16},{10,18},{12,20},{14,22},{16,8},{18,... | collective-permute-start | bytes 393224 | tf_op jit(solution)/shard_map/ppermute | solution.py:459
  33.6 3.7 %collective-permute-start.8 = (bf16[2,8,512]{2,1,0:T(8,128)(2,1)S(1)}, bf16[2,8,512]{2,1,0:T(8,128)(2,1)S(1)}, u32[]{:S(2)}, u32[]{:S(2)}) collective-permute-start(bf16[2,8,512]{2,1,0:T(8,128)(2,1)S(1)} %shard_map.64), channel_id=1, source_target_pairs={{0,1},{1,0},{2,3},{3,2},{4,5},{5,4},{6,7},{7,6},{8,9},{9,8},{10,11... | collective-permute-start | bytes 49160 | tf_op jit(solution)/shard_map/ppermute | solution.py:446

commit v12 on v11

--- a/solution.py
+++ b/solution.py
@@ -515,7 +515,7 @@
         deep = call(
             on(depth_body, *both),
             [VMEM((rows, channels, cols * width), BF16)] * deep_swaps,
-            (*block, near[1]),
+            (*block, near[0]),
             {base: pl.ANY},
         )
         deeper = [swap_first(deep[0], "trow")]
@@ -532,8 +532,8 @@
         a, b, side = call(
             far_body,
             [owed_side, owed_side, VMEM((2, *line.shape), BF16)],
-            (*beside, operator["beside"], *parts, accs[0]),
-            {5: pl.ANY},
+            (*beside, operator["beside"], *parts, accs[0], *deeper),
+            {5 + n: pl.ANY for n in range(1 + deep_swaps)},
         )
         far_got = swap_first(a, "srow"), swap_second(b, "srow", "scol")
         if layer < layers - 1:

time: 39.2 us -> 38.3 us (0.977)
  waiting for transfers between devices: 7.95 us -> 7.52 us
  starting transfers between devices: 15.2 us -> 14.8 us
    ppermute x6, waiting for transfers between devices: 4.67 us -> 0.02 us  [swap_second(): return lax.ppermute(value, (axis, other), pairs)]
    ppermute x8, waiting for transfers between devices: 3.28 us -> 7.5 us  [swap_first(): lax.ppermute(value, axis, [(n, n ^ 1) for n in range(lax.axis_size(axis))])]
  transfers between devices with their start and end apart: 14 -> 14, of which waited for: 6 -> 5; matrix products, arithmetic and copies ran while one was open for 0% -> 0% of each run, Pallas kernels for 32% -> 32%
where the time goes in v12:
time: 38.3 us; the launch traced here: 38.2 us
  Pallas kernels  15.6 us (41%)
  starting transfers between devices  14.8 us (39%)
  waiting for transfers between devices  7.52 us (20%)
    pallas_call x27, Pallas kernels, call(): pl.pallas_call(body, out_shape=tuple(outs), in_specs=[pl.BlockSpec(memory...  15.6 us
    ppermute x8, starting transfers between devices, swap_first(): lax.ppermute(value, axis, [(n, n ^ 1) for n in range(lax.axis_size(axis))])  11.6 us
    ppermute x8, waiting for transfers between devices, swap_first(): lax.ppermute(value, axis, [(n, n ^ 1) for n in range(lax.axis_size(axis))])  7.5 us
    ppermute x6, starting transfers between devices, swap_second(): return lax.ppermute(value, (axis, other), pairs)  3.24 us
  transfers between devices with their start and end apart: 14, of which 5 were waited for; matrix products, arithmetic and copies ran while one was open for 0% of the time, Pallas kernels for 32%

profile of v12, /device:TPU:0, one launch (start us, length us, event | category | flops | bytes accessed | tf_op | source)
XLA Modules:
  0.0 38.2 jit_solution(15795475773555143638)
XLA Ops:
  0.0 0.0 copy-start
  0.0 1.2 %shard_map.46 = (bf16[2,8,8,9]{3,2,1,0:T(8,128)(2,1)S(1)}, bf16[2,8,8,9]{3,2,1,0:T(8,128)(2,1)S(1)}, f32[2,8]{1,0:T(2,128)S(1)}, bf16[2,256,768]{2,1,0:T(8,128)(...) custom-call(bf16[8,2,4,64,128]{4,3,2,1,0:T(8,128)(2,1)} %x_ref.19, ...), custom_call_target="tpu_custom_call" | custom-call | flops 1000000 | bytes 10000 | tf_op jit(solution)/shard_map/pallas_call | solution.py:29
  1.2 0.5 %collective-permute-start = (bf16[8,2,64,128]{3,2,1,0:T(8,128)(2,1)S(1)}, bf16[8,2,64,128]{3,2,1,0:T(8,128)(2,1)S(1)}, u32[]{:S(2)}, u32[]{:S(2)}) collective-permute-start(bf16[8,2,64,128]{3,2,1,0:T(8,128)(2,1)S(1)} %get-tuple-element.52), channel_id=1, source_target_pairs={{0,2},{2,0},{4,6},{6,4},{1,3},{3,1},{5,7},{7,5},{8,10},{10,8},{12,... | collective-permute-start | bytes 786440 | tf_op jit(solution)/shard_map/ppermute | solution.py:446
  1.7 0.0 copy-done
  1.7 0.6 %shard_map.47 = (bf16[8,3,64,128]{3,2,1,0:T(8,128)(2,1)S(1)}, bf16[8,3,64,128]{3,2,1,0:T(8,128)(2,1)S(1)}) custom-call(bf16[8,2,4,64,128]{4,3,2,1,0:T(8,128)(2,1)S(1)} %copy-done, bf16[2,256,768]{2,1,0:T(8,128)(2,1)S(1)} %get-tuple-element.49.refs_0_.refs_1_.beside_ref.refs_2_), custom_call_target="tpu_custom_call" | custom-call | flops 1000000 | bytes 10000 | tf_op jit(solution)/shard_map/pallas_call | solution.py:29
  2.3 0.3 shard_map.51
  2.6 0.5 %shard_map.48 = (bf16[256,768]{1,0:T(8,128)(2,1)S(1)}, bf16[256,768]{1,0:T(8,128)(2,1)S(1)}, bf16[2,256,384]{2,1,0:T(8,128)(2,1)S(1)}, bf16[2,256,24]{2,1,0:T(8,128)(2,1)S(1)}) custom-call(bf16[2,8,8,9]{3,2,1,0:T(8,128)(2,1)S(1)} %get-tuple-element.47.src_w_ref, bf16[2,8,8,9]{3,2,1,0:T(8,128)(2,1)S(1)} %get-tuple-element.48.tgt_w_ref, ...), custom_call_target="tpu_custom_call" | custom-call | flops 1000000 | bytes 10000 | tf_op jit(solution)/shard_map/pallas_call | solution.py:29
  3.2 0.0 collective-permute-done.refs_0_.cola_ref
  3.2 0.4 %shard_map.49 = (bf16[8,3,64,128]{3,2,1,0:T(8,128)(2,1)S(1)}, bf16[8,3,64,128]{3,2,1,0:T(8,128)(2,1)S(1)}) custom-call(bf16[8,2,4,64,128]{4,3,2,1,0:T(8,128)(2,1)S(1)} %copy-done, bf16[8,2,64,128]{3,2,1,0:T(8,128)(2,1)S(1)} %collective-permute-done.refs_0_.cola_ref, ...), custom_call_target="tpu_custom_call", output_to_operand_aliasing={{0}: (3, {}), {1}: (4, {})} | custom-call | flops 1000000 | bytes 10000 | tf_op jit(solution)/shard_map/pallas_call | solution.py:29
  3.6 0.2 shard_map.50
  3.8 2.7 %collective-permute-start.3 = (bf16[8,3,64,128]{3,2,1,0:T(8,128)(2,1)S(1)}, bf16[8,3,64,128]{3,2,1,0:T(8,128)(2,1)S(1)}, u32[]{:S(2)}, u32[]{:S(2)}) collective-permute-start(bf16[8,3,64,128]{3,2,1,0:T(8,128)(2,1)S(1)} %get-tuple-element.54.refs_0_.after_ref), channel_id=1, source_target_pairs={{0,8},{8,0},{16,24},{24,16},{1,9},{9,1},{17,25},{25,17},{2,10},{10... | collective-permute-start | bytes 1179656 | tf_op jit(solution)/shard_map/ppermute | solution.py:446
  6.5 0.1 collective-permute-start.4
  6.6 1.6 %collective-permute-start.2 = (bf16[8,2,64,128]{3,2,1,0:T(8,128)(2,1)S(1)}, bf16[8,2,64,128]{3,2,1,0:T(8,128)(2,1)S(1)}, u32[]{:S(2)}, u32[]{:S(2)}) collective-permute-start(bf16[8,2,64,128]{3,2,1,0:T(8,128)(2,1)S(1)} %shard_map.53), channel_id=1, source_target_pairs={{0,1},{1,0},{2,4},{3,5},{4,2},{5,3},{6,7},{7,6},{8,9},{9,8},{10,12... | collective-permute-start | bytes 786440 | tf_op jit(solution)/shard_map/ppermute | solution.py:459
  8.2 0.5 %collective-permute-start.1 = (bf16[2,8,512]{2,1,0:T(8,128)(2,1)S(1)}, bf16[2,8,512]{2,1,0:T(8,128)(2,1)S(1)}, u32[]{:S(2)}, u32[]{:S(2)}) collective-permute-start(bf16[2,8,512]{2,1,0:T(8,128)(2,1)S(1)} %shard_map.50), channel_id=1, source_target_pairs={{0,1},{1,0},{2,3},{3,2},{4,5},{5,4},{6,7},{7,6},{8,9},{9,8},{10,11... | collective-permute-start | bytes 49160 | tf_op jit(solution)/shard_map/ppermute | solution.py:446
  8.7 2.5 %shard_map.52 = (f32[8,2,2,64,128]{4,3,2,1,0:T(8,128)S(1)}, f32[8,2,2,64,128]{4,3,2,1,0:T(8,128)S(1)}) custom-call(bf16[8,2,4,64,128]{4,3,2,1,0:T(8,128)(2,1)S(1)} %copy-done, bf16[256,768]{1,0:T(8,128)(2,1)S(1)} %get-tuple-element.55.refs_0_.refs_1_, bf16[2,256,768]{2,1,0:T(8,128)(2,1)S(1)} %get-tuple-element.49.refs_0_.refs_1_.beside_ref.refs_2_, ...), custom_call_target="tpu_custom_call" | custom-call | flops 10000000000 | bytes 10000 | tf_op jit(solution)/shard_map/pallas_call | solution.py:29
  11.2 2.2 %collective-permute-done.1.refs_1_.refs_0_ = bf16[2,8,512]{2,1,0:T(8,128)(2,1)S(1)} collective-permute-done((bf16[2,8,512]{2,1,0:T(8,128)(2,1)S(1)}, bf16[2,8,512]{2,1,0:T(8,128)(2,1)S(1)}, u32[]{:S(2)}, u32[]{:S(2)}) %collective-permute-start.1) | collective-permute-done | bytes 16416 | tf_op jit(solution)/shard_map/ppermute | solution.py:446
  13.4 0.0 collective-permute-done.2.colb_ref
  13.4 0.3 shard_map.54
  13.7 3.2 %collective-permute-start.6 = (bf16[8,1,64,128]{3,2,1,0:T(8,128)(2,1)S(1)}, bf16[8,1,64,128]{3,2,1,0:T(8,128)(2,1)S(1)}, u32[]{:S(2)}, u32[]{:S(2)}) collective-permute-start(bf16[8,1,64,128]{3,2,1,0:T(8,128)(2,1)S(1)} %get-tuple-element.70), channel_id=1, source_target_pairs={{0,8},{8,0},{16,24},{24,16},{1,9},{9,1},{17,25},{25,17},{2,10},{10... | collective-permute-start | bytes 393224 | tf_op jit(solution)/shard_map/ppermute | solution.py:446
  16.8 0.0 collective-permute-start.5
  16.8 0.6 %shard_map.58 = (bf16[256,768]{1,0:T(8,128)(2,1)S(1)}, bf16[2,256,768]{2,1,0:T(8,128)(2,1)S(1)}, bf16[256,768]{1,0:T(8,128)(2,1)S(1)}, bf16[2,256,384]{2,1,0:T(8,128)(2,1)S(1)}, bf16[2,256,24]{2,1,0:T(8,128)(2,1)S(1)}) custom-call(bf16[2,8,8,9]{3,2,1,0:T(8,128)(2,1)S(1)} %get-tuple-element.47.src_w_ref, ...), custom_call_target="tpu_custom_call" | custom-call | flops 1000000 | bytes 10000 | tf_op jit(solution)/shard_map/pallas_call | solution.py:29
  17.5 1.0 %shard_map.55.refs_2_ = f32[8,2,2,64,128]{4,3,2,1,0:T(8,128)S(1)} custom-call(bf16[8,2,4,64,128]{4,3,2,1,0:T(8,128)(2,1)S(1)} %copy-done, bf16[2,8,2,64,128]{4,3,2,1,0:T(8,128)(2,1)S(1)} %get-tuple-element.64.refs_0_, bf16[256,768]{1,0:T(8,128)(2,1)S(1)} %get-tuple-element.55.refs_0_.refs_1_, ...), custom_call_target="tpu_custom_call", output_to_operand_aliasing={{}: (4, {})} | custom-call | flops 1000000 | bytes 10000 | tf_op jit(solution)/shard_map/pallas_call | solution.py:29
  18.5 0.3 shard_map.56
  18.8 0.0 collective-permute-done.3.refs_1_
  18.8 0.0 collective-permute-done.4.refs_2_.refs_1_
  18.8 0.2 shard_map.57.refs_3_.mid_ref.x_ref
  19.1 0.7 %collective-permute-done.6.refs_2_ = bf16[8,1,64,128]{3,2,1,0:T(8,128)(2,1)S(1)} collective-permute-done((bf16[8,1,64,128]{3,2,1,0:T(8,128)(2,1)S(1)}, bf16[8,1,64,128]{3,2,1,0:T(8,128)(2,1)S(1)}, u32[]{:S(2)}, u32[]{:S(2)}) %collective-permute-start.6) | collective-permute-done | bytes 131104 | tf_op jit(solution)/shard_map/ppermute | solution.py:446
  19.8 0.1 shard_map.59.rim_ref.refs_3_
  19.9 0.4 shard_map.60.refs_4_.refs_0_
  20.3 0.0 collective-permute-done.5.refs_2_
  20.3 0.2 shard_map.61
  20.5 0.1 collective-permute-start.7
  20.6 0.4 shard_map.62.refs_1_.after_ref
  21.0 0.3 shard_map.65
  21.3 0.8 %collective-permute-done.7.cola_ref = bf16[8,2,64,128]{3,2,1,0:T(8,128)(2,1)S(1)} collective-permute-done((bf16[8,2,64,128]{3,2,1,0:T(8,128)(2,1)S(1)}, bf16[8,2,64,128]{3,2,1,0:T(8,128)(2,1)S(1)}, u32[]{:S(2)}, u32[]{:S(2)}) %collective-permute-start.7) | collective-permute-done | bytes 262176 | tf_op jit(solution)/shard_map/ppermute | solution.py:446
  22.1 0.4 shard_map.63
  22.5 0.2 shard_map.64
  22.7 2.0 %collective-permute-start.10 = (bf16[8,3,64,128]{3,2,1,0:T(8,128)(2,1)S(1)}, bf16[8,3,64,128]{3,2,1,0:T(8,128)(2,1)S(1)}, u32[]{:S(2)}, u32[]{:S(2)}) collective-permute-start(bf16[8,3,64,128]{3,2,1,0:T(8,128)(2,1)S(1)} %get-tuple-element.74.after_ref), channel_id=1, source_target_pairs={{0,8},{8,0},{16,24},{24,16},{1,9},{9,1},{17,25},{25,17},{2,10},{10... | collective-permute-start | bytes 1179656 | tf_op jit(solution)/shard_map/ppermute | solution.py:446
  24.7 0.0 collective-permute-start.11
  24.7 1.6 %collective-permute-start.9 = (bf16[8,2,64,128]{3,2,1,0:T(8,128)(2,1)S(1)}, bf16[8,2,64,128]{3,2,1,0:T(8,128)(2,1)S(1)}, u32[]{:S(2)}, u32[]{:S(2)}) collective-permute-start(bf16[8,2,64,128]{3,2,1,0:T(8,128)(2,1)S(1)} %shard_map.67), channel_id=1, source_target_pairs={{0,1},{1,0},{2,4},{3,5},{4,2},{5,3},{6,7},{7,6},{8,9},{9,8},{10,12... | collective-permute-start | bytes 786440 | tf_op jit(solution)/shard_map/ppermute | solution.py:459
  26.3 0.5 %collective-permute-start.8 = (bf16[2,8,512]{2,1,0:T(8,128)(2,1)S(1)}, bf16[2,8,512]{2,1,0:T(8,128)(2,1)S(1)}, u32[]{:S(2)}, u32[]{:S(2)}) collective-permute-start(bf16[2,8,512]{2,1,0:T(8,128)(2,1)S(1)} %shard_map.64), channel_id=1, source_target_pairs={{0,1},{1,0},{2,3},{3,2},{4,5},{5,4},{6,7},{7,6},{8,9},{9,8},{10,11... | collective-permute-start | bytes 49160 | tf_op jit(solution)/shard_map/ppermute | solution.py:446
  26.8 2.5 %shard_map.66 = (f32[8,2,2,64,128]{4,3,2,1,0:T(8,128)S(1)}, f32[8,2,2,64,128]{4,3,2,1,0:T(8,128)S(1)}) custom-call(bf16[8,2,2,64,128]{4,3,2,1,0:T(8,128)(2,1)S(1)} %shard_map.57.refs_3_.mid_ref.x_ref, bf16[8,2,2,64,128]{4,3,2,1,0:T(8,128)(2,1)S(1)} %get-tuple-element.72.rim_ref, bf16[256,768]{1,0:T(8,128)(2,1)S(1)} %get-tuple-element.75.middle_ref, ...), custom_call_target="tpu_custom_call" | custom-call | flops 10000000000 | bytes 10000 | tf_op jit(solution)/shard_map/pallas_call | solution.py:29
  29.4 2.2 %collective-permute-done.8.refs_1_.refs_0_ = bf16[2,8,512]{2,1,0:T(8,128)(2,1)S(1)} collective-permute-done((bf16[2,8,512]{2,1,0:T(8,128)(2,1)S(1)}, bf16[2,8,512]{2,1,0:T(8,128)(2,1)S(1)}, u32[]{:S(2)}, u32[]{:S(2)}) %collective-permute-start.8) | collective-permute-done | bytes 16416 | tf_op jit(solution)/shard_map/ppermute | solution.py:446
  31.5 0.0 collective-permute-done.9.colb_ref
  31.5 0.3 shard_map.68
  31.8 2.1 %collective-permute-start.12 = (bf16[8,1,64,128]{3,2,1,0:T(8,128)(2,1)S(1)}, bf16[8,1,64,128]{3,2,1,0:T(8,128)(2,1)S(1)}, u32[]{:S(2)}, u32[]{:S(2)}) collective-permute-start(bf16[8,1,64,128]{3,2,1,0:T(8,128)(2,1)S(1)} %get-tuple-element.87), channel_id=1, source_target_pairs={{0,8},{8,0},{16,24},{24,16},{1,9},{9,1},{17,25},{25,17},{2,10},{10... | collective-permute-start | bytes 393224 | tf_op jit(solution)/shard_map/ppermute | solution.py:446
  33.9 0.0 collective-permute-start.13
  33.9 1.0 %shard_map.69.refs_2_ = f32[8,2,2,64,128]{4,3,2,1,0:T(8,128)S(1)} custom-call(bf16[8,2,2,64,128]{4,3,2,1,0:T(8,128)(2,1)S(1)} %shard_map.57.refs_3_.mid_ref.x_ref, bf16[8,2,2,64,128]{4,3,2,1,0:T(8,128)(2,1)S(1)} %get-tuple-element.72.rim_ref, bf16[2,8,2,64,128]{4,3,2,1,0:T(8,128)(2,1)S(1)} %get-tuple-element.83.side_ref, ...), custom_call_target="tpu_custom_call", output_to_operand_aliasing={{}: (5, {})} | custom-call | flops 1000000 | bytes 10000 | tf_op jit(solution)/shard_map/pallas_call | solution.py:29
  34.9 0.3 shard_map.70
  35.3 0.0 collective-permute-done.10.a_ref.neara_ref
  35.3 0.0 collective-permute-done.11.b_ref.nearb_ref
  35.3 0.2 shard_map.71.mid_ref
  35.5 1.6 %collective-permute-done.12.fara_ref = bf16[8,1,64,128]{3,2,1,0:T(8,128)(2,1)S(1)} collective-permute-done((bf16[8,1,64,128]{3,2,1,0:T(8,128)(2,1)S(1)}, bf16[8,1,64,128]{3,2,1,0:T(8,128)(2,1)S(1)}, u32[]{:S(2)}, u32[]{:S(2)}) %collective-permute-start.12) | collective-permute-done | bytes 131104 | tf_op jit(solution)/shard_map/ppermute | solution.py:446
  37.2 0.0 collective-permute-done.13.farb_ref
  37.2 1.0 %shard_map.72 = bf16[8,2,4,64,128]{4,3,2,1,0:T(8,128)(2,1)} custom-call(bf16[8,2,2,64,128]{4,3,2,1,0:T(8,128)(2,1)S(1)} %shard_map.71.mid_ref, bf16[8,2,2,64,128]{4,3,2,1,0:T(8,128)(2,1)S(1)} %get-tuple-element.72.rim_ref, f32[8,2,2,64,128]{4,3,2,1,0:T(8,128)S(1)} %get-tuple-element.86.acc_ref, ...), custom_call_target="tpu_custom_call" | custom-call | flops 1000000 | bytes 10000 | tf_op jit(solution)/shard_map/pallas_call | solution.py:29
  (2 shorter events, 0.0 us)
Async XLA Ops:
  0.0 1.7 %copy-start = (bf16[8,2,4,64,128]{4,3,2,1,0:T(8,128)(2,1)S(1)}, bf16[8,2,4,64,128]{4,3,2,1,0:T(8,128)(2,1)}, u32[]{:S(2)}) copy-start(bf16[8,2,4,64,128]{4,3,2,1,0:T(8,128)(2,1)} %x_ref.19) | copy-start | bytes 3145732
  1.2 2.0 %collective-permute-start = (bf16[8,2,64,128]{3,2,1,0:T(8,128)(2,1)S(1)}, bf16[8,2,64,128]{3,2,1,0:T(8,128)(2,1)S(1)}, u32[]{:S(2)}, u32[]{:S(2)}) collective-permute-start(bf16[8,2,64,128]{3,2,1,0:T(8,128)(2,1)S(1)} %get-tuple-element.52), channel_id=1, source_target_pairs={{0,2},{2,0},{4,6},{6,4},{1,3},{3,1},{5,7},{7,5},{8,10},{10,8},{12,... | collective-permute-start | bytes 786440 | tf_op jit(solution)/shard_map/ppermute | solution.py:446
  3.8 15.1 %collective-permute-start.3 = (bf16[8,3,64,128]{3,2,1,0:T(8,128)(2,1)S(1)}, bf16[8,3,64,128]{3,2,1,0:T(8,128)(2,1)S(1)}, u32[]{:S(2)}, u32[]{:S(2)}) collective-permute-start(bf16[8,3,64,128]{3,2,1,0:T(8,128)(2,1)S(1)} %get-tuple-element.54.refs_0_.after_ref), channel_id=1, source_target_pairs={{0,8},{8,0},{16,24},{24,16},{1,9},{9,1},{17,25},{25,17},{2,10},{10... | collective-permute-start | bytes 1179656 | tf_op jit(solution)/shard_map/ppermute | solution.py:446
  6.5 12.3 %collective-permute-start.4 = (bf16[8,3,64,128]{3,2,1,0:T(8,128)(2,1)S(1)}, bf16[8,3,64,128]{3,2,1,0:T(8,128)(2,1)S(1)}, u32[]{:S(2)}, u32[]{:S(2)}) collective-permute-start(bf16[8,3,64,128]{3,2,1,0:T(8,128)(2,1)S(1)} %get-tuple-element.62.also_ref), channel_id=1, source_target_pairs={{0,2},{2,0},{4,6},{6,4},{8,16},{10,18},{12,20},{14,22},{16,8},{18,... | collective-permute-start | bytes 1179656 | tf_op jit(solution)/shard_map/ppermute | solution.py:459
  6.6 6.8 %collective-permute-start.2 = (bf16[8,2,64,128]{3,2,1,0:T(8,128)(2,1)S(1)}, bf16[8,2,64,128]{3,2,1,0:T(8,128)(2,1)S(1)}, u32[]{:S(2)}, u32[]{:S(2)}) collective-permute-start(bf16[8,2,64,128]{3,2,1,0:T(8,128)(2,1)S(1)} %shard_map.53), channel_id=1, source_target_pairs={{0,1},{1,0},{2,4},{3,5},{4,2},{5,3},{6,7},{7,6},{8,9},{9,8},{10,12... | collective-permute-start | bytes 786440 | tf_op jit(solution)/shard_map/ppermute | solution.py:459
  8.2 5.2 %collective-permute-start.1 = (bf16[2,8,512]{2,1,0:T(8,128)(2,1)S(1)}, bf16[2,8,512]{2,1,0:T(8,128)(2,1)S(1)}, u32[]{:S(2)}, u32[]{:S(2)}) collective-permute-start(bf16[2,8,512]{2,1,0:T(8,128)(2,1)S(1)} %shard_map.50), channel_id=1, source_target_pairs={{0,1},{1,0},{2,3},{3,2},{4,5},{5,4},{6,7},{7,6},{8,9},{9,8},{10,11... | collective-permute-start | bytes 49160 | tf_op jit(solution)/shard_map/ppermute | solution.py:446
  13.7 6.1 %collective-permute-start.6 = (bf16[8,1,64,128]{3,2,1,0:T(8,128)(2,1)S(1)}, bf16[8,1,64,128]{3,2,1,0:T(8,128)(2,1)S(1)}, u32[]{:S(2)}, u32[]{:S(2)}) collective-permute-start(bf16[8,1,64,128]{3,2,1,0:T(8,128)(2,1)S(1)} %get-tuple-element.70), channel_id=1, source_target_pairs={{0,8},{8,0},{16,24},{24,16},{1,9},{9,1},{17,25},{25,17},{2,10},{10... | collective-permute-start | bytes 393224 | tf_op jit(solution)/shard_map/ppermute | solution.py:446
  16.8 3.5 %collective-permute-start.5 = (bf16[8,1,64,128]{3,2,1,0:T(8,128)(2,1)S(1)}, bf16[8,1,64,128]{3,2,1,0:T(8,128)(2,1)S(1)}, u32[]{:S(2)}, u32[]{:S(2)}) collective-permute-start(bf16[8,1,64,128]{3,2,1,0:T(8,128)(2,1)S(1)} %get-tuple-element.67.after_ref), channel_id=1, source_target_pairs={{0,2},{2,0},{4,6},{6,4},{8,16},{10,18},{12,20},{14,22},{16,8},{18,... | collective-permute-start | bytes 393224 | tf_op jit(solution)/shard_map/ppermute | solution.py:459
  20.5 1.6 %collective-permute-start.7 = (bf16[8,2,64,128]{3,2,1,0:T(8,128)(2,1)S(1)}, bf16[8,2,64,128]{3,2,1,0:T(8,128)(2,1)S(1)}, u32[]{:S(2)}, u32[]{:S(2)}) collective-permute-start(bf16[8,2,64,128]{3,2,1,0:T(8,128)(2,1)S(1)} %get-tuple-element.73), channel_id=1, source_target_pairs={{0,2},{2,0},{4,6},{6,4},{1,3},{3,1},{5,7},{7,5},{8,10},{10,8},{12,... | collective-permute-start | bytes 786440 | tf_op jit(solution)/shard_map/ppermute | solution.py:446
  22.7 12.6 %collective-permute-start.10 = (bf16[8,3,64,128]{3,2,1,0:T(8,128)(2,1)S(1)}, bf16[8,3,64,128]{3,2,1,0:T(8,128)(2,1)S(1)}, u32[]{:S(2)}, u32[]{:S(2)}) collective-permute-start(bf16[8,3,64,128]{3,2,1,0:T(8,128)(2,1)S(1)} %get-tuple-element.74.after_ref), channel_id=1, source_target_pairs={{0,8},{8,0},{16,24},{24,16},{1,9},{9,1},{17,25},{25,17},{2,10},{10... | collective-permute-start | bytes 1179656 | tf_op jit(solution)/shard_map/ppermute | solution.py:446
  24.7 10.6 %collective-permute-start.11 = (bf16[8,3,64,128]{3,2,1,0:T(8,128)(2,1)S(1)}, bf16[8,3,64,128]{3,2,1,0:T(8,128)(2,1)S(1)}, u32[]{:S(2)}, u32[]{:S(2)}) collective-permute-start(bf16[8,3,64,128]{3,2,1,0:T(8,128)(2,1)S(1)} %get-tuple-element.81.also_ref), channel_id=1, source_target_pairs={{0,2},{2,0},{4,6},{6,4},{8,16},{10,18},{12,20},{14,22},{16,8},{18,... | collective-permute-start | bytes 1179656 | tf_op jit(solution)/shard_map/ppermute | solution.py:459
  24.7 6.8 %collective-permute-start.9 = (bf16[8,2,64,128]{3,2,1,0:T(8,128)(2,1)S(1)}, bf16[8,2,64,128]{3,2,1,0:T(8,128)(2,1)S(1)}, u32[]{:S(2)}, u32[]{:S(2)}) collective-permute-start(bf16[8,2,64,128]{3,2,1,0:T(8,128)(2,1)S(1)} %shard_map.67), channel_id=1, source_target_pairs={{0,1},{1,0},{2,4},{3,5},{4,2},{5,3},{6,7},{7,6},{8,9},{9,8},{10,12... | collective-permute-start | bytes 786440 | tf_op jit(solution)/shard_map/ppermute | solution.py:459
  26.3 5.2 %collective-permute-start.8 = (bf16[2,8,512]{2,1,0:T(8,128)(2,1)S(1)}, bf16[2,8,512]{2,1,0:T(8,128)(2,1)S(1)}, u32[]{:S(2)}, u32[]{:S(2)}) collective-permute-start(bf16[2,8,512]{2,1,0:T(8,128)(2,1)S(1)} %shard_map.64), channel_id=1, source_target_pairs={{0,1},{1,0},{2,3},{3,2},{4,5},{5,4},{6,7},{7,6},{8,9},{9,8},{10,11... | collective-permute-start | bytes 49160 | tf_op jit(solution)/shard_map/ppermute | solution.py:446
  31.8 5.3 %collective-permute-start.12 = (bf16[8,1,64,128]{3,2,1,0:T(8,128)(2,1)S(1)}, bf16[8,1,64,128]{3,2,1,0:T(8,128)(2,1)S(1)}, u32[]{:S(2)}, u32[]{:S(2)}) collective-permute-start(bf16[8,1,64,128]{3,2,1,0:T(8,128)(2,1)S(1)} %get-tuple-element.87), channel_id=1, source_target_pairs={{0,8},{8,0},{16,24},{24,16},{1,9},{9,1},{17,25},{25,17},{2,10},{10... | collective-permute-start | bytes 393224 | tf_op jit(solution)/shard_map/ppermute | solution.py:446
  33.9 3.3 %collective-permute-start.13 = (bf16[8,1,64,128]{3,2,1,0:T(8,128)(2,1)S(1)}, bf16[8,1,64,128]{3,2,1,0:T(8,128)(2,1)S(1)}, u32[]{:S(2)}, u32[]{:S(2)}) collective-permute-start(bf16[8,1,64,128]{3,2,1,0:T(8,128)(2,1)S(1)} %get-tuple-element.88), channel_id=1, source_target_pairs={{0,2},{2,0},{4,6},{6,4},{8,16},{10,18},{12,20},{14,22},{16,8},{18,... | collective-permute-start | bytes 393224 | tf_op jit(solution)/shard_map/ppermute | solution.py:459

commit v13 on v8

--- a/solution.py
+++ b/solution.py
@@ -357,22 +357,16 @@
     sent_columns(out_ref, (cola_ref, colb_ref))
 
 
-def last_body(mid_ref, rim_ref, acc_ref, a_ref, b_ref, out_ref, hold_ref, sems):
-    rows, mids = mid_ref.shape[1:3]
+def write_body(first, step, x_ref, acc_ref, a_ref, b_ref, *refs):
+    out_ref, hold_ref, sems = refs[-3:]
     copies = []
-    for i in range(rows):
-        for j in range(mids):
-            copy = pltpu.make_async_copy(mid_ref.at[:, i, j], out_ref.at[:, i, j + 1], sems.at[len(copies)])
-            copy.start()
-            copies.append(copy)
 
     def store(i, j, value):
         hold_ref[:, i, j] = value
-        copy = pltpu.make_async_copy(hold_ref.at[:, i, j], out_ref.at[:, i, j * (mids + 1)], sems.at[len(copies)])
-        copy.start()
-        copies.append(copy)
-
-    finished(rim_ref, acc_ref, (a_ref, b_ref), store)
+        copies.append(pltpu.make_async_copy(hold_ref.at[:, i, j], out_ref.at[:, i, first + step * j], sems.at[len(copies)]))
+        copies[-1].start()
+
+    finished(x_ref, acc_ref, (a_ref, b_ref), store)
     for copy in copies:
         copy.wait()
 
@@ -489,8 +483,8 @@
             (*block, side, *(operator[kind] for kind in ("middle", "beside", "deep")), *accs, *deeper),
             aliases={base + 4: 0, base + 5: 1},
         )
-        (mid,) = call(on(mid_body, middle), [VMEM(mid_shape, BF16)], (mid, acc_mid, *inner))
         if layer < layers - 1:
+            (mid,) = call(on(mid_body, middle), [VMEM(mid_shape, BF16)], (mid, acc_mid, *inner))
             whole_rim = [VMEM(rim_shape, BF16)]
             (begun,) = call(on(begin_body, sides), whole_rim, (rim, acc_rim, outer[0], mid), {3: pl.ANY})
             (sum_a,) = call(functools.partial(inner_body, (0,)), owed_inner, (mid, begun, made["beside", layer + 1]))
@@ -504,14 +498,21 @@
             )
             block = (mid, rim)
         else:
-            (state,) = call(
-                last_body,
-                [jax.ShapeDtypeStruct(volume.shape, BF16)],
-                (mid, rim, acc_rim, *outer),
-                out_place=HBM,
-                scratch=[VMEM(rim_shape, BF16), pltpu.SemaphoreType.DMA((rows * cols,))],
-            )
-    return state
+            result, state = [jax.ShapeDtypeStruct(volume.shape, BF16)], ()
+            for first, step, shape, operands in (
+                (1, 1, mid_shape, (mid, acc_mid, *inner)),
+                (0, cols - 1, rim_shape, (rim, acc_rim, *outer)),
+            ):
+                state = call(
+                    functools.partial(write_body, first, step),
+                    result,
+                    (*operands, *state),
+                    {4: HBM},
+                    out_place=HBM,
+                    scratch=[VMEM(shape, BF16), pltpu.SemaphoreType.DMA((shape[1] * shape[2],))],
+                    aliases={4: 0} if state else None,
+                )
+    return state[0]
 
 
 def solution(mesh):

time: 36.6 us -> 36.5 us (level)
  waiting for transfers between devices: 5.72 us -> 5.05 us
  Pallas kernels: 14.7 us -> 15.3 us
    ppermute x8, waiting for transfers between devices: 3.28 us -> 2.61 us  [swap_first(): lax.ppermute(value, axis, [(n, n ^ 1) for n in range(lax.axis_size(axis))])]
    pallas_call x20, Pallas kernels: 14.7 us -> 15.3 us  [call(): pl.pallas_call(body, out_shape=tuple(outs), in_specs=[pl.BlockSpec(memory...]
  transfers between devices with their start and end apart: 14 -> 14, of which waited for: 5 -> 5; matrix products, arithmetic and copies ran while one was open for 0% -> 0% of each run, Pallas kernels for 34% -> 36%
where the time goes in v13:
time: 36.5 us; the launch traced here: 36.4 us
  starting transfers between devices  15.9 us (44%)
  Pallas kernels  15.3 us (42%)
  waiting for transfers between devices  5.05 us (14%)
    pallas_call x20, Pallas kernels, call(): pl.pallas_call(body, out_shape=tuple(outs), in_specs=[pl.BlockSpec(memory...  15.3 us
    ppermute x8, starting transfers between devices, swap_first(): lax.ppermute(value, axis, [(n, n ^ 1) for n in range(lax.axis_size(axis))])  12.2 us
    ppermute x6, starting transfers between devices, swap_second(): return lax.ppermute(value, (axis, other), pairs)  3.71 us
    ppermute x8, waiting for transfers between devices, swap_first(): lax.ppermute(value, axis, [(n, n ^ 1) for n in range(lax.axis_size(axis))])  2.61 us
    ppermute x6, waiting for transfers between devices, swap_second(): return lax.ppermute(value, (axis, other), pairs)  2.44 us
  transfers between devices with their start and end apart: 14, of which 5 were waited for; matrix products, arithmetic and copies ran while one was open for 0% of the time, Pallas kernels for 36%

profile of v13, /device:TPU:0, one launch (start us, length us, event | category | flops | bytes accessed | tf_op | source)
XLA Modules:
  0.0 36.4 jit_solution(209206866675085944)
XLA Ops:
  0.0 0.0 copy-start
  0.0 1.2 %shard_map.46 = (bf16[2,8,8,9]{3,2,1,0:T(8,128)(2,1)S(1)}, bf16[2,8,8,9]{3,2,1,0:T(8,128)(2,1)S(1)}, f32[2,8]{1,0:T(2,128)S(1)}, bf16[2,256,768]{2,1,0:T(8,128)(...) custom-call(bf16[8,2,4,64,128]{4,3,2,1,0:T(8,128)(2,1)} %x_ref.17, ...), custom_call_target="tpu_custom_call" | custom-call | flops 1000000 | bytes 10000 | tf_op jit(solution)/shard_map/pallas_call | solution.py:29
  1.2 0.5 %collective-permute-start = (bf16[8,2,64,128]{3,2,1,0:T(8,128)(2,1)S(1)}, bf16[8,2,64,128]{3,2,1,0:T(8,128)(2,1)S(1)}, u32[]{:S(2)}, u32[]{:S(2)}) collective-permute-start(bf16[8,2,64,128]{3,2,1,0:T(8,128)(2,1)S(1)} %get-tuple-element.43), channel_id=1, source_target_pairs={{0,2},{2,0},{4,6},{6,4},{1,3},{3,1},{5,7},{7,5},{8,10},{10,8},{12,... | collective-permute-start | bytes 786440 | tf_op jit(solution)/shard_map/ppermute | solution.py:395
  1.7 2.6 %collective-permute-start.1 = (bf16[8,2,64,128]{3,2,1,0:T(8,128)(2,1)S(1)}, bf16[8,2,64,128]{3,2,1,0:T(8,128)(2,1)S(1)}, u32[]{:S(2)}, u32[]{:S(2)}) collective-permute-start(bf16[8,2,64,128]{3,2,1,0:T(8,128)(2,1)S(1)} %get-tuple-element.44), channel_id=1, source_target_pairs={{0,1},{1,0},{2,4},{3,5},{4,2},{5,3},{6,7},{7,6},{8,9},{9,8},{10,12... | collective-permute-start | bytes 786440 | tf_op jit(solution)/shard_map/ppermute | solution.py:408
  4.3 0.0 copy-done
  4.3 0.6 %shard_map.47 = (bf16[8,2,64,128]{3,2,1,0:T(8,128)(2,1)S(1)}, bf16[8,2,64,128]{3,2,1,0:T(8,128)(2,1)S(1)}) custom-call(bf16[8,2,4,64,128]{4,3,2,1,0:T(8,128)(2,1)S(1)} %copy-done, bf16[2,256,768]{2,1,0:T(8,128)(2,1)S(1)} %get-tuple-element.45.refs_0_.beside_ref.refs_1_.refs_2_), custom_call_target="tpu_custom_call" | custom-call | flops 1000000 | bytes 10000 | tf_op jit(solution)/shard_map/pallas_call | solution.py:29
  4.9 1.6 %collective-permute-start.5 = (bf16[8,2,64,128]{3,2,1,0:T(8,128)(2,1)S(1)}, bf16[8,2,64,128]{3,2,1,0:T(8,128)(2,1)S(1)}, u32[]{:S(2)}, u32[]{:S(2)}) collective-permute-start(bf16[8,2,64,128]{3,2,1,0:T(8,128)(2,1)S(1)} %get-tuple-element.63), channel_id=1, source_target_pairs={{0,8},{8,0},{16,24},{24,16},{1,9},{9,1},{17,25},{25,17},{2,10},{10... | collective-permute-start | bytes 786440 | tf_op jit(solution)/shard_map/ppermute | solution.py:395
  6.5 0.0 collective-permute-start.6
  6.5 0.4 %shard_map.48 = (f32[2,256,256]{2,1,0:T(8,128)S(1)}, f32[2,256,256]{2,1,0:T(8,128)S(1)}) custom-call(bf16[8,2,4,64,128]{4,3,2,1,0:T(8,128)(2,1)S(1)} %copy-done, bf16[2,256,768]{2,1,0:T(8,128)(2,1)S(1)} %get-tuple-element.45.refs_0_.beside_ref.refs_1_.refs_2_, bf16[8,2,64,128]{3,2,1,0:T(8,128)(2,1)S(1)} %get-tuple-element.46.refs_1_.after_ref), custom_call_target="tpu_custom_call" | custom-call | flops 1000000 | bytes 10000 | tf_op jit(solution)/shard_map/pallas_call | solution.py:29
  7.0 1.1 %shard_map.49 = (bf16[256,768]{1,0:T(8,128)(2,1)S(1)}, bf16[256,768]{1,0:T(8,128)(2,1)S(1)}, bf16[2,256,384]{2,1,0:T(8,128)(2,1)S(1)}, bf16[2,256,24]{2,1,0:T(8,...) custom-call(bf16[2,8,8,9]{3,2,1,0:T(8,128)(2,1)S(1)} %get-tuple-elem, ...), custom_call_target="tpu_custom_call" | custom-call | flops 1000000 | bytes 10000 | tf_op jit(solution)/shard_map/pallas_call | solution.py:29
  8.1 0.0 collective-permute-done.cola_ref
  8.1 0.6 %collective-permute-done.1.colb_ref = bf16[8,2,64,128]{3,2,1,0:T(8,128)(2,1)S(1)} collective-permute-done((bf16[8,2,64,128]{3,2,1,0:T(8,128)(2,1)S(1)}, bf16[8,2,64,128]{3,2,1,0:T(8,128)(2,1)S(1)}, u32[]{:S(2)}, u32[]{:S(2)}) %collective-permute-start.1) | collective-permute-done | bytes 262176 | tf_op jit(solution)/shard_map/ppermute | solution.py:408
  8.7 0.4 %shard_map.50 = (bf16[8,2,64,128]{3,2,1,0:T(8,128)(2,1)S(1)}, bf16[8,2,64,128]{3,2,1,0:T(8,128)(2,1)S(1)}, bf16[2,8,2,64,128]{4,3,2,1,0:T(8,128)(2,1)S(1)}) custom-call(bf16[8,2,64,128]{3,2,1,0:T(8,128)(2,1)S(1)} %collective-permute-done.cola_ref, bf16[8,2,64,128]{3,2,1,0:T(8,128)(2,1)S(1)} %collective-permute-done.1.colb_ref, ...), custom_call_target="tpu_custom_call" | custom-call | flops 1000000 | bytes 10000 | tf_op jit(solution)/shard_map/pallas_call | solution.py:29
  9.0 2.7 %collective-permute-start.4 = (bf16[8,2,64,128]{3,2,1,0:T(8,128)(2,1)S(1)}, bf16[8,2,64,128]{3,2,1,0:T(8,128)(2,1)S(1)}, u32[]{:S(2)}, u32[]{:S(2)}) collective-permute-start(bf16[8,2,64,128]{3,2,1,0:T(8,128)(2,1)S(1)} %get-tuple-element.61), channel_id=1, source_target_pairs={{0,8},{8,0},{16,24},{24,16},{1,9},{9,1},{17,25},{25,17},{2,10},{10... | collective-permute-start | bytes 786440 | tf_op jit(solution)/shard_map/ppermute | solution.py:395
  11.7 0.0 collective-permute-start.3
  11.7 0.2 shard_map.52
  11.9 1.0 %collective-permute-start.2 = (bf16[2,8,512]{2,1,0:T(8,128)(2,1)S(1)}, bf16[2,8,512]{2,1,0:T(8,128)(2,1)S(1)}, u32[]{:S(2)}, u32[]{:S(2)}) collective-permute-start(bf16[2,8,512]{2,1,0:T(8,128)(2,1)S(1)} %shard_map.52), channel_id=1, source_target_pairs={{0,1},{1,0},{2,3},{3,2},{4,5},{5,4},{6,7},{7,6},{8,9},{9,8},{10,11... | collective-permute-start | bytes 49160 | tf_op jit(solution)/shard_map/ppermute | solution.py:395
  12.9 2.5 %shard_map.51 = (f32[8,2,2,64,128]{4,3,2,1,0:T(8,128)S(1)}, f32[8,2,2,64,128]{4,3,2,1,0:T(8,128)S(1)}) custom-call(bf16[8,2,4,64,128]{4,3,2,1,0:T(8,128)(2,1)S(1)} %copy-done, bf16[256,768]{1,0:T(8,128)(2,1)S(1)} %get-tuple-element.51.after_ref.refs_0_.refs_1_, bf16[2,256,768]{2,1,0:T(8,128)(2,1)S(1)} %get-tuple-element.45.refs_0_.beside_ref.refs_1_.refs_2_, ...), custom_call_target="tpu_custom_call" | custom-call | flops 1000000 | bytes 10000 | tf_op jit(solution)/shard_map/pallas_call | solution.py:29
  15.4 0.2 collective-permute-done.2.refs_6_
  15.7 1.1 %shard_map.53 = (f32[8,2,2,64,128]{4,3,2,1,0:T(8,128)S(1)}, f32[8,2,2,64,128]{4,3,2,1,0:T(8,128)S(1)}) custom-call(bf16[8,2,4,64,128]{4,3,2,1,0:T(8,128)(2,1)S(1)} %copy-done, bf16[2,8,2,64,128]{4,3,2,1,0:T(8,128)(2,1)S(1)} %get-tuple-element.52.refs_0_, ...), custom_call_target="tpu_custom_call", output_to_operand_aliasing={{0}: (5, {}), {1}: (6, {})} | custom-call | flops 1000000 | bytes 10000 | tf_op jit(solution)/shard_map/pallas_call | solution.py:29
  16.8 0.0 collective-permute-done.5.refs_1_
  16.8 0.0 collective-permute-done.6.refs_2_
  16.8 0.2 shard_map.54.refs_2_.mid_ref.x_ref
  17.0 1.8 %collective-permute-done.4.refs_1_ = bf16[8,2,64,128]{3,2,1,0:T(8,128)(2,1)S(1)} collective-permute-done((bf16[8,2,64,128]{3,2,1,0:T(8,128)(2,1)S(1)}, bf16[8,2,64,128]{3,2,1,0:T(8,128)(2,1)S(1)}, u32[]{:S(2)}, u32[]{:S(2)}) %collective-permute-start.4) | collective-permute-done | bytes 262176 | tf_op jit(solution)/shard_map/ppermute | solution.py:395
  18.9 0.1 shard_map.55.rim_ref.refs_2_
  19.0 0.4 %shard_map.56.refs_3_ = bf16[8,2,64,128]{3,2,1,0:T(8,128)(2,1)S(1)} custom-call(bf16[8,2,2,64,128]{4,3,2,1,0:T(8,128)(2,1)S(1)} %shard_map.54.refs_2_.mid_ref.x_ref, bf16[8,2,2,64,128]{4,3,2,1,0:T(8,128)(2,1)S(1)} %shard_map.55.rim_ref.refs_2_, bf16[2,256,768]{2,1,0:T(8,128)(2,1)S(1)} %get-tuple-element.64.beside_ref), custom_call_target="tpu_custom_call" | custom-call | flops 1000000 | bytes 10000 | tf_op jit(solution)/shard_map/pallas_call | solution.py:29
  19.4 0.0 collective-permute-done.3.refs_1_
  19.4 0.2 shard_map.57
  19.6 0.1 collective-permute-start.7
  19.7 1.0 %collective-permute-start.8 = (bf16[8,2,64,128]{3,2,1,0:T(8,128)(2,1)S(1)}, bf16[8,2,64,128]{3,2,1,0:T(8,128)(2,1)S(1)}, u32[]{:S(2)}, u32[]{:S(2)}) collective-permute-start(bf16[8,2,64,128]{3,2,1,0:T(8,128)(2,1)S(1)} %get-tuple-element.67), channel_id=1, source_target_pairs={{0,1},{1,0},{2,4},{3,5},{4,2},{5,3},{6,7},{7,6},{8,9},{9,8},{10,12... | collective-permute-start | bytes 786440 | tf_op jit(solution)/shard_map/ppermute | solution.py:408
  20.7 2.6 %collective-permute-start.12 = (bf16[8,2,64,128]{3,2,1,0:T(8,128)(2,1)S(1)}, bf16[8,2,64,128]{3,2,1,0:T(8,128)(2,1)S(1)}, u32[]{:S(2)}, u32[]{:S(2)}) collective-permute-start(bf16[8,2,64,128]{3,2,1,0:T(8,128)(2,1)S(1)} %shard_map.56.refs_3_), channel_id=1, source_target_pairs={{0,8},{8,0},{16,24},{24,16},{1,9},{9,1},{17,25},{25,17},{2,10},{10... | collective-permute-start | bytes 786440 | tf_op jit(solution)/shard_map/ppermute | solution.py:395
  23.3 0.4 %shard_map.58.after_ref = bf16[8,2,64,128]{3,2,1,0:T(8,128)(2,1)S(1)} custom-call(bf16[8,2,2,64,128]{4,3,2,1,0:T(8,128)(2,1)S(1)} %shard_map.54.refs_2_.mid_ref.x_ref, bf16[8,2,2,64,128]{4,3,2,1,0:T(8,128)(2,1)S(1)} %get-tuple-element.65.rim_ref.x_ref, bf16[2,256,768]{2,1,0:T(8,128)(2,1)S(1)} %get-tuple-element.64.beside_ref), custom_call_target="tpu_custom_call" | custom-call | flops 1000000 | bytes 10000 | tf_op jit(solution)/shard_map/pallas_call | solution.py:29
  23.7 0.1 collective-permute-start.13
  23.8 0.4 %shard_map.59 = (f32[2,256,256]{2,1,0:T(8,128)S(1)}, f32[2,256,256]{2,1,0:T(8,128)S(1)}) custom-call(bf16[8,2,2,64,128]{4,3,2,1,0:T(8,128)(2,1)S(1)} %shard_map.54.refs_2_.mid_ref.x_ref, bf16[8,2,2,64,128]{4,3,2,1,0:T(8,128)(2,1)S(1)} %get-tuple-element.65.rim_ref.x_ref, bf16[2,256,768]{2,1,0:T(8,128)(2,1)S(1)} %get-tuple-element.64.beside_ref, ...), custom_call_target="tpu_custom_call" | custom-call | flops 1000000 | bytes 10000 | tf_op jit(solution)/shard_map/pallas_call | solution.py:29
  24.2 0.0 collective-permute-done.7.cola_ref
  24.2 1.9 %collective-permute-done.8.colb_ref = bf16[8,2,64,128]{3,2,1,0:T(8,128)(2,1)S(1)} collective-permute-done((bf16[8,2,64,128]{3,2,1,0:T(8,128)(2,1)S(1)}, bf16[8,2,64,128]{3,2,1,0:T(8,128)(2,1)S(1)}, u32[]{:S(2)}, u32[]{:S(2)}) %collective-permute-start.8) | collective-permute-done | bytes 262176 | tf_op jit(solution)/shard_map/ppermute | solution.py:408
  26.1 0.4 %shard_map.60 = (bf16[8,2,64,128]{3,2,1,0:T(8,128)(2,1)S(1)}, bf16[8,2,64,128]{3,2,1,0:T(8,128)(2,1)S(1)}, bf16[2,8,2,64,128]{4,3,2,1,0:T(8,128)(2,1)S(1)}) custom-call(bf16[8,2,64,128]{3,2,1,0:T(8,128)(2,1)S(1)} %collective-permute-done.7.cola_ref, bf16[8,2,64,128]{3,2,1,0:T(8,128)(2,1)S(1)} %collective-permute-done.8.colb_ref, ...), custom_call_target="tpu_custom_call" | custom-call | flops 1000000 | bytes 10000 | tf_op jit(solution)/shard_map/pallas_call | solution.py:29
  26.5 2.3 %collective-permute-start.10 = (bf16[8,2,64,128]{3,2,1,0:T(8,128)(2,1)S(1)}, bf16[8,2,64,128]{3,2,1,0:T(8,128)(2,1)S(1)}, u32[]{:S(2)}, u32[]{:S(2)}) collective-permute-start(bf16[8,2,64,128]{3,2,1,0:T(8,128)(2,1)S(1)} %get-tuple-element.79), channel_id=1, source_target_pairs={{0,8},{8,0},{16,24},{24,16},{1,9},{9,1},{17,25},{25,17},{2,10},{10... | collective-permute-start | bytes 786440 | tf_op jit(solution)/shard_map/ppermute | solution.py:395
  28.7 0.0 collective-permute-start.11
  28.7 0.2 shard_map.62
  28.9 1.4 %collective-permute-start.9 = (bf16[2,8,512]{2,1,0:T(8,128)(2,1)S(1)}, bf16[2,8,512]{2,1,0:T(8,128)(2,1)S(1)}, u32[]{:S(2)}, u32[]{:S(2)}) collective-permute-start(bf16[2,8,512]{2,1,0:T(8,128)(2,1)S(1)} %shard_map.62), channel_id=1, source_target_pairs={{0,1},{1,0},{2,3},{3,2},{4,5},{5,4},{6,7},{7,6},{8,9},{9,8},{10,11... | collective-permute-start | bytes 49160 | tf_op jit(solution)/shard_map/ppermute | solution.py:395
  30.3 2.5 %shard_map.61 = (f32[8,2,2,64,128]{4,3,2,1,0:T(8,128)S(1)}, f32[8,2,2,64,128]{4,3,2,1,0:T(8,128)S(1)}) custom-call(bf16[8,2,2,64,128]{4,3,2,1,0:T(8,128)(2,1)S(1)} %shard_map.54.refs_2_.mid_ref.x_ref, bf16[8,2,2,64,128]{4,3,2,1,0:T(8,128)(2,1)S(1)} %get-tuple-element.65.rim_ref.x_ref, bf16[256,768]{1,0:T(8,128)(2,1)S(1)} %get-tuple-element.70.after_ref.middle_ref, ...), custom_call_target="tpu_custom_call" | custom-call | flops 1000000 | bytes 10000 | tf_op jit(solution)/shard_map/pallas_call | solution.py:29
  32.8 0.0 collective-permute-done.9.rest_0_
  32.9 1.1 %shard_map.63 = (f32[8,2,2,64,128]{4,3,2,1,0:T(8,128)S(1)}, f32[8,2,2,64,128]{4,3,2,1,0:T(8,128)S(1)}) custom-call(bf16[8,2,2,64,128]{4,3,2,1,0:T(8,128)(2,1)S(1)} %shard_map.54.refs_2_.mid_ref.x_ref, bf16[8,2,2,64,128]{4,3,2,1,0:T(8,128)(2,1)S(1)} %get-tuple-element.65.rim_ref.x_ref, ...), custom_call_target="tpu_custom_call", output_to_operand_aliasing={{0}: (6, {}), {1}: (7, {})} | custom-call | flops 1000000 | bytes 10000 | tf_op jit(solution)/shard_map/pallas_call | solution.py:29
  34.0 0.0 collective-permute-done.13.b_ref
  34.0 0.0 collective-permute-done.12.a_ref
  34.0 0.9 %shard_map.64.refs_0_ = bf16[8,2,4,64,128]{4,3,2,1,0:T(8,128)(2,1)} custom-call(bf16[8,2,2,64,128]{4,3,2,1,0:T(8,128)(2,1)S(1)} %shard_map.54.refs_2_.mid_ref.x_ref, f32[8,2,2,64,128]{4,3,2,1,0:T(8,128)S(1)} %get-tuple-element.80.acc_ref, bf16[8,2,64,128]{3,2,1,0:T(8,128)(2,1)S(1)} %collective-permute-done.12.a_ref, ...), custom_call_target="tpu_custom_call" | custom-call | flops 1000000 | bytes 10000 | tf_op jit(solution)/shard_map/pallas_call | solution.py:29
  34.9 0.5 %collective-permute-done.10.a_ref = bf16[8,2,64,128]{3,2,1,0:T(8,128)(2,1)S(1)} collective-permute-done((bf16[8,2,64,128]{3,2,1,0:T(8,128)(2,1)S(1)}, bf16[8,2,64,128]{3,2,1,0:T(8,128)(2,1)S(1)}, u32[]{:S(2)}, u32[]{:S(2)}) %collective-permute-start.10) | collective-permute-done | bytes 262176 | tf_op jit(solution)/shard_map/ppermute | solution.py:395
  35.5 0.0 collective-permute-done.11.b_ref
  35.5 0.9 %shard_map.65 = bf16[8,2,4,64,128]{4,3,2,1,0:T(8,128)(2,1)} custom-call(bf16[8,2,2,64,128]{4,3,2,1,0:T(8,128)(2,1)S(1)} %get-tuple-element.65.rim_ref.x_ref, f32[8,2,2,64,128]{4,3,2,1,0:T(8,128)S(1)} %get-tuple-element.78.acc_ref, bf16[8,2,64,128]{3,2,1,0:T(8,128)(2,1)S(1)} %collective-permute-done.10.a_ref, ...), custom_call_target="tpu_custom_call", output_to_operand_aliasing={{}: (4, {})} | custom-call | flops 1000000 | bytes 10000 | tf_op jit(solution)/shard_map/pallas_call | solution.py:29
Async XLA Ops:
  0.0 4.3 %copy-start = (bf16[8,2,4,64,128]{4,3,2,1,0:T(8,128)(2,1)S(1)}, bf16[8,2,4,64,128]{4,3,2,1,0:T(8,128)(2,1)}, u32[]{:S(2)}) copy-start(bf16[8,2,4,64,128]{4,3,2,1,0:T(8,128)(2,1)} %x_ref.17) | copy-start | bytes 3145732
  1.2 6.9 %collective-permute-start = (bf16[8,2,64,128]{3,2,1,0:T(8,128)(2,1)S(1)}, bf16[8,2,64,128]{3,2,1,0:T(8,128)(2,1)S(1)}, u32[]{:S(2)}, u32[]{:S(2)}) collective-permute-start(bf16[8,2,64,128]{3,2,1,0:T(8,128)(2,1)S(1)} %get-tuple-element.43), channel_id=1, source_target_pairs={{0,2},{2,0},{4,6},{6,4},{1,3},{3,1},{5,7},{7,5},{8,10},{10,8},{12,... | collective-permute-start | bytes 786440 | tf_op jit(solution)/shard_map/ppermute | solution.py:395
  1.7 6.9 %collective-permute-start.1 = (bf16[8,2,64,128]{3,2,1,0:T(8,128)(2,1)S(1)}, bf16[8,2,64,128]{3,2,1,0:T(8,128)(2,1)S(1)}, u32[]{:S(2)}, u32[]{:S(2)}) collective-permute-start(bf16[8,2,64,128]{3,2,1,0:T(8,128)(2,1)S(1)} %get-tuple-element.44), channel_id=1, source_target_pairs={{0,1},{1,0},{2,4},{3,5},{4,2},{5,3},{6,7},{7,6},{8,9},{9,8},{10,12... | collective-permute-start | bytes 786440 | tf_op jit(solution)/shard_map/ppermute | solution.py:408
  4.9 11.9 %collective-permute-start.5 = (bf16[8,2,64,128]{3,2,1,0:T(8,128)(2,1)S(1)}, bf16[8,2,64,128]{3,2,1,0:T(8,128)(2,1)S(1)}, u32[]{:S(2)}, u32[]{:S(2)}) collective-permute-start(bf16[8,2,64,128]{3,2,1,0:T(8,128)(2,1)S(1)} %get-tuple-element.63), channel_id=1, source_target_pairs={{0,8},{8,0},{16,24},{24,16},{1,9},{9,1},{17,25},{25,17},{2,10},{10... | collective-permute-start | bytes 786440 | tf_op jit(solution)/shard_map/ppermute | solution.py:395
  6.5 10.3 %collective-permute-start.6 = (bf16[8,2,64,128]{3,2,1,0:T(8,128)(2,1)S(1)}, bf16[8,2,64,128]{3,2,1,0:T(8,128)(2,1)S(1)}, u32[]{:S(2)}, u32[]{:S(2)}) collective-permute-start(bf16[8,2,64,128]{3,2,1,0:T(8,128)(2,1)S(1)} %get-tuple-element.46.refs_1_.after_ref), channel_id=1, source_target_pairs={{0,2},{2,0},{4,6},{6,4},{8,16},{10,18},{12,20},{14,22},{16,8},{18,... | collective-permute-start | bytes 786440 | tf_op jit(solution)/shard_map/ppermute | solution.py:408
  9.0 9.8 %collective-permute-start.4 = (bf16[8,2,64,128]{3,2,1,0:T(8,128)(2,1)S(1)}, bf16[8,2,64,128]{3,2,1,0:T(8,128)(2,1)S(1)}, u32[]{:S(2)}, u32[]{:S(2)}) collective-permute-start(bf16[8,2,64,128]{3,2,1,0:T(8,128)(2,1)S(1)} %get-tuple-element.61), channel_id=1, source_target_pairs={{0,8},{8,0},{16,24},{24,16},{1,9},{9,1},{17,25},{25,17},{2,10},{10... | collective-permute-start | bytes 786440 | tf_op jit(solution)/shard_map/ppermute | solution.py:395
  11.7 7.7 %collective-permute-start.3 = (bf16[8,2,64,128]{3,2,1,0:T(8,128)(2,1)S(1)}, bf16[8,2,64,128]{3,2,1,0:T(8,128)(2,1)S(1)}, u32[]{:S(2)}, u32[]{:S(2)}) collective-permute-start(bf16[8,2,64,128]{3,2,1,0:T(8,128)(2,1)S(1)} %get-tuple-element.57.refs_5_.refs_0_), channel_id=1, source_target_pairs={{0,2},{2,0},{4,6},{6,4},{8,16},{10,18},{12,20},{14,22},{16,8},{18,... | collective-permute-start | bytes 786440 | tf_op jit(solution)/shard_map/ppermute | solution.py:408
  11.9 3.7 %collective-permute-start.2 = (bf16[2,8,512]{2,1,0:T(8,128)(2,1)S(1)}, bf16[2,8,512]{2,1,0:T(8,128)(2,1)S(1)}, u32[]{:S(2)}, u32[]{:S(2)}) collective-permute-start(bf16[2,8,512]{2,1,0:T(8,128)(2,1)S(1)} %shard_map.52), channel_id=1, source_target_pairs={{0,1},{1,0},{2,3},{3,2},{4,5},{5,4},{6,7},{7,6},{8,9},{9,8},{10,11... | collective-permute-start | bytes 49160 | tf_op jit(solution)/shard_map/ppermute | solution.py:395
  19.6 4.6 %collective-permute-start.7 = (bf16[8,2,64,128]{3,2,1,0:T(8,128)(2,1)S(1)}, bf16[8,2,64,128]{3,2,1,0:T(8,128)(2,1)S(1)}, u32[]{:S(2)}, u32[]{:S(2)}) collective-permute-start(bf16[8,2,64,128]{3,2,1,0:T(8,128)(2,1)S(1)} %get-tuple-element.66), channel_id=1, source_target_pairs={{0,2},{2,0},{4,6},{6,4},{1,3},{3,1},{5,7},{7,5},{8,10},{10,8},{12,... | collective-permute-start | bytes 786440 | tf_op jit(solution)/shard_map/ppermute | solution.py:395
  19.7 6.4 %collective-permute-start.8 = (bf16[8,2,64,128]{3,2,1,0:T(8,128)(2,1)S(1)}, bf16[8,2,64,128]{3,2,1,0:T(8,128)(2,1)S(1)}, u32[]{:S(2)}, u32[]{:S(2)}) collective-permute-start(bf16[8,2,64,128]{3,2,1,0:T(8,128)(2,1)S(1)} %get-tuple-element.67), channel_id=1, source_target_pairs={{0,1},{1,0},{2,4},{3,5},{4,2},{5,3},{6,7},{7,6},{8,9},{9,8},{10,12... | collective-permute-start | bytes 786440 | tf_op jit(solution)/shard_map/ppermute | solution.py:408
  20.7 13.3 %collective-permute-start.12 = (bf16[8,2,64,128]{3,2,1,0:T(8,128)(2,1)S(1)}, bf16[8,2,64,128]{3,2,1,0:T(8,128)(2,1)S(1)}, u32[]{:S(2)}, u32[]{:S(2)}) collective-permute-start(bf16[8,2,64,128]{3,2,1,0:T(8,128)(2,1)S(1)} %shard_map.56.refs_3_), channel_id=1, source_target_pairs={{0,8},{8,0},{16,24},{24,16},{1,9},{9,1},{17,25},{25,17},{2,10},{10... | collective-permute-start | bytes 786440 | tf_op jit(solution)/shard_map/ppermute | solution.py:395
  23.7 10.3 %collective-permute-start.13 = (bf16[8,2,64,128]{3,2,1,0:T(8,128)(2,1)S(1)}, bf16[8,2,64,128]{3,2,1,0:T(8,128)(2,1)S(1)}, u32[]{:S(2)}, u32[]{:S(2)}) collective-permute-start(bf16[8,2,64,128]{3,2,1,0:T(8,128)(2,1)S(1)} %shard_map.58.after_ref), channel_id=1, source_target_pairs={{0,2},{2,0},{4,6},{6,4},{8,16},{10,18},{12,20},{14,22},{16,8},{18,... | collective-permute-start | bytes 786440 | tf_op jit(solution)/shard_map/ppermute | solution.py:408
  26.5 9.0 %collective-permute-start.10 = (bf16[8,2,64,128]{3,2,1,0:T(8,128)(2,1)S(1)}, bf16[8,2,64,128]{3,2,1,0:T(8,128)(2,1)S(1)}, u32[]{:S(2)}, u32[]{:S(2)}) collective-permute-start(bf16[8,2,64,128]{3,2,1,0:T(8,128)(2,1)S(1)} %get-tuple-element.79), channel_id=1, source_target_pairs={{0,8},{8,0},{16,24},{24,16},{1,9},{9,1},{17,25},{25,17},{2,10},{10... | collective-permute-start | bytes 786440 | tf_op jit(solution)/shard_map/ppermute | solution.py:395
  28.7 6.7 %collective-permute-start.11 = (bf16[8,2,64,128]{3,2,1,0:T(8,128)(2,1)S(1)}, bf16[8,2,64,128]{3,2,1,0:T(8,128)(2,1)S(1)}, u32[]{:S(2)}, u32[]{:S(2)}) collective-permute-start(bf16[8,2,64,128]{3,2,1,0:T(8,128)(2,1)S(1)} %get-tuple-element.75.after_ref), channel_id=1, source_target_pairs={{0,2},{2,0},{4,6},{6,4},{8,16},{10,18},{12,20},{14,22},{16,8},{18,... | collective-permute-start | bytes 786440 | tf_op jit(solution)/shard_map/ppermute | solution.py:408
  28.9 3.9 %collective-permute-start.9 = (bf16[2,8,512]{2,1,0:T(8,128)(2,1)S(1)}, bf16[2,8,512]{2,1,0:T(8,128)(2,1)S(1)}, u32[]{:S(2)}, u32[]{:S(2)}) collective-permute-start(bf16[2,8,512]{2,1,0:T(8,128)(2,1)S(1)} %shard_map.62), channel_id=1, source_target_pairs={{0,1},{1,0},{2,3},{3,2},{4,5},{5,4},{6,7},{7,6},{8,9},{9,8},{10,11... | collective-permute-start | bytes 49160 | tf_op jit(solution)/shard_map/ppermute | solution.py:395

commit v14 on v13

--- a/solution.py
+++ b/solution.py
@@ -22,7 +22,7 @@
     return (at > 0) & (at < lax.axis_size(axis) - 1)
 
 
-def call(body, outs, args, places=None, out_place=VMEM, scratch=(), aliases=None):
+def call(body, outs, args, places=None, out_place=VMEM, scratch=(), aliases=None, flops=10**6):
     places = places or {}
     spaces = [places.get(n, VMEM) for n in range(len(args))]
     held = [pltpu.with_memory_space_constraint(a, m) if m in (VMEM, HBM) else a for a, m in zip(args, spaces)]
@@ -34,7 +34,7 @@
         scratch_shapes=list(scratch),
         input_output_aliases=aliases or {},
         compiler_params=pltpu.CompilerParams(vmem_limit_bytes=SCOPED),
-        cost_estimate=pl.CostEstimate(flops=10**6, bytes_accessed=10**4, transcendentals=0),
+        cost_estimate=pl.CostEstimate(flops=flops, bytes_accessed=10**4, transcendentals=0),
     )(*held)
 
 
@@ -453,6 +453,7 @@
             [VMEM((2, channels * BAND, depth // BAND * width), F32)] * 2,
             (*block, operator["beside"], sum_b),
             {base + 1: pl.ANY},
+            flops=10**10 if layer else 10**6,
         )
         a, b, side = call(
             edge_body,

time: 36.5 us -> 39.3 us (1.077)
  waiting for transfers between devices: 5.05 us -> 7.56 us
    ppermute x6, waiting for transfers between devices: 2.44 us -> 5.1 us  [swap_second(): return lax.ppermute(value, (axis, other), pairs)]
  transfers between devices with their start and end apart: 14 -> 14, of which waited for: 5 -> 5; matrix products, arithmetic and copies ran while one was open for 0% -> 0% of each run, Pallas kernels for 36% -> 34%
where the time goes in v14:
time: 39.3 us; the launch traced here: 39.2 us
  starting transfers between devices  16.1 us (41%)
  Pallas kernels  15.3 us (39%)
  waiting for transfers between devices  7.56 us (19%)
    pallas_call x20, Pallas kernels, call(): pl.pallas_call(body, out_shape=tuple(outs), in_specs=[pl.BlockSpec(memory...  15.3 us
    ppermute x8, starting transfers between devices, swap_first(): lax.ppermute(value, axis, [(n, n ^ 1) for n in range(lax.axis_size(axis))])  12.1 us
    ppermute x6, waiting for transfers between devices, swap_second(): return lax.ppermute(value, (axis, other), pairs)  5.1 us
    ppermute x6, starting transfers between devices, swap_second(): return lax.ppermute(value, (axis, other), pairs)  4.06 us
    ppermute x8, waiting for transfers between devices, swap_first(): lax.ppermute(value, axis, [(n, n ^ 1) for n in range(lax.axis_size(axis))])  2.46 us
  transfers between devices with their start and end apart: 14, of which 5 were waited for; matrix products, arithmetic and copies ran while one was open for 0% of the time, Pallas kernels for 34%

profile of v14, /device:TPU:0, one launch (start us, length us, event | category | flops | bytes accessed | tf_op | source)
XLA Modules:
  0.0 39.2 jit_solution(6875030184458547495)
XLA Ops:
  0.0 0.0 copy-start
  0.0 1.2 %shard_map.46 = (bf16[2,8,8,9]{3,2,1,0:T(8,128)(2,1)S(1)}, bf16[2,8,8,9]{3,2,1,0:T(8,128)(2,1)S(1)}, f32[2,8]{1,0:T(2,128)S(1)}, bf16[2,256,768]{2,1,0:T(8,128)(...) custom-call(bf16[8,2,4,64,128]{4,3,2,1,0:T(8,128)(2,1)} %x_ref.17, ...), custom_call_target="tpu_custom_call" | custom-call | flops 1000000 | bytes 10000 | tf_op jit(solution)/shard_map/pallas_call | solution.py:29
  1.2 0.5 %collective-permute-start = (bf16[8,2,64,128]{3,2,1,0:T(8,128)(2,1)S(1)}, bf16[8,2,64,128]{3,2,1,0:T(8,128)(2,1)S(1)}, u32[]{:S(2)}, u32[]{:S(2)}) collective-permute-start(bf16[8,2,64,128]{3,2,1,0:T(8,128)(2,1)S(1)} %get-tuple-element.43), channel_id=1, source_target_pairs={{0,2},{2,0},{4,6},{6,4},{1,3},{3,1},{5,7},{7,5},{8,10},{10,8},{12,... | collective-permute-start | bytes 786440 | tf_op jit(solution)/shard_map/ppermute | solution.py:395
  1.7 2.6 %collective-permute-start.1 = (bf16[8,2,64,128]{3,2,1,0:T(8,128)(2,1)S(1)}, bf16[8,2,64,128]{3,2,1,0:T(8,128)(2,1)S(1)}, u32[]{:S(2)}, u32[]{:S(2)}) collective-permute-start(bf16[8,2,64,128]{3,2,1,0:T(8,128)(2,1)S(1)} %get-tuple-element.44), channel_id=1, source_target_pairs={{0,1},{1,0},{2,4},{3,5},{4,2},{5,3},{6,7},{7,6},{8,9},{9,8},{10,12... | collective-permute-start | bytes 786440 | tf_op jit(solution)/shard_map/ppermute | solution.py:408
  4.3 0.0 copy-done
  4.3 0.6 %shard_map.47 = (bf16[8,2,64,128]{3,2,1,0:T(8,128)(2,1)S(1)}, bf16[8,2,64,128]{3,2,1,0:T(8,128)(2,1)S(1)}) custom-call(bf16[8,2,4,64,128]{4,3,2,1,0:T(8,128)(2,1)S(1)} %copy-done, bf16[2,256,768]{2,1,0:T(8,128)(2,1)S(1)} %get-tuple-element.45.refs_0_.beside_ref.refs_1_.refs_2_), custom_call_target="tpu_custom_call" | custom-call | flops 1000000 | bytes 10000 | tf_op jit(solution)/shard_map/pallas_call | solution.py:29
  4.9 1.6 %collective-permute-start.5 = (bf16[8,2,64,128]{3,2,1,0:T(8,128)(2,1)S(1)}, bf16[8,2,64,128]{3,2,1,0:T(8,128)(2,1)S(1)}, u32[]{:S(2)}, u32[]{:S(2)}) collective-permute-start(bf16[8,2,64,128]{3,2,1,0:T(8,128)(2,1)S(1)} %get-tuple-element.63), channel_id=1, source_target_pairs={{0,8},{8,0},{16,24},{24,16},{1,9},{9,1},{17,25},{25,17},{2,10},{10... | collective-permute-start | bytes 786440 | tf_op jit(solution)/shard_map/ppermute | solution.py:395
  6.5 0.0 collective-permute-start.6
  6.5 0.4 %shard_map.48 = (f32[2,256,256]{2,1,0:T(8,128)S(1)}, f32[2,256,256]{2,1,0:T(8,128)S(1)}) custom-call(bf16[8,2,4,64,128]{4,3,2,1,0:T(8,128)(2,1)S(1)} %copy-done, bf16[2,256,768]{2,1,0:T(8,128)(2,1)S(1)} %get-tuple-element.45.refs_0_.beside_ref.refs_1_.refs_2_, bf16[8,2,64,128]{3,2,1,0:T(8,128)(2,1)S(1)} %get-tuple-element.46.refs_1_.after_ref), custom_call_target="tpu_custom_call" | custom-call | flops 1000000 | bytes 10000 | tf_op jit(solution)/shard_map/pallas_call | solution.py:29
  7.0 1.1 %shard_map.49 = (bf16[256,768]{1,0:T(8,128)(2,1)S(1)}, bf16[256,768]{1,0:T(8,128)(2,1)S(1)}, bf16[2,256,384]{2,1,0:T(8,128)(2,1)S(1)}, bf16[2,256,24]{2,1,0:T(8,...) custom-call(bf16[2,8,8,9]{3,2,1,0:T(8,128)(2,1)S(1)} %get-tuple-elem, ...), custom_call_target="tpu_custom_call" | custom-call | flops 1000000 | bytes 10000 | tf_op jit(solution)/shard_map/pallas_call | solution.py:29
  8.1 0.0 collective-permute-done.cola_ref
  8.1 0.6 %collective-permute-done.1.colb_ref = bf16[8,2,64,128]{3,2,1,0:T(8,128)(2,1)S(1)} collective-permute-done((bf16[8,2,64,128]{3,2,1,0:T(8,128)(2,1)S(1)}, bf16[8,2,64,128]{3,2,1,0:T(8,128)(2,1)S(1)}, u32[]{:S(2)}, u32[]{:S(2)}) %collective-permute-start.1) | collective-permute-done | bytes 262176 | tf_op jit(solution)/shard_map/ppermute | solution.py:408
  8.7 0.4 shard_map.50
  9.0 2.7 %collective-permute-start.4 = (bf16[8,2,64,128]{3,2,1,0:T(8,128)(2,1)S(1)}, bf16[8,2,64,128]{3,2,1,0:T(8,128)(2,1)S(1)}, u32[]{:S(2)}, u32[]{:S(2)}) collective-permute-start(bf16[8,2,64,128]{3,2,1,0:T(8,128)(2,1)S(1)} %get-tuple-element.61), channel_id=1, source_target_pairs={{0,8},{8,0},{16,24},{24,16},{1,9},{9,1},{17,25},{25,17},{2,10},{10... | collective-permute-start | bytes 786440 | tf_op jit(solution)/shard_map/ppermute | solution.py:395
  11.7 0.0 collective-permute-start.3
  11.7 0.2 shard_map.52
  11.9 1.0 %collective-permute-start.2 = (bf16[2,8,512]{2,1,0:T(8,128)(2,1)S(1)}, bf16[2,8,512]{2,1,0:T(8,128)(2,1)S(1)}, u32[]{:S(2)}, u32[]{:S(2)}) collective-permute-start(bf16[2,8,512]{2,1,0:T(8,128)(2,1)S(1)} %shard_map.52), channel_id=1, source_target_pairs={{0,1},{1,0},{2,3},{3,2},{4,5},{5,4},{6,7},{7,6},{8,9},{9,8},{10,11... | collective-permute-start | bytes 49160 | tf_op jit(solution)/shard_map/ppermute | solution.py:395
  12.9 2.5 %shard_map.51 = (f32[8,2,2,64,128]{4,3,2,1,0:T(8,128)S(1)}, f32[8,2,2,64,128]{4,3,2,1,0:T(8,128)S(1)}) custom-call(bf16[8,2,4,64,128]{4,3,2,1,0:T(8,128)(2,1)S(1)} %copy-done, bf16[256,768]{1,0:T(8,128)(2,1)S(1)} %get-tuple-element.51.after_ref.refs_0_.refs_1_, bf16[2,256,768]{2,1,0:T(8,128)(2,1)S(1)} %get-tuple-element.45.refs_0_.beside_ref.refs_1_.refs_2_, ...), custom_call_target="tpu_custom_call" | custom-call | flops 1000000 | bytes 10000 | tf_op jit(solution)/shard_map/pallas_call | solution.py:29
  15.4 0.2 collective-permute-done.2.refs_6_
  15.7 1.1 %shard_map.53 = (f32[8,2,2,64,128]{4,3,2,1,0:T(8,128)S(1)}, f32[8,2,2,64,128]{4,3,2,1,0:T(8,128)S(1)}) custom-call(bf16[8,2,4,64,128]{4,3,2,1,0:T(8,128)(2,1)S(1)} %copy-done, bf16[2,8,2,64,128]{4,3,2,1,0:T(8,128)(2,1)S(1)} %get-tuple-element.52.refs_0_, ...), custom_call_target="tpu_custom_call", output_to_operand_aliasing={{0}: (5, {}), {1}: (6, {})} | custom-call | flops 1000000 | bytes 10000 | tf_op jit(solution)/shard_map/pallas_call | solution.py:29
  16.8 0.0 collective-permute-done.5.refs_1_
  16.8 0.0 collective-permute-done.6.refs_2_
  16.8 0.2 shard_map.54.refs_2_.mid_ref.x_ref
  17.0 1.8 %collective-permute-done.4.refs_1_ = bf16[8,2,64,128]{3,2,1,0:T(8,128)(2,1)S(1)} collective-permute-done((bf16[8,2,64,128]{3,2,1,0:T(8,128)(2,1)S(1)}, bf16[8,2,64,128]{3,2,1,0:T(8,128)(2,1)S(1)}, u32[]{:S(2)}, u32[]{:S(2)}) %collective-permute-start.4) | collective-permute-done | bytes 262176 | tf_op jit(solution)/shard_map/ppermute | solution.py:395
  18.9 0.1 shard_map.55.rim_ref.refs_2_
  19.0 0.4 shard_map.56.refs_3_
  19.4 1.6 %collective-permute-start.12 = (bf16[8,2,64,128]{3,2,1,0:T(8,128)(2,1)S(1)}, bf16[8,2,64,128]{3,2,1,0:T(8,128)(2,1)S(1)}, u32[]{:S(2)}, u32[]{:S(2)}) collective-permute-start(bf16[8,2,64,128]{3,2,1,0:T(8,128)(2,1)S(1)} %shard_map.56.refs_3_), channel_id=1, source_target_pairs={{0,8},{8,0},{16,24},{24,16},{1,9},{9,1},{17,25},{25,17},{2,10},{10... | collective-permute-start | bytes 786440 | tf_op jit(solution)/shard_map/ppermute | solution.py:395
  21.0 0.0 collective-permute-done.3.refs_1_
  21.0 0.2 shard_map.57
  21.2 0.4 shard_map.58.after_ref
  21.6 0.1 collective-permute-start.13
  21.7 0.5 %collective-permute-start.7 = (bf16[8,2,64,128]{3,2,1,0:T(8,128)(2,1)S(1)}, bf16[8,2,64,128]{3,2,1,0:T(8,128)(2,1)S(1)}, u32[]{:S(2)}, u32[]{:S(2)}) collective-permute-start(bf16[8,2,64,128]{3,2,1,0:T(8,128)(2,1)S(1)} %get-tuple-element.66), channel_id=1, source_target_pairs={{0,2},{2,0},{4,6},{6,4},{1,3},{3,1},{5,7},{7,5},{8,10},{10,8},{12,... | collective-permute-start | bytes 786440 | tf_op jit(solution)/shard_map/ppermute | solution.py:395
  22.2 1.4 %collective-permute-start.8 = (bf16[8,2,64,128]{3,2,1,0:T(8,128)(2,1)S(1)}, bf16[8,2,64,128]{3,2,1,0:T(8,128)(2,1)S(1)}, u32[]{:S(2)}, u32[]{:S(2)}) collective-permute-start(bf16[8,2,64,128]{3,2,1,0:T(8,128)(2,1)S(1)} %get-tuple-element.67), channel_id=1, source_target_pairs={{0,1},{1,0},{2,4},{3,5},{4,2},{5,3},{6,7},{7,6},{8,9},{9,8},{10,12... | collective-permute-start | bytes 786440 | tf_op jit(solution)/shard_map/ppermute | solution.py:408
  23.6 0.4 %shard_map.59 = (f32[2,256,256]{2,1,0:T(8,128)S(1)}, f32[2,256,256]{2,1,0:T(8,128)S(1)}) custom-call(bf16[8,2,2,64,128]{4,3,2,1,0:T(8,128)(2,1)S(1)} %shard_map.54.refs_2_.mid_ref.x_ref, bf16[8,2,2,64,128]{4,3,2,1,0:T(8,128)(2,1)S(1)} %get-tuple-element.65.rim_ref.x_ref, bf16[2,256,768]{2,1,0:T(8,128)(2,1)S(1)} %get-tuple-element.64.beside_ref, ...), custom_call_target="tpu_custom_call" | custom-call | flops 10000000000 | bytes 10000 | tf_op jit(solution)/shard_map/pallas_call | solution.py:29
  24.0 0.0 collective-permute-done.7.cola_ref
  24.0 4.5 %collective-permute-done.8.colb_ref = bf16[8,2,64,128]{3,2,1,0:T(8,128)(2,1)S(1)} collective-permute-done((bf16[8,2,64,128]{3,2,1,0:T(8,128)(2,1)S(1)}, bf16[8,2,64,128]{3,2,1,0:T(8,128)(2,1)S(1)}, u32[]{:S(2)}, u32[]{:S(2)}) %collective-permute-start.8) | collective-permute-done | bytes 262176 | tf_op jit(solution)/shard_map/ppermute | solution.py:408
  28.6 0.4 shard_map.60
  28.9 2.7 %collective-permute-start.10 = (bf16[8,2,64,128]{3,2,1,0:T(8,128)(2,1)S(1)}, bf16[8,2,64,128]{3,2,1,0:T(8,128)(2,1)S(1)}, u32[]{:S(2)}, u32[]{:S(2)}) collective-permute-start(bf16[8,2,64,128]{3,2,1,0:T(8,128)(2,1)S(1)} %get-tuple-element.79), channel_id=1, source_target_pairs={{0,8},{8,0},{16,24},{24,16},{1,9},{9,1},{17,25},{25,17},{2,10},{10... | collective-permute-start | bytes 786440 | tf_op jit(solution)/shard_map/ppermute | solution.py:395
  31.7 0.0 collective-permute-start.11
  31.7 0.2 shard_map.62
  31.8 1.4 %collective-permute-start.9 = (bf16[2,8,512]{2,1,0:T(8,128)(2,1)S(1)}, bf16[2,8,512]{2,1,0:T(8,128)(2,1)S(1)}, u32[]{:S(2)}, u32[]{:S(2)}) collective-permute-start(bf16[2,8,512]{2,1,0:T(8,128)(2,1)S(1)} %shard_map.62), channel_id=1, source_target_pairs={{0,1},{1,0},{2,3},{3,2},{4,5},{5,4},{6,7},{7,6},{8,9},{9,8},{10,11... | collective-permute-start | bytes 49160 | tf_op jit(solution)/shard_map/ppermute | solution.py:395
  33.2 2.5 %shard_map.61 = (f32[8,2,2,64,128]{4,3,2,1,0:T(8,128)S(1)}, f32[8,2,2,64,128]{4,3,2,1,0:T(8,128)S(1)}) custom-call(bf16[8,2,2,64,128]{4,3,2,1,0:T(8,128)(2,1)S(1)} %shard_map.54.refs_2_.mid_ref.x_ref, bf16[8,2,2,64,128]{4,3,2,1,0:T(8,128)(2,1)S(1)} %get-tuple-element.65.rim_ref.x_ref, bf16[256,768]{1,0:T(8,128)(2,1)S(1)} %get-tuple-element.70.after_ref.middle_ref, ...), custom_call_target="tpu_custom_call" | custom-call | flops 1000000 | bytes 10000 | tf_op jit(solution)/shard_map/pallas_call | solution.py:29
  35.8 0.0 collective-permute-done.9.rest_0_
  35.8 1.1 %shard_map.63 = (f32[8,2,2,64,128]{4,3,2,1,0:T(8,128)S(1)}, f32[8,2,2,64,128]{4,3,2,1,0:T(8,128)S(1)}) custom-call(bf16[8,2,2,64,128]{4,3,2,1,0:T(8,128)(2,1)S(1)} %shard_map.54.refs_2_.mid_ref.x_ref, bf16[8,2,2,64,128]{4,3,2,1,0:T(8,128)(2,1)S(1)} %get-tuple-element.65.rim_ref.x_ref, ...), custom_call_target="tpu_custom_call", output_to_operand_aliasing={{0}: (6, {}), {1}: (7, {})} | custom-call | flops 1000000 | bytes 10000 | tf_op jit(solution)/shard_map/pallas_call | solution.py:29
  36.9 0.0 collective-permute-done.13.b_ref
  36.9 0.0 collective-permute-done.12.a_ref
  36.9 0.9 %shard_map.64.refs_0_ = bf16[8,2,4,64,128]{4,3,2,1,0:T(8,128)(2,1)} custom-call(bf16[8,2,2,64,128]{4,3,2,1,0:T(8,128)(2,1)S(1)} %shard_map.54.refs_2_.mid_ref.x_ref, f32[8,2,2,64,128]{4,3,2,1,0:T(8,128)S(1)} %get-tuple-element.80.acc_ref, bf16[8,2,64,128]{3,2,1,0:T(8,128)(2,1)S(1)} %collective-permute-done.12.a_ref, ...), custom_call_target="tpu_custom_call" | custom-call | flops 1000000 | bytes 10000 | tf_op jit(solution)/shard_map/pallas_call | solution.py:29
  37.8 0.4 collective-permute-done.10.a_ref
  38.2 0.0 collective-permute-done.11.b_ref
  38.2 0.9 %shard_map.65 = bf16[8,2,4,64,128]{4,3,2,1,0:T(8,128)(2,1)} custom-call(bf16[8,2,2,64,128]{4,3,2,1,0:T(8,128)(2,1)S(1)} %get-tuple-element.65.rim_ref.x_ref, f32[8,2,2,64,128]{4,3,2,1,0:T(8,128)S(1)} %get-tuple-element.78.acc_ref, bf16[8,2,64,128]{3,2,1,0:T(8,128)(2,1)S(1)} %collective-permute-done.10.a_ref, ...), custom_call_target="tpu_custom_call", output_to_operand_aliasing={{}: (4, {})} | custom-call | flops 1000000 | bytes 10000 | tf_op jit(solution)/shard_map/pallas_call | solution.py:29
Async XLA Ops:
  0.0 4.3 %copy-start = (bf16[8,2,4,64,128]{4,3,2,1,0:T(8,128)(2,1)S(1)}, bf16[8,2,4,64,128]{4,3,2,1,0:T(8,128)(2,1)}, u32[]{:S(2)}) copy-start(bf16[8,2,4,64,128]{4,3,2,1,0:T(8,128)(2,1)} %x_ref.17) | copy-start | bytes 3145732
  1.2 6.9 %collective-permute-start = (bf16[8,2,64,128]{3,2,1,0:T(8,128)(2,1)S(1)}, bf16[8,2,64,128]{3,2,1,0:T(8,128)(2,1)S(1)}, u32[]{:S(2)}, u32[]{:S(2)}) collective-permute-start(bf16[8,2,64,128]{3,2,1,0:T(8,128)(2,1)S(1)} %get-tuple-element.43), channel_id=1, source_target_pairs={{0,2},{2,0},{4,6},{6,4},{1,3},{3,1},{5,7},{7,5},{8,10},{10,8},{12,... | collective-permute-start | bytes 786440 | tf_op jit(solution)/shard_map/ppermute | solution.py:395
  1.7 6.9 %collective-permute-start.1 = (bf16[8,2,64,128]{3,2,1,0:T(8,128)(2,1)S(1)}, bf16[8,2,64,128]{3,2,1,0:T(8,128)(2,1)S(1)}, u32[]{:S(2)}, u32[]{:S(2)}) collective-permute-start(bf16[8,2,64,128]{3,2,1,0:T(8,128)(2,1)S(1)} %get-tuple-element.44), channel_id=1, source_target_pairs={{0,1},{1,0},{2,4},{3,5},{4,2},{5,3},{6,7},{7,6},{8,9},{9,8},{10,12... | collective-permute-start | bytes 786440 | tf_op jit(solution)/shard_map/ppermute | solution.py:408
  4.9 11.9 %collective-permute-start.5 = (bf16[8,2,64,128]{3,2,1,0:T(8,128)(2,1)S(1)}, bf16[8,2,64,128]{3,2,1,0:T(8,128)(2,1)S(1)}, u32[]{:S(2)}, u32[]{:S(2)}) collective-permute-start(bf16[8,2,64,128]{3,2,1,0:T(8,128)(2,1)S(1)} %get-tuple-element.63), channel_id=1, source_target_pairs={{0,8},{8,0},{16,24},{24,16},{1,9},{9,1},{17,25},{25,17},{2,10},{10... | collective-permute-start | bytes 786440 | tf_op jit(solution)/shard_map/ppermute | solution.py:395
  6.5 10.3 %collective-permute-start.6 = (bf16[8,2,64,128]{3,2,1,0:T(8,128)(2,1)S(1)}, bf16[8,2,64,128]{3,2,1,0:T(8,128)(2,1)S(1)}, u32[]{:S(2)}, u32[]{:S(2)}) collective-permute-start(bf16[8,2,64,128]{3,2,1,0:T(8,128)(2,1)S(1)} %get-tuple-element.46.refs_1_.after_ref), channel_id=1, source_target_pairs={{0,2},{2,0},{4,6},{6,4},{8,16},{10,18},{12,20},{14,22},{16,8},{18,... | collective-permute-start | bytes 786440 | tf_op jit(solution)/shard_map/ppermute | solution.py:408
  9.0 9.8 %collective-permute-start.4 = (bf16[8,2,64,128]{3,2,1,0:T(8,128)(2,1)S(1)}, bf16[8,2,64,128]{3,2,1,0:T(8,128)(2,1)S(1)}, u32[]{:S(2)}, u32[]{:S(2)}) collective-permute-start(bf16[8,2,64,128]{3,2,1,0:T(8,128)(2,1)S(1)} %get-tuple-element.61), channel_id=1, source_target_pairs={{0,8},{8,0},{16,24},{24,16},{1,9},{9,1},{17,25},{25,17},{2,10},{10... | collective-permute-start | bytes 786440 | tf_op jit(solution)/shard_map/ppermute | solution.py:395
  11.7 9.3 %collective-permute-start.3 = (bf16[8,2,64,128]{3,2,1,0:T(8,128)(2,1)S(1)}, bf16[8,2,64,128]{3,2,1,0:T(8,128)(2,1)S(1)}, u32[]{:S(2)}, u32[]{:S(2)}) collective-permute-start(bf16[8,2,64,128]{3,2,1,0:T(8,128)(2,1)S(1)} %get-tuple-element.57.refs_5_.refs_0_), channel_id=1, source_target_pairs={{0,2},{2,0},{4,6},{6,4},{8,16},{10,18},{12,20},{14,22},{16,8},{18,... | collective-permute-start | bytes 786440 | tf_op jit(solution)/shard_map/ppermute | solution.py:408
  11.9 3.7 %collective-permute-start.2 = (bf16[2,8,512]{2,1,0:T(8,128)(2,1)S(1)}, bf16[2,8,512]{2,1,0:T(8,128)(2,1)S(1)}, u32[]{:S(2)}, u32[]{:S(2)}) collective-permute-start(bf16[2,8,512]{2,1,0:T(8,128)(2,1)S(1)} %shard_map.52), channel_id=1, source_target_pairs={{0,1},{1,0},{2,3},{3,2},{4,5},{5,4},{6,7},{7,6},{8,9},{9,8},{10,11... | collective-permute-start | bytes 49160 | tf_op jit(solution)/shard_map/ppermute | solution.py:395
  19.4 17.5 %collective-permute-start.12 = (bf16[8,2,64,128]{3,2,1,0:T(8,128)(2,1)S(1)}, bf16[8,2,64,128]{3,2,1,0:T(8,128)(2,1)S(1)}, u32[]{:S(2)}, u32[]{:S(2)}) collective-permute-start(bf16[8,2,64,128]{3,2,1,0:T(8,128)(2,1)S(1)} %shard_map.56.refs_3_), channel_id=1, source_target_pairs={{0,8},{8,0},{16,24},{24,16},{1,9},{9,1},{17,25},{25,17},{2,10},{10... | collective-permute-start | bytes 786440 | tf_op jit(solution)/shard_map/ppermute | solution.py:395
  21.6 15.3 %collective-permute-start.13 = (bf16[8,2,64,128]{3,2,1,0:T(8,128)(2,1)S(1)}, bf16[8,2,64,128]{3,2,1,0:T(8,128)(2,1)S(1)}, u32[]{:S(2)}, u32[]{:S(2)}) collective-permute-start(bf16[8,2,64,128]{3,2,1,0:T(8,128)(2,1)S(1)} %shard_map.58.after_ref), channel_id=1, source_target_pairs={{0,2},{2,0},{4,6},{6,4},{8,16},{10,18},{12,20},{14,22},{16,8},{18,... | collective-permute-start | bytes 786440 | tf_op jit(solution)/shard_map/ppermute | solution.py:408
  21.7 2.3 %collective-permute-start.7 = (bf16[8,2,64,128]{3,2,1,0:T(8,128)(2,1)S(1)}, bf16[8,2,64,128]{3,2,1,0:T(8,128)(2,1)S(1)}, u32[]{:S(2)}, u32[]{:S(2)}) collective-permute-start(bf16[8,2,64,128]{3,2,1,0:T(8,128)(2,1)S(1)} %get-tuple-element.66), channel_id=1, source_target_pairs={{0,2},{2,0},{4,6},{6,4},{1,3},{3,1},{5,7},{7,5},{8,10},{10,8},{12,... | collective-permute-start | bytes 786440 | tf_op jit(solution)/shard_map/ppermute | solution.py:395
  22.2 6.4 %collective-permute-start.8 = (bf16[8,2,64,128]{3,2,1,0:T(8,128)(2,1)S(1)}, bf16[8,2,64,128]{3,2,1,0:T(8,128)(2,1)S(1)}, u32[]{:S(2)}, u32[]{:S(2)}) collective-permute-start(bf16[8,2,64,128]{3,2,1,0:T(8,128)(2,1)S(1)} %get-tuple-element.67), channel_id=1, source_target_pairs={{0,1},{1,0},{2,4},{3,5},{4,2},{5,3},{6,7},{7,6},{8,9},{9,8},{10,12... | collective-permute-start | bytes 786440 | tf_op jit(solution)/shard_map/ppermute | solution.py:408
  28.9 9.3 %collective-permute-start.10 = (bf16[8,2,64,128]{3,2,1,0:T(8,128)(2,1)S(1)}, bf16[8,2,64,128]{3,2,1,0:T(8,128)(2,1)S(1)}, u32[]{:S(2)}, u32[]{:S(2)}) collective-permute-start(bf16[8,2,64,128]{3,2,1,0:T(8,128)(2,1)S(1)} %get-tuple-element.79), channel_id=1, source_target_pairs={{0,8},{8,0},{16,24},{24,16},{1,9},{9,1},{17,25},{25,17},{2,10},{10... | collective-permute-start | bytes 786440 | tf_op jit(solution)/shard_map/ppermute | solution.py:395
  31.7 6.6 %collective-permute-start.11 = (bf16[8,2,64,128]{3,2,1,0:T(8,128)(2,1)S(1)}, bf16[8,2,64,128]{3,2,1,0:T(8,128)(2,1)S(1)}, u32[]{:S(2)}, u32[]{:S(2)}) collective-permute-start(bf16[8,2,64,128]{3,2,1,0:T(8,128)(2,1)S(1)} %get-tuple-element.75.after_ref), channel_id=1, source_target_pairs={{0,2},{2,0},{4,6},{6,4},{8,16},{10,18},{12,20},{14,22},{16,8},{18,... | collective-permute-start | bytes 786440 | tf_op jit(solution)/shard_map/ppermute | solution.py:408
  31.8 3.9 %collective-permute-start.9 = (bf16[2,8,512]{2,1,0:T(8,128)(2,1)S(1)}, bf16[2,8,512]{2,1,0:T(8,128)(2,1)S(1)}, u32[]{:S(2)}, u32[]{:S(2)}) collective-permute-start(bf16[2,8,512]{2,1,0:T(8,128)(2,1)S(1)} %shard_map.62), channel_id=1, source_target_pairs={{0,1},{1,0},{2,3},{3,2},{4,5},{5,4},{6,7},{7,6},{8,9},{9,8},{10,11... | collective-permute-start | bytes 49160 | tf_op jit(solution)/shard_map/ppermute | solution.py:395

commit v15 on v13

--- a/solution.py
+++ b/solution.py
@@ -408,6 +408,11 @@
     return lax.ppermute(value, (axis, other), pairs)
 
 
+def swap_inside(value, axis):
+    pairs = [(n, n + 1 if n % 2 else n - 1) for n in range(1, lax.axis_size(axis) - 1)]
+    return lax.ppermute(value, axis, pairs)
+
+
 def shards(volume, src_weight, tgt_weight, bias):
     layers = src_weight.shape[0]
     channels, rows, cols, depth, width = volume.shape
@@ -439,7 +444,7 @@
 
         both, base = (middle, sides), len(block)
         mid, rim = block[0], block[-1]
-        beside = swap_first(col_a, "scol"), swap_second(col_b, "scol", "trow")
+        beside = swap_first(col_a, "scol"), swap_inside(col_b, "scol")
         which = (0, 1) if sum_a is None else (1,)
         sums = call(on(functools.partial(inner_body, which), *both), owed_inner * len(which), (*block, made["beside", layer]))
         sum_b = sums[-1]

time: 36.5 us -> 37.2 us (1.019)
  starting transfers between devices: 15.9 us -> 20.9 us
  waiting for transfers between devices: 5.05 us -> 0.67 us
    ppermute x6 -> x4, starting transfers between devices: 3.71 us -> 10.7 us  [swap_second(): return lax.ppermute(value, (axis, other), pairs)]
    ppermute x8, starting transfers between devices: 12.2 us -> 8.8 us  [swap_first(): lax.ppermute(value, axis, [(n, n ^ 1) for n in range(lax.axis_size(axis))])]
    ppermute x6 -> x4, waiting for transfers between devices: 2.44 us -> 0.01 us  [swap_second(): return lax.ppermute(value, (axis, other), pairs)]
    ppermute x8, waiting for transfers between devices: 2.61 us -> 0.65 us  [swap_first(): lax.ppermute(value, axis, [(n, n ^ 1) for n in range(lax.axis_size(axis))])]
    ppermute x0 -> x2, starting transfers between devices: none -> 1.33 us  [swap_inside(): return lax.ppermute(value, axis, pairs)]
  transfers between devices with their start and end apart: 14 -> 14, of which waited for: 5 -> 1; matrix products, arithmetic and copies ran while one was open for 0% -> 0% of each run, Pallas kernels for 36% -> 35%
where the time goes in v15:
time: 37.2 us; the launch traced here: 37.1 us
  starting transfers between devices  20.9 us (56%)
  Pallas kernels  15.3 us (41%)
  waiting for transfers between devices  0.67 us (2%)
    pallas_call x20, Pallas kernels, call(): pl.pallas_call(body, out_shape=tuple(outs), in_specs=[pl.BlockSpec(memory...  15.3 us
    ppermute x4, starting transfers between devices, swap_second(): return lax.ppermute(value, (axis, other), pairs)  10.7 us
    ppermute x8, starting transfers between devices, swap_first(): lax.ppermute(value, axis, [(n, n ^ 1) for n in range(lax.axis_size(axis))])  8.8 us
    ppermute x2, starting transfers between devices, swap_inside(): return lax.ppermute(value, axis, pairs)  1.33 us
  transfers between devices with their start and end apart: 14, of which 1 were waited for; matrix products, arithmetic and copies ran while one was open for 0% of the time, Pallas kernels for 35%

profile of v15, /device:TPU:0, one launch (start us, length us, event | category | flops | bytes accessed | tf_op | source)
XLA Modules:
  0.0 37.1 jit_solution(13106499809457819140)
XLA Ops:
  0.0 0.0 copy-start
  0.0 1.2 %shard_map.46 = (bf16[2,8,8,9]{3,2,1,0:T(8,128)(2,1)S(1)}, bf16[2,8,8,9]{3,2,1,0:T(8,128)(2,1)S(1)}, f32[2,8]{1,0:T(2,128)S(1)}, bf16[2,256,768]{2,1,0:T(8,128)(...) custom-call(bf16[8,2,4,64,128]{4,3,2,1,0:T(8,128)(2,1)} %x_ref.17, ...), custom_call_target="tpu_custom_call" | custom-call | flops 1000000 | bytes 10000 | tf_op jit(solution)/shard_map/pallas_call | solution.py:29
  1.2 0.5 %collective-permute-start = (bf16[8,2,64,128]{3,2,1,0:T(8,128)(2,1)S(1)}, bf16[8,2,64,128]{3,2,1,0:T(8,128)(2,1)S(1)}, u32[]{:S(2)}, u32[]{:S(2)}) collective-permute-start(bf16[8,2,64,128]{3,2,1,0:T(8,128)(2,1)S(1)} %get-tuple-element.43), channel_id=1, source_target_pairs={{0,2},{2,0},{4,6},{6,4},{1,3},{3,1},{5,7},{7,5},{8,10},{10,8},{12,... | collective-permute-start | bytes 786440 | tf_op jit(solution)/shard_map/ppermute | solution.py:395
  1.7 0.7 %collective-permute-start.1 = (bf16[8,2,64,128]{3,2,1,0:T(8,128)(2,1)S(1)}, bf16[8,2,64,128]{3,2,1,0:T(8,128)(2,1)S(1)}, u32[]{:S(2)}, u32[]{:S(2)}) collective-permute-start(bf16[8,2,64,128]{3,2,1,0:T(8,128)(2,1)S(1)} %get-tuple-element.44), channel_id=1, source_target_pairs={{2,4},{4,2},{3,5},{5,3},{10,12},{12,10},{11,13},{13,11},{18,20},{2... | collective-permute-start | bytes 786440 | tf_op jit(solution)/shard_map/ppermute | solution.py:413
  2.4 0.0 copy-done
  2.4 0.6 %shard_map.47 = (bf16[8,2,64,128]{3,2,1,0:T(8,128)(2,1)S(1)}, bf16[8,2,64,128]{3,2,1,0:T(8,128)(2,1)S(1)}) custom-call(bf16[8,2,4,64,128]{4,3,2,1,0:T(8,128)(2,1)S(1)} %copy-done, bf16[2,256,768]{2,1,0:T(8,128)(2,1)S(1)} %get-tuple-element.45.refs_0_.beside_ref.refs_1_.refs_2_), custom_call_target="tpu_custom_call" | custom-call | flops 1000000 | bytes 10000 | tf_op jit(solution)/shard_map/pallas_call | solution.py:29
  3.0 2.7 %collective-permute-start.5 = (bf16[8,2,64,128]{3,2,1,0:T(8,128)(2,1)S(1)}, bf16[8,2,64,128]{3,2,1,0:T(8,128)(2,1)S(1)}, u32[]{:S(2)}, u32[]{:S(2)}) collective-permute-start(bf16[8,2,64,128]{3,2,1,0:T(8,128)(2,1)S(1)} %get-tuple-element.63), channel_id=1, source_target_pairs={{0,8},{8,0},{16,24},{24,16},{1,9},{9,1},{17,25},{25,17},{2,10},{10... | collective-permute-start | bytes 786440 | tf_op jit(solution)/shard_map/ppermute | solution.py:395
  5.7 2.6 %collective-permute-start.6 = (bf16[8,2,64,128]{3,2,1,0:T(8,128)(2,1)S(1)}, bf16[8,2,64,128]{3,2,1,0:T(8,128)(2,1)S(1)}, u32[]{:S(2)}, u32[]{:S(2)}) collective-permute-start(bf16[8,2,64,128]{3,2,1,0:T(8,128)(2,1)S(1)} %get-tuple-element.46.refs_1_.after_ref), channel_id=1, source_target_pairs={{0,2},{2,0},{4,6},{6,4},{8,16},{10,18},{12,20},{14,22},{16,8},{18,... | collective-permute-start | bytes 786440 | tf_op jit(solution)/shard_map/ppermute | solution.py:408
  8.2 0.4 %shard_map.48 = (f32[2,256,256]{2,1,0:T(8,128)S(1)}, f32[2,256,256]{2,1,0:T(8,128)S(1)}) custom-call(bf16[8,2,4,64,128]{4,3,2,1,0:T(8,128)(2,1)S(1)} %copy-done, bf16[2,256,768]{2,1,0:T(8,128)(2,1)S(1)} %get-tuple-element.45.refs_0_.beside_ref.refs_1_.refs_2_, bf16[8,2,64,128]{3,2,1,0:T(8,128)(2,1)S(1)} %get-tuple-element.46.refs_1_.after_ref), custom_call_target="tpu_custom_call" | custom-call | flops 1000000 | bytes 10000 | tf_op jit(solution)/shard_map/pallas_call | solution.py:29
  8.6 1.1 %shard_map.49 = (bf16[256,768]{1,0:T(8,128)(2,1)S(1)}, bf16[256,768]{1,0:T(8,128)(2,1)S(1)}, bf16[2,256,384]{2,1,0:T(8,128)(2,1)S(1)}, bf16[2,256,24]{2,1,0:T(8,...) custom-call(bf16[2,8,8,9]{3,2,1,0:T(8,128)(2,1)S(1)} %get-tuple-elem, ...), custom_call_target="tpu_custom_call" | custom-call | flops 1000000 | bytes 10000 | tf_op jit(solution)/shard_map/pallas_call | solution.py:29
  9.8 0.0 collective-permute-done.cola_ref
  9.8 0.0 collective-permute-done.1.colb_ref
  9.8 0.4 %shard_map.50 = (bf16[8,2,64,128]{3,2,1,0:T(8,128)(2,1)S(1)}, bf16[8,2,64,128]{3,2,1,0:T(8,128)(2,1)S(1)}, bf16[2,8,2,64,128]{4,3,2,1,0:T(8,128)(2,1)S(1)}) custom-call(bf16[8,2,64,128]{3,2,1,0:T(8,128)(2,1)S(1)} %collective-permute-done.cola_ref, bf16[8,2,64,128]{3,2,1,0:T(8,128)(2,1)S(1)} %collective-permute-done.1.colb_ref, ...), custom_call_target="tpu_custom_call" | custom-call | flops 1000000 | bytes 10000 | tf_op jit(solution)/shard_map/pallas_call | solution.py:29
  10.2 0.7 %collective-permute-start.4 = (bf16[8,2,64,128]{3,2,1,0:T(8,128)(2,1)S(1)}, bf16[8,2,64,128]{3,2,1,0:T(8,128)(2,1)S(1)}, u32[]{:S(2)}, u32[]{:S(2)}) collective-permute-start(bf16[8,2,64,128]{3,2,1,0:T(8,128)(2,1)S(1)} %get-tuple-element.61), channel_id=1, source_target_pairs={{0,8},{8,0},{16,24},{24,16},{1,9},{9,1},{17,25},{25,17},{2,10},{10... | collective-permute-start | bytes 786440 | tf_op jit(solution)/shard_map/ppermute | solution.py:395
  10.8 2.1 %collective-permute-start.3 = (bf16[8,2,64,128]{3,2,1,0:T(8,128)(2,1)S(1)}, bf16[8,2,64,128]{3,2,1,0:T(8,128)(2,1)S(1)}, u32[]{:S(2)}, u32[]{:S(2)}) collective-permute-start(bf16[8,2,64,128]{3,2,1,0:T(8,128)(2,1)S(1)} %get-tuple-element.57.refs_5_.refs_0_), channel_id=1, source_target_pairs={{0,2},{2,0},{4,6},{6,4},{8,16},{10,18},{12,20},{14,22},{16,8},{18,... | collective-permute-start | bytes 786440 | tf_op jit(solution)/shard_map/ppermute | solution.py:408
  12.9 0.2 shard_map.52
  13.1 1.5 %collective-permute-start.2 = (bf16[2,8,512]{2,1,0:T(8,128)(2,1)S(1)}, bf16[2,8,512]{2,1,0:T(8,128)(2,1)S(1)}, u32[]{:S(2)}, u32[]{:S(2)}) collective-permute-start(bf16[2,8,512]{2,1,0:T(8,128)(2,1)S(1)} %shard_map.52), channel_id=1, source_target_pairs={{0,1},{1,0},{2,3},{3,2},{4,5},{5,4},{6,7},{7,6},{8,9},{9,8},{10,11... | collective-permute-start | bytes 49160 | tf_op jit(solution)/shard_map/ppermute | solution.py:395
  14.6 2.5 %shard_map.51 = (f32[8,2,2,64,128]{4,3,2,1,0:T(8,128)S(1)}, f32[8,2,2,64,128]{4,3,2,1,0:T(8,128)S(1)}) custom-call(bf16[8,2,4,64,128]{4,3,2,1,0:T(8,128)(2,1)S(1)} %copy-done, bf16[256,768]{1,0:T(8,128)(2,1)S(1)} %get-tuple-element.51.after_ref.refs_0_.refs_1_, bf16[2,256,768]{2,1,0:T(8,128)(2,1)S(1)} %get-tuple-element.45.refs_0_.beside_ref.refs_1_.refs_2_, ...), custom_call_target="tpu_custom_call" | custom-call | flops 1000000 | bytes 10000 | tf_op jit(solution)/shard_map/pallas_call | solution.py:29
  17.1 0.0 collective-permute-done.2.refs_6_
  17.2 1.1 %shard_map.53 = (f32[8,2,2,64,128]{4,3,2,1,0:T(8,128)S(1)}, f32[8,2,2,64,128]{4,3,2,1,0:T(8,128)S(1)}) custom-call(bf16[8,2,4,64,128]{4,3,2,1,0:T(8,128)(2,1)S(1)} %copy-done, bf16[2,8,2,64,128]{4,3,2,1,0:T(8,128)(2,1)S(1)} %get-tuple-element.52.refs_0_, ...), custom_call_target="tpu_custom_call", output_to_operand_aliasing={{0}: (5, {}), {1}: (6, {})} | custom-call | flops 1000000 | bytes 10000 | tf_op jit(solution)/shard_map/pallas_call | solution.py:29
  18.3 0.0 collective-permute-done.5.refs_1_
  18.3 0.0 collective-permute-done.6.refs_2_
  18.3 0.2 shard_map.54.refs_2_.mid_ref.x_ref
  18.6 0.6 %collective-permute-done.4.refs_1_ = bf16[8,2,64,128]{3,2,1,0:T(8,128)(2,1)S(1)} collective-permute-done((bf16[8,2,64,128]{3,2,1,0:T(8,128)(2,1)S(1)}, bf16[8,2,64,128]{3,2,1,0:T(8,128)(2,1)S(1)}, u32[]{:S(2)}, u32[]{:S(2)}) %collective-permute-start.4) | collective-permute-done | bytes 262176 | tf_op jit(solution)/shard_map/ppermute | solution.py:395
  19.2 0.1 shard_map.55.rim_ref.refs_2_
  19.3 0.4 %shard_map.56.refs_3_ = bf16[8,2,64,128]{3,2,1,0:T(8,128)(2,1)S(1)} custom-call(bf16[8,2,2,64,128]{4,3,2,1,0:T(8,128)(2,1)S(1)} %shard_map.54.refs_2_.mid_ref.x_ref, bf16[8,2,2,64,128]{4,3,2,1,0:T(8,128)(2,1)S(1)} %shard_map.55.rim_ref.refs_2_, bf16[2,256,768]{2,1,0:T(8,128)(2,1)S(1)} %get-tuple-element.64.beside_ref), custom_call_target="tpu_custom_call" | custom-call | flops 1000000 | bytes 10000 | tf_op jit(solution)/shard_map/pallas_call | solution.py:29
  19.7 0.0 collective-permute-done.3.refs_1_
  19.7 0.2 shard_map.57
  19.9 0.2 collective-permute-start.7
  20.1 0.7 %collective-permute-start.8 = (bf16[8,2,64,128]{3,2,1,0:T(8,128)(2,1)S(1)}, bf16[8,2,64,128]{3,2,1,0:T(8,128)(2,1)S(1)}, u32[]{:S(2)}, u32[]{:S(2)}) collective-permute-start(bf16[8,2,64,128]{3,2,1,0:T(8,128)(2,1)S(1)} %get-tuple-element.67), channel_id=1, source_target_pairs={{2,4},{4,2},{3,5},{5,3},{10,12},{12,10},{11,13},{13,11},{18,20},{2... | collective-permute-start | bytes 786440 | tf_op jit(solution)/shard_map/ppermute | solution.py:413
  20.8 1.9 %collective-permute-start.12 = (bf16[8,2,64,128]{3,2,1,0:T(8,128)(2,1)S(1)}, bf16[8,2,64,128]{3,2,1,0:T(8,128)(2,1)S(1)}, u32[]{:S(2)}, u32[]{:S(2)}) collective-permute-start(bf16[8,2,64,128]{3,2,1,0:T(8,128)(2,1)S(1)} %shard_map.56.refs_3_), channel_id=1, source_target_pairs={{0,8},{8,0},{16,24},{24,16},{1,9},{9,1},{17,25},{25,17},{2,10},{10... | collective-permute-start | bytes 786440 | tf_op jit(solution)/shard_map/ppermute | solution.py:395
  22.7 0.4 shard_map.58.after_ref
  23.1 2.7 %collective-permute-start.13 = (bf16[8,2,64,128]{3,2,1,0:T(8,128)(2,1)S(1)}, bf16[8,2,64,128]{3,2,1,0:T(8,128)(2,1)S(1)}, u32[]{:S(2)}, u32[]{:S(2)}) collective-permute-start(bf16[8,2,64,128]{3,2,1,0:T(8,128)(2,1)S(1)} %shard_map.58.after_ref), channel_id=1, source_target_pairs={{0,2},{2,0},{4,6},{6,4},{8,16},{10,18},{12,20},{14,22},{16,8},{18,... | collective-permute-start | bytes 786440 | tf_op jit(solution)/shard_map/ppermute | solution.py:408
  25.8 0.4 %shard_map.59 = (f32[2,256,256]{2,1,0:T(8,128)S(1)}, f32[2,256,256]{2,1,0:T(8,128)S(1)}) custom-call(bf16[8,2,2,64,128]{4,3,2,1,0:T(8,128)(2,1)S(1)} %shard_map.54.refs_2_.mid_ref.x_ref, bf16[8,2,2,64,128]{4,3,2,1,0:T(8,128)(2,1)S(1)} %get-tuple-element.65.rim_ref.x_ref, bf16[2,256,768]{2,1,0:T(8,128)(2,1)S(1)} %get-tuple-element.64.beside_ref, ...), custom_call_target="tpu_custom_call" | custom-call | flops 1000000 | bytes 10000 | tf_op jit(solution)/shard_map/pallas_call | solution.py:29
  26.2 0.0 collective-permute-done.7.cola_ref
  26.2 0.0 collective-permute-done.8.colb_ref
  26.2 0.4 %shard_map.60 = (bf16[8,2,64,128]{3,2,1,0:T(8,128)(2,1)S(1)}, bf16[8,2,64,128]{3,2,1,0:T(8,128)(2,1)S(1)}, bf16[2,8,2,64,128]{4,3,2,1,0:T(8,128)(2,1)S(1)}) custom-call(bf16[8,2,64,128]{3,2,1,0:T(8,128)(2,1)S(1)} %collective-permute-done.7.cola_ref, bf16[8,2,64,128]{3,2,1,0:T(8,128)(2,1)S(1)} %collective-permute-done.8.colb_ref, ...), custom_call_target="tpu_custom_call" | custom-call | flops 1000000 | bytes 10000 | tf_op jit(solution)/shard_map/pallas_call | solution.py:29
  26.6 0.1 collective-permute-start.10
  26.7 3.4 %collective-permute-start.11 = (bf16[8,2,64,128]{3,2,1,0:T(8,128)(2,1)S(1)}, bf16[8,2,64,128]{3,2,1,0:T(8,128)(2,1)S(1)}, u32[]{:S(2)}, u32[]{:S(2)}) collective-permute-start(bf16[8,2,64,128]{3,2,1,0:T(8,128)(2,1)S(1)} %get-tuple-element.75.after_ref), channel_id=1, source_target_pairs={{0,2},{2,0},{4,6},{6,4},{8,16},{10,18},{12,20},{14,22},{16,8},{18,... | collective-permute-start | bytes 786440 | tf_op jit(solution)/shard_map/ppermute | solution.py:408
  30.1 0.2 shard_map.62
  30.3 1.3 %collective-permute-start.9 = (bf16[2,8,512]{2,1,0:T(8,128)(2,1)S(1)}, bf16[2,8,512]{2,1,0:T(8,128)(2,1)S(1)}, u32[]{:S(2)}, u32[]{:S(2)}) collective-permute-start(bf16[2,8,512]{2,1,0:T(8,128)(2,1)S(1)} %shard_map.62), channel_id=1, source_target_pairs={{0,1},{1,0},{2,3},{3,2},{4,5},{5,4},{6,7},{7,6},{8,9},{9,8},{10,11... | collective-permute-start | bytes 49160 | tf_op jit(solution)/shard_map/ppermute | solution.py:395
  31.5 2.5 %shard_map.61 = (f32[8,2,2,64,128]{4,3,2,1,0:T(8,128)S(1)}, f32[8,2,2,64,128]{4,3,2,1,0:T(8,128)S(1)}) custom-call(bf16[8,2,2,64,128]{4,3,2,1,0:T(8,128)(2,1)S(1)} %shard_map.54.refs_2_.mid_ref.x_ref, bf16[8,2,2,64,128]{4,3,2,1,0:T(8,128)(2,1)S(1)} %get-tuple-element.65.rim_ref.x_ref, bf16[256,768]{1,0:T(8,128)(2,1)S(1)} %get-tuple-element.70.after_ref.middle_ref, ...), custom_call_target="tpu_custom_call" | custom-call | flops 1000000 | bytes 10000 | tf_op jit(solution)/shard_map/pallas_call | solution.py:29
  34.1 0.0 collective-permute-done.9.rest_0_
  34.1 1.1 %shard_map.63 = (f32[8,2,2,64,128]{4,3,2,1,0:T(8,128)S(1)}, f32[8,2,2,64,128]{4,3,2,1,0:T(8,128)S(1)}) custom-call(bf16[8,2,2,64,128]{4,3,2,1,0:T(8,128)(2,1)S(1)} %shard_map.54.refs_2_.mid_ref.x_ref, bf16[8,2,2,64,128]{4,3,2,1,0:T(8,128)(2,1)S(1)} %get-tuple-element.65.rim_ref.x_ref, ...), custom_call_target="tpu_custom_call", output_to_operand_aliasing={{0}: (6, {}), {1}: (7, {})} | custom-call | flops 1000000 | bytes 10000 | tf_op jit(solution)/shard_map/pallas_call | solution.py:29
  35.2 0.0 collective-permute-done.13.b_ref
  35.2 0.0 collective-permute-done.12.a_ref
  35.2 0.9 %shard_map.64.refs_0_ = bf16[8,2,4,64,128]{4,3,2,1,0:T(8,128)(2,1)} custom-call(bf16[8,2,2,64,128]{4,3,2,1,0:T(8,128)(2,1)S(1)} %shard_map.54.refs_2_.mid_ref.x_ref, f32[8,2,2,64,128]{4,3,2,1,0:T(8,128)S(1)} %get-tuple-element.80.acc_ref, bf16[8,2,64,128]{3,2,1,0:T(8,128)(2,1)S(1)} %collective-permute-done.12.a_ref, ...), custom_call_target="tpu_custom_call" | custom-call | flops 1000000 | bytes 10000 | tf_op jit(solution)/shard_map/pallas_call | solution.py:29
  36.1 0.0 collective-permute-done.10.a_ref
  36.1 0.0 collective-permute-done.11.b_ref
  36.2 0.9 %shard_map.65 = bf16[8,2,4,64,128]{4,3,2,1,0:T(8,128)(2,1)} custom-call(bf16[8,2,2,64,128]{4,3,2,1,0:T(8,128)(2,1)S(1)} %get-tuple-element.65.rim_ref.x_ref, f32[8,2,2,64,128]{4,3,2,1,0:T(8,128)S(1)} %get-tuple-element.78.acc_ref, bf16[8,2,64,128]{3,2,1,0:T(8,128)(2,1)S(1)} %collective-permute-done.10.a_ref, ...), custom_call_target="tpu_custom_call", output_to_operand_aliasing={{}: (4, {})} | custom-call | flops 1000000 | bytes 10000 | tf_op jit(solution)/shard_map/pallas_call | solution.py:29
Async XLA Ops:
  0.0 2.4 %copy-start = (bf16[8,2,4,64,128]{4,3,2,1,0:T(8,128)(2,1)S(1)}, bf16[8,2,4,64,128]{4,3,2,1,0:T(8,128)(2,1)}, u32[]{:S(2)}) copy-start(bf16[8,2,4,64,128]{4,3,2,1,0:T(8,128)(2,1)} %x_ref.17) | copy-start | bytes 3145732
  1.2 8.6 %collective-permute-start = (bf16[8,2,64,128]{3,2,1,0:T(8,128)(2,1)S(1)}, bf16[8,2,64,128]{3,2,1,0:T(8,128)(2,1)S(1)}, u32[]{:S(2)}, u32[]{:S(2)}) collective-permute-start(bf16[8,2,64,128]{3,2,1,0:T(8,128)(2,1)S(1)} %get-tuple-element.43), channel_id=1, source_target_pairs={{0,2},{2,0},{4,6},{6,4},{1,3},{3,1},{5,7},{7,5},{8,10},{10,8},{12,... | collective-permute-start | bytes 786440 | tf_op jit(solution)/shard_map/ppermute | solution.py:395
  1.7 8.1 %collective-permute-start.1 = (bf16[8,2,64,128]{3,2,1,0:T(8,128)(2,1)S(1)}, bf16[8,2,64,128]{3,2,1,0:T(8,128)(2,1)S(1)}, u32[]{:S(2)}, u32[]{:S(2)}) collective-permute-start(bf16[8,2,64,128]{3,2,1,0:T(8,128)(2,1)S(1)} %get-tuple-element.44), channel_id=1, source_target_pairs={{2,4},{4,2},{3,5},{5,3},{10,12},{12,10},{11,13},{13,11},{18,20},{2... | collective-permute-start | bytes 786440 | tf_op jit(solution)/shard_map/ppermute | solution.py:413
  3.0 15.3 %collective-permute-start.5 = (bf16[8,2,64,128]{3,2,1,0:T(8,128)(2,1)S(1)}, bf16[8,2,64,128]{3,2,1,0:T(8,128)(2,1)S(1)}, u32[]{:S(2)}, u32[]{:S(2)}) collective-permute-start(bf16[8,2,64,128]{3,2,1,0:T(8,128)(2,1)S(1)} %get-tuple-element.63), channel_id=1, source_target_pairs={{0,8},{8,0},{16,24},{24,16},{1,9},{9,1},{17,25},{25,17},{2,10},{10... | collective-permute-start | bytes 786440 | tf_op jit(solution)/shard_map/ppermute | solution.py:395
  5.7 12.7 %collective-permute-start.6 = (bf16[8,2,64,128]{3,2,1,0:T(8,128)(2,1)S(1)}, bf16[8,2,64,128]{3,2,1,0:T(8,128)(2,1)S(1)}, u32[]{:S(2)}, u32[]{:S(2)}) collective-permute-start(bf16[8,2,64,128]{3,2,1,0:T(8,128)(2,1)S(1)} %get-tuple-element.46.refs_1_.after_ref), channel_id=1, source_target_pairs={{0,2},{2,0},{4,6},{6,4},{8,16},{10,18},{12,20},{14,22},{16,8},{18,... | collective-permute-start | bytes 786440 | tf_op jit(solution)/shard_map/ppermute | solution.py:408
  10.2 9.0 %collective-permute-start.4 = (bf16[8,2,64,128]{3,2,1,0:T(8,128)(2,1)S(1)}, bf16[8,2,64,128]{3,2,1,0:T(8,128)(2,1)S(1)}, u32[]{:S(2)}, u32[]{:S(2)}) collective-permute-start(bf16[8,2,64,128]{3,2,1,0:T(8,128)(2,1)S(1)} %get-tuple-element.61), channel_id=1, source_target_pairs={{0,8},{8,0},{16,24},{24,16},{1,9},{9,1},{17,25},{25,17},{2,10},{10... | collective-permute-start | bytes 786440 | tf_op jit(solution)/shard_map/ppermute | solution.py:395
  10.8 8.8 %collective-permute-start.3 = (bf16[8,2,64,128]{3,2,1,0:T(8,128)(2,1)S(1)}, bf16[8,2,64,128]{3,2,1,0:T(8,128)(2,1)S(1)}, u32[]{:S(2)}, u32[]{:S(2)}) collective-permute-start(bf16[8,2,64,128]{3,2,1,0:T(8,128)(2,1)S(1)} %get-tuple-element.57.refs_5_.refs_0_), channel_id=1, source_target_pairs={{0,2},{2,0},{4,6},{6,4},{8,16},{10,18},{12,20},{14,22},{16,8},{18,... | collective-permute-start | bytes 786440 | tf_op jit(solution)/shard_map/ppermute | solution.py:408
  13.1 4.0 %collective-permute-start.2 = (bf16[2,8,512]{2,1,0:T(8,128)(2,1)S(1)}, bf16[2,8,512]{2,1,0:T(8,128)(2,1)S(1)}, u32[]{:S(2)}, u32[]{:S(2)}) collective-permute-start(bf16[2,8,512]{2,1,0:T(8,128)(2,1)S(1)} %shard_map.52), channel_id=1, source_target_pairs={{0,1},{1,0},{2,3},{3,2},{4,5},{5,4},{6,7},{7,6},{8,9},{9,8},{10,11... | collective-permute-start | bytes 49160 | tf_op jit(solution)/shard_map/ppermute | solution.py:395
  19.9 6.3 %collective-permute-start.7 = (bf16[8,2,64,128]{3,2,1,0:T(8,128)(2,1)S(1)}, bf16[8,2,64,128]{3,2,1,0:T(8,128)(2,1)S(1)}, u32[]{:S(2)}, u32[]{:S(2)}) collective-permute-start(bf16[8,2,64,128]{3,2,1,0:T(8,128)(2,1)S(1)} %get-tuple-element.66), channel_id=1, source_target_pairs={{0,2},{2,0},{4,6},{6,4},{1,3},{3,1},{5,7},{7,5},{8,10},{10,8},{12,... | collective-permute-start | bytes 786440 | tf_op jit(solution)/shard_map/ppermute | solution.py:395
  20.1 6.1 %collective-permute-start.8 = (bf16[8,2,64,128]{3,2,1,0:T(8,128)(2,1)S(1)}, bf16[8,2,64,128]{3,2,1,0:T(8,128)(2,1)S(1)}, u32[]{:S(2)}, u32[]{:S(2)}) collective-permute-start(bf16[8,2,64,128]{3,2,1,0:T(8,128)(2,1)S(1)} %get-tuple-element.67), channel_id=1, source_target_pairs={{2,4},{4,2},{3,5},{5,3},{10,12},{12,10},{11,13},{13,11},{18,20},{2... | collective-permute-start | bytes 786440 | tf_op jit(solution)/shard_map/ppermute | solution.py:413
  20.8 14.4 %collective-permute-start.12 = (bf16[8,2,64,128]{3,2,1,0:T(8,128)(2,1)S(1)}, bf16[8,2,64,128]{3,2,1,0:T(8,128)(2,1)S(1)}, u32[]{:S(2)}, u32[]{:S(2)}) collective-permute-start(bf16[8,2,64,128]{3,2,1,0:T(8,128)(2,1)S(1)} %shard_map.56.refs_3_), channel_id=1, source_target_pairs={{0,8},{8,0},{16,24},{24,16},{1,9},{9,1},{17,25},{25,17},{2,10},{10... | collective-permute-start | bytes 786440 | tf_op jit(solution)/shard_map/ppermute | solution.py:395
  23.1 12.1 %collective-permute-start.13 = (bf16[8,2,64,128]{3,2,1,0:T(8,128)(2,1)S(1)}, bf16[8,2,64,128]{3,2,1,0:T(8,128)(2,1)S(1)}, u32[]{:S(2)}, u32[]{:S(2)}) collective-permute-start(bf16[8,2,64,128]{3,2,1,0:T(8,128)(2,1)S(1)} %shard_map.58.after_ref), channel_id=1, source_target_pairs={{0,2},{2,0},{4,6},{6,4},{8,16},{10,18},{12,20},{14,22},{16,8},{18,... | collective-permute-start | bytes 786440 | tf_op jit(solution)/shard_map/ppermute | solution.py:408
  26.6 9.5 %collective-permute-start.10 = (bf16[8,2,64,128]{3,2,1,0:T(8,128)(2,1)S(1)}, bf16[8,2,64,128]{3,2,1,0:T(8,128)(2,1)S(1)}, u32[]{:S(2)}, u32[]{:S(2)}) collective-permute-start(bf16[8,2,64,128]{3,2,1,0:T(8,128)(2,1)S(1)} %get-tuple-element.79), channel_id=1, source_target_pairs={{0,8},{8,0},{16,24},{24,16},{1,9},{9,1},{17,25},{25,17},{2,10},{10... | collective-permute-start | bytes 786440 | tf_op jit(solution)/shard_map/ppermute | solution.py:395
  26.7 9.4 %collective-permute-start.11 = (bf16[8,2,64,128]{3,2,1,0:T(8,128)(2,1)S(1)}, bf16[8,2,64,128]{3,2,1,0:T(8,128)(2,1)S(1)}, u32[]{:S(2)}, u32[]{:S(2)}) collective-permute-start(bf16[8,2,64,128]{3,2,1,0:T(8,128)(2,1)S(1)} %get-tuple-element.75.after_ref), channel_id=1, source_target_pairs={{0,2},{2,0},{4,6},{6,4},{8,16},{10,18},{12,20},{14,22},{16,8},{18,... | collective-permute-start | bytes 786440 | tf_op jit(solution)/shard_map/ppermute | solution.py:408
  30.3 3.8 %collective-permute-start.9 = (bf16[2,8,512]{2,1,0:T(8,128)(2,1)S(1)}, bf16[2,8,512]{2,1,0:T(8,128)(2,1)S(1)}, u32[]{:S(2)}, u32[]{:S(2)}) collective-permute-start(bf16[2,8,512]{2,1,0:T(8,128)(2,1)S(1)} %shard_map.62), channel_id=1, source_target_pairs={{0,1},{1,0},{2,3},{3,2},{4,5},{5,4},{6,7},{7,6},{8,9},{9,8},{10,11... | collective-permute-start | bytes 49160 | tf_op jit(solution)/shard_map/ppermute | solution.py:395

commit v16 on v13

--- a/solution.py
+++ b/solution.py
@@ -444,9 +444,8 @@
         sums = call(on(functools.partial(inner_body, which), *both), owed_inner * len(which), (*block, made["beside", layer]))
         sum_b = sums[-1]
         inner = swap_first(sums[0], "srow") if sum_a is None else got_a, swap_second(sum_b, "srow", "scol")
-        if layer == 0:
-            late = [(kind, n) for n in range(layers) for kind in kinds]
-            made |= build([part for part in late if part not in early], src_w, tgt_w, sum_b)
+        late = [(kind, layer) for kind in kinds] + [("beside", n) for n in range(layer + 1, min(layer + 2, layers))]
+        made |= build([part for part in late if part not in made], src_w, tgt_w, sum_b)
         operator = {kind: made[kind, layer] for kind in kinds}
         parts = call(
             on(part_body, *both),

time: 36.5 us -> 36.5 us (level)
    pallas_call x20 -> x21, Pallas kernels: 15.3 us -> 15.3 us  [call(): pl.pallas_call(body, out_shape=tuple(outs), in_specs=[pl.BlockSpec(memory...]
  transfers between devices with their start and end apart: 14 -> 14, of which waited for: 5 -> 4; matrix products, arithmetic and copies ran while one was open for 0% -> 0% of each run, Pallas kernels for 36% -> 36%
where the time goes in v16:
time: 36.5 us; the launch traced here: 36.4 us
  starting transfers between devices  15.9 us (44%)
  Pallas kernels  15.3 us (42%)
  waiting for transfers between devices  4.99 us (14%)
    pallas_call x21, Pallas kernels, call(): pl.pallas_call(body, out_shape=tuple(outs), in_specs=[pl.BlockSpec(memory...  15.3 us
    ppermute x8, starting transfers between devices, swap_first(): lax.ppermute(value, axis, [(n, n ^ 1) for n in range(lax.axis_size(axis))])  12.2 us
    ppermute x6, starting transfers between devices, swap_second(): return lax.ppermute(value, (axis, other), pairs)  3.71 us
    ppermute x8, waiting for transfers between devices, swap_first(): lax.ppermute(value, axis, [(n, n ^ 1) for n in range(lax.axis_size(axis))])  2.58 us
    ppermute x6, waiting for transfers between devices, swap_second(): return lax.ppermute(value, (axis, other), pairs)  2.41 us
  transfers between devices with their start and end apart: 14, of which 4 were waited for; matrix products, arithmetic and copies ran while one was open for 0% of the time, Pallas kernels for 36%

profile of v16, /device:TPU:0, one launch (start us, length us, event | category | flops | bytes accessed | tf_op | source)
XLA Modules:
  0.0 36.4 jit_solution(10609728692458862179)
XLA Ops:
  0.0 0.0 copy-start
  0.0 1.2 %shard_map.46 = (bf16[2,8,8,9]{3,2,1,0:T(8,128)(2,1)S(1)}, bf16[2,8,8,9]{3,2,1,0:T(8,128)(2,1)S(1)}, f32[2,8]{1,0:T(2,128)S(1)}, bf16[2,256,768]{2,1,0:T(8,128)(...) custom-call(bf16[8,2,4,64,128]{4,3,2,1,0:T(8,128)(2,1)} %x_ref.17, ...), custom_call_target="tpu_custom_call" | custom-call | flops 1000000 | bytes 10000 | tf_op jit(solution)/shard_map/pallas_call | solution.py:29
  1.2 0.5 %collective-permute-start = (bf16[8,2,64,128]{3,2,1,0:T(8,128)(2,1)S(1)}, bf16[8,2,64,128]{3,2,1,0:T(8,128)(2,1)S(1)}, u32[]{:S(2)}, u32[]{:S(2)}) collective-permute-start(bf16[8,2,64,128]{3,2,1,0:T(8,128)(2,1)S(1)} %get-tuple-element.43), channel_id=1, source_target_pairs={{0,2},{2,0},{4,6},{6,4},{1,3},{3,1},{5,7},{7,5},{8,10},{10,8},{12,... | collective-permute-start | bytes 786440 | tf_op jit(solution)/shard_map/ppermute | solution.py:395
  1.7 2.6 %collective-permute-start.1 = (bf16[8,2,64,128]{3,2,1,0:T(8,128)(2,1)S(1)}, bf16[8,2,64,128]{3,2,1,0:T(8,128)(2,1)S(1)}, u32[]{:S(2)}, u32[]{:S(2)}) collective-permute-start(bf16[8,2,64,128]{3,2,1,0:T(8,128)(2,1)S(1)} %get-tuple-element.44), channel_id=1, source_target_pairs={{0,1},{1,0},{2,4},{3,5},{4,2},{5,3},{6,7},{7,6},{8,9},{9,8},{10,12... | collective-permute-start | bytes 786440 | tf_op jit(solution)/shard_map/ppermute | solution.py:408
  4.3 0.0 copy-done
  4.3 0.6 %shard_map.47 = (bf16[8,2,64,128]{3,2,1,0:T(8,128)(2,1)S(1)}, bf16[8,2,64,128]{3,2,1,0:T(8,128)(2,1)S(1)}) custom-call(bf16[8,2,4,64,128]{4,3,2,1,0:T(8,128)(2,1)S(1)} %copy-done, bf16[2,256,768]{2,1,0:T(8,128)(2,1)S(1)} %get-tuple-element.45.refs_0_.beside_ref.refs_1_.refs_2_), custom_call_target="tpu_custom_call" | custom-call | flops 1000000 | bytes 10000 | tf_op jit(solution)/shard_map/pallas_call | solution.py:29
  4.9 1.6 %collective-permute-start.5 = (bf16[8,2,64,128]{3,2,1,0:T(8,128)(2,1)S(1)}, bf16[8,2,64,128]{3,2,1,0:T(8,128)(2,1)S(1)}, u32[]{:S(2)}, u32[]{:S(2)}) collective-permute-start(bf16[8,2,64,128]{3,2,1,0:T(8,128)(2,1)S(1)} %get-tuple-element.63), channel_id=1, source_target_pairs={{0,8},{8,0},{16,24},{24,16},{1,9},{9,1},{17,25},{25,17},{2,10},{10... | collective-permute-start | bytes 786440 | tf_op jit(solution)/shard_map/ppermute | solution.py:395
  6.5 0.0 collective-permute-start.6
  6.5 0.4 %shard_map.48 = (f32[2,256,256]{2,1,0:T(8,128)S(1)}, f32[2,256,256]{2,1,0:T(8,128)S(1)}) custom-call(bf16[8,2,4,64,128]{4,3,2,1,0:T(8,128)(2,1)S(1)} %copy-done, bf16[2,256,768]{2,1,0:T(8,128)(2,1)S(1)} %get-tuple-element.45.refs_0_.beside_ref.refs_1_.refs_2_, bf16[8,2,64,128]{3,2,1,0:T(8,128)(2,1)S(1)} %get-tuple-element.46.refs_1_.after_ref), custom_call_target="tpu_custom_call" | custom-call | flops 1000000 | bytes 10000 | tf_op jit(solution)/shard_map/pallas_call | solution.py:29
  7.0 0.6 %shard_map.49 = (bf16[256,768]{1,0:T(8,128)(2,1)S(1)}, bf16[256,768]{1,0:T(8,128)(2,1)S(1)}, bf16[2,256,384]{2,1,0:T(8,128)(2,1)S(1)}, bf16[2,256,24]{2,1,0:T(8,128)(2,1)S(1)}, bf16[2,256,768]{2,1,0:T(8,128)(2,1)S(1)}) custom-call(bf16[2,8,8,9]{3,2,1,0:T(8,128)(2,1)S(1)} %get-tuple-element.49.src_w_ref, ...), custom_call_target="tpu_custom_call" | custom-call | flops 1000000 | bytes 10000 | tf_op jit(solution)/shard_map/pallas_call | solution.py:29
  7.6 0.0 collective-permute-done.cola_ref
  7.6 1.1 %collective-permute-done.1.colb_ref = bf16[8,2,64,128]{3,2,1,0:T(8,128)(2,1)S(1)} collective-permute-done((bf16[8,2,64,128]{3,2,1,0:T(8,128)(2,1)S(1)}, bf16[8,2,64,128]{3,2,1,0:T(8,128)(2,1)S(1)}, u32[]{:S(2)}, u32[]{:S(2)}) %collective-permute-start.1) | collective-permute-done | bytes 262176 | tf_op jit(solution)/shard_map/ppermute | solution.py:408
  8.7 0.4 %shard_map.50 = (bf16[8,2,64,128]{3,2,1,0:T(8,128)(2,1)S(1)}, bf16[8,2,64,128]{3,2,1,0:T(8,128)(2,1)S(1)}, bf16[2,8,2,64,128]{4,3,2,1,0:T(8,128)(2,1)S(1)}) custom-call(bf16[8,2,64,128]{3,2,1,0:T(8,128)(2,1)S(1)} %collective-permute-done.cola_ref, bf16[8,2,64,128]{3,2,1,0:T(8,128)(2,1)S(1)} %collective-permute-done.1.colb_ref, ...), custom_call_target="tpu_custom_call" | custom-call | flops 1000000 | bytes 10000 | tf_op jit(solution)/shard_map/pallas_call | solution.py:29
  9.0 2.2 %collective-permute-start.4 = (bf16[8,2,64,128]{3,2,1,0:T(8,128)(2,1)S(1)}, bf16[8,2,64,128]{3,2,1,0:T(8,128)(2,1)S(1)}, u32[]{:S(2)}, u32[]{:S(2)}) collective-permute-start(bf16[8,2,64,128]{3,2,1,0:T(8,128)(2,1)S(1)} %get-tuple-element.61), channel_id=1, source_target_pairs={{0,8},{8,0},{16,24},{24,16},{1,9},{9,1},{17,25},{25,17},{2,10},{10... | collective-permute-start | bytes 786440 | tf_op jit(solution)/shard_map/ppermute | solution.py:395
  11.2 0.0 collective-permute-start.3
  11.2 0.2 shard_map.52
  11.4 1.5 %collective-permute-start.2 = (bf16[2,8,512]{2,1,0:T(8,128)(2,1)S(1)}, bf16[2,8,512]{2,1,0:T(8,128)(2,1)S(1)}, u32[]{:S(2)}, u32[]{:S(2)}) collective-permute-start(bf16[2,8,512]{2,1,0:T(8,128)(2,1)S(1)} %shard_map.52), channel_id=1, source_target_pairs={{0,1},{1,0},{2,3},{3,2},{4,5},{5,4},{6,7},{7,6},{8,9},{9,8},{10,11... | collective-permute-start | bytes 49160 | tf_op jit(solution)/shard_map/ppermute | solution.py:395
  12.9 2.5 %shard_map.51 = (f32[8,2,2,64,128]{4,3,2,1,0:T(8,128)S(1)}, f32[8,2,2,64,128]{4,3,2,1,0:T(8,128)S(1)}) custom-call(bf16[8,2,4,64,128]{4,3,2,1,0:T(8,128)(2,1)S(1)} %copy-done, bf16[256,768]{1,0:T(8,128)(2,1)S(1)} %get-tuple-element.51.after_ref.refs_0_.refs_1_, bf16[2,256,768]{2,1,0:T(8,128)(2,1)S(1)} %get-tuple-element.45.refs_0_.beside_ref.refs_1_.refs_2_, ...), custom_call_target="tpu_custom_call" | custom-call | flops 1000000 | bytes 10000 | tf_op jit(solution)/shard_map/pallas_call | solution.py:29
  15.4 0.0 collective-permute-done.2.refs_6_
  15.4 1.1 %shard_map.53 = (f32[8,2,2,64,128]{4,3,2,1,0:T(8,128)S(1)}, f32[8,2,2,64,128]{4,3,2,1,0:T(8,128)S(1)}) custom-call(bf16[8,2,4,64,128]{4,3,2,1,0:T(8,128)(2,1)S(1)} %copy-done, bf16[2,8,2,64,128]{4,3,2,1,0:T(8,128)(2,1)S(1)} %get-tuple-element.52.refs_0_, ...), custom_call_target="tpu_custom_call", output_to_operand_aliasing={{0}: (5, {}), {1}: (6, {})} | custom-call | flops 1000000 | bytes 10000 | tf_op jit(solution)/shard_map/pallas_call | solution.py:29
  16.6 0.0 collective-permute-done.5.refs_1_
  16.6 0.0 collective-permute-done.6.refs_2_
  16.6 0.2 shard_map.54.refs_2_.mid_ref.x_ref
  16.8 2.0 %collective-permute-done.4.refs_1_ = bf16[8,2,64,128]{3,2,1,0:T(8,128)(2,1)S(1)} collective-permute-done((bf16[8,2,64,128]{3,2,1,0:T(8,128)(2,1)S(1)}, bf16[8,2,64,128]{3,2,1,0:T(8,128)(2,1)S(1)}, u32[]{:S(2)}, u32[]{:S(2)}) %collective-permute-start.4) | collective-permute-done | bytes 262176 | tf_op jit(solution)/shard_map/ppermute | solution.py:395
  18.9 0.1 shard_map.55.rim_ref.refs_2_
  19.0 0.4 %shard_map.56.refs_3_ = bf16[8,2,64,128]{3,2,1,0:T(8,128)(2,1)S(1)} custom-call(bf16[8,2,2,64,128]{4,3,2,1,0:T(8,128)(2,1)S(1)} %shard_map.54.refs_2_.mid_ref.x_ref, bf16[8,2,2,64,128]{4,3,2,1,0:T(8,128)(2,1)S(1)} %shard_map.55.rim_ref.refs_2_, bf16[2,256,768]{2,1,0:T(8,128)(2,1)S(1)} %get-tuple-element.64.beside_ref), custom_call_target="tpu_custom_call" | custom-call | flops 1000000 | bytes 10000 | tf_op jit(solution)/shard_map/pallas_call | solution.py:29
  19.4 0.0 collective-permute-done.3.refs_1_
  19.4 0.2 shard_map.57
  19.6 0.1 collective-permute-start.7
  19.7 1.0 %collective-permute-start.8 = (bf16[8,2,64,128]{3,2,1,0:T(8,128)(2,1)S(1)}, bf16[8,2,64,128]{3,2,1,0:T(8,128)(2,1)S(1)}, u32[]{:S(2)}, u32[]{:S(2)}) collective-permute-start(bf16[8,2,64,128]{3,2,1,0:T(8,128)(2,1)S(1)} %get-tuple-element.67), channel_id=1, source_target_pairs={{0,1},{1,0},{2,4},{3,5},{4,2},{5,3},{6,7},{7,6},{8,9},{9,8},{10,12... | collective-permute-start | bytes 786440 | tf_op jit(solution)/shard_map/ppermute | solution.py:408
  20.7 2.6 %collective-permute-start.12 = (bf16[8,2,64,128]{3,2,1,0:T(8,128)(2,1)S(1)}, bf16[8,2,64,128]{3,2,1,0:T(8,128)(2,1)S(1)}, u32[]{:S(2)}, u32[]{:S(2)}) collective-permute-start(bf16[8,2,64,128]{3,2,1,0:T(8,128)(2,1)S(1)} %shard_map.56.refs_3_), channel_id=1, source_target_pairs={{0,8},{8,0},{16,24},{24,16},{1,9},{9,1},{17,25},{25,17},{2,10},{10... | collective-permute-start | bytes 786440 | tf_op jit(solution)/shard_map/ppermute | solution.py:395
  23.3 0.4 %shard_map.58.after_ref = bf16[8,2,64,128]{3,2,1,0:T(8,128)(2,1)S(1)} custom-call(bf16[8,2,2,64,128]{4,3,2,1,0:T(8,128)(2,1)S(1)} %shard_map.54.refs_2_.mid_ref.x_ref, bf16[8,2,2,64,128]{4,3,2,1,0:T(8,128)(2,1)S(1)} %get-tuple-element.65.rim_ref.x_ref, bf16[2,256,768]{2,1,0:T(8,128)(2,1)S(1)} %get-tuple-element.64.beside_ref), custom_call_target="tpu_custom_call" | custom-call | flops 1000000 | bytes 10000 | tf_op jit(solution)/shard_map/pallas_call | solution.py:29
  23.7 0.1 collective-permute-start.13
  23.8 0.4 %shard_map.59 = (f32[2,256,256]{2,1,0:T(8,128)S(1)}, f32[2,256,256]{2,1,0:T(8,128)S(1)}) custom-call(bf16[8,2,2,64,128]{4,3,2,1,0:T(8,128)(2,1)S(1)} %shard_map.54.refs_2_.mid_ref.x_ref, bf16[8,2,2,64,128]{4,3,2,1,0:T(8,128)(2,1)S(1)} %get-tuple-element.65.rim_ref.x_ref, bf16[2,256,768]{2,1,0:T(8,128)(2,1)S(1)} %get-tuple-element.64.beside_ref, ...), custom_call_target="tpu_custom_call" | custom-call | flops 1000000 | bytes 10000 | tf_op jit(solution)/shard_map/pallas_call | solution.py:29
  24.2 0.5 %shard_map.60 = (bf16[256,768]{1,0:T(8,128)(2,1)S(1)}, bf16[256,768]{1,0:T(8,128)(2,1)S(1)}, bf16[2,256,384]{2,1,0:T(8,128)(2,1)S(1)}, bf16[2,256,24]{2,1,0:T(8,128)(2,1)S(1)}) custom-call(bf16[2,8,8,9]{3,2,1,0:T(8,128)(2,1)S(1)} %get-tuple-element.49.src_w_ref, bf16[2,8,8,9]{3,2,1,0:T(8,128)(2,1)S(1)} %get-tuple-element.50.tgt_w_ref, ...), custom_call_target="tpu_custom_call" | custom-call | flops 1000000 | bytes 10000 | tf_op jit(solution)/shard_map/pallas_call | solution.py:29
  24.7 0.0 collective-permute-done.7.cola_ref
  24.8 1.3 %collective-permute-done.8.colb_ref = bf16[8,2,64,128]{3,2,1,0:T(8,128)(2,1)S(1)} collective-permute-done((bf16[8,2,64,128]{3,2,1,0:T(8,128)(2,1)S(1)}, bf16[8,2,64,128]{3,2,1,0:T(8,128)(2,1)S(1)}, u32[]{:S(2)}, u32[]{:S(2)}) %collective-permute-start.8) | collective-permute-done | bytes 262176 | tf_op jit(solution)/shard_map/ppermute | solution.py:408
  26.1 0.4 %shard_map.61 = (bf16[8,2,64,128]{3,2,1,0:T(8,128)(2,1)S(1)}, bf16[8,2,64,128]{3,2,1,0:T(8,128)(2,1)S(1)}, bf16[2,8,2,64,128]{4,3,2,1,0:T(8,128)(2,1)S(1)}) custom-call(bf16[8,2,64,128]{3,2,1,0:T(8,128)(2,1)S(1)} %collective-permute-done.7.cola_ref, bf16[8,2,64,128]{3,2,1,0:T(8,128)(2,1)S(1)} %collective-permute-done.8.colb_ref, ...), custom_call_target="tpu_custom_call" | custom-call | flops 1000000 | bytes 10000 | tf_op jit(solution)/shard_map/pallas_call | solution.py:29
  26.5 2.3 %collective-permute-start.10 = (bf16[8,2,64,128]{3,2,1,0:T(8,128)(2,1)S(1)}, bf16[8,2,64,128]{3,2,1,0:T(8,128)(2,1)S(1)}, u32[]{:S(2)}, u32[]{:S(2)}) collective-permute-start(bf16[8,2,64,128]{3,2,1,0:T(8,128)(2,1)S(1)} %get-tuple-element.79), channel_id=1, source_target_pairs={{0,8},{8,0},{16,24},{24,16},{1,9},{9,1},{17,25},{25,17},{2,10},{10... | collective-permute-start | bytes 786440 | tf_op jit(solution)/shard_map/ppermute | solution.py:395
  28.7 0.0 collective-permute-start.11
  28.7 0.2 shard_map.63
  28.9 1.4 %collective-permute-start.9 = (bf16[2,8,512]{2,1,0:T(8,128)(2,1)S(1)}, bf16[2,8,512]{2,1,0:T(8,128)(2,1)S(1)}, u32[]{:S(2)}, u32[]{:S(2)}) collective-permute-start(bf16[2,8,512]{2,1,0:T(8,128)(2,1)S(1)} %shard_map.63), channel_id=1, source_target_pairs={{0,1},{1,0},{2,3},{3,2},{4,5},{5,4},{6,7},{7,6},{8,9},{9,8},{10,11... | collective-permute-start | bytes 49160 | tf_op jit(solution)/shard_map/ppermute | solution.py:395
  30.3 2.5 %shard_map.62 = (f32[8,2,2,64,128]{4,3,2,1,0:T(8,128)S(1)}, f32[8,2,2,64,128]{4,3,2,1,0:T(8,128)S(1)}) custom-call(bf16[8,2,2,64,128]{4,3,2,1,0:T(8,128)(2,1)S(1)} %shard_map.54.refs_2_.mid_ref.x_ref, bf16[8,2,2,64,128]{4,3,2,1,0:T(8,128)(2,1)S(1)} %get-tuple-element.65.rim_ref.x_ref, bf16[256,768]{1,0:T(8,128)(2,1)S(1)} %get-tuple-element.70.after_ref.middle_ref, ...), custom_call_target="tpu_custom_call" | custom-call | flops 1000000 | bytes 10000 | tf_op jit(solution)/shard_map/pallas_call | solution.py:29
  32.9 0.0 collective-permute-done.9.rest_0_
  32.9 1.1 %shard_map.64 = (f32[8,2,2,64,128]{4,3,2,1,0:T(8,128)S(1)}, f32[8,2,2,64,128]{4,3,2,1,0:T(8,128)S(1)}) custom-call(bf16[8,2,2,64,128]{4,3,2,1,0:T(8,128)(2,1)S(1)} %shard_map.54.refs_2_.mid_ref.x_ref, bf16[8,2,2,64,128]{4,3,2,1,0:T(8,128)(2,1)S(1)} %get-tuple-element.65.rim_ref.x_ref, ...), custom_call_target="tpu_custom_call", output_to_operand_aliasing={{0}: (6, {}), {1}: (7, {})} | custom-call | flops 1000000 | bytes 10000 | tf_op jit(solution)/shard_map/pallas_call | solution.py:29
  34.0 0.0 collective-permute-done.13.b_ref
  34.0 0.0 collective-permute-done.12.a_ref
  34.0 0.9 %shard_map.65.refs_0_ = bf16[8,2,4,64,128]{4,3,2,1,0:T(8,128)(2,1)} custom-call(bf16[8,2,2,64,128]{4,3,2,1,0:T(8,128)(2,1)S(1)} %shard_map.54.refs_2_.mid_ref.x_ref, f32[8,2,2,64,128]{4,3,2,1,0:T(8,128)S(1)} %get-tuple-element.80.acc_ref, bf16[8,2,64,128]{3,2,1,0:T(8,128)(2,1)S(1)} %collective-permute-done.12.a_ref, ...), custom_call_target="tpu_custom_call" | custom-call | flops 1000000 | bytes 10000 | tf_op jit(solution)/shard_map/pallas_call | solution.py:29
  34.9 0.5 %collective-permute-done.10.a_ref = bf16[8,2,64,128]{3,2,1,0:T(8,128)(2,1)S(1)} collective-permute-done((bf16[8,2,64,128]{3,2,1,0:T(8,128)(2,1)S(1)}, bf16[8,2,64,128]{3,2,1,0:T(8,128)(2,1)S(1)}, u32[]{:S(2)}, u32[]{:S(2)}) %collective-permute-start.10) | collective-permute-done | bytes 262176 | tf_op jit(solution)/shard_map/ppermute | solution.py:395
  35.5 0.0 collective-permute-done.11.b_ref
  35.5 0.9 %shard_map.66 = bf16[8,2,4,64,128]{4,3,2,1,0:T(8,128)(2,1)} custom-call(bf16[8,2,2,64,128]{4,3,2,1,0:T(8,128)(2,1)S(1)} %get-tuple-element.65.rim_ref.x_ref, f32[8,2,2,64,128]{4,3,2,1,0:T(8,128)S(1)} %get-tuple-element.78.acc_ref, bf16[8,2,64,128]{3,2,1,0:T(8,128)(2,1)S(1)} %collective-permute-done.10.a_ref, ...), custom_call_target="tpu_custom_call", output_to_operand_aliasing={{}: (4, {})} | custom-call | flops 1000000 | bytes 10000 | tf_op jit(solution)/shard_map/pallas_call | solution.py:29
Async XLA Ops:
  0.0 4.3 %copy-start = (bf16[8,2,4,64,128]{4,3,2,1,0:T(8,128)(2,1)S(1)}, bf16[8,2,4,64,128]{4,3,2,1,0:T(8,128)(2,1)}, u32[]{:S(2)}) copy-start(bf16[8,2,4,64,128]{4,3,2,1,0:T(8,128)(2,1)} %x_ref.17) | copy-start | bytes 3145732
  1.2 6.4 %collective-permute-start = (bf16[8,2,64,128]{3,2,1,0:T(8,128)(2,1)S(1)}, bf16[8,2,64,128]{3,2,1,0:T(8,128)(2,1)S(1)}, u32[]{:S(2)}, u32[]{:S(2)}) collective-permute-start(bf16[8,2,64,128]{3,2,1,0:T(8,128)(2,1)S(1)} %get-tuple-element.43), channel_id=1, source_target_pairs={{0,2},{2,0},{4,6},{6,4},{1,3},{3,1},{5,7},{7,5},{8,10},{10,8},{12,... | collective-permute-start | bytes 786440 | tf_op jit(solution)/shard_map/ppermute | solution.py:395
  1.7 6.9 %collective-permute-start.1 = (bf16[8,2,64,128]{3,2,1,0:T(8,128)(2,1)S(1)}, bf16[8,2,64,128]{3,2,1,0:T(8,128)(2,1)S(1)}, u32[]{:S(2)}, u32[]{:S(2)}) collective-permute-start(bf16[8,2,64,128]{3,2,1,0:T(8,128)(2,1)S(1)} %get-tuple-element.44), channel_id=1, source_target_pairs={{0,1},{1,0},{2,4},{3,5},{4,2},{5,3},{6,7},{7,6},{8,9},{9,8},{10,12... | collective-permute-start | bytes 786440 | tf_op jit(solution)/shard_map/ppermute | solution.py:408
  4.9 11.7 %collective-permute-start.5 = (bf16[8,2,64,128]{3,2,1,0:T(8,128)(2,1)S(1)}, bf16[8,2,64,128]{3,2,1,0:T(8,128)(2,1)S(1)}, u32[]{:S(2)}, u32[]{:S(2)}) collective-permute-start(bf16[8,2,64,128]{3,2,1,0:T(8,128)(2,1)S(1)} %get-tuple-element.63), channel_id=1, source_target_pairs={{0,8},{8,0},{16,24},{24,16},{1,9},{9,1},{17,25},{25,17},{2,10},{10... | collective-permute-start | bytes 786440 | tf_op jit(solution)/shard_map/ppermute | solution.py:395
  6.5 10.1 %collective-permute-start.6 = (bf16[8,2,64,128]{3,2,1,0:T(8,128)(2,1)S(1)}, bf16[8,2,64,128]{3,2,1,0:T(8,128)(2,1)S(1)}, u32[]{:S(2)}, u32[]{:S(2)}) collective-permute-start(bf16[8,2,64,128]{3,2,1,0:T(8,128)(2,1)S(1)} %get-tuple-element.46.refs_1_.after_ref), channel_id=1, source_target_pairs={{0,2},{2,0},{4,6},{6,4},{8,16},{10,18},{12,20},{14,22},{16,8},{18,... | collective-permute-start | bytes 786440 | tf_op jit(solution)/shard_map/ppermute | solution.py:408
  9.0 9.8 %collective-permute-start.4 = (bf16[8,2,64,128]{3,2,1,0:T(8,128)(2,1)S(1)}, bf16[8,2,64,128]{3,2,1,0:T(8,128)(2,1)S(1)}, u32[]{:S(2)}, u32[]{:S(2)}) collective-permute-start(bf16[8,2,64,128]{3,2,1,0:T(8,128)(2,1)S(1)} %get-tuple-element.61), channel_id=1, source_target_pairs={{0,8},{8,0},{16,24},{24,16},{1,9},{9,1},{17,25},{25,17},{2,10},{10... | collective-permute-start | bytes 786440 | tf_op jit(solution)/shard_map/ppermute | solution.py:395
  11.2 8.2 %collective-permute-start.3 = (bf16[8,2,64,128]{3,2,1,0:T(8,128)(2,1)S(1)}, bf16[8,2,64,128]{3,2,1,0:T(8,128)(2,1)S(1)}, u32[]{:S(2)}, u32[]{:S(2)}) collective-permute-start(bf16[8,2,64,128]{3,2,1,0:T(8,128)(2,1)S(1)} %get-tuple-element.57.refs_5_.refs_0_), channel_id=1, source_target_pairs={{0,2},{2,0},{4,6},{6,4},{8,16},{10,18},{12,20},{14,22},{16,8},{18,... | collective-permute-start | bytes 786440 | tf_op jit(solution)/shard_map/ppermute | solution.py:408
  11.4 4.0 %collective-permute-start.2 = (bf16[2,8,512]{2,1,0:T(8,128)(2,1)S(1)}, bf16[2,8,512]{2,1,0:T(8,128)(2,1)S(1)}, u32[]{:S(2)}, u32[]{:S(2)}) collective-permute-start(bf16[2,8,512]{2,1,0:T(8,128)(2,1)S(1)} %shard_map.52), channel_id=1, source_target_pairs={{0,1},{1,0},{2,3},{3,2},{4,5},{5,4},{6,7},{7,6},{8,9},{9,8},{10,11... | collective-permute-start | bytes 49160 | tf_op jit(solution)/shard_map/ppermute | solution.py:395
  19.6 5.2 %collective-permute-start.7 = (bf16[8,2,64,128]{3,2,1,0:T(8,128)(2,1)S(1)}, bf16[8,2,64,128]{3,2,1,0:T(8,128)(2,1)S(1)}, u32[]{:S(2)}, u32[]{:S(2)}) collective-permute-start(bf16[8,2,64,128]{3,2,1,0:T(8,128)(2,1)S(1)} %get-tuple-element.66), channel_id=1, source_target_pairs={{0,2},{2,0},{4,6},{6,4},{1,3},{3,1},{5,7},{7,5},{8,10},{10,8},{12,... | collective-permute-start | bytes 786440 | tf_op jit(solution)/shard_map/ppermute | solution.py:395
  19.7 6.4 %collective-permute-start.8 = (bf16[8,2,64,128]{3,2,1,0:T(8,128)(2,1)S(1)}, bf16[8,2,64,128]{3,2,1,0:T(8,128)(2,1)S(1)}, u32[]{:S(2)}, u32[]{:S(2)}) collective-permute-start(bf16[8,2,64,128]{3,2,1,0:T(8,128)(2,1)S(1)} %get-tuple-element.67), channel_id=1, source_target_pairs={{0,1},{1,0},{2,4},{3,5},{4,2},{5,3},{6,7},{7,6},{8,9},{9,8},{10,12... | collective-permute-start | bytes 786440 | tf_op jit(solution)/shard_map/ppermute | solution.py:408
  20.7 13.3 %collective-permute-start.12 = (bf16[8,2,64,128]{3,2,1,0:T(8,128)(2,1)S(1)}, bf16[8,2,64,128]{3,2,1,0:T(8,128)(2,1)S(1)}, u32[]{:S(2)}, u32[]{:S(2)}) collective-permute-start(bf16[8,2,64,128]{3,2,1,0:T(8,128)(2,1)S(1)} %shard_map.56.refs_3_), channel_id=1, source_target_pairs={{0,8},{8,0},{16,24},{24,16},{1,9},{9,1},{17,25},{25,17},{2,10},{10... | collective-permute-start | bytes 786440 | tf_op jit(solution)/shard_map/ppermute | solution.py:395
  23.7 10.3 %collective-permute-start.13 = (bf16[8,2,64,128]{3,2,1,0:T(8,128)(2,1)S(1)}, bf16[8,2,64,128]{3,2,1,0:T(8,128)(2,1)S(1)}, u32[]{:S(2)}, u32[]{:S(2)}) collective-permute-start(bf16[8,2,64,128]{3,2,1,0:T(8,128)(2,1)S(1)} %shard_map.58.after_ref), channel_id=1, source_target_pairs={{0,2},{2,0},{4,6},{6,4},{8,16},{10,18},{12,20},{14,22},{16,8},{18,... | collective-permute-start | bytes 786440 | tf_op jit(solution)/shard_map/ppermute | solution.py:408
  26.5 9.0 %collective-permute-start.10 = (bf16[8,2,64,128]{3,2,1,0:T(8,128)(2,1)S(1)}, bf16[8,2,64,128]{3,2,1,0:T(8,128)(2,1)S(1)}, u32[]{:S(2)}, u32[]{:S(2)}) collective-permute-start(bf16[8,2,64,128]{3,2,1,0:T(8,128)(2,1)S(1)} %get-tuple-element.79), channel_id=1, source_target_pairs={{0,8},{8,0},{16,24},{24,16},{1,9},{9,1},{17,25},{25,17},{2,10},{10... | collective-permute-start | bytes 786440 | tf_op jit(solution)/shard_map/ppermute | solution.py:395
  28.7 6.7 %collective-permute-start.11 = (bf16[8,2,64,128]{3,2,1,0:T(8,128)(2,1)S(1)}, bf16[8,2,64,128]{3,2,1,0:T(8,128)(2,1)S(1)}, u32[]{:S(2)}, u32[]{:S(2)}) collective-permute-start(bf16[8,2,64,128]{3,2,1,0:T(8,128)(2,1)S(1)} %get-tuple-element.75.after_ref), channel_id=1, source_target_pairs={{0,2},{2,0},{4,6},{6,4},{8,16},{10,18},{12,20},{14,22},{16,8},{18,... | collective-permute-start | bytes 786440 | tf_op jit(solution)/shard_map/ppermute | solution.py:408
  28.9 3.9 %collective-permute-start.9 = (bf16[2,8,512]{2,1,0:T(8,128)(2,1)S(1)}, bf16[2,8,512]{2,1,0:T(8,128)(2,1)S(1)}, u32[]{:S(2)}, u32[]{:S(2)}) collective-permute-start(bf16[2,8,512]{2,1,0:T(8,128)(2,1)S(1)} %shard_map.63), channel_id=1, source_target_pairs={{0,1},{1,0},{2,3},{3,2},{4,5},{5,4},{6,7},{7,6},{8,9},{9,8},{10,11... | collective-permute-start | bytes 49160 | tf_op jit(solution)/shard_map/ppermute | solution.py:395

commit v17 on v13

--- a/solution.py
+++ b/solution.py
@@ -440,10 +440,11 @@
         both, base = (middle, sides), len(block)
         mid, rim = block[0], block[-1]
         beside = swap_first(col_a, "scol"), swap_second(col_b, "scol", "trow")
-        which = (0, 1) if sum_a is None else (1,)
-        sums = call(on(functools.partial(inner_body, which), *both), owed_inner * len(which), (*block, made["beside", layer]))
-        sum_b = sums[-1]
-        inner = swap_first(sums[0], "srow") if sum_a is None else got_a, swap_second(sum_b, "srow", "scol")
+        if sum_a is None:
+            (sum_a,) = call(on(functools.partial(inner_body, (0,)), *both), owed_inner, (*block, made["beside", layer]))
+            got_a = swap_first(sum_a, "srow")
+        (sum_b,) = call(on(functools.partial(inner_body, (1,)), *both), owed_inner, (*block, made["beside", layer]))
+        inner = got_a, swap_second(sum_b, "srow", "scol")
         if layer == 0:
             late = [(kind, n) for n in range(layers) for kind in kinds]
             made |= build([part for part in late if part not in early], src_w, tgt_w, sum_b)

time: 36.5 us -> 37.7 us (1.033)
  waiting for transfers between devices: 5.05 us -> 6.26 us
    ppermute x8, waiting for transfers between devices: 2.61 us -> 4.06 us  [swap_first(): lax.ppermute(value, axis, [(n, n ^ 1) for n in range(lax.axis_size(axis))])]
    ppermute x8, starting transfers between devices: 12.2 us -> 11.4 us  [swap_first(): lax.ppermute(value, axis, [(n, n ^ 1) for n in range(lax.axis_size(axis))])]
    ppermute x6, starting transfers between devices: 3.71 us -> 4.18 us  [swap_second(): return lax.ppermute(value, (axis, other), pairs)]
    pallas_call x20 -> x21, Pallas kernels: 15.3 us -> 15.4 us  [call(): pl.pallas_call(body, out_shape=tuple(outs), in_specs=[pl.BlockSpec(memory...]
  transfers between devices with their start and end apart: 14 -> 14, of which waited for: 5 -> 3; matrix products, arithmetic and copies ran while one was open for 0% -> 0% of each run, Pallas kernels for 36% -> 35%
where the time goes in v17:
time: 37.7 us; the launch traced here: 37.5 us
  starting transfers between devices  15.6 us (41%)
  Pallas kernels  15.4 us (41%)
  waiting for transfers between devices  6.26 us (17%)
    pallas_call x21, Pallas kernels, call(): pl.pallas_call(body, out_shape=tuple(outs), in_specs=[pl.BlockSpec(memory...  15.4 us
    ppermute x8, starting transfers between devices, swap_first(): lax.ppermute(value, axis, [(n, n ^ 1) for n in range(lax.axis_size(axis))])  11.4 us
    ppermute x6, starting transfers between devices, swap_second(): return lax.ppermute(value, (axis, other), pairs)  4.18 us
    ppermute x8, waiting for transfers between devices, swap_first(): lax.ppermute(value, axis, [(n, n ^ 1) for n in range(lax.axis_size(axis))])  4.06 us
    ppermute x6, waiting for transfers between devices, swap_second(): return lax.ppermute(value, (axis, other), pairs)  2.21 us
  transfers between devices with their start and end apart: 14, of which 3 were waited for; matrix products, arithmetic and copies ran while one was open for 0% of the time, Pallas kernels for 35%

profile of v17, /device:TPU:0, one launch (start us, length us, event | category | flops | bytes accessed | tf_op | source)
XLA Modules:
  0.0 37.5 jit_solution(4339321537417776955)
XLA Ops:
  0.0 0.0 copy-start
  0.0 1.2 %shard_map.46 = (bf16[2,8,8,9]{3,2,1,0:T(8,128)(2,1)S(1)}, bf16[2,8,8,9]{3,2,1,0:T(8,128)(2,1)S(1)}, f32[2,8]{1,0:T(2,128)S(1)}, bf16[2,256,768]{2,1,0:T(8,128)(...) custom-call(bf16[8,2,4,64,128]{4,3,2,1,0:T(8,128)(2,1)} %x_ref.19, ...), custom_call_target="tpu_custom_call" | custom-call | flops 1000000 | bytes 10000 | tf_op jit(solution)/shard_map/pallas_call | solution.py:29
  1.2 0.5 %collective-permute-start = (bf16[8,2,64,128]{3,2,1,0:T(8,128)(2,1)S(1)}, bf16[8,2,64,128]{3,2,1,0:T(8,128)(2,1)S(1)}, u32[]{:S(2)}, u32[]{:S(2)}) collective-permute-start(bf16[8,2,64,128]{3,2,1,0:T(8,128)(2,1)S(1)} %get-tuple-element.41), channel_id=1, source_target_pairs={{0,2},{2,0},{4,6},{6,4},{1,3},{3,1},{5,7},{7,5},{8,10},{10,8},{12,... | collective-permute-start | bytes 786440 | tf_op jit(solution)/shard_map/ppermute | solution.py:395
  1.7 2.6 %collective-permute-start.1 = (bf16[8,2,64,128]{3,2,1,0:T(8,128)(2,1)S(1)}, bf16[8,2,64,128]{3,2,1,0:T(8,128)(2,1)S(1)}, u32[]{:S(2)}, u32[]{:S(2)}) collective-permute-start(bf16[8,2,64,128]{3,2,1,0:T(8,128)(2,1)S(1)} %get-tuple-element.42), channel_id=1, source_target_pairs={{0,1},{1,0},{2,4},{3,5},{4,2},{5,3},{6,7},{7,6},{8,9},{9,8},{10,12... | collective-permute-start | bytes 786440 | tf_op jit(solution)/shard_map/ppermute | solution.py:408
  4.3 0.0 copy-done
  4.3 0.4 shard_map.47.refs_1_.after_ref
  4.7 0.2 collective-permute-start.6
  4.8 0.4 shard_map.54
  5.2 3.1 %collective-permute-start.5 = (bf16[8,2,64,128]{3,2,1,0:T(8,128)(2,1)S(1)}, bf16[8,2,64,128]{3,2,1,0:T(8,128)(2,1)S(1)}, u32[]{:S(2)}, u32[]{:S(2)}) collective-permute-start(bf16[8,2,64,128]{3,2,1,0:T(8,128)(2,1)S(1)} %shard_map.54), channel_id=1, source_target_pairs={{0,8},{8,0},{16,24},{24,16},{1,9},{9,1},{17,25},{25,17},{2,10},{10... | collective-permute-start | bytes 786440 | tf_op jit(solution)/shard_map/ppermute | solution.py:395
  8.3 0.4 %shard_map.48 = (f32[2,256,256]{2,1,0:T(8,128)S(1)}, f32[2,256,256]{2,1,0:T(8,128)S(1)}) custom-call(bf16[8,2,4,64,128]{4,3,2,1,0:T(8,128)(2,1)S(1)} %copy-done, bf16[2,256,768]{2,1,0:T(8,128)(2,1)S(1)} %get-tuple-element.43.refs_0_.beside_ref.refs_1_.refs_2_, bf16[8,2,64,128]{3,2,1,0:T(8,128)(2,1)S(1)} %shard_map.47.refs_1_.after_ref), custom_call_target="tpu_custom_call" | custom-call | flops 1000000 | bytes 10000 | tf_op jit(solution)/shard_map/pallas_call | solution.py:29
  8.8 1.1 %shard_map.49 = (bf16[256,768]{1,0:T(8,128)(2,1)S(1)}, bf16[256,768]{1,0:T(8,128)(2,1)S(1)}, bf16[2,256,384]{2,1,0:T(8,128)(2,1)S(1)}, bf16[2,256,24]{2,1,0:T(8,...) custom-call(bf16[2,8,8,9]{3,2,1,0:T(8,128)(2,1)S(1)} %get-tuple-elem, ...), custom_call_target="tpu_custom_call" | custom-call | flops 1000000 | bytes 10000 | tf_op jit(solution)/shard_map/pallas_call | solution.py:29
  9.9 0.0 collective-permute-done.cola_ref
  9.9 0.0 collective-permute-done.1.colb_ref
  9.9 0.4 %shard_map.50 = (bf16[8,2,64,128]{3,2,1,0:T(8,128)(2,1)S(1)}, bf16[8,2,64,128]{3,2,1,0:T(8,128)(2,1)S(1)}, bf16[2,8,2,64,128]{4,3,2,1,0:T(8,128)(2,1)S(1)}) custom-call(bf16[8,2,64,128]{3,2,1,0:T(8,128)(2,1)S(1)} %collective-permute-done.cola_ref, bf16[8,2,64,128]{3,2,1,0:T(8,128)(2,1)S(1)} %collective-permute-done.1.colb_ref, ...), custom_call_target="tpu_custom_call" | custom-call | flops 1000000 | bytes 10000 | tf_op jit(solution)/shard_map/pallas_call | solution.py:29
  10.3 0.9 %collective-permute-start.4 = (bf16[8,2,64,128]{3,2,1,0:T(8,128)(2,1)S(1)}, bf16[8,2,64,128]{3,2,1,0:T(8,128)(2,1)S(1)}, u32[]{:S(2)}, u32[]{:S(2)}) collective-permute-start(bf16[8,2,64,128]{3,2,1,0:T(8,128)(2,1)S(1)} %get-tuple-element.58), channel_id=1, source_target_pairs={{0,8},{8,0},{16,24},{24,16},{1,9},{9,1},{17,25},{25,17},{2,10},{10... | collective-permute-start | bytes 786440 | tf_op jit(solution)/shard_map/ppermute | solution.py:395
  11.2 0.0 collective-permute-start.3
  11.2 0.2 shard_map.52
  11.4 1.5 %collective-permute-start.2 = (bf16[2,8,512]{2,1,0:T(8,128)(2,1)S(1)}, bf16[2,8,512]{2,1,0:T(8,128)(2,1)S(1)}, u32[]{:S(2)}, u32[]{:S(2)}) collective-permute-start(bf16[2,8,512]{2,1,0:T(8,128)(2,1)S(1)} %shard_map.52), channel_id=1, source_target_pairs={{0,1},{1,0},{2,3},{3,2},{4,5},{5,4},{6,7},{7,6},{8,9},{9,8},{10,11... | collective-permute-start | bytes 49160 | tf_op jit(solution)/shard_map/ppermute | solution.py:395
  12.9 2.5 %shard_map.51 = (f32[8,2,2,64,128]{4,3,2,1,0:T(8,128)S(1)}, f32[8,2,2,64,128]{4,3,2,1,0:T(8,128)S(1)}) custom-call(bf16[8,2,4,64,128]{4,3,2,1,0:T(8,128)(2,1)S(1)} %copy-done, bf16[256,768]{1,0:T(8,128)(2,1)S(1)} %get-tuple-element.48.after_ref.refs_0_.refs_1_, bf16[2,256,768]{2,1,0:T(8,128)(2,1)S(1)} %get-tuple-element.43.refs_0_.beside_ref.refs_1_.refs_2_, ...), custom_call_target="tpu_custom_call" | custom-call | flops 1000000 | bytes 10000 | tf_op jit(solution)/shard_map/pallas_call | solution.py:29
  15.4 0.0 collective-permute-done.2.refs_6_
  15.4 1.1 %shard_map.53 = (f32[8,2,2,64,128]{4,3,2,1,0:T(8,128)S(1)}, f32[8,2,2,64,128]{4,3,2,1,0:T(8,128)S(1)}) custom-call(bf16[8,2,4,64,128]{4,3,2,1,0:T(8,128)(2,1)S(1)} %copy-done, bf16[2,8,2,64,128]{4,3,2,1,0:T(8,128)(2,1)S(1)} %get-tuple-element.49.refs_0_, ...), custom_call_target="tpu_custom_call", output_to_operand_aliasing={{0}: (5, {}), {1}: (6, {})} | custom-call | flops 1000000 | bytes 10000 | tf_op jit(solution)/shard_map/pallas_call | solution.py:29
  16.6 0.0 collective-permute-done.6.refs_2_
  16.6 0.0 collective-permute-done.5.refs_1_
  16.6 0.2 shard_map.55.refs_2_.mid_ref.x_ref
  16.8 3.4 %collective-permute-done.4.refs_1_ = bf16[8,2,64,128]{3,2,1,0:T(8,128)(2,1)S(1)} collective-permute-done((bf16[8,2,64,128]{3,2,1,0:T(8,128)(2,1)S(1)}, bf16[8,2,64,128]{3,2,1,0:T(8,128)(2,1)S(1)}, u32[]{:S(2)}, u32[]{:S(2)}) %collective-permute-start.4) | collective-permute-done | bytes 262176 | tf_op jit(solution)/shard_map/ppermute | solution.py:395
  20.2 0.1 shard_map.56.rim_ref.refs_2_
  20.3 0.4 %shard_map.57.refs_3_ = bf16[8,2,64,128]{3,2,1,0:T(8,128)(2,1)S(1)} custom-call(bf16[8,2,2,64,128]{4,3,2,1,0:T(8,128)(2,1)S(1)} %shard_map.55.refs_2_.mid_ref.x_ref, bf16[8,2,2,64,128]{4,3,2,1,0:T(8,128)(2,1)S(1)} %shard_map.56.rim_ref.refs_2_, bf16[2,256,768]{2,1,0:T(8,128)(2,1)S(1)} %get-tuple-element.60.beside_ref), custom_call_target="tpu_custom_call" | custom-call | flops 1000000 | bytes 10000 | tf_op jit(solution)/shard_map/pallas_call | solution.py:29
  20.7 0.0 collective-permute-done.3.refs_1_
  20.7 0.2 shard_map.58
  21.0 0.1 collective-permute-start.7
  21.0 1.4 %collective-permute-start.8 = (bf16[8,2,64,128]{3,2,1,0:T(8,128)(2,1)S(1)}, bf16[8,2,64,128]{3,2,1,0:T(8,128)(2,1)S(1)}, u32[]{:S(2)}, u32[]{:S(2)}) collective-permute-start(bf16[8,2,64,128]{3,2,1,0:T(8,128)(2,1)S(1)} %get-tuple-element.63), channel_id=1, source_target_pairs={{0,1},{1,0},{2,4},{3,5},{4,2},{5,3},{6,7},{7,6},{8,9},{9,8},{10,12... | collective-permute-start | bytes 786440 | tf_op jit(solution)/shard_map/ppermute | solution.py:408
  22.4 2.0 %collective-permute-start.12 = (bf16[8,2,64,128]{3,2,1,0:T(8,128)(2,1)S(1)}, bf16[8,2,64,128]{3,2,1,0:T(8,128)(2,1)S(1)}, u32[]{:S(2)}, u32[]{:S(2)}) collective-permute-start(bf16[8,2,64,128]{3,2,1,0:T(8,128)(2,1)S(1)} %shard_map.57.refs_3_), channel_id=1, source_target_pairs={{0,8},{8,0},{16,24},{24,16},{1,9},{9,1},{17,25},{25,17},{2,10},{10... | collective-permute-start | bytes 786440 | tf_op jit(solution)/shard_map/ppermute | solution.py:395
  24.4 0.4 shard_map.59.after_ref
  24.7 0.1 collective-permute-start.13
  24.8 0.4 %shard_map.60 = (f32[2,256,256]{2,1,0:T(8,128)S(1)}, f32[2,256,256]{2,1,0:T(8,128)S(1)}) custom-call(bf16[8,2,2,64,128]{4,3,2,1,0:T(8,128)(2,1)S(1)} %shard_map.55.refs_2_.mid_ref.x_ref, bf16[8,2,2,64,128]{4,3,2,1,0:T(8,128)(2,1)S(1)} %get-tuple-element.61.rim_ref.x_ref, bf16[2,256,768]{2,1,0:T(8,128)(2,1)S(1)} %get-tuple-element.60.beside_ref, ...), custom_call_target="tpu_custom_call" | custom-call | flops 1000000 | bytes 10000 | tf_op jit(solution)/shard_map/pallas_call | solution.py:29
  25.3 0.0 collective-permute-done.7.cola_ref
  25.3 2.2 %collective-permute-done.8.colb_ref = bf16[8,2,64,128]{3,2,1,0:T(8,128)(2,1)S(1)} collective-permute-done((bf16[8,2,64,128]{3,2,1,0:T(8,128)(2,1)S(1)}, bf16[8,2,64,128]{3,2,1,0:T(8,128)(2,1)S(1)}, u32[]{:S(2)}, u32[]{:S(2)}) %collective-permute-start.8) | collective-permute-done | bytes 262176 | tf_op jit(solution)/shard_map/ppermute | solution.py:408
  27.5 0.4 shard_map.61
  27.9 1.8 %collective-permute-start.10 = (bf16[8,2,64,128]{3,2,1,0:T(8,128)(2,1)S(1)}, bf16[8,2,64,128]{3,2,1,0:T(8,128)(2,1)S(1)}, u32[]{:S(2)}, u32[]{:S(2)}) collective-permute-start(bf16[8,2,64,128]{3,2,1,0:T(8,128)(2,1)S(1)} %get-tuple-element.75), channel_id=1, source_target_pairs={{0,8},{8,0},{16,24},{24,16},{1,9},{9,1},{17,25},{25,17},{2,10},{10... | collective-permute-start | bytes 786440 | tf_op jit(solution)/shard_map/ppermute | solution.py:395
  29.7 0.0 collective-permute-start.11
  29.7 0.2 shard_map.63
  29.8 1.5 %collective-permute-start.9 = (bf16[2,8,512]{2,1,0:T(8,128)(2,1)S(1)}, bf16[2,8,512]{2,1,0:T(8,128)(2,1)S(1)}, u32[]{:S(2)}, u32[]{:S(2)}) collective-permute-start(bf16[2,8,512]{2,1,0:T(8,128)(2,1)S(1)} %shard_map.63), channel_id=1, source_target_pairs={{0,1},{1,0},{2,3},{3,2},{4,5},{5,4},{6,7},{7,6},{8,9},{9,8},{10,11... | collective-permute-start | bytes 49160 | tf_op jit(solution)/shard_map/ppermute | solution.py:395
  31.4 2.5 %shard_map.62 = (f32[8,2,2,64,128]{4,3,2,1,0:T(8,128)S(1)}, f32[8,2,2,64,128]{4,3,2,1,0:T(8,128)S(1)}) custom-call(bf16[8,2,2,64,128]{4,3,2,1,0:T(8,128)(2,1)S(1)} %shard_map.55.refs_2_.mid_ref.x_ref, bf16[8,2,2,64,128]{4,3,2,1,0:T(8,128)(2,1)S(1)} %get-tuple-element.61.rim_ref.x_ref, bf16[256,768]{1,0:T(8,128)(2,1)S(1)} %get-tuple-element.66.after_ref.middle_ref, ...), custom_call_target="tpu_custom_call" | custom-call | flops 1000000 | bytes 10000 | tf_op jit(solution)/shard_map/pallas_call | solution.py:29
  33.9 0.0 collective-permute-done.9.rest_0_
  33.9 1.1 %shard_map.64 = (f32[8,2,2,64,128]{4,3,2,1,0:T(8,128)S(1)}, f32[8,2,2,64,128]{4,3,2,1,0:T(8,128)S(1)}) custom-call(bf16[8,2,2,64,128]{4,3,2,1,0:T(8,128)(2,1)S(1)} %shard_map.55.refs_2_.mid_ref.x_ref, bf16[8,2,2,64,128]{4,3,2,1,0:T(8,128)(2,1)S(1)} %get-tuple-element.61.rim_ref.x_ref, ...), custom_call_target="tpu_custom_call", output_to_operand_aliasing={{0}: (6, {}), {1}: (7, {})} | custom-call | flops 1000000 | bytes 10000 | tf_op jit(solution)/shard_map/pallas_call | solution.py:29
  35.0 0.0 collective-permute-done.13.b_ref
  35.0 0.0 collective-permute-done.12.a_ref
  35.0 0.9 %shard_map.65.refs_0_ = bf16[8,2,4,64,128]{4,3,2,1,0:T(8,128)(2,1)} custom-call(bf16[8,2,2,64,128]{4,3,2,1,0:T(8,128)(2,1)S(1)} %shard_map.55.refs_2_.mid_ref.x_ref, f32[8,2,2,64,128]{4,3,2,1,0:T(8,128)S(1)} %get-tuple-element.76.acc_ref, bf16[8,2,64,128]{3,2,1,0:T(8,128)(2,1)S(1)} %collective-permute-done.12.a_ref, ...), custom_call_target="tpu_custom_call" | custom-call | flops 1000000 | bytes 10000 | tf_op jit(solution)/shard_map/pallas_call | solution.py:29
  36.0 0.6 %collective-permute-done.10.a_ref = bf16[8,2,64,128]{3,2,1,0:T(8,128)(2,1)S(1)} collective-permute-done((bf16[8,2,64,128]{3,2,1,0:T(8,128)(2,1)S(1)}, bf16[8,2,64,128]{3,2,1,0:T(8,128)(2,1)S(1)}, u32[]{:S(2)}, u32[]{:S(2)}) %collective-permute-start.10) | collective-permute-done | bytes 262176 | tf_op jit(solution)/shard_map/ppermute | solution.py:395
  36.6 0.0 collective-permute-done.11.b_ref
  36.6 0.9 %shard_map.66 = bf16[8,2,4,64,128]{4,3,2,1,0:T(8,128)(2,1)} custom-call(bf16[8,2,2,64,128]{4,3,2,1,0:T(8,128)(2,1)S(1)} %get-tuple-element.61.rim_ref.x_ref, f32[8,2,2,64,128]{4,3,2,1,0:T(8,128)S(1)} %get-tuple-element.74.acc_ref, bf16[8,2,64,128]{3,2,1,0:T(8,128)(2,1)S(1)} %collective-permute-done.10.a_ref, ...), custom_call_target="tpu_custom_call", output_to_operand_aliasing={{}: (4, {})} | custom-call | flops 1000000 | bytes 10000 | tf_op jit(solution)/shard_map/pallas_call | solution.py:29
Async XLA Ops:
  0.0 4.3 %copy-start = (bf16[8,2,4,64,128]{4,3,2,1,0:T(8,128)(2,1)S(1)}, bf16[8,2,4,64,128]{4,3,2,1,0:T(8,128)(2,1)}, u32[]{:S(2)}) copy-start(bf16[8,2,4,64,128]{4,3,2,1,0:T(8,128)(2,1)} %x_ref.19) | copy-start | bytes 3145732
  1.2 8.7 %collective-permute-start = (bf16[8,2,64,128]{3,2,1,0:T(8,128)(2,1)S(1)}, bf16[8,2,64,128]{3,2,1,0:T(8,128)(2,1)S(1)}, u32[]{:S(2)}, u32[]{:S(2)}) collective-permute-start(bf16[8,2,64,128]{3,2,1,0:T(8,128)(2,1)S(1)} %get-tuple-element.41), channel_id=1, source_target_pairs={{0,2},{2,0},{4,6},{6,4},{1,3},{3,1},{5,7},{7,5},{8,10},{10,8},{12,... | collective-permute-start | bytes 786440 | tf_op jit(solution)/shard_map/ppermute | solution.py:395
  1.7 8.2 %collective-permute-start.1 = (bf16[8,2,64,128]{3,2,1,0:T(8,128)(2,1)S(1)}, bf16[8,2,64,128]{3,2,1,0:T(8,128)(2,1)S(1)}, u32[]{:S(2)}, u32[]{:S(2)}) collective-permute-start(bf16[8,2,64,128]{3,2,1,0:T(8,128)(2,1)S(1)} %get-tuple-element.42), channel_id=1, source_target_pairs={{0,1},{1,0},{2,4},{3,5},{4,2},{5,3},{6,7},{7,6},{8,9},{9,8},{10,12... | collective-permute-start | bytes 786440 | tf_op jit(solution)/shard_map/ppermute | solution.py:408
  4.7 11.9 %collective-permute-start.6 = (bf16[8,2,64,128]{3,2,1,0:T(8,128)(2,1)S(1)}, bf16[8,2,64,128]{3,2,1,0:T(8,128)(2,1)S(1)}, u32[]{:S(2)}, u32[]{:S(2)}) collective-permute-start(bf16[8,2,64,128]{3,2,1,0:T(8,128)(2,1)S(1)} %shard_map.47.refs_1_.after_ref), channel_id=1, source_target_pairs={{0,2},{2,0},{4,6},{6,4},{8,16},{10,18},{12,20},{14,22},{16,8},{18,... | collective-permute-start | bytes 786440 | tf_op jit(solution)/shard_map/ppermute | solution.py:408
  5.2 11.4 %collective-permute-start.5 = (bf16[8,2,64,128]{3,2,1,0:T(8,128)(2,1)S(1)}, bf16[8,2,64,128]{3,2,1,0:T(8,128)(2,1)S(1)}, u32[]{:S(2)}, u32[]{:S(2)}) collective-permute-start(bf16[8,2,64,128]{3,2,1,0:T(8,128)(2,1)S(1)} %shard_map.54), channel_id=1, source_target_pairs={{0,8},{8,0},{16,24},{24,16},{1,9},{9,1},{17,25},{25,17},{2,10},{10... | collective-permute-start | bytes 786440 | tf_op jit(solution)/shard_map/ppermute | solution.py:395
  10.3 9.9 %collective-permute-start.4 = (bf16[8,2,64,128]{3,2,1,0:T(8,128)(2,1)S(1)}, bf16[8,2,64,128]{3,2,1,0:T(8,128)(2,1)S(1)}, u32[]{:S(2)}, u32[]{:S(2)}) collective-permute-start(bf16[8,2,64,128]{3,2,1,0:T(8,128)(2,1)S(1)} %get-tuple-element.58), channel_id=1, source_target_pairs={{0,8},{8,0},{16,24},{24,16},{1,9},{9,1},{17,25},{25,17},{2,10},{10... | collective-permute-start | bytes 786440 | tf_op jit(solution)/shard_map/ppermute | solution.py:395
  11.2 9.6 %collective-permute-start.3 = (bf16[8,2,64,128]{3,2,1,0:T(8,128)(2,1)S(1)}, bf16[8,2,64,128]{3,2,1,0:T(8,128)(2,1)S(1)}, u32[]{:S(2)}, u32[]{:S(2)}) collective-permute-start(bf16[8,2,64,128]{3,2,1,0:T(8,128)(2,1)S(1)} %get-tuple-element.54.refs_5_.refs_0_), channel_id=1, source_target_pairs={{0,2},{2,0},{4,6},{6,4},{8,16},{10,18},{12,20},{14,22},{16,8},{18,... | collective-permute-start | bytes 786440 | tf_op jit(solution)/shard_map/ppermute | solution.py:408
  11.4 4.0 %collective-permute-start.2 = (bf16[2,8,512]{2,1,0:T(8,128)(2,1)S(1)}, bf16[2,8,512]{2,1,0:T(8,128)(2,1)S(1)}, u32[]{:S(2)}, u32[]{:S(2)}) collective-permute-start(bf16[2,8,512]{2,1,0:T(8,128)(2,1)S(1)} %shard_map.52), channel_id=1, source_target_pairs={{0,1},{1,0},{2,3},{3,2},{4,5},{5,4},{6,7},{7,6},{8,9},{9,8},{10,11... | collective-permute-start | bytes 49160 | tf_op jit(solution)/shard_map/ppermute | solution.py:395
  21.0 4.3 %collective-permute-start.7 = (bf16[8,2,64,128]{3,2,1,0:T(8,128)(2,1)S(1)}, bf16[8,2,64,128]{3,2,1,0:T(8,128)(2,1)S(1)}, u32[]{:S(2)}, u32[]{:S(2)}) collective-permute-start(bf16[8,2,64,128]{3,2,1,0:T(8,128)(2,1)S(1)} %get-tuple-element.62), channel_id=1, source_target_pairs={{0,2},{2,0},{4,6},{6,4},{1,3},{3,1},{5,7},{7,5},{8,10},{10,8},{12,... | collective-permute-start | bytes 786440 | tf_op jit(solution)/shard_map/ppermute | solution.py:395
  21.0 6.4 %collective-permute-start.8 = (bf16[8,2,64,128]{3,2,1,0:T(8,128)(2,1)S(1)}, bf16[8,2,64,128]{3,2,1,0:T(8,128)(2,1)S(1)}, u32[]{:S(2)}, u32[]{:S(2)}) collective-permute-start(bf16[8,2,64,128]{3,2,1,0:T(8,128)(2,1)S(1)} %get-tuple-element.63), channel_id=1, source_target_pairs={{0,1},{1,0},{2,4},{3,5},{4,2},{5,3},{6,7},{7,6},{8,9},{9,8},{10,12... | collective-permute-start | bytes 786440 | tf_op jit(solution)/shard_map/ppermute | solution.py:408
  22.4 12.6 %collective-permute-start.12 = (bf16[8,2,64,128]{3,2,1,0:T(8,128)(2,1)S(1)}, bf16[8,2,64,128]{3,2,1,0:T(8,128)(2,1)S(1)}, u32[]{:S(2)}, u32[]{:S(2)}) collective-permute-start(bf16[8,2,64,128]{3,2,1,0:T(8,128)(2,1)S(1)} %shard_map.57.refs_3_), channel_id=1, source_target_pairs={{0,8},{8,0},{16,24},{24,16},{1,9},{9,1},{17,25},{25,17},{2,10},{10... | collective-permute-start | bytes 786440 | tf_op jit(solution)/shard_map/ppermute | solution.py:395
  24.7 10.3 %collective-permute-start.13 = (bf16[8,2,64,128]{3,2,1,0:T(8,128)(2,1)S(1)}, bf16[8,2,64,128]{3,2,1,0:T(8,128)(2,1)S(1)}, u32[]{:S(2)}, u32[]{:S(2)}) collective-permute-start(bf16[8,2,64,128]{3,2,1,0:T(8,128)(2,1)S(1)} %shard_map.59.after_ref), channel_id=1, source_target_pairs={{0,2},{2,0},{4,6},{6,4},{8,16},{10,18},{12,20},{14,22},{16,8},{18,... | collective-permute-start | bytes 786440 | tf_op jit(solution)/shard_map/ppermute | solution.py:408
  27.9 8.7 %collective-permute-start.10 = (bf16[8,2,64,128]{3,2,1,0:T(8,128)(2,1)S(1)}, bf16[8,2,64,128]{3,2,1,0:T(8,128)(2,1)S(1)}, u32[]{:S(2)}, u32[]{:S(2)}) collective-permute-start(bf16[8,2,64,128]{3,2,1,0:T(8,128)(2,1)S(1)} %get-tuple-element.75), channel_id=1, source_target_pairs={{0,8},{8,0},{16,24},{24,16},{1,9},{9,1},{17,25},{25,17},{2,10},{10... | collective-permute-start | bytes 786440 | tf_op jit(solution)/shard_map/ppermute | solution.py:395
  29.7 6.9 %collective-permute-start.11 = (bf16[8,2,64,128]{3,2,1,0:T(8,128)(2,1)S(1)}, bf16[8,2,64,128]{3,2,1,0:T(8,128)(2,1)S(1)}, u32[]{:S(2)}, u32[]{:S(2)}) collective-permute-start(bf16[8,2,64,128]{3,2,1,0:T(8,128)(2,1)S(1)} %get-tuple-element.71.after_ref), channel_id=1, source_target_pairs={{0,2},{2,0},{4,6},{6,4},{8,16},{10,18},{12,20},{14,22},{16,8},{18,... | collective-permute-start | bytes 786440 | tf_op jit(solution)/shard_map/ppermute | solution.py:408
  29.8 4.0 %collective-permute-start.9 = (bf16[2,8,512]{2,1,0:T(8,128)(2,1)S(1)}, bf16[2,8,512]{2,1,0:T(8,128)(2,1)S(1)}, u32[]{:S(2)}, u32[]{:S(2)}) collective-permute-start(bf16[2,8,512]{2,1,0:T(8,128)(2,1)S(1)} %shard_map.63), channel_id=1, source_target_pairs={{0,1},{1,0},{2,3},{3,2},{4,5},{5,4},{6,7},{7,6},{8,9},{9,8},{10,11... | collective-permute-start | bytes 49160 | tf_op jit(solution)/shard_map/ppermute | solution.py:395

commit v18 on v17

--- a/solution.py
+++ b/solution.py
@@ -178,7 +178,7 @@
 
 def inner_body(which, mid_ref, rim_ref, beside_ref, *out_refs):
     rows, cols = mid_ref.shape[1:3]
-    for n, out_ref in zip(which, out_refs):
+    for n, out_ref in zip(which, out_refs[-len(which) :]):
         i, side = sent_rows(rows)[n]
         owed_sums(
             beside_ref[side], lambda cut, b: [column(mid_ref, rim_ref, i, j + b, cut) for j in range(cols)], out_ref
@@ -443,7 +443,12 @@
         if sum_a is None:
             (sum_a,) = call(on(functools.partial(inner_body, (0,)), *both), owed_inner, (*block, made["beside", layer]))
             got_a = swap_first(sum_a, "srow")
-        (sum_b,) = call(on(functools.partial(inner_body, (1,)), *both), owed_inner, (*block, made["beside", layer]))
+        (sum_b,) = call(
+            on(functools.partial(inner_body, (1,)), *both),
+            owed_inner,
+            (*block, made["beside", layer], sum_a),
+            {base + 1: pl.ANY},
+        )
         inner = got_a, swap_second(sum_b, "srow", "scol")
         if layer == 0:
             late = [(kind, n) for n in range(layers) for kind in kinds]

time: 37.7 us -> 36.8 us (0.976)
  waiting for transfers between devices: 6.26 us -> 4.33 us
  starting transfers between devices: 15.6 us -> 16.6 us
    ppermute x8, waiting for transfers between devices: 4.06 us -> 2.5 us  [swap_first(): lax.ppermute(value, axis, [(n, n ^ 1) for n in range(lax.axis_size(axis))])]
    ppermute x8, starting transfers between devices: 11.4 us -> 12.9 us  [swap_first(): lax.ppermute(value, axis, [(n, n ^ 1) for n in range(lax.axis_size(axis))])]
    ppermute x6, starting transfers between devices: 4.18 us -> 3.78 us  [swap_second(): return lax.ppermute(value, (axis, other), pairs)]
    ppermute x6, waiting for transfers between devices: 2.21 us -> 1.83 us  [swap_second(): return lax.ppermute(value, (axis, other), pairs)]
  transfers between devices with their start and end apart: 14 -> 14, of which waited for: 3 -> 5; matrix products, arithmetic and copies ran while one was open for 0% -> 0% of each run, Pallas kernels for 35% -> 36%
where the time goes in v18:
time: 36.8 us; the launch traced here: 36.6 us
  starting transfers between devices  16.6 us (45%)
  Pallas kernels  15.4 us (42%)
  waiting for transfers between devices  4.33 us (12%)
    pallas_call x21, Pallas kernels, call(): pl.pallas_call(body, out_shape=tuple(outs), in_specs=[pl.BlockSpec(memory...  15.4 us
    ppermute x8, starting transfers between devices, swap_first(): lax.ppermute(value, axis, [(n, n ^ 1) for n in range(lax.axis_size(axis))])  12.9 us
    ppermute x6, starting transfers between devices, swap_second(): return lax.ppermute(value, (axis, other), pairs)  3.78 us
    ppermute x8, waiting for transfers between devices, swap_first(): lax.ppermute(value, axis, [(n, n ^ 1) for n in range(lax.axis_size(axis))])  2.5 us
    ppermute x6, waiting for transfers between devices, swap_second(): return lax.ppermute(value, (axis, other), pairs)  1.83 us
  transfers between devices with their start and end apart: 14, of which 5 were waited for; matrix products, arithmetic and copies ran while one was open for 0% of the time, Pallas kernels for 36%

profile of v18, /device:TPU:0, one launch (start us, length us, event | category | flops | bytes accessed | tf_op | source)
XLA Modules:
  0.0 36.6 jit_solution(1463910430025743470)
XLA Ops:
  0.0 0.0 copy-start
  0.0 1.2 %shard_map.46 = (bf16[2,8,8,9]{3,2,1,0:T(8,128)(2,1)S(1)}, bf16[2,8,8,9]{3,2,1,0:T(8,128)(2,1)S(1)}, f32[2,8]{1,0:T(2,128)S(1)}, bf16[2,256,768]{2,1,0:T(8,128)(...) custom-call(bf16[8,2,4,64,128]{4,3,2,1,0:T(8,128)(2,1)} %x_ref.19, ...), custom_call_target="tpu_custom_call" | custom-call | flops 1000000 | bytes 10000 | tf_op jit(solution)/shard_map/pallas_call | solution.py:29
  1.2 0.5 %collective-permute-start = (bf16[8,2,64,128]{3,2,1,0:T(8,128)(2,1)S(1)}, bf16[8,2,64,128]{3,2,1,0:T(8,128)(2,1)S(1)}, u32[]{:S(2)}, u32[]{:S(2)}) collective-permute-start(bf16[8,2,64,128]{3,2,1,0:T(8,128)(2,1)S(1)} %get-tuple-element.41), channel_id=1, source_target_pairs={{0,2},{2,0},{4,6},{6,4},{1,3},{3,1},{5,7},{7,5},{8,10},{10,8},{12,... | collective-permute-start | bytes 786440 | tf_op jit(solution)/shard_map/ppermute | solution.py:395
  1.7 2.6 %collective-permute-start.1 = (bf16[8,2,64,128]{3,2,1,0:T(8,128)(2,1)S(1)}, bf16[8,2,64,128]{3,2,1,0:T(8,128)(2,1)S(1)}, u32[]{:S(2)}, u32[]{:S(2)}) collective-permute-start(bf16[8,2,64,128]{3,2,1,0:T(8,128)(2,1)S(1)} %get-tuple-element.42), channel_id=1, source_target_pairs={{0,1},{1,0},{2,4},{3,5},{4,2},{5,3},{6,7},{7,6},{8,9},{9,8},{10,12... | collective-permute-start | bytes 786440 | tf_op jit(solution)/shard_map/ppermute | solution.py:408
  4.3 0.0 copy-done
  4.3 0.4 shard_map.47.refs_1_
  4.7 1.6 %collective-permute-start.5 = (bf16[8,2,64,128]{3,2,1,0:T(8,128)(2,1)S(1)}, bf16[8,2,64,128]{3,2,1,0:T(8,128)(2,1)S(1)}, u32[]{:S(2)}, u32[]{:S(2)}) collective-permute-start(bf16[8,2,64,128]{3,2,1,0:T(8,128)(2,1)S(1)} %shard_map.47.refs_1_), channel_id=1, source_target_pairs={{0,8},{8,0},{16,24},{24,16},{1,9},{9,1},{17,25},{25,17},{2,10},{10... | collective-permute-start | bytes 786440 | tf_op jit(solution)/shard_map/ppermute | solution.py:395
  6.3 0.4 shard_map.48.refs_1_.after_ref
  6.7 0.1 collective-permute-start.6
  6.8 0.4 %shard_map.49 = (f32[2,256,256]{2,1,0:T(8,128)S(1)}, f32[2,256,256]{2,1,0:T(8,128)S(1)}) custom-call(bf16[8,2,4,64,128]{4,3,2,1,0:T(8,128)(2,1)S(1)} %copy-done, bf16[2,256,768]{2,1,0:T(8,128)(2,1)S(1)} %get-tuple-element.43.refs_0_.beside_ref.refs_1_.refs_2_, bf16[8,2,64,128]{3,2,1,0:T(8,128)(2,1)S(1)} %shard_map.48.refs_1_.after_ref), custom_call_target="tpu_custom_call" | custom-call | flops 1000000 | bytes 10000 | tf_op jit(solution)/shard_map/pallas_call | solution.py:29
  7.2 1.1 %shard_map.50 = (bf16[256,768]{1,0:T(8,128)(2,1)S(1)}, bf16[256,768]{1,0:T(8,128)(2,1)S(1)}, bf16[2,256,384]{2,1,0:T(8,128)(2,1)S(1)}, bf16[2,256,24]{2,1,0:T(8,...) custom-call(bf16[2,8,8,9]{3,2,1,0:T(8,128)(2,1)S(1)} %get-tuple-elem, ...), custom_call_target="tpu_custom_call" | custom-call | flops 1000000 | bytes 10000 | tf_op jit(solution)/shard_map/pallas_call | solution.py:29
  8.4 0.0 collective-permute-done.cola_ref
  8.4 0.3 collective-permute-done.1.colb_ref
  8.7 0.4 %shard_map.51 = (bf16[8,2,64,128]{3,2,1,0:T(8,128)(2,1)S(1)}, bf16[8,2,64,128]{3,2,1,0:T(8,128)(2,1)S(1)}, bf16[2,8,2,64,128]{4,3,2,1,0:T(8,128)(2,1)S(1)}) custom-call(bf16[8,2,64,128]{3,2,1,0:T(8,128)(2,1)S(1)} %collective-permute-done.cola_ref, bf16[8,2,64,128]{3,2,1,0:T(8,128)(2,1)S(1)} %collective-permute-done.1.colb_ref, ...), custom_call_target="tpu_custom_call" | custom-call | flops 1000000 | bytes 10000 | tf_op jit(solution)/shard_map/pallas_call | solution.py:29
  9.0 2.9 %collective-permute-start.4 = (bf16[8,2,64,128]{3,2,1,0:T(8,128)(2,1)S(1)}, bf16[8,2,64,128]{3,2,1,0:T(8,128)(2,1)S(1)}, u32[]{:S(2)}, u32[]{:S(2)}) collective-permute-start(bf16[8,2,64,128]{3,2,1,0:T(8,128)(2,1)S(1)} %get-tuple-element.58), channel_id=1, source_target_pairs={{0,8},{8,0},{16,24},{24,16},{1,9},{9,1},{17,25},{25,17},{2,10},{10... | collective-permute-start | bytes 786440 | tf_op jit(solution)/shard_map/ppermute | solution.py:395
  12.0 0.0 collective-permute-start.3
  12.0 0.2 shard_map.53
  12.1 0.8 %collective-permute-start.2 = (bf16[2,8,512]{2,1,0:T(8,128)(2,1)S(1)}, bf16[2,8,512]{2,1,0:T(8,128)(2,1)S(1)}, u32[]{:S(2)}, u32[]{:S(2)}) collective-permute-start(bf16[2,8,512]{2,1,0:T(8,128)(2,1)S(1)} %shard_map.53), channel_id=1, source_target_pairs={{0,1},{1,0},{2,3},{3,2},{4,5},{5,4},{6,7},{7,6},{8,9},{9,8},{10,11... | collective-permute-start | bytes 49160 | tf_op jit(solution)/shard_map/ppermute | solution.py:395
  12.9 2.5 %shard_map.52 = (f32[8,2,2,64,128]{4,3,2,1,0:T(8,128)S(1)}, f32[8,2,2,64,128]{4,3,2,1,0:T(8,128)S(1)}) custom-call(bf16[8,2,4,64,128]{4,3,2,1,0:T(8,128)(2,1)S(1)} %copy-done, bf16[256,768]{1,0:T(8,128)(2,1)S(1)} %get-tuple-element.48.after_ref.refs_0_.refs_1_, bf16[2,256,768]{2,1,0:T(8,128)(2,1)S(1)} %get-tuple-element.43.refs_0_.beside_ref.refs_1_.refs_2_, ...), custom_call_target="tpu_custom_call" | custom-call | flops 1000000 | bytes 10000 | tf_op jit(solution)/shard_map/pallas_call | solution.py:29
  15.4 0.5 %collective-permute-done.2.refs_6_ = bf16[2,8,512]{2,1,0:T(8,128)(2,1)S(1)} collective-permute-done((bf16[2,8,512]{2,1,0:T(8,128)(2,1)S(1)}, bf16[2,8,512]{2,1,0:T(8,128)(2,1)S(1)}, u32[]{:S(2)}, u32[]{:S(2)}) %collective-permute-start.2) | collective-permute-done | bytes 16416 | tf_op jit(solution)/shard_map/ppermute | solution.py:395
  15.9 1.1 %shard_map.54 = (f32[8,2,2,64,128]{4,3,2,1,0:T(8,128)S(1)}, f32[8,2,2,64,128]{4,3,2,1,0:T(8,128)S(1)}) custom-call(bf16[8,2,4,64,128]{4,3,2,1,0:T(8,128)(2,1)S(1)} %copy-done, bf16[2,8,2,64,128]{4,3,2,1,0:T(8,128)(2,1)S(1)} %get-tuple-element.49.refs_0_, ...), custom_call_target="tpu_custom_call", output_to_operand_aliasing={{0}: (5, {}), {1}: (6, {})} | custom-call | flops 1000000 | bytes 10000 | tf_op jit(solution)/shard_map/pallas_call | solution.py:29
  17.0 0.0 collective-permute-done.6.refs_2_
  17.0 0.0 collective-permute-done.5.refs_1_
  17.1 0.2 shard_map.55.refs_2_.mid_ref.x_ref
  17.3 1.4 %collective-permute-done.4.refs_1_ = bf16[8,2,64,128]{3,2,1,0:T(8,128)(2,1)S(1)} collective-permute-done((bf16[8,2,64,128]{3,2,1,0:T(8,128)(2,1)S(1)}, bf16[8,2,64,128]{3,2,1,0:T(8,128)(2,1)S(1)}, u32[]{:S(2)}, u32[]{:S(2)}) %collective-permute-start.4) | collective-permute-done | bytes 262176 | tf_op jit(solution)/shard_map/ppermute | solution.py:395
  18.7 0.1 shard_map.56.rim_ref.refs_2_
  18.8 0.4 %shard_map.57.refs_3_.out_refs_0_ = bf16[8,2,64,128]{3,2,1,0:T(8,128)(2,1)S(1)} custom-call(bf16[8,2,2,64,128]{4,3,2,1,0:T(8,128)(2,1)S(1)} %shard_map.55.refs_2_.mid_ref.x_ref, bf16[8,2,2,64,128]{4,3,2,1,0:T(8,128)(2,1)S(1)} %shard_map.56.rim_ref.refs_2_, bf16[2,256,768]{2,1,0:T(8,128)(2,1)S(1)} %get-tuple-element.60.beside_ref), custom_call_target="tpu_custom_call" | custom-call | flops 1000000 | bytes 10000 | tf_op jit(solution)/shard_map/pallas_call | solution.py:29
  19.2 0.0 collective-permute-done.3.refs_1_
  19.2 0.2 shard_map.58
  19.4 0.1 collective-permute-start.7
  19.5 1.0 %collective-permute-start.8 = (bf16[8,2,64,128]{3,2,1,0:T(8,128)(2,1)S(1)}, bf16[8,2,64,128]{3,2,1,0:T(8,128)(2,1)S(1)}, u32[]{:S(2)}, u32[]{:S(2)}) collective-permute-start(bf16[8,2,64,128]{3,2,1,0:T(8,128)(2,1)S(1)} %get-tuple-element.63), channel_id=1, source_target_pairs={{0,1},{1,0},{2,4},{3,5},{4,2},{5,3},{6,7},{7,6},{8,9},{9,8},{10,12... | collective-permute-start | bytes 786440 | tf_op jit(solution)/shard_map/ppermute | solution.py:408
  20.5 3.0 %collective-permute-start.12 = (bf16[8,2,64,128]{3,2,1,0:T(8,128)(2,1)S(1)}, bf16[8,2,64,128]{3,2,1,0:T(8,128)(2,1)S(1)}, u32[]{:S(2)}, u32[]{:S(2)}) collective-permute-start(bf16[8,2,64,128]{3,2,1,0:T(8,128)(2,1)S(1)} %shard_map.57.refs_3_.out_refs_0_), channel_id=1, source_target_pairs={{0,8},{8,0},{16,24},{24,16},{1,9},{9,1},{17,25},{25,17},{2,10},{10... | collective-permute-start | bytes 786440 | tf_op jit(solution)/shard_map/ppermute | solution.py:395
  23.5 0.4 shard_map.59.after_ref
  23.8 0.1 collective-permute-start.13
  23.9 0.4 %shard_map.60 = (f32[2,256,256]{2,1,0:T(8,128)S(1)}, f32[2,256,256]{2,1,0:T(8,128)S(1)}) custom-call(bf16[8,2,2,64,128]{4,3,2,1,0:T(8,128)(2,1)S(1)} %shard_map.55.refs_2_.mid_ref.x_ref, bf16[8,2,2,64,128]{4,3,2,1,0:T(8,128)(2,1)S(1)} %get-tuple-element.61.rim_ref.x_ref, bf16[2,256,768]{2,1,0:T(8,128)(2,1)S(1)} %get-tuple-element.60.beside_ref, ...), custom_call_target="tpu_custom_call" | custom-call | flops 1000000 | bytes 10000 | tf_op jit(solution)/shard_map/pallas_call | solution.py:29
  24.4 0.0 collective-permute-done.7.cola_ref
  24.4 1.5 %collective-permute-done.8.colb_ref = bf16[8,2,64,128]{3,2,1,0:T(8,128)(2,1)S(1)} collective-permute-done((bf16[8,2,64,128]{3,2,1,0:T(8,128)(2,1)S(1)}, bf16[8,2,64,128]{3,2,1,0:T(8,128)(2,1)S(1)}, u32[]{:S(2)}, u32[]{:S(2)}) %collective-permute-start.8) | collective-permute-done | bytes 262176 | tf_op jit(solution)/shard_map/ppermute | solution.py:408
  25.9 0.4 %shard_map.61 = (bf16[8,2,64,128]{3,2,1,0:T(8,128)(2,1)S(1)}, bf16[8,2,64,128]{3,2,1,0:T(8,128)(2,1)S(1)}, bf16[2,8,2,64,128]{4,3,2,1,0:T(8,128)(2,1)S(1)}) custom-call(bf16[8,2,64,128]{3,2,1,0:T(8,128)(2,1)S(1)} %collective-permute-done.7.cola_ref, bf16[8,2,64,128]{3,2,1,0:T(8,128)(2,1)S(1)} %collective-permute-done.8.colb_ref, ...), custom_call_target="tpu_custom_call" | custom-call | flops 1000000 | bytes 10000 | tf_op jit(solution)/shard_map/pallas_call | solution.py:29
  26.3 2.7 %collective-permute-start.10 = (bf16[8,2,64,128]{3,2,1,0:T(8,128)(2,1)S(1)}, bf16[8,2,64,128]{3,2,1,0:T(8,128)(2,1)S(1)}, u32[]{:S(2)}, u32[]{:S(2)}) collective-permute-start(bf16[8,2,64,128]{3,2,1,0:T(8,128)(2,1)S(1)} %get-tuple-element.75), channel_id=1, source_target_pairs={{0,8},{8,0},{16,24},{24,16},{1,9},{9,1},{17,25},{25,17},{2,10},{10... | collective-permute-start | bytes 786440 | tf_op jit(solution)/shard_map/ppermute | solution.py:395
  29.0 0.0 collective-permute-start.11
  29.0 0.2 shard_map.63
  29.2 1.3 %collective-permute-start.9 = (bf16[2,8,512]{2,1,0:T(8,128)(2,1)S(1)}, bf16[2,8,512]{2,1,0:T(8,128)(2,1)S(1)}, u32[]{:S(2)}, u32[]{:S(2)}) collective-permute-start(bf16[2,8,512]{2,1,0:T(8,128)(2,1)S(1)} %shard_map.63), channel_id=1, source_target_pairs={{0,1},{1,0},{2,3},{3,2},{4,5},{5,4},{6,7},{7,6},{8,9},{9,8},{10,11... | collective-permute-start | bytes 49160 | tf_op jit(solution)/shard_map/ppermute | solution.py:395
  30.5 2.5 %shard_map.62 = (f32[8,2,2,64,128]{4,3,2,1,0:T(8,128)S(1)}, f32[8,2,2,64,128]{4,3,2,1,0:T(8,128)S(1)}) custom-call(bf16[8,2,2,64,128]{4,3,2,1,0:T(8,128)(2,1)S(1)} %shard_map.55.refs_2_.mid_ref.x_ref, bf16[8,2,2,64,128]{4,3,2,1,0:T(8,128)(2,1)S(1)} %get-tuple-element.61.rim_ref.x_ref, bf16[256,768]{1,0:T(8,128)(2,1)S(1)} %get-tuple-element.66.after_ref.middle_ref, ...), custom_call_target="tpu_custom_call" | custom-call | flops 1000000 | bytes 10000 | tf_op jit(solution)/shard_map/pallas_call | solution.py:29
  33.0 0.0 collective-permute-done.9.rest_0_
  33.0 1.1 %shard_map.64 = (f32[8,2,2,64,128]{4,3,2,1,0:T(8,128)S(1)}, f32[8,2,2,64,128]{4,3,2,1,0:T(8,128)S(1)}) custom-call(bf16[8,2,2,64,128]{4,3,2,1,0:T(8,128)(2,1)S(1)} %shard_map.55.refs_2_.mid_ref.x_ref, bf16[8,2,2,64,128]{4,3,2,1,0:T(8,128)(2,1)S(1)} %get-tuple-element.61.rim_ref.x_ref, ...), custom_call_target="tpu_custom_call", output_to_operand_aliasing={{0}: (6, {}), {1}: (7, {})} | custom-call | flops 1000000 | bytes 10000 | tf_op jit(solution)/shard_map/pallas_call | solution.py:29
  34.1 0.0 collective-permute-done.13.b_ref
  34.1 0.0 collective-permute-done.12.a_ref
  34.1 0.9 %shard_map.65.refs_0_ = bf16[8,2,4,64,128]{4,3,2,1,0:T(8,128)(2,1)} custom-call(bf16[8,2,2,64,128]{4,3,2,1,0:T(8,128)(2,1)S(1)} %shard_map.55.refs_2_.mid_ref.x_ref, f32[8,2,2,64,128]{4,3,2,1,0:T(8,128)S(1)} %get-tuple-element.76.acc_ref, bf16[8,2,64,128]{3,2,1,0:T(8,128)(2,1)S(1)} %collective-permute-done.12.a_ref, ...), custom_call_target="tpu_custom_call" | custom-call | flops 1000000 | bytes 10000 | tf_op jit(solution)/shard_map/pallas_call | solution.py:29
  35.1 0.6 %collective-permute-done.10.a_ref = bf16[8,2,64,128]{3,2,1,0:T(8,128)(2,1)S(1)} collective-permute-done((bf16[8,2,64,128]{3,2,1,0:T(8,128)(2,1)S(1)}, bf16[8,2,64,128]{3,2,1,0:T(8,128)(2,1)S(1)}, u32[]{:S(2)}, u32[]{:S(2)}) %collective-permute-start.10) | collective-permute-done | bytes 262176 | tf_op jit(solution)/shard_map/ppermute | solution.py:395
  35.7 0.0 collective-permute-done.11.b_ref
  35.7 0.9 %shard_map.66 = bf16[8,2,4,64,128]{4,3,2,1,0:T(8,128)(2,1)} custom-call(bf16[8,2,2,64,128]{4,3,2,1,0:T(8,128)(2,1)S(1)} %get-tuple-element.61.rim_ref.x_ref, f32[8,2,2,64,128]{4,3,2,1,0:T(8,128)S(1)} %get-tuple-element.74.acc_ref, bf16[8,2,64,128]{3,2,1,0:T(8,128)(2,1)S(1)} %collective-permute-done.10.a_ref, ...), custom_call_target="tpu_custom_call", output_to_operand_aliasing={{}: (4, {})} | custom-call | flops 1000000 | bytes 10000 | tf_op jit(solution)/shard_map/pallas_call | solution.py:29
Async XLA Ops:
  0.0 4.3 %copy-start = (bf16[8,2,4,64,128]{4,3,2,1,0:T(8,128)(2,1)S(1)}, bf16[8,2,4,64,128]{4,3,2,1,0:T(8,128)(2,1)}, u32[]{:S(2)}) copy-start(bf16[8,2,4,64,128]{4,3,2,1,0:T(8,128)(2,1)} %x_ref.19) | copy-start | bytes 3145732
  1.2 7.2 %collective-permute-start = (bf16[8,2,64,128]{3,2,1,0:T(8,128)(2,1)S(1)}, bf16[8,2,64,128]{3,2,1,0:T(8,128)(2,1)S(1)}, u32[]{:S(2)}, u32[]{:S(2)}) collective-permute-start(bf16[8,2,64,128]{3,2,1,0:T(8,128)(2,1)S(1)} %get-tuple-element.41), channel_id=1, source_target_pairs={{0,2},{2,0},{4,6},{6,4},{1,3},{3,1},{5,7},{7,5},{8,10},{10,8},{12,... | collective-permute-start | bytes 786440 | tf_op jit(solution)/shard_map/ppermute | solution.py:395
  1.7 6.9 %collective-permute-start.1 = (bf16[8,2,64,128]{3,2,1,0:T(8,128)(2,1)S(1)}, bf16[8,2,64,128]{3,2,1,0:T(8,128)(2,1)S(1)}, u32[]{:S(2)}, u32[]{:S(2)}) collective-permute-start(bf16[8,2,64,128]{3,2,1,0:T(8,128)(2,1)S(1)} %get-tuple-element.42), channel_id=1, source_target_pairs={{0,1},{1,0},{2,4},{3,5},{4,2},{5,3},{6,7},{7,6},{8,9},{9,8},{10,12... | collective-permute-start | bytes 786440 | tf_op jit(solution)/shard_map/ppermute | solution.py:408
  4.7 12.4 %collective-permute-start.5 = (bf16[8,2,64,128]{3,2,1,0:T(8,128)(2,1)S(1)}, bf16[8,2,64,128]{3,2,1,0:T(8,128)(2,1)S(1)}, u32[]{:S(2)}, u32[]{:S(2)}) collective-permute-start(bf16[8,2,64,128]{3,2,1,0:T(8,128)(2,1)S(1)} %shard_map.47.refs_1_), channel_id=1, source_target_pairs={{0,8},{8,0},{16,24},{24,16},{1,9},{9,1},{17,25},{25,17},{2,10},{10... | collective-permute-start | bytes 786440 | tf_op jit(solution)/shard_map/ppermute | solution.py:395
  6.7 10.3 %collective-permute-start.6 = (bf16[8,2,64,128]{3,2,1,0:T(8,128)(2,1)S(1)}, bf16[8,2,64,128]{3,2,1,0:T(8,128)(2,1)S(1)}, u32[]{:S(2)}, u32[]{:S(2)}) collective-permute-start(bf16[8,2,64,128]{3,2,1,0:T(8,128)(2,1)S(1)} %shard_map.48.refs_1_.after_ref), channel_id=1, source_target_pairs={{0,2},{2,0},{4,6},{6,4},{8,16},{10,18},{12,20},{14,22},{16,8},{18,... | collective-permute-start | bytes 786440 | tf_op jit(solution)/shard_map/ppermute | solution.py:408
  9.0 9.6 %collective-permute-start.4 = (bf16[8,2,64,128]{3,2,1,0:T(8,128)(2,1)S(1)}, bf16[8,2,64,128]{3,2,1,0:T(8,128)(2,1)S(1)}, u32[]{:S(2)}, u32[]{:S(2)}) collective-permute-start(bf16[8,2,64,128]{3,2,1,0:T(8,128)(2,1)S(1)} %get-tuple-element.58), channel_id=1, source_target_pairs={{0,8},{8,0},{16,24},{24,16},{1,9},{9,1},{17,25},{25,17},{2,10},{10... | collective-permute-start | bytes 786440 | tf_op jit(solution)/shard_map/ppermute | solution.py:395
  12.0 7.2 %collective-permute-start.3 = (bf16[8,2,64,128]{3,2,1,0:T(8,128)(2,1)S(1)}, bf16[8,2,64,128]{3,2,1,0:T(8,128)(2,1)S(1)}, u32[]{:S(2)}, u32[]{:S(2)}) collective-permute-start(bf16[8,2,64,128]{3,2,1,0:T(8,128)(2,1)S(1)} %get-tuple-element.54.refs_5_.refs_0_), channel_id=1, source_target_pairs={{0,2},{2,0},{4,6},{6,4},{8,16},{10,18},{12,20},{14,22},{16,8},{18,... | collective-permute-start | bytes 786440 | tf_op jit(solution)/shard_map/ppermute | solution.py:408
  12.1 3.7 %collective-permute-start.2 = (bf16[2,8,512]{2,1,0:T(8,128)(2,1)S(1)}, bf16[2,8,512]{2,1,0:T(8,128)(2,1)S(1)}, u32[]{:S(2)}, u32[]{:S(2)}) collective-permute-start(bf16[2,8,512]{2,1,0:T(8,128)(2,1)S(1)} %shard_map.53), channel_id=1, source_target_pairs={{0,1},{1,0},{2,3},{3,2},{4,5},{5,4},{6,7},{7,6},{8,9},{9,8},{10,11... | collective-permute-start | bytes 49160 | tf_op jit(solution)/shard_map/ppermute | solution.py:395
  19.4 5.0 %collective-permute-start.7 = (bf16[8,2,64,128]{3,2,1,0:T(8,128)(2,1)S(1)}, bf16[8,2,64,128]{3,2,1,0:T(8,128)(2,1)S(1)}, u32[]{:S(2)}, u32[]{:S(2)}) collective-permute-start(bf16[8,2,64,128]{3,2,1,0:T(8,128)(2,1)S(1)} %get-tuple-element.62), channel_id=1, source_target_pairs={{0,2},{2,0},{4,6},{6,4},{1,3},{3,1},{5,7},{7,5},{8,10},{10,8},{12,... | collective-permute-start | bytes 786440 | tf_op jit(solution)/shard_map/ppermute | solution.py:395
  19.5 6.4 %collective-permute-start.8 = (bf16[8,2,64,128]{3,2,1,0:T(8,128)(2,1)S(1)}, bf16[8,2,64,128]{3,2,1,0:T(8,128)(2,1)S(1)}, u32[]{:S(2)}, u32[]{:S(2)}) collective-permute-start(bf16[8,2,64,128]{3,2,1,0:T(8,128)(2,1)S(1)} %get-tuple-element.63), channel_id=1, source_target_pairs={{0,1},{1,0},{2,4},{3,5},{4,2},{5,3},{6,7},{7,6},{8,9},{9,8},{10,12... | collective-permute-start | bytes 786440 | tf_op jit(solution)/shard_map/ppermute | solution.py:408
  20.5 13.6 %collective-permute-start.12 = (bf16[8,2,64,128]{3,2,1,0:T(8,128)(2,1)S(1)}, bf16[8,2,64,128]{3,2,1,0:T(8,128)(2,1)S(1)}, u32[]{:S(2)}, u32[]{:S(2)}) collective-permute-start(bf16[8,2,64,128]{3,2,1,0:T(8,128)(2,1)S(1)} %shard_map.57.refs_3_.out_refs_0_), channel_id=1, source_target_pairs={{0,8},{8,0},{16,24},{24,16},{1,9},{9,1},{17,25},{25,17},{2,10},{10... | collective-permute-start | bytes 786440 | tf_op jit(solution)/shard_map/ppermute | solution.py:395
  23.8 10.3 %collective-permute-start.13 = (bf16[8,2,64,128]{3,2,1,0:T(8,128)(2,1)S(1)}, bf16[8,2,64,128]{3,2,1,0:T(8,128)(2,1)S(1)}, u32[]{:S(2)}, u32[]{:S(2)}) collective-permute-start(bf16[8,2,64,128]{3,2,1,0:T(8,128)(2,1)S(1)} %shard_map.59.after_ref), channel_id=1, source_target_pairs={{0,2},{2,0},{4,6},{6,4},{8,16},{10,18},{12,20},{14,22},{16,8},{18,... | collective-permute-start | bytes 786440 | tf_op jit(solution)/shard_map/ppermute | solution.py:408
  26.3 9.4 %collective-permute-start.10 = (bf16[8,2,64,128]{3,2,1,0:T(8,128)(2,1)S(1)}, bf16[8,2,64,128]{3,2,1,0:T(8,128)(2,1)S(1)}, u32[]{:S(2)}, u32[]{:S(2)}) collective-permute-start(bf16[8,2,64,128]{3,2,1,0:T(8,128)(2,1)S(1)} %get-tuple-element.75), channel_id=1, source_target_pairs={{0,8},{8,0},{16,24},{24,16},{1,9},{9,1},{17,25},{25,17},{2,10},{10... | collective-permute-start | bytes 786440 | tf_op jit(solution)/shard_map/ppermute | solution.py:395
  29.0 6.7 %collective-permute-start.11 = (bf16[8,2,64,128]{3,2,1,0:T(8,128)(2,1)S(1)}, bf16[8,2,64,128]{3,2,1,0:T(8,128)(2,1)S(1)}, u32[]{:S(2)}, u32[]{:S(2)}) collective-permute-start(bf16[8,2,64,128]{3,2,1,0:T(8,128)(2,1)S(1)} %get-tuple-element.71.after_ref), channel_id=1, source_target_pairs={{0,2},{2,0},{4,6},{6,4},{8,16},{10,18},{12,20},{14,22},{16,8},{18,... | collective-permute-start | bytes 786440 | tf_op jit(solution)/shard_map/ppermute | solution.py:408
  29.2 3.8 %collective-permute-start.9 = (bf16[2,8,512]{2,1,0:T(8,128)(2,1)S(1)}, bf16[2,8,512]{2,1,0:T(8,128)(2,1)S(1)}, u32[]{:S(2)}, u32[]{:S(2)}) collective-permute-start(bf16[2,8,512]{2,1,0:T(8,128)(2,1)S(1)} %shard_map.63), channel_id=1, source_target_pairs={{0,1},{1,0},{2,3},{3,2},{4,5},{5,4},{6,7},{7,6},{8,9},{9,8},{10,11... | collective-permute-start | bytes 49160 | tf_op jit(solution)/shard_map/ppermute | solution.py:395
